TPU v7x, 128 devices: a whole 4x4x4 slice. The times are simulated.
128 devices in a mesh: gx: 8 (over x, core), gy: 16 (over y, z).
Axes of the slice: x: 4, y: 4, z: 4, core: 2. Of those that a mesh axis runs over, the one named last changes fastest.
Arguments:
- source_term: float32 [384, 32768], P(('gx', 'gy')), may hold values from -4 to 4
- inverse_density: float32 [384, 32768], P(('gx', 'gy')), may hold values from 1 to 8
- box_counts: int32 [128], P(('gx', 'gy')), may hold values from 1 to 3, as said below
- ghost_from: int32 [384, 4], P(('gx', 'gy')), may hold values from -1 to 383, as said below
Outputs:
- correction: float32 [384, 32768], P(('gx', 'gy'))
- residual: float32 [384, 32768], P(('gx', 'gy'))
- residual_norm: float32 [], replicated
Inputs may be any that keep to these rules, and one draw needn't show every extreme that they name: `box_counts`: every device owns at least one box and at least one device owns 3. `ghost_from`: entries name global slots (device times 3 plus local slot) of used slots; unused slots and faces on the domain's walls hold -1. Neighbours are mutual across the opposite face. The owner of a neighbour lies within 3 devices of the slot's owner in the order of gx+gy: across face 0 at or before it, across face 1 at or after it, across faces 2 and 3 at most one device away.
All inputs are finite; a program needn't handle non-finite values.
Results may differ from a plain program's by a relative error of at most 0.0003.
Values sent between devices are 32-bit elements; how exact they have to be, the bound alone decides.
No kernel may reach another device: no remote copies, remote signals or barrier semaphores. Data moves between devices by JAX's collectives and lax.ppermute only.
A program may use at most 192 MiB of HBM per device.

v0:
```python
import jax
import jax.numpy as jnp
from jax import lax
from jax.sharding import PartitionSpec as P

EDGE = 32
SWEEPS = 2
BOTTOM_ITERS = 8


RELAXATION = 2.0 / 3.0
OPPOSITE = (1, 0, 3, 2)


def passed_along(block, axis, distance):
    devices = range(lax.axis_size(axis))
    route = [(i - distance, i) for i in devices if i - distance in devices]
    return lax.ppermute(block, axis, route)


def face_table(level_field, box_edge):
    slot_total = level_field.shape[0]
    cube_view = level_field.reshape(slot_total, box_edge, box_edge, box_edge)
    side_area = box_edge * box_edge
    return jnp.stack(
        [
            cube_view[:, 0].reshape(slot_total, side_area),
            cube_view[:, box_edge - 1].reshape(slot_total, side_area),
            cube_view[:, :, 0].reshape(slot_total, side_area),
            cube_view[:, :, box_edge - 1].reshape(slot_total, side_area),
        ],
        axis=1,
    )


def neighbours(level_field, ghost_faces, box_edge):
    slot_total = level_field.shape[0]
    cube_view = level_field.reshape(slot_total, box_edge, box_edge, box_edge)
    west_ghost = ghost_faces[:, 0].reshape(slot_total, 1, box_edge, box_edge)
    east_ghost = ghost_faces[:, 1].reshape(slot_total, 1, box_edge, box_edge)
    south_ghost = ghost_faces[:, 2].reshape(slot_total, box_edge, 1, box_edge)
    north_ghost = ghost_faces[:, 3].reshape(slot_total, box_edge, 1, box_edge)
    along_xdir = jnp.concatenate([west_ghost, cube_view, east_ghost], axis=1)
    along_ydir = jnp.concatenate([south_ghost, cube_view, north_ghost], axis=2)
    zero_layer = jnp.zeros_like(cube_view[:, :, :, :1])
    along_zdir = jnp.concatenate([zero_layer, cube_view, zero_layer], axis=3)
    return (
        along_xdir[:, :-2],
        along_xdir[:, 2:],
        along_ydir[:, :, :-2],
        along_ydir[:, :, 2:],
        along_zdir[:, :, :, :-2],
        along_zdir[:, :, :, 2:],
    )


def weights(present_float, box_edge):
    ramp_cells = jnp.arange(box_edge)
    first_cell = ramp_cells == 0
    last_cell = ramp_cells == box_edge - 1
    across_face = present_float[:, :, None, None, None]
    west_weight = jnp.where(first_cell[None, :, None, None], across_face[:, 0], 1.0)
    east_weight = jnp.where(last_cell[None, :, None, None], across_face[:, 1], 1.0)
    south_weight = jnp.where(first_cell[None, None, :, None], across_face[:, 2], 1.0)
    north_weight = jnp.where(last_cell[None, None, :, None], across_face[:, 3], 1.0)
    below_weight = jnp.where(first_cell, 0.0, 1.0).astype(jnp.float32)
    above_weight = jnp.where(last_cell, 0.0, 1.0).astype(jnp.float32)
    return (west_weight, east_weight, south_weight, north_weight, below_weight, above_weight)


def operate(
    level_field, coefficient, ghost_faces, beta_faces, present_float, box_edge, level_scale
):
    slot_total = level_field.shape[0]
    field_cube = level_field.reshape(slot_total, box_edge, box_edge, box_edge)
    beta_cube = coefficient.reshape(slot_total, box_edge, box_edge, box_edge)
    cell_sides = neighbours(level_field, ghost_faces, box_edge)
    beta_sides = neighbours(coefficient, beta_faces, box_edge)
    flux_sum = jnp.zeros_like(field_cube)
    for neighbour, beta_near, weight in zip(
        cell_sides, beta_sides, weights(present_float, box_edge)
    ):
        flux_sum = flux_sum + 0.5 * (beta_cube + beta_near) * weight * (field_cube - neighbour)
    return (level_scale * flux_sum).reshape(level_field.shape)


def diagonal(coefficient, beta_faces, present_float, box_edge, level_scale):
    slot_total = coefficient.shape[0]
    beta_cube = coefficient.reshape(slot_total, box_edge, box_edge, box_edge)
    beta_sides = neighbours(coefficient, beta_faces, box_edge)
    coef_sum = jnp.zeros_like(beta_cube)
    for beta_near, weight in zip(beta_sides, weights(present_float, box_edge)):
        coef_sum = coef_sum + 0.5 * (beta_cube + beta_near) * weight
    return (level_scale * coef_sum).reshape(coefficient.shape)


def restrict(level_field, box_edge):
    half_edge = box_edge // 2
    slot_total = level_field.shape[0]
    blocks = level_field.reshape(slot_total, half_edge, 2, half_edge, 2, half_edge, 2)
    return jnp.mean(blocks, axis=(2, 4, 6)).reshape(slot_total, half_edge**3)


def prolong(level_field, coarse_edge):
    slot_total = level_field.shape[0]
    blocks = level_field.reshape(slot_total, coarse_edge, 1, coarse_edge, 1, coarse_edge, 1)
    blocks = jnp.broadcast_to(blocks, (slot_total, coarse_edge, 2, coarse_edge, 2, coarse_edge, 2))
    return blocks.reshape(slot_total, (2 * coarse_edge) ** 3)


def smooth(level_field, target, apply_level, diag_level, sweep_total):
    for sweep_index in range(sweep_total):
        level_field = level_field + RELAXATION * (target - apply_level(level_field)) / diag_level
    return level_field


def conjugate(shifted, apply_level, reduce_curve, reduce_norm):
    solution = jnp.zeros_like(shifted)
    remainder = shifted
    direction = shifted
    norm_now = reduce_norm(jnp.sum(remainder * remainder))
    for iteration in range(BOTTOM_ITERS):
        image = apply_level(direction)
        step_size = norm_now / reduce_curve(jnp.sum(direction * image))
        solution = solution + step_size * direction
        if iteration + 1 < BOTTOM_ITERS:
            remainder = remainder - step_size * image
            norm_next = reduce_norm(jnp.sum(remainder * remainder))
            direction = remainder + norm_next / norm_now * direction
            norm_now = norm_next
    return solution


def routes(ghost_from, slot_count, device):
    present = ghost_from >= 0
    owner_index = jnp.where(present, ghost_from // slot_count, device)
    offset = owner_index - device
    local_slot = jnp.where(present, ghost_from % slot_count, 0)
    opposite = jnp.array(OPPOSITE, jnp.int32)
    position = ((offset + 3) * slot_count + local_slot) * 4 + opposite[None, :]
    return (jnp.where(present, position, 0), present)


def fetch(face_rows, position, present):
    slot_count, face_count, face_width = face_rows.shape
    lowers = {}
    uppers = {}
    for distance in (1, 2, 3):
        lowers[distance] = passed_along(face_rows, ("gx", "gy"), distance)
        uppers[distance] = passed_along(face_rows, ("gx", "gy"), -distance)
    stacked = jnp.concatenate(
        [lowers[3], lowers[2], lowers[1], face_rows, uppers[1], uppers[2], uppers[3]], axis=0
    )
    flat_rows = stacked.reshape(-1, face_width)
    picked = flat_rows[position]
    return jnp.where(present[:, :, None], picked, jnp.zeros_like(picked))


def shards(source_term, inverse_density, box_counts, ghost_from):
    slot_count = source_term.shape[0]
    device = lax.axis_index(("gx", "gy"))
    valid_mask = (jnp.arange(slot_count, dtype=jnp.int32) < box_counts[0]).astype(jnp.float32)[
        :, None
    ]
    position, present = routes(ghost_from, slot_count, device)
    present_float = present.astype(jnp.float32)
    source = source_term * valid_mask
    fine_edge = EDGE
    middle_edge = EDGE // 2
    bottom_edge = EDGE // 4
    middle_beta = restrict(inverse_density, fine_edge)
    bottom_beta = restrict(middle_beta, middle_edge)

    def local_level(coefficient, box_edge, level_scale):
        beta_faces = fetch(face_table(coefficient, box_edge), position, present)
        diag_level = diagonal(coefficient, beta_faces, present_float, box_edge, level_scale)

        def apply_level(level_field):
            ghost_faces = fetch(face_table(level_field, box_edge), position, present)
            return operate(
                level_field,
                coefficient,
                ghost_faces,
                beta_faces,
                present_float,
                box_edge,
                level_scale,
            )

        return (apply_level, diag_level)

    fine_apply, fine_diag = local_level(inverse_density, fine_edge, 1.0)
    middle_apply, middle_diag = local_level(middle_beta, middle_edge, 0.25)
    fine_field = RELAXATION * source / fine_diag
    fine_field = smooth(fine_field, source, fine_apply, fine_diag, SWEEPS - 1)
    middle_source = restrict(source - fine_apply(fine_field), fine_edge)
    middle_field = RELAXATION * middle_source / middle_diag
    middle_field = smooth(middle_field, middle_source, middle_apply, middle_diag, SWEEPS - 1)
    bottom_source = restrict(middle_source - middle_apply(middle_field), middle_edge)
    bottom_apply, bottom_diag = local_level(bottom_beta, bottom_edge, 0.0625)
    rhs_total, box_total = lax.psum(
        (jnp.sum(bottom_source), box_counts[0].astype(jnp.float32)), ("gx", "gy")
    )
    shifted = (bottom_source - rhs_total / (box_total * bottom_edge**3)) * valid_mask

    def curve_total(value):
        return lax.psum(value, ("gx", "gy"))

    def square_total(value):
        return lax.psum(value, ("gx", "gy"))

    solution = conjugate(shifted, bottom_apply, curve_total, square_total)
    middle_field = middle_field + prolong(solution, bottom_edge)
    middle_field = smooth(middle_field, middle_source, middle_apply, middle_diag, SWEEPS)
    fine_field = fine_field + prolong(middle_field, middle_edge)
    fine_field = smooth(fine_field, source, fine_apply, fine_diag, SWEEPS)
    cell_total = box_total * fine_edge**3
    field_sum = lax.psum(jnp.sum(fine_field), ("gx", "gy"))
    correction = (fine_field - field_sum / cell_total) * valid_mask
    residual = source - fine_apply(correction)
    square_sum = lax.psum(jnp.sum(residual * residual), ("gx", "gy"))
    residual_norm = jnp.sqrt(square_sum / cell_total)
    return (correction, residual, residual_norm)


def solution(mesh):
    in_specs = (
        P(("gx", "gy"), None),
        P(("gx", "gy"), None),
        P(("gx", "gy")),
        P(("gx", "gy"), None),
    )
    out_specs = (P(("gx", "gy"), None), P(("gx", "gy"), None), P())
    return jax.shard_map(shards, mesh=mesh, in_specs=in_specs, out_specs=out_specs, check_vma=False)
```

profile of v0, /device:TPU:1, one launch (start us, length us, event | category | flops | bytes accessed | tf_op | source)
XLA Modules:
  0.0 2406.0 jit_solution(2548926657130442409)
XLA Ops:
  3.0 6.5 collective-permute-start
  15.1 5.9 collective-permute-start.3
  21.0 37.4 %reshape.919 = f32[3,16,2,16,2,16,2]{6,5,4,3,2,1,0:T(8,128)} reshape(f32[3,32768]{1,0:T(4,128)S(1)} %copy-done.7) | data formatting | bytes 786432 | tf_op jit(solution)/shard_map/reshape | solution.py:100
  58.4 9.4 reduce_sum.208
  84.2 6.1 collective-permute-done.37
  93.2 5.6 collective-permute-done.38
  100.7 5.2 collective-permute-done.18
  107.8 6.7 collective-permute-done.19
  116.4 6.4 collective-permute-done.20
  139.1 6.4 collective-permute-start.4
  149.2 4.8 collective-permute-start.39
  184.3 4.7 collective-permute-start.6
  199.4 4.8 collective-permute-start.9
  228.7 8.5 fusion.56
  275.0 4.8 collective-permute-start.15
  305.9 8.7 fusion.43
  319.8 36.9 %reshape.918 = f32[3,16,2,16,2,16,2]{6,5,4,3,2,1,0:T(8,128)} reshape(f32[3,32768]{1,0:T(4,128)} %fusion.274) | data formatting | bytes 786432 | tf_op jit(solution)/shard_map/reshape | solution.py:100
  356.7 10.2 reduce_sum.207
  377.1 6.9 collective-permute-start.24
  385.3 7.1 collective-permute-start.25
  395.0 7.0 collective-permute-start.27
  441.0 6.3 collective-permute-start.31
  449.2 7.0 collective-permute-start.33
  490.2 73.2 %all-reduce.41 = (f32[]{:T(128)}, f32[]{:T(128)}) all-reduce(f32[]{:T(128)} %multiply_reduce_fusion.16, f32[]{:T(128)S(6)} %convert_element_type.12), channel_id=1, replica_groups=mesh['gx'=8,'gy'=16] {'gx','gy'}, use_global_device_ids=true, to_apply=%region_4.5 | all-reduce | flops 2 | bytes 16 | tf_op jit(solution)/shard_map/psum | solution.py:201
  585.3 7.0 collective-permute-start.45
  624.7 63.4 %all-reduce.40 = (f32[]{:T(128)}, f32[]{:T(128)}) all-reduce(f32[]{:T(128)} %get-tuple-element.40, f32[]{:T(128)} %get-tuple-element.39), channel_id=1, replica_groups=mesh['gx'=8,'gy'=16] {'gx','gy'}, use_global_device_ids=true, to_apply=%region_7.8 | all-reduce | flops 2 | bytes 16 | tf_op jit(solution)/shard_map/psum | solution.py:210
  691.1 63.9 %psum.144 = f32[]{:T(128)} all-reduce(f32[]{:T(128)} %multiply_reduce_fusion.13), channel_id=1, replica_groups=mesh['gx'=8,'gy'=16] {'gx','gy'}, use_global_device_ids=true, to_apply=%region_12.13 | all-reduce | flops 1 | bytes 8 | tf_op jit(solution)/shard_map/psum | solution.py:210
  772.2 7.0 collective-permute-start.51
  805.8 62.7 %psum.145 = f32[]{:T(128)} all-reduce(f32[]{:T(128)} %get-tuple-element.157), channel_id=1, replica_groups=mesh['gx'=8,'gy'=16] {'gx','gy'}, use_global_device_ids=true, to_apply=%region_14.15 | all-reduce | flops 1 | bytes 8 | tf_op jit(solution)/shard_map/psum | solution.py:207
  872.1 64.1 %psum.146 = f32[]{:T(128)} all-reduce(f32[]{:T(128)} %get-tuple-element.155), channel_id=1, replica_groups=mesh['gx'=8,'gy'=16] {'gx','gy'}, use_global_device_ids=true, to_apply=%region_16.17 | all-reduce | flops 1 | bytes 8 | tf_op jit(solution)/shard_map/psum | solution.py:210
  953.4 7.0 collective-permute-start.57
  963.5 4.3 collective-permute-start.59
  987.0 62.7 %psum.147 = f32[]{:T(128)} all-reduce(f32[]{:T(128)} %get-tuple-element.153), channel_id=1, replica_groups=mesh['gx'=8,'gy'=16] {'gx','gy'}, use_global_device_ids=true, to_apply=%region_18.19 | all-reduce | flops 1 | bytes 8 | tf_op jit(solution)/shard_map/psum | solution.py:207
  1053.2 64.3 %psum.148 = f32[]{:T(128)} all-reduce(f32[]{:T(128)} %get-tuple-element.151), channel_id=1, replica_groups=mesh['gx'=8,'gy'=16] {'gx','gy'}, use_global_device_ids=true, to_apply=%region_20.21 | all-reduce | flops 1 | bytes 8 | tf_op jit(solution)/shard_map/psum | solution.py:210
  1134.6 7.0 collective-permute-start.63
  1168.5 62.7 %psum.149 = f32[]{:T(128)} all-reduce(f32[]{:T(128)} %get-tuple-element.149), channel_id=1, replica_groups=mesh['gx'=8,'gy'=16] {'gx','gy'}, use_global_device_ids=true, to_apply=%region_22.23 | all-reduce | flops 1 | bytes 8 | tf_op jit(solution)/shard_map/psum | solution.py:207
  1234.7 64.1 %psum.150 = f32[]{:T(128)} all-reduce(f32[]{:T(128)} %get-tuple-element.147), channel_id=1, replica_groups=mesh['gx'=8,'gy'=16] {'gx','gy'}, use_global_device_ids=true, to_apply=%region_24.25 | all-reduce | flops 1 | bytes 8 | tf_op jit(solution)/shard_map/psum | solution.py:210
  1315.9 7.0 collective-permute-start.69
  1326.0 4.3 collective-permute-start.71
  1349.6 62.7 %psum.151 = f32[]{:T(128)} all-reduce(f32[]{:T(128)} %get-tuple-element.145), channel_id=1, replica_groups=mesh['gx'=8,'gy'=16] {'gx','gy'}, use_global_device_ids=true, to_apply=%region_26.27 | all-reduce | flops 1 | bytes 8 | tf_op jit(solution)/shard_map/psum | solution.py:207
  1415.8 64.1 %psum.152 = f32[]{:T(128)} all-reduce(f32[]{:T(128)} %get-tuple-element.143), channel_id=1, replica_groups=mesh['gx'=8,'gy'=16] {'gx','gy'}, use_global_device_ids=true, to_apply=%region_28.29 | all-reduce | flops 1 | bytes 8 | tf_op jit(solution)/shard_map/psum | solution.py:210
  1497.0 7.0 collective-permute-start.75
  1530.9 62.7 %psum.153 = f32[]{:T(128)} all-reduce(f32[]{:T(128)} %get-tuple-element.141), channel_id=1, replica_groups=mesh['gx'=8,'gy'=16] {'gx','gy'}, use_global_device_ids=true, to_apply=%region_30.31 | all-reduce | flops 1 | bytes 8 | tf_op jit(solution)/shard_map/psum | solution.py:207
  1597.1 64.1 %psum.154 = f32[]{:T(128)} all-reduce(f32[]{:T(128)} %get-tuple-element.139), channel_id=1, replica_groups=mesh['gx'=8,'gy'=16] {'gx','gy'}, use_global_device_ids=true, to_apply=%region_32.33 | all-reduce | flops 1 | bytes 8 | tf_op jit(solution)/shard_map/psum | solution.py:210
  1678.6 7.0 collective-permute-start.81
  1712.2 62.7 %psum.155 = f32[]{:T(128)} all-reduce(f32[]{:T(128)} %get-tuple-element.137), channel_id=1, replica_groups=mesh['gx'=8,'gy'=16] {'gx','gy'}, use_global_device_ids=true, to_apply=%region_34.35 | all-reduce | flops 1 | bytes 8 | tf_op jit(solution)/shard_map/psum | solution.py:207
  1777.8 64.1 %psum.156 = f32[]{:T(128)} all-reduce(f32[]{:T(128)} %multiply_reduce_fusion.1), channel_id=1, replica_groups=mesh['gx'=8,'gy'=16] {'gx','gy'}, use_global_device_ids=true, to_apply=%region_36.37 | all-reduce | flops 1 | bytes 8 | tf_op jit(solution)/shard_map/psum | solution.py:210
  1859.1 7.0 collective-permute-start.87
  1892.2 62.7 %psum.157 = f32[]{:T(128)} all-reduce(f32[]{:T(128)} %fusion.265), channel_id=1, replica_groups=mesh['gx'=8,'gy'=16] {'gx','gy'}, use_global_device_ids=true, to_apply=%region_38.39 | all-reduce | flops 1 | bytes 8 | tf_op jit(solution)/shard_map/psum | solution.py:207
  1980.2 6.3 collective-permute-start.93
  2030.1 6.7 collective-permute-start.99
  2040.2 4.8 collective-permute-start.101
  2065.1 9.0 broadcast_in_dim.1043
  2074.1 34.2 %reshape.935 = f32[3,32768]{1,0:T(4,128)} reshape(f32[3,16,2,16,2,16,2]{6,5,4,3,2,1,0:T(8,128)} %broadcast_in_dim.1043) | data formatting | bytes 786432 | tf_op jit(solution)/shard_map/reshape | solution.py:108
  2125.4 6.7 collective-permute-start.105
  2135.5 4.8 collective-permute-start.107
  2150.7 8.2 fusion.30
  2179.9 6.7 collective-permute-start.111
  2190.0 4.8 collective-permute-start.113
  2206.0 8.4 fusion.17
  2220.6 65.8 %psum.158 = f32[]{:T(128)} all-reduce(f32[]{:T(128)} %get-tuple-element.135), channel_id=1, replica_groups=mesh['gx'=8,'gy'=16] {'gx','gy'}, use_global_device_ids=true, to_apply=%region_40.41 | all-reduce | flops 1 | bytes 8 | tf_op jit(solution)/shard_map/psum | solution.py:218
  2304.3 6.1 collective-permute-start.117
  2328.0 8.1 fusion.4
  2340.0 63.7 %psum.159 = f32[]{:T(128)} all-reduce(f32[]{:T(128)} %get-tuple-element.133), channel_id=1, replica_groups=mesh['gx'=8,'gy'=16] {'gx','gy'}, use_global_device_ids=true, to_apply=%region_42.43 | all-reduce | flops 1 | bytes 8 | tf_op jit(solution)/shard_map/psum | solution.py:221
  (828 shorter events, 831.8 us)
Async XLA Ops:
  3.0 143.7 %collective-permute-start = (f32[3,4,1024]{2,1,0:T(4,128)S(1)}, f32[3,4,1024]{2,1,0:T(4,128)S(1)}, u32[]{:S(2)}, u32[]{:S(2)}) collective-permute-start(f32[3,4,1024]{2,1,0:T(4,128)S(1)} %pad_maximum_fusion.80), channel_id=1, source_target_pairs={{0,3},{1,4},{2,5},{3,6},{4,7},{5,8},{6,9},{7,10},{8,11},{9,12},{10... | collective-permute-start | bytes 147464 | tf_op jit(solution)/shard_map/ppermute | solution.py:18
  9.5 139.6 %collective-permute-start.1 = (f32[3,4,1024]{2,1,0:T(4,128)S(1)}, f32[3,4,1024]{2,1,0:T(4,128)S(1)}, u32[]{:S(2)}, u32[]{:S(2)}) collective-permute-start(f32[3,4,1024]{2,1,0:T(4,128)S(1)} %pad_maximum_fusion.80), channel_id=1, source_target_pairs={{0,2},{1,3},{2,4},{3,5},{4,6},{5,7},{6,8},{7,9},{8,10},{9,11},{10,... | collective-permute-start | bytes 147464 | tf_op jit(solution)/shard_map/ppermute | solution.py:18
  12.1 141.8 %collective-permute-start.2 = (f32[3,4,1024]{2,1,0:T(4,128)S(1)}, f32[3,4,1024]{2,1,0:T(4,128)S(1)}, u32[]{:S(2)}, u32[]{:S(2)}) collective-permute-start(f32[3,4,1024]{2,1,0:T(4,128)S(1)} %pad_maximum_fusion.80), channel_id=1, source_target_pairs={{0,1},{1,2},{2,3},{3,4},{4,5},{5,6},{6,7},{7,8},{8,9},{9,10},{10,1... | collective-permute-start | bytes 147464 | tf_op jit(solution)/shard_map/ppermute | solution.py:18
  15.1 140.9 %collective-permute-start.3 = (f32[3,4,1024]{2,1,0:T(4,128)S(1)}, f32[3,4,1024]{2,1,0:T(4,128)S(1)}, u32[]{:S(2)}, u32[]{:S(2)}) collective-permute-start(f32[3,4,1024]{2,1,0:T(4,128)S(1)} %pad_maximum_fusion.80), channel_id=1, source_target_pairs={{1,0},{2,1},{3,2},{4,3},{5,4},{6,5},{7,6},{8,7},{9,8},{10,9},{11,1... | collective-permute-start | bytes 147464 | tf_op jit(solution)/shard_map/ppermute | solution.py:18
  139.1 18.9 collective-permute-start.4
  149.2 290.6 %collective-permute-start.39 = (f32[3,4,64]{2,1,0:T(4,128)}, f32[3,4,64]{2,1,0:T(4,128)}, u32[]{:S(2)}, u32[]{:S(2)}) collective-permute-start(f32[3,4,64]{2,1,0:T(4,128)} %pad_maximum_fusion.91), channel_id=1, source_target_pairs={{1,0},{2,1},{3,2},{4,3},{5,4},{6,5},{7,6},{8,7},{9,8},{10,9},{11,1... | collective-permute-start | bytes 9224 | tf_op jit(solution)/shard_map/ppermute | solution.py:18
  153.9 335.0 %collective-permute-start.40 = (f32[3,4,64]{2,1,0:T(4,128)}, f32[3,4,64]{2,1,0:T(4,128)}, u32[]{:S(2)}, u32[]{:S(2)}) collective-permute-start(f32[3,4,64]{2,1,0:T(4,128)} %pad_maximum_fusion.91), channel_id=1, source_target_pairs={{2,0},{3,1},{4,2},{5,3},{6,4},{7,5},{8,6},{9,7},{10,8},{11,9},{12,... | collective-permute-start | bytes 9224 | tf_op jit(solution)/shard_map/ppermute | solution.py:18
  156.0 419.8 %collective-permute-start.41 = (f32[3,4,64]{2,1,0:T(4,128)}, f32[3,4,64]{2,1,0:T(4,128)}, u32[]{:S(2)}, u32[]{:S(2)}) collective-permute-start(f32[3,4,64]{2,1,0:T(4,128)} %pad_maximum_fusion.91), channel_id=1, source_target_pairs={{3,0},{4,1},{5,2},{6,3},{7,4},{8,5},{9,6},{10,7},{11,8},{12,9},{13... | collective-permute-start | bytes 9224 | tf_op jit(solution)/shard_map/ppermute | solution.py:18
  377.1 15.3 collective-permute-start.24
  435.6 13.6 collective-permute-start.30
  441.0 15.8 collective-permute-start.31
  449.2 13.9 collective-permute-start.33
  572.5 23.0 collective-permute-start.42
  580.4 19.8 collective-permute-start.43
  583.4 17.5 collective-permute-start.44
  585.3 17.5 collective-permute-start.45
  764.7 17.5 collective-permute-start.48
  767.2 20.0 collective-permute-start.49
  770.2 17.5 collective-permute-start.50
  772.2 17.5 collective-permute-start.51
  946.0 17.5 collective-permute-start.54
  948.4 20.0 collective-permute-start.55
  951.4 17.5 collective-permute-start.56
  953.4 17.5 collective-permute-start.57
  1127.2 17.5 collective-permute-start.60
  1129.7 20.0 collective-permute-start.61
  1132.7 17.5 collective-permute-start.62
  1134.6 17.5 collective-permute-start.63
  1308.5 17.5 collective-permute-start.66
  1311.0 20.0 collective-permute-start.67
  1314.0 17.5 collective-permute-start.68
  1315.9 17.5 collective-permute-start.69
  1489.6 17.5 collective-permute-start.72
  1492.0 20.0 collective-permute-start.73
  1495.0 17.5 collective-permute-start.74
  1497.0 17.5 collective-permute-start.75
  1670.9 17.7 collective-permute-start.78
  1673.6 20.0 collective-permute-start.79
  1676.6 17.5 collective-permute-start.80
  1678.6 17.5 collective-permute-start.81
  1851.7 17.5 collective-permute-start.84
  1854.1 20.0 collective-permute-start.85
  1857.2 17.5 collective-permute-start.86
  1859.1 17.5 collective-permute-start.87
  1971.6 19.1 collective-permute-start.90
  1975.6 19.1 collective-permute-start.91
  1977.6 17.7 collective-permute-start.92
  1980.2 17.0 collective-permute-start.93
  2022.0 18.2 collective-permute-start.96
  2025.1 20.6 collective-permute-start.97
  2027.4 18.8 collective-permute-start.98
  2030.1 18.0 collective-permute-start.99
  2117.3 18.2 collective-permute-start.102
  2119.2 21.7 collective-permute-start.103
  2122.1 19.5 collective-permute-start.104
  2125.4 18.2 collective-permute-start.105
  2171.2 18.8 collective-permute-start.108
  2173.7 22.5 collective-permute-start.109
  2176.6 20.3 collective-permute-start.110
  2179.9 19.0 collective-permute-start.111
  2295.8 18.2 collective-permute-start.114
  2299.0 19.3 collective-permute-start.115
  2301.3 17.6 collective-permute-start.116
  2304.3 16.5 collective-permute-start.117
  (99 other events, 2514.1 us)
where the time goes:
time: 2430 us; the launch traced here: 2410 us
  blocking collectives  1150 us (47%)
  local copies, waits for them, and re-layouts  527 us (22%)
  starting transfers between devices  436 us (18%)
  other arithmetic  213 us (9%)
  waiting for transfers between devices  48.2 us (2%)
  between operations  28.1 us (1%)
    psum x8, blocking collectives, square_total(): return lax.psum(value, ('gx', 'gy'))  512 us
    psum x7, blocking collectives, curve_total(): return lax.psum(value, ('gx', 'gy'))  439 us
    ppermute x120, starting transfers between devices, passed_along(): return lax.ppermute(block, axis, route)  436 us
    another operation x80, local copies, waits for them, and re-layouts, face_table(): jnp.stack([cube_view[:, 0].reshape(slot_total, side_area), cube_view[:, b...  80.1 us
    reshape x2, local copies, waits for them, and re-layouts, restrict(): level_field.reshape(slot_total, half_edge, 2, half_edge, 2, half_edge, 2)  74.3 us
    psum x1, blocking collectives, shards(): lax.psum((jnp.sum(bottom_source), box_counts[0].astype(jnp.float32)), ('g...  73.2 us
    psum x1, blocking collectives, shards(): field_sum = lax.psum(jnp.sum(fine_field), ('gx', 'gy'))  65.8 us
    psum x1, blocking collectives, shards(): square_sum = lax.psum(jnp.sum(residual * residual), ('gx', 'gy'))  63.7 us
  transfers between devices with their start and end apart: 120, of which 14 were waited for; matrix products, arithmetic and copies ran while one was open for 15% of the time, Pallas kernels for 0%

commit v1 on v0

v1 whole, which is shorter than its diff:
```python
import functools

import jax
import jax.numpy as jnp
from jax import lax
from jax.experimental import pallas as pl
from jax.experimental.pallas import tpu as pltpu
from jax.sharding import PartitionSpec as P

AX = ("gx", "gy")
DEVICES = 128
SLOTS = 3
BOTTOM_ITERS = 8
RELAXATION = 2.0 / 3.0
F32 = jnp.float32
I32 = jnp.int32

PLANES = (32, 16)


def iota(shape, dim):
    return lax.broadcasted_iota(I32, shape, dim)


def lanes():
    return iota((8, 128), 1)


def subs():
    return iota((8, 128), 0)


def roll(x, shift, axis):
    return pltpu.roll(x, shift, axis)


class Tile:
    def __init__(self, lv):
        self.zs, self.ys = 1 << lv, 32 << lv
        lane, sub = lanes(), subs()
        self.south_in = lane >= self.ys
        self.north_in = lane < 128 - self.ys
        self.first_row = sub == 0
        self.last_row = sub == 7
        self.south_edge = self.first_row & (lane < self.ys)
        self.z_low = (lane & 31) < self.zs

    def south(self, v, row):
        r = roll(v, self.ys, 1)
        return jnp.where(self.south_in, r, jnp.where(self.first_row, row, roll(r, 1, 0)))

    def north(self, v, edge):
        r = roll(v, 128 - self.ys, 1)
        return jnp.where(self.north_in, r, jnp.where(self.last_row, edge, roll(r, 7, 0)))

    def below(self, v):
        return roll(v, self.zs, 1)

    def above(self, v):
        return roll(v, 128 - self.zs, 1)


def pair_sum(t, lv):
    lane = lanes()
    zs, ys = 1 << lv, 32 << lv
    t = t + jnp.where((lane & zs) == 0, roll(t, 128 - zs, 1), roll(t, zs, 1))
    return t + jnp.where((lane & ys) == 0, roll(t, 128 - ys, 1), roll(t, ys, 1))


def pack_faces(v, s, lv, out, t0):
    n = PLANES[lv]
    out[s, t0] = v[s, 0]
    out[s, t0 + 1] = v[s, n - 1]
    y0 = v[s, :, 0, :]
    y7 = v[s, :, 7, :]
    if lv == 0:
        lane = iota((32, 128), 1)
        p = jnp.where(lane >= 96, roll(y0, 96, 1), roll(y7, 32, 1))
        lane = iota((16, 128), 1)
        q = jnp.where((lane < 32) | (lane >= 96), p[:16], roll(p[16:], 64, 1))
    else:
        lane = iota((16, 128), 1)
        q = roll(jnp.where(lane < 64, y0, y7), 64, 1)
    out[s, t0 + 2] = q[:8]
    out[s, t0 + 3] = q[8:]


def pick(tab, own, near, far, s, f, tile):
    src = tab[s * 4 + f]
    at = tab[12 + s * 4 + f]
    return jnp.where(src == 0, own[at, tile], jnp.where(src == 1, near[at, tile], far[at, tile]))


def take_ghosts(tab, win, s, lv, t0, gx, gy):
    own, near, far = win
    gx[s, 0] = pick(tab, own, near, far, s, 0, t0 + 1)
    gx[s, 1] = pick(tab, own, near, far, s, 1, t0)
    low = lanes() < 64
    for t in range(2):
        sv = pick(tab, own, near, far, s, 2, t0 + 2 + t)
        nv = pick(tab, own, near, far, s, 3, t0 + 2 + t)
        gy[s, 8 * t : 8 * t + 8, :] = jnp.where(low, sv, nv)
        if lv == 0:
            gy[s, 16 + 8 * t : 24 + 8 * t, :] = roll(jnp.where(low, nv, sv), 64, 1)


def planes_loop(n, body, carry, unroll=8):
    def chunk(c, carry):
        for u in range(unroll):
            carry = body(c * unroll + u, carry, u == unroll - 1)
        return carry

    return lax.fori_loop(0, n // unroll, chunk, carry)


def following(ref, s, i, n, edge, at_end):
    if not at_end:
        return ref[s, i + 1]
    return jnp.where(i == n - 1, edge, ref[s, jnp.minimum(i + 1, n - 1)])


def make_weights(b, gx, gy, pres, lv, cx, cy, cz, wn, rd, extra):
    n = PLANES[lv]
    h = 0.5 * 0.25**lv
    tl = Tile(lv)
    first = []
    for s in range(SLOTS):
        v = b[s, 0]
        w = h * (v + gx[s, 0]) * pres[s * 4]
        cx[s, 0] = w
        first.append((v, w))

    def body(i, carry, at_end):
        out = []
        for s in range(SLOTS):
            v, w = carry[s]
            nxt = following(b, s, i, n, gx[s, 1], at_end)
            wnext = h * (v + nxt)
            if at_end:
                wnext = wnext * jnp.where(i == n - 1, pres[s * 4 + 1], 1.0)
            row = gy[s, pl.ds(i, 1), :]
            wy = h * (v + tl.south(v, row))
            wy = jnp.where(tl.south_edge, wy * pres[s * 4 + 2], wy)
            wrow = h * (v + row) * pres[s * 4 + 3]
            wz = jnp.where(tl.z_low, 0.0, h * (v + tl.below(v)))
            d = (w + wnext) + (wy + tl.north(wy, wrow)) + (wz + tl.above(wz))
            r = RELAXATION / d
            cx[s, i + 1] = wnext
            cy[s, i] = wy
            cz[s, i] = wz
            wn[s, pl.ds(i, 1), :] = wrow[7:8, :]
            rd[s, i] = r
            extra(s, i, r)
            out.append((nxt, wnext))
        return tuple(out)

    planes_loop(n, body, tuple(first))


def apply_level(v, gx, gy, lv, cx, cy, cz, wn, emit):
    n = PLANES[lv]
    tl = Tile(lv)
    first = []
    for s in range(SLOTS):
        v0 = v[s, 0]
        first.append((v0, cx[s, 0] * (v0 - gx[s, 0])))

    def body(i, carry, at_end):
        out = []
        for s in range(SLOTS):
            here, fx = carry[s]
            nxt = following(v, s, i, n, gx[s, 1], at_end)
            fnext = cx[s, i + 1] * (nxt - here)
            row = gy[s, pl.ds(i, 1), :]
            wrow = wn[s, pl.ds(i, 1), :]
            fy = cy[s, i] * (here - tl.south(here, row))
            fn = tl.north(fy, wrow * (row - here))
            fz = cz[s, i] * (here - tl.below(here))
            emit(s, i, here, (fx - fnext) + (fy - fn) + (fz - tl.above(fz)))
            out.append((nxt, fnext))
        return tuple(out)

    planes_loop(n, body, tuple(first))


def restrict_planes(v, s, lv, scale):
    out = []
    for c in range(PLANES[lv] // 2):
        out.append(pair_sum(v[s, 2 * c] + v[s, 2 * c + 1], lv) * scale)
    return out


def pack_bottom(planes, out):
    lane = lanes()
    at = (lane & 7) * 4
    part = lane >> 3
    top = None
    for s in range(2):
        for i in range(8):
            g = jnp.take_along_axis(planes[s][i], at, axis=1)
            top = g if top is None else jnp.where(part == s * 8 + i, g, top)
    low = None
    for i in range(8):
        g = jnp.take_along_axis(planes[2][i], at, axis=1)
        low = g if low is None else jnp.where((part & 7) == i, g, low)
    low = jnp.where(lane < 64, low, roll(low, 4, 0))
    out[0:8, :] = top
    out[8:12, :] = low[0:4]


def k_start(mask, src, inv, note, s_out, b_out, b1_out, faces, gathered):
    bottom = []
    for s in range(SLOTS):
        s_out[s] = src[:, s, :].reshape(32, 8, 128) * mask[s]
        b_out[s] = inv[:, s, :].reshape(32, 8, 128)
        for c, t in enumerate(restrict_planes(b_out, s, 0, 0.125)):
            b1_out[s, c] = t
        bottom.append(restrict_planes(b1_out, s, 1, 0.125))
        pack_faces(b_out, s, 0, faces, 0)
        pack_faces(b1_out, s, 1, faces, 4)
    pack_bottom(bottom, gathered)
    gathered[12:24, :] = jnp.zeros((12, 128), F32)
    gathered[12:13, :] = note[...]


def k_weights(tab, pres, s_in, b, b1, own, near, far, cx, cy, cz, wn, rd, u, cx1, cy1, cz1, wn1, rd1, faces, gx, gy, gx1, gy1):
    win = (own, near, far)
    for s in range(SLOTS):
        take_ghosts(tab, win, s, 0, 0, gx, gy)
        take_ghosts(tab, win, s, 1, 4, gx1, gy1)

    def first(s, i, r):
        u[s, i] = s_in[s, i] * r

    make_weights(b, gx, gy, pres, 0, cx, cy, cz, wn, rd, first)
    make_weights(b1, gx1, gy1, pres, 1, cx1, cy1, cz1, wn1, rd1, lambda s, i, r: None)
    for s in range(SLOTS):
        pack_faces(u, s, 0, faces, 0)


def k_sweep(lv, tab, t, u, own, near, far, cx, cy, cz, wn, rd, out, faces, gx, gy):
    for s in range(SLOTS):
        take_ghosts(tab, (own, near, far), s, lv, 0, gx, gy)

    def emit(s, i, here, av):
        out[s, i] = here + (t[s, i] - av) * rd[s, i]

    apply_level(u, gx, gy, lv, cx, cy, cz, wn, emit)
    for s in range(SLOTS):
        pack_faces(out, s, lv, faces, 0)


def k_down(tab, t, u, own, near, far, cx, cy, cz, wn, rd1, f1, u1, faces, gx, gy, res):
    for s in range(SLOTS):
        take_ghosts(tab, (own, near, far), s, 0, 0, gx, gy)

    def emit(s, i, here, av):
        res[s, i] = t[s, i] - av

    apply_level(u, gx, gy, 0, cx, cy, cz, wn, emit)
    for s in range(SLOTS):
        for c, p in enumerate(restrict_planes(res, s, 0, 0.125)):
            f1[s, c] = p
            u1[s, c] = p * rd1[s, c]
        pack_faces(u1, s, 1, faces, 0)


def k_bottom_rhs(tab, t, u, own, near, far, cx, cy, cz, wn, packed, gx, gy, res):
    for s in range(SLOTS):
        take_ghosts(tab, (own, near, far), s, 1, 0, gx, gy)

    def emit(s, i, here, av):
        res[s, i] = t[s, i] - av

    apply_level(u, gx, gy, 1, cx, cy, cz, wn, emit)
    pack_bottom([restrict_planes(res, s, 1, 0.125) for s in range(SLOTS)], packed)


def total(v):
    return jnp.sum(v, axis=(0, 1), keepdims=True)


def unpack_bottom(rows, put):
    for r in range(12):
        t = rows[:, r, :].T
        for half in range(2):
            s, j = (half, r) if r < 8 else (2, r - 8 + 4 * half)
            for i in range(8):
                put(s, j, i, t[half * 64 + i * 8 : half * 64 + i * 8 + 8, :])


def face_gather(v, dev_at, slot_at, place, s):
    out = jnp.take_along_axis(place(0), dev_at, axis=1)
    for other in range(1, SLOTS):
        g = jnp.take_along_axis(place(other), dev_at, axis=1)
        out = jnp.where(slot_at == other, g, out)
    return out


def k_bottom(tab, t, u, gx0, gy0, cx1, cy1, cz1, wn1, rd1, beta_rows, rhs_rows, out, faces, boxes_out,
             p, r, x, q, cx, cy, cz, back, sq, v1, gx, gy):
    note = beta_rows[:, 12, :].T
    at, slot, pres = [], [], []
    for f in range(12):
        gf = jnp.broadcast_to(note[f : f + 1, :], (8, 128))
        has = gf >= 0.0
        gf = jnp.where(has, gf, 0.0)
        dv = ((gf + 0.5) * (1.0 / 3.0)).astype(I32)
        at.append(dv)
        slot.append(gf.astype(I32) - 3 * dv)
        pres.append(jnp.where(has, 1.0, 0.0))
    counts = note[12:13, :]
    boxes = jnp.sum(counts, axis=1, keepdims=True)
    boxes_out[...] = jnp.broadcast_to(boxes, (8, 128))

    def fill_ghosts():
        def along(m, _):
            for s in range(SLOTS):
                for f, (src, dst) in enumerate(((7, 0), (0, 9))):
                    k = s * 4 + f
                    p[s, m + 1, dst] = face_gather(p, at[k], slot[k], lambda o: p[o, m + 1, src + 1], s)
                for f, (src, dst) in enumerate(((7, 0), (0, 9))):
                    k = s * 4 + 2 + f
                    p[s, dst, m + 1] = face_gather(p, at[k], slot[k], lambda o: p[o, src + 1, m + 1], s)
            return 0

        lax.fori_loop(0, 8, along, 0)

    def put_beta(s, j, i, tile):
        p[s, j + 1, i + 1] = tile

    unpack_bottom(beta_rows, put_beta)
    fill_ghosts()
    h = 0.5 * 0.0625
    low = subs() == 0

    def weights(m, _):
        for s in range(SLOTS):
            for i in range(9):
                w = h * (p[s, m + 1, i] + p[s, m + 1, i + 1])
                if i == 0:
                    w = w * pres[s * 4]
                if i == 8:
                    w = w * pres[s * 4 + 1]
                cx[s, m, i] = w
                w = h * (p[s, i, m + 1] + p[s, i + 1, m + 1])
                if i == 0:
                    w = w * pres[s * 4 + 2]
                if i == 8:
                    w = w * pres[s * 4 + 3]
                cy[s, i, m] = w
            for i in range(8):
                b = p[s, m + 1, i + 1]
                cz[s, m, i] = jnp.where(low, 0.0, h * (b + roll(b, 1, 0)))
        return 0

    lax.fori_loop(0, 8, weights, 0)

    def put_rhs(s, j, i, tile):
        r[s, j, i] = tile

    unpack_bottom(rhs_rows, put_rhs)

    def each(fn, init):
        def step(j, acc):
            for s in range(SLOTS):
                for i in range(8):
                    acc = fn(s, j, i, acc)
            return acc

        return lax.fori_loop(0, 8, step, init)

    zero = jnp.zeros((8, 128), F32)
    mean = total(each(lambda s, j, i, acc: acc + r[s, j, i], zero)) / (boxes * 512.0)
    valid = [jnp.where(jnp.broadcast_to(counts, (8, 128)) > s + 0.5, 1.0, 0.0) for s in range(SLOTS)]

    def shift(s, j, i, acc):
        v = (r[s, j, i] - mean) * valid[s]
        r[s, j, i] = v
        p[s, j + 1, i + 1] = v
        x[s, j, i] = zero
        return acc + v * v

    rr = total(each(shift, zero))

    def image(s, j, i, acc):
        here = p[s, j + 1, i + 1]
        a = cx[s, j, i] * (here - p[s, j + 1, i]) + cx[s, j, i + 1] * (here - p[s, j + 1, i + 2])
        b = cy[s, j, i] * (here - p[s, j, i + 1]) + cy[s, j + 1, i] * (here - p[s, j + 2, i + 1])
        fz = cz[s, j, i] * (here - roll(here, 1, 0))
        v = a + b + (fz - roll(fz, 7, 0))
        q[s, j, i] = v
        return acc + here * v

    def iteration(it, rr):
        fill_ghosts()
        alpha = rr / total(each(image, zero))

        def step(s, j, i, acc):
            x[s, j, i] = x[s, j, i] + alpha * p[s, j + 1, i + 1]
            v = r[s, j, i] - alpha * q[s, j, i]
            r[s, j, i] = v
            return acc + v * v

        rr_next = total(each(step, zero))
        ratio = rr_next / rr

        def turn(s, j, i, acc):
            p[s, j + 1, i + 1] = r[s, j, i] + ratio * p[s, j + 1, i + 1]
            return acc

        each(turn, 0)
        return rr_next

    rr = lax.fori_loop(0, BOTTOM_ITERS - 1, iteration, rr)
    fill_ghosts()
    alpha = rr / total(each(image, zero))

    def last(s, j, i, acc):
        x[s, j, i] = x[s, j, i] + alpha * p[s, j + 1, i + 1]
        return acc

    each(last, 0)

    for row in range(12):
        for half in range(2):
            s, j = (half, row) if row < 8 else (2, row - 8 + 4 * half)
            for i in range(8):
                sq[half * 64 + i * 8 : half * 64 + i * 8 + 8, :] = x[s, j, i]
        tr = sq[...].T
        if row < 8:
            back[:, row, :] = tr
            back[:, 8 + row, :] = roll(tr, 64, 1)
        else:
            back[:, 8 + row, :] = tr
            back[:, 12 + row, :] = roll(tr, 64, 1)

    lane, sub = lanes(), subs()
    kat = (lane & 31) >> 2

    def box(dev, s):
        return back[dev, pl.ds(pl.multiple_of(8 * s, 8), 8), :]

    for s in range(SLOTS):
        mine = box(tab[48], s)
        for i in range(8):
            g = jnp.take_along_axis(mine, kat + i * 8, axis=1)
            v1[s, 2 * i] = u[s, 2 * i] + g
            v1[s, 2 * i + 1] = u[s, 2 * i + 1] + g
        for f, i in ((0, 7), (1, 0)):
            nb = box(tab[24 + s * 4 + f], tab[36 + s * 4 + f])
            gx[s, f] = gx0[s, f] + jnp.take_along_axis(nb, kat + i * 8, axis=1)
        sb = jnp.broadcast_to(box(tab[24 + s * 4 + 2], tab[36 + s * 4 + 2])[7:8, :], (8, 128))
        nb = jnp.broadcast_to(box(tab[24 + s * 4 + 3], tab[36 + s * 4 + 3])[0:1, :], (8, 128))
        for part in range(2):
            idx = kat + (part * 4 + (sub >> 1)) * 8
            g = jnp.where(lane < 64, jnp.take_along_axis(sb, idx, axis=1), jnp.take_along_axis(nb, idx, axis=1))
            gy[s, 8 * part : 8 * part + 8, :] = gy0[s, 8 * part : 8 * part + 8, :] + g

    def emit(s, i, here, av):
        out[s, i] = here + (t[s, i] - av) * rd1[s, i]

    apply_level(v1, gx, gy, 1, cx1, cy1, cz1, wn1, emit)
    for s in range(SLOTS):
        pack_faces(out, s, 1, faces, 0)


def k_up(tab, t, u0, gx0, gy0, u1, own, near, far, cx, cy, cz, wn, rd, out, faces, v, gx, gy, gx1, gy1):
    for s in range(SLOTS):
        take_ghosts(tab, (own, near, far), s, 1, 0, gx1, gy1)
        for f in range(2):
            gx[s, f] = gx0[s, f] + gx1[s, f]
        for i in range(16):
            c = u1[s, i]
            v[s, 2 * i] = u0[s, 2 * i] + c
            v[s, 2 * i + 1] = u0[s, 2 * i + 1] + c
            gy[s, 2 * i : 2 * i + 2, :] = gy0[s, 2 * i : 2 * i + 2, :] + gy1[s, i : i + 1, :]

    def emit(s, i, here, av):
        out[s, i] = here + (t[s, i] - av) * rd[s, i]

    apply_level(v, gx, gy, 0, cx, cy, cz, wn, emit)
    for s in range(SLOTS):
        pack_faces(out, s, 0, faces, 0)


def k_residual(tab, t, u, own, near, far, cx, cy, cz, wn, res_out, sums, gx, gy, res):
    for s in range(SLOTS):
        take_ghosts(tab, (own, near, far), s, 0, 0, gx, gy)

    def emit(s, i, here, av):
        res[s, i] = t[s, i] - av

    apply_level(u, gx, gy, 0, cx, cy, cz, wn, emit)
    su = jnp.zeros((8, 128), F32)
    sr = jnp.zeros((8, 128), F32)
    for s in range(SLOTS):
        for i in range(32):
            w = res[s, i]
            sr = sr + w * w
            su = su + u[s, i]
        res_out[:, s, :] = res[s].reshape(256, 128)
    lane = iota((1, 128), 1)
    sums[...] = jnp.where(lane == 0, total(su), jnp.where(lane == 1, total(sr), 0.0))


def k_finish(mask, u, sums, boxes, corr, norm):
    tot = jnp.sum(sums[...], axis=0, keepdims=True)
    cells = boxes[0:1, 0:1] * 32768.0
    mean = tot[:, 0:1] / cells
    for s in range(SLOTS):
        corr[:, s, :] = ((u[s] - mean) * mask[s]).reshape(256, 128)
    norm[...] = jnp.broadcast_to(jnp.sqrt(tot[:, 1:2] / cells), (1, 128))


VMEM = pl.BlockSpec(memory_space=pltpu.VMEM)
SMEM = pl.BlockSpec(memory_space=pltpu.SMEM)


def call(kernel, smem, args, outs, scratch=(), vmem=24):
    shape = lambda s: jax.ShapeDtypeStruct(s, F32)
    return pl.pallas_call(
        kernel,
        out_shape=[shape(s) for s in outs],
        in_specs=[SMEM] * smem + [VMEM] * (len(args) - smem),
        out_specs=[VMEM] * len(outs),
        scratch_shapes=[pltpu.VMEM(s, F32) for s in scratch],
        compiler_params=pltpu.CompilerParams(vmem_limit_bytes=vmem * 1024 * 1024),
    )(*args)


def swapped(block, pairs):
    route = sorted([(a, b) for a, b in pairs] + [(b, a) for a, b in pairs])
    return lax.ppermute(block, AX, route)


def exchange(faces):
    tiles = faces.shape[1]
    got = [faces]
    for m in (1, 2, 3):
        got.append(swapped(faces, [(i, i ^ m) for i in range(DEVICES) if i < i ^ m]))
    own = jnp.concatenate(got, axis=0)
    sides = []
    for odd in (0, 1):
        pairs = [(i, i + 4) for i in range(DEVICES - 4) if (i // 4) % 2 == odd]
        sides.append(swapped(own, pairs))
    return own, sides[0], sides[1]


def to_all(rows):
    spread = jnp.broadcast_to(rows[None], (DEVICES,) + rows.shape)
    return lax.all_to_all(spread, AX, 0, 0)


def shards(source_term, inverse_density, box_counts, ghost_from):
    dev = lax.axis_index(AX).astype(I32)
    mask = (jnp.arange(SLOTS, dtype=I32) < box_counts[0]).astype(F32)
    flat = ghost_from.reshape(-1)
    present = flat >= 0
    pres = present.astype(F32)
    at = jnp.where(present, flat, dev * SLOTS)
    owner = at // SLOTS
    local = at - owner * SLOTS
    block = dev // 4
    ahead = owner // 4 - block
    even = (block & 1) == 0
    src = jnp.where(ahead == 0, 0, jnp.where((ahead == 1) == even, 1, 2))
    tab = jnp.concatenate(
        [src, ((owner & 3) ^ (dev & 3)) * SLOTS + local, owner, local, jnp.full((16,), dev)]
    ).astype(I32)
    note = jnp.concatenate([flat, box_counts, jnp.zeros((115,), I32)]).astype(F32).reshape(1, 128)

    view = lambda a: a.reshape(SLOTS, 256, 128).transpose(1, 0, 2)
    fine = (SLOTS, 32, 8, 128)
    mid = (SLOTS, 16, 8, 128)
    face = (SLOTS, 4, 8, 128)
    gx, gyf, gym = (SLOTS, 2, 8, 128), (SLOTS, 32, 128), (SLOTS, 16, 128)
    source, beta, beta1, faces, notes = call(
        k_start, 1, (mask, view(source_term), view(inverse_density), note),
        [fine, fine, mid, (SLOTS, 8, 8, 128), (24, 128)],
    )
    beta_rows = lax.all_gather(notes, AX)
    win = exchange(faces)
    cx, cy, cz, wn, rd, u, cx1, cy1, cz1, wn1, rd1, faces = call(
        k_weights, 2, (tab, pres, source, beta, beta1) + win,
        [(SLOTS, 33, 8, 128), fine, fine, gyf, fine, fine, (SLOTS, 17, 8, 128), mid, mid, gym, mid, face],
        [gx, gyf, gx, gym],
    )
    fine_w, mid_w = (cx, cy, cz, wn), (cx1, cy1, cz1, wn1)

    def sweep(lv, t, u, faces, w, d):
        return call(
            functools.partial(k_sweep, lv), 1, (tab, t, u) + exchange(faces) + w + (d,),
            [(fine, mid)[lv], face], [gx, (gyf, gym)[lv]],
        )

    u, faces = sweep(0, source, u, faces, fine_w, rd)
    f1, u1, faces, gx0, gy0 = call(
        k_down, 1, (tab, source, u) + exchange(faces) + fine_w + (rd1,), [mid, mid, face, gx, gyf], [fine],
    )
    u1, faces = sweep(1, f1, u1, faces, mid_w, rd1)
    rows, gx1, gy1 = call(
        k_bottom_rhs, 1, (tab, f1, u1) + exchange(faces) + mid_w, [(12, 128), gx, gym], [mid],
    )
    cube = (SLOTS, 8, 8, 8, 128)
    u1, faces, boxes = call(
        k_bottom, 1, (tab, f1, u1, gx1, gy1) + mid_w + (rd1, beta_rows, to_all(rows)), [mid, face, (8, 128)],
        [(SLOTS, 10, 10, 8, 128), cube, cube, cube, (SLOTS, 8, 9, 8, 128), (SLOTS, 9, 8, 8, 128), cube,
         (DEVICES, 24, 128), (128, 128), mid, gx, gym],
    )
    u1, faces = sweep(1, f1, u1, faces, mid_w, rd1)
    u, faces = call(
        k_up, 1, (tab, source, u, gx0, gy0, u1) + exchange(faces) + fine_w + (rd,), [fine, face],
        [fine, gx, gyf, gx, gym],
    )
    u, faces = sweep(0, source, u, faces, fine_w, rd)
    residual, sums = call(
        k_residual, 1, (tab, source, u) + exchange(faces) + fine_w, [(256, SLOTS, 128), (1, 128)], [gx, gyf, fine],
    )
    parts = to_all(sums).reshape(DEVICES, 128)
    correction, norm = call(k_finish, 1, (mask, u, parts, boxes), [(256, SLOTS, 128), (1, 128)])
    back = lambda a: a.transpose(1, 0, 2).reshape(SLOTS, 32768)
    return back(correction), back(residual), norm[0, 0]


def solution(mesh):
    rows = P(AX, None)
    return jax.shard_map(
        shards, mesh=mesh, in_specs=(rows, rows, P(AX), rows), out_specs=(rows, rows, P()), check_vma=False
    )
```

time: 2430 us -> 309 us (0.13)
  blocking collectives: 1150 us -> 40.4 us
  local copies, waits for them, and re-layouts: 527 us -> 14.6 us
  starting transfers between devices: 436 us -> 99.7 us
  other arithmetic: 213 us -> 0.12 us
  Pallas kernels: 0 us -> 68.5 us
    psum x18 -> x0, blocking collectives: 1150 us -> none  [the longest x8 512 us: square_total(): return lax.psum(value, ('gx', 'gy'))]
    ppermute x120 -> x45, starting transfers between devices: 436 us -> 99.7 us  [swapped(): return lax.ppermute(block, AX, route)]
    another operation x160 -> x0, local copies, waits for them, and re-layouts: 172 us -> none  [the longest x80 80.1 us: face_table(): jnp.stack([cube_view[:, 0].reshape(slot_total, side_area), cube_view[:, b...]
    reshape x36 -> x1, local copies, waits for them, and re-layouts: 172 us -> 0.76 us  [shards(): flat = ghost_from.reshape(-1)]
    add x21 -> x1, other arithmetic: 72.9 us -> 0.02 us  [shards(): (owner & 3 ^ dev & 3) * SLOTS + local]
    reduce_sum x22 -> x0, other arithmetic: 70.2 us -> none  [the longest x8 24.8 us: conjugate(): step_size = norm_now / reduce_curve(jnp.sum(direction * image))]
    pallas_call x0 -> x12, Pallas kernels: none -> 68.5 us  [call(): pl.pallas_call(kernel, out_shape=[shape(s) for s in outs], in_specs=[SMEM...]
    gather x40 -> x0, local copies, waits for them, and re-layouts: 53.7 us -> none  [fetch(): picked = flat_rows[position]]
  transfers between devices with their start and end apart: 120 -> 46, of which waited for: 14 -> 29; matrix products, arithmetic and copies ran while one was open for 15% -> 0% of each run, Pallas kernels for 0% -> 3%
where the time goes in v1:
time: 309 us; the launch traced here: 308 us
  starting transfers between devices  99.7 us (32%)
  waiting for transfers between devices  69.6 us (23%)
  Pallas kernels  68.5 us (22%)
  blocking collectives  40.4 us (13%)
  between operations  15.2 us (5%)
  local copies, waits for them, and re-layouts  14.6 us (5%)
    ppermute x45, starting transfers between devices, swapped(): return lax.ppermute(block, AX, route)  99.7 us
    ppermute x45, waiting for transfers between devices, swapped(): return lax.ppermute(block, AX, route)  69.6 us
    pallas_call x12, Pallas kernels, call(): pl.pallas_call(kernel, out_shape=[shape(s) for s in outs], in_specs=[SMEM...  68.5 us
    all_to_all x2, blocking collectives, to_all(): return lax.all_to_all(spread, AX, 0, 0)  40.4 us
    unnamed x73, local copies, waits for them, and re-layouts  12.8 us
  transfers between devices with their start and end apart: 46, of which 29 were waited for; matrix products, arithmetic and copies ran while one was open for 0% of the time, Pallas kernels for 3%

profile of v1, /device:TPU:1, one launch (start us, length us, event | category | flops | bytes accessed | tf_op | source)
XLA Modules:
  0.0 308.1 jit_solution(13614284289106241014)
XLA Ops:
  8.7 1.0 copy-done.11
  9.8 1.0 copy-done.12
  10.8 3.2 %shard_map.67 = (f32[3,32,8,128]{3,2,1,0:T(8,128)S(1)}, f32[3,32,8,128]{3,2,1,0:T(8,128)S(1)}, f32[3,16,8,128]{3,2,1,0:T(8,128)S(1)}, f32[3,8,8,128]{3,2,1,0:T(8,128)S(1)}, f32[24,128]{1,0:T(8,128)}) custom-call(f32[3]{0:T(128)S(1)} %compare_convert_fusion.1.mask, f32[256,3,128]{2,1,0:T(4,128)S(1)} %bitcast.26, f32[256,3,128]{2,1,0:T(4,128)S(1)} %bitcast.27, ...), custom_call_target="tpu_custom_call" | custom-call | tf_op jit(solution)/shard_map/pallas_call | solution.py:522
  14.0 2.5 collective-permute-start
  16.5 3.3 %collective-permute-start.1 = (f32[3,8,8,128]{3,2,1,0:T(8,128)S(1)}, f32[3,8,8,128]{3,2,1,0:T(8,128)S(1)}, u32[]{:S(2)}, u32[]{:S(2)}) collective-permute-start(f32[3,8,8,128]{3,2,1,0:T(8,128)S(1)} %get-tuple-element.48), channel_id=1, source_target_pairs={{0,2},{1,3},{2,0},{3,1},{4,6},{5,7},{6,4},{7,5},{8,10},{9,11},{10,... | collective-permute-start | bytes 294920 | tf_op jit(solution)/shard_map/ppermute | solution.py:534
  20.6 3.1 %collective-permute-done.1 = f32[3,8,8,128]{3,2,1,0:T(8,128)S(1)} collective-permute-done((f32[3,8,8,128]{3,2,1,0:T(8,128)S(1)}, f32[3,8,8,128]{3,2,1,0:T(8,128)S(1)}, u32[]{:S(2)}, u32[]{:S(2)}) %collective-permute-start.1) | collective-permute-done | bytes 98336 | tf_op jit(solution)/shard_map/ppermute | solution.py:534
  23.8 2.7 collective-permute-done.2
  26.5 1.4 collective-permute-start.3
  27.9 4.9 %collective-permute-start.4 = (f32[12,8,8,128]{3,2,1,0:T(8,128)S(1)}, f32[12,8,8,128]{3,2,1,0:T(8,128)S(1)}, u32[]{:S(2)}, u32[]{:S(2)}) collective-permute-start(f32[12,8,8,128]{3,2,1,0:T(8,128)S(1)} %constant_dynamic-update-slice_fusion.own), channel_id=1, source_target_pairs={{4,8},{5,9},{6,10},{7,11},{8,4},{9,5},{10,6},{11,7},{12,16},{13,17... | collective-permute-start | bytes 1179656 | tf_op jit(solution)/shard_map/ppermute | solution.py:534
  32.9 3.6 %collective-permute-done.3.near = f32[12,8,8,128]{3,2,1,0:T(8,128)S(1)} collective-permute-done((f32[12,8,8,128]{3,2,1,0:T(8,128)S(1)}, f32[12,8,8,128]{3,2,1,0:T(8,128)S(1)}, u32[]{:S(2)}, u32[]{:S(2)}) %collective-permute-start.3) | collective-permute-done | bytes 393248 | tf_op jit(solution)/shard_map/ppermute | solution.py:534
  37.2 4.6 %collective-permute-done.4.far = f32[12,8,8,128]{3,2,1,0:T(8,128)S(1)} collective-permute-done((f32[12,8,8,128]{3,2,1,0:T(8,128)S(1)}, f32[12,8,8,128]{3,2,1,0:T(8,128)S(1)}, u32[]{:S(2)}, u32[]{:S(2)}) %collective-permute-start.4) | collective-permute-done | bytes 393248 | tf_op jit(solution)/shard_map/ppermute | solution.py:534
  44.5 2.0 shard_map.68
  46.7 1.3 collective-permute-start.6
  47.9 2.6 collective-permute-start.7
  52.1 7.3 %collective-permute-start.9 = (f32[12,4,8,128]{3,2,1,0:T(8,128)S(1)}, f32[12,4,8,128]{3,2,1,0:T(8,128)S(1)}, u32[]{:S(2)}, u32[]{:S(2)}) collective-permute-start(f32[12,4,8,128]{3,2,1,0:T(8,128)S(1)} %constant_dynamic-update-slice_fusion.4.own), channel_id=1, source_target_pairs={{4,8},{5,9},{6,10},{7,11},{8,4},{9,5},{10,6},{11,7},{12,16},{13,17... | collective-permute-start | bytes 589832 | tf_op jit(solution)/shard_map/ppermute | solution.py:534
  59.4 3.5 %collective-permute-done.9.far = f32[12,4,8,128]{3,2,1,0:T(8,128)S(1)} collective-permute-done((f32[12,4,8,128]{3,2,1,0:T(8,128)S(1)}, f32[12,4,8,128]{3,2,1,0:T(8,128)S(1)}, u32[]{:S(2)}, u32[]{:S(2)}) %collective-permute-start.9) | collective-permute-done | bytes 196640 | tf_op jit(solution)/shard_map/ppermute | solution.py:534
  62.9 1.6 shard_map.69
  65.3 3.3 %collective-permute-start.11 = (f32[3,4,8,128]{3,2,1,0:T(8,128)S(1)}, f32[3,4,8,128]{3,2,1,0:T(8,128)S(1)}, u32[]{:S(2)}, u32[]{:S(2)}) collective-permute-start(f32[3,4,8,128]{3,2,1,0:T(8,128)S(1)} %get-tuple-element.57), channel_id=1, source_target_pairs={{0,2},{1,3},{2,0},{3,1},{4,6},{5,7},{6,4},{7,5},{8,10},{9,11},{10,... | collective-permute-start | bytes 147464 | tf_op jit(solution)/shard_map/ppermute | solution.py:534
  68.6 2.1 collective-permute-done.11
  70.6 2.0 collective-permute-done.12
  72.7 7.8 %collective-permute-start.14 = (f32[12,4,8,128]{3,2,1,0:T(8,128)S(1)}, f32[12,4,8,128]{3,2,1,0:T(8,128)S(1)}, u32[]{:S(2)}, u32[]{:S(2)}) collective-permute-start(f32[12,4,8,128]{3,2,1,0:T(8,128)S(1)} %constant_dynamic-update-slice_fusion.8.own), channel_id=1, source_target_pairs={{4,8},{5,9},{6,10},{7,11},{8,4},{9,5},{10,6},{11,7},{12,16},{13,17... | collective-permute-start | bytes 589832 | tf_op jit(solution)/shard_map/ppermute | solution.py:534
  80.5 4.4 %collective-permute-done.14.far = f32[12,4,8,128]{3,2,1,0:T(8,128)S(1)} collective-permute-done((f32[12,4,8,128]{3,2,1,0:T(8,128)S(1)}, f32[12,4,8,128]{3,2,1,0:T(8,128)S(1)}, u32[]{:S(2)}, u32[]{:S(2)}) %collective-permute-start.14) | collective-permute-done | bytes 196640 | tf_op jit(solution)/shard_map/ppermute | solution.py:534
  84.9 2.1 shard_map.70
  87.2 1.4 collective-permute-start.16
  88.5 2.5 collective-permute-start.17
  92.8 7.3 %collective-permute-start.19 = (f32[12,4,8,128]{3,2,1,0:T(8,128)S(1)}, f32[12,4,8,128]{3,2,1,0:T(8,128)S(1)}, u32[]{:S(2)}, u32[]{:S(2)}) collective-permute-start(f32[12,4,8,128]{3,2,1,0:T(8,128)S(1)} %constant_dynamic-update-slice_fusion.12.own), channel_id=1, source_target_pairs={{4,8},{5,9},{6,10},{7,11},{8,4},{9,5},{10,6},{11,7},{12,16},{13,17... | collective-permute-start | bytes 589832 | tf_op jit(solution)/shard_map/ppermute | solution.py:534
  100.1 4.2 %collective-permute-done.19.far = f32[12,4,8,128]{3,2,1,0:T(8,128)S(1)} collective-permute-done((f32[12,4,8,128]{3,2,1,0:T(8,128)S(1)}, f32[12,4,8,128]{3,2,1,0:T(8,128)S(1)}, u32[]{:S(2)}, u32[]{:S(2)}) %collective-permute-start.19) | collective-permute-done | bytes 196640 | tf_op jit(solution)/shard_map/ppermute | solution.py:534
  104.3 1.1 shard_map.71
  105.6 3.5 %collective-permute-start.21 = (f32[3,4,8,128]{3,2,1,0:T(8,128)S(1)}, f32[3,4,8,128]{3,2,1,0:T(8,128)S(1)}, u32[]{:S(2)}, u32[]{:S(2)}) collective-permute-start(f32[3,4,8,128]{3,2,1,0:T(8,128)S(1)} %get-tuple-element.69), channel_id=1, source_target_pairs={{0,2},{1,3},{2,0},{3,1},{4,6},{5,7},{6,4},{7,5},{8,10},{9,11},{10,... | collective-permute-start | bytes 147464 | tf_op jit(solution)/shard_map/ppermute | solution.py:534
  109.3 1.8 collective-permute-done.21
  111.2 2.1 collective-permute-done.22
  113.3 7.3 %collective-permute-start.24 = (f32[12,4,8,128]{3,2,1,0:T(8,128)S(1)}, f32[12,4,8,128]{3,2,1,0:T(8,128)S(1)}, u32[]{:S(2)}, u32[]{:S(2)}) collective-permute-start(f32[12,4,8,128]{3,2,1,0:T(8,128)S(1)} %constant_dynamic-update-slice_fusion.16.own), channel_id=1, source_target_pairs={{4,8},{5,9},{6,10},{7,11},{8,4},{9,5},{10,6},{11,7},{12,16},{13,17... | collective-permute-start | bytes 589832 | tf_op jit(solution)/shard_map/ppermute | solution.py:534
  120.6 4.2 %collective-permute-done.24.far = f32[12,4,8,128]{3,2,1,0:T(8,128)S(1)} collective-permute-done((f32[12,4,8,128]{3,2,1,0:T(8,128)S(1)}, f32[12,4,8,128]{3,2,1,0:T(8,128)S(1)}, u32[]{:S(2)}, u32[]{:S(2)}) %collective-permute-start.24) | collective-permute-done | bytes 196640 | tf_op jit(solution)/shard_map/ppermute | solution.py:534
  124.8 1.3 shard_map.72
  126.7 24.5 %all_to_all.10.rhs_rows = f32[128,12,128]{2,1,0:T(8,128)S(1)} all-to-all(f32[128,12,128]{2,1,0:T(8,128)S(1)} %broadcast_in_dim.33), channel_id=1, replica_groups=mesh['gx'=8,'gy'=16] {'gx','gy'}, dimensions={0} | all-to-all | bytes 1572864 | tf_op jit(solution)/shard_map/all_to_all | solution.py:552
  154.0 1.4 copy-done.6
  157.8 48.5 %shard_map.73 = (f32[3,16,8,128]{3,2,1,0:T(8,128)S(1)}, f32[3,4,8,128]{3,2,1,0:T(8,128)S(1)}, f32[8,128]{1,0:T(8,128)S(1)}) custom-call(s32[64]{0:T(128)S(1)} %concatenate.44.tab, f32[3,16,8,128]{3,2,1,0:T(8,128)S(1)} %copy-done.5, f32[3,16,8,128]{3,2,1,0:T(8,128)S(1)} %copy-done.10, f32[3,2,8,128]{3,2,1,0:T(8,128)S(1)} %copy-done.20, ...), custom_call_target="tpu_custom_call" | custom-call | tf_op jit(solution)/shard_map/pallas_call | solution.py:522
  206.7 2.2 collective-permute-start.26
  208.9 1.4 collective-permute-start.27
  210.3 1.2 collective-permute-done.26
  211.5 2.1 collective-permute-done.27
  213.7 4.2 %collective-permute-start.29 = (f32[12,4,8,128]{3,2,1,0:T(8,128)S(1)}, f32[12,4,8,128]{3,2,1,0:T(8,128)S(1)}, u32[]{:S(2)}, u32[]{:S(2)}) collective-permute-start(f32[12,4,8,128]{3,2,1,0:T(8,128)S(1)} %constant_dynamic-update-slice_fusion.20.own), channel_id=1, source_target_pairs={{4,8},{5,9},{6,10},{7,11},{8,4},{9,5},{10,6},{11,7},{12,16},{13,17... | collective-permute-start | bytes 589832 | tf_op jit(solution)/shard_map/ppermute | solution.py:534
  218.2 4.3 %collective-permute-done.29.far = f32[12,4,8,128]{3,2,1,0:T(8,128)S(1)} collective-permute-done((f32[12,4,8,128]{3,2,1,0:T(8,128)S(1)}, f32[12,4,8,128]{3,2,1,0:T(8,128)S(1)}, u32[]{:S(2)}, u32[]{:S(2)}) %collective-permute-start.29) | collective-permute-done | bytes 196640 | tf_op jit(solution)/shard_map/ppermute | solution.py:534
  222.5 1.1 shard_map.74
  223.8 3.5 %collective-permute-start.31 = (f32[3,4,8,128]{3,2,1,0:T(8,128)S(1)}, f32[3,4,8,128]{3,2,1,0:T(8,128)S(1)}, u32[]{:S(2)}, u32[]{:S(2)}) collective-permute-start(f32[3,4,8,128]{3,2,1,0:T(8,128)S(1)} %get-tuple-element.77), channel_id=1, source_target_pairs={{0,2},{1,3},{2,0},{3,1},{4,6},{5,7},{6,4},{7,5},{8,10},{9,11},{10,... | collective-permute-start | bytes 147464 | tf_op jit(solution)/shard_map/ppermute | solution.py:534
  227.6 1.7 collective-permute-done.31
  229.2 2.1 collective-permute-done.32
  231.4 7.3 %collective-permute-start.34 = (f32[12,4,8,128]{3,2,1,0:T(8,128)S(1)}, f32[12,4,8,128]{3,2,1,0:T(8,128)S(1)}, u32[]{:S(2)}, u32[]{:S(2)}) collective-permute-start(f32[12,4,8,128]{3,2,1,0:T(8,128)S(1)} %constant_dynamic-update-slice_fusion.24.own), channel_id=1, source_target_pairs={{4,8},{5,9},{6,10},{7,11},{8,4},{9,5},{10,6},{11,7},{12,16},{13,17... | collective-permute-start | bytes 589832 | tf_op jit(solution)/shard_map/ppermute | solution.py:534
  238.7 3.5 %collective-permute-done.34.far = f32[12,4,8,128]{3,2,1,0:T(8,128)S(1)} collective-permute-done((f32[12,4,8,128]{3,2,1,0:T(8,128)S(1)}, f32[12,4,8,128]{3,2,1,0:T(8,128)S(1)}, u32[]{:S(2)}, u32[]{:S(2)}) %collective-permute-start.34) | collective-permute-done | bytes 196640 | tf_op jit(solution)/shard_map/ppermute | solution.py:534
  242.2 1.6 shard_map.75
  243.9 1.6 collective-permute-start.36
  245.5 2.3 collective-permute-start.37
  248.5 1.2 collective-permute-done.37
  249.7 7.7 %collective-permute-start.39 = (f32[12,4,8,128]{3,2,1,0:T(8,128)S(1)}, f32[12,4,8,128]{3,2,1,0:T(8,128)S(1)}, u32[]{:S(2)}, u32[]{:S(2)}) collective-permute-start(f32[12,4,8,128]{3,2,1,0:T(8,128)S(1)} %constant_dynamic-update-slice_fusion.28.own), channel_id=1, source_target_pairs={{4,8},{5,9},{6,10},{7,11},{8,4},{9,5},{10,6},{11,7},{12,16},{13,17... | collective-permute-start | bytes 589832 | tf_op jit(solution)/shard_map/ppermute | solution.py:534
  257.4 3.6 %collective-permute-done.39.far = f32[12,4,8,128]{3,2,1,0:T(8,128)S(1)} collective-permute-done((f32[12,4,8,128]{3,2,1,0:T(8,128)S(1)}, f32[12,4,8,128]{3,2,1,0:T(8,128)S(1)}, u32[]{:S(2)}, u32[]{:S(2)}) %collective-permute-start.39) | collective-permute-done | bytes 196640 | tf_op jit(solution)/shard_map/ppermute | solution.py:534
  260.9 1.6 shard_map.76
  262.7 3.4 %collective-permute-start.41 = (f32[3,4,8,128]{3,2,1,0:T(8,128)S(1)}, f32[3,4,8,128]{3,2,1,0:T(8,128)S(1)}, u32[]{:S(2)}, u32[]{:S(2)}) collective-permute-start(f32[3,4,8,128]{3,2,1,0:T(8,128)S(1)} %get-tuple-element.81), channel_id=1, source_target_pairs={{0,2},{1,3},{2,0},{3,1},{4,6},{5,7},{6,4},{7,5},{8,10},{9,11},{10,... | collective-permute-start | bytes 147464 | tf_op jit(solution)/shard_map/ppermute | solution.py:534
  266.5 1.6 collective-permute-done.41
  268.1 2.1 collective-permute-done.42
  270.3 7.3 %collective-permute-start.44 = (f32[12,4,8,128]{3,2,1,0:T(8,128)S(1)}, f32[12,4,8,128]{3,2,1,0:T(8,128)S(1)}, u32[]{:S(2)}, u32[]{:S(2)}) collective-permute-start(f32[12,4,8,128]{3,2,1,0:T(8,128)S(1)} %constant_dynamic-update-slice_fusion.32.own), channel_id=1, source_target_pairs={{4,8},{5,9},{6,10},{7,11},{8,4},{9,5},{10,6},{11,7},{12,16},{13,17... | collective-permute-start | bytes 589832 | tf_op jit(solution)/shard_map/ppermute | solution.py:534
  277.6 3.5 %collective-permute-done.44.far = f32[12,4,8,128]{3,2,1,0:T(8,128)S(1)} collective-permute-done((f32[12,4,8,128]{3,2,1,0:T(8,128)S(1)}, f32[12,4,8,128]{3,2,1,0:T(8,128)S(1)}, u32[]{:S(2)}, u32[]{:S(2)}) %collective-permute-start.44) | collective-permute-done | bytes 196640 | tf_op jit(solution)/shard_map/ppermute | solution.py:534
  281.1 2.6 shard_map.77
  283.7 15.9 %all_to_all.11 = f32[128,1,128]{2,1,0:T(1,128)S(1)} all-to-all(f32[128,1,128]{2,1,0:T(1,128)S(1)} %broadcast_in_dim.35), channel_id=1, replica_groups=mesh['gx'=8,'gy'=16] {'gx','gy'}, dimensions={0} | all-to-all | bytes 131072 | tf_op jit(solution)/shard_map/all_to_all | solution.py:552
  299.6 1.6 shard_map.78
  (137 shorter events, 18.3 us)
Async XLA Ops:
  7.2 144.1 %all-gather.3.cloned.1.call-start = ((), (), s32[]{:S(2)}) async-start(), calls=%async_computation.2 | async-start | bytes 1585152 | tf_op jit(solution)/shard_map/all_gather | solution.py:582
  8.7 1.0 copy-start.11
  9.8 1.0 copy-start.12
  14.0 6.6 %collective-permute-start = (f32[3,8,8,128]{3,2,1,0:T(8,128)S(1)}, f32[3,8,8,128]{3,2,1,0:T(8,128)S(1)}, u32[]{:S(2)}, u32[]{:S(2)}) collective-permute-start(f32[3,8,8,128]{3,2,1,0:T(8,128)S(1)} %get-tuple-element.48), channel_id=1, source_target_pairs={{0,1},{1,0},{2,3},{3,2},{4,5},{5,4},{6,7},{7,6},{8,9},{9,8},{10,11... | collective-permute-start | bytes 294920 | tf_op jit(solution)/shard_map/ppermute | solution.py:534
  16.5 7.3 %collective-permute-start.1 = (f32[3,8,8,128]{3,2,1,0:T(8,128)S(1)}, f32[3,8,8,128]{3,2,1,0:T(8,128)S(1)}, u32[]{:S(2)}, u32[]{:S(2)}) collective-permute-start(f32[3,8,8,128]{3,2,1,0:T(8,128)S(1)} %get-tuple-element.48), channel_id=1, source_target_pairs={{0,2},{1,3},{2,0},{3,1},{4,6},{5,7},{6,4},{7,5},{8,10},{9,11},{10,... | collective-permute-start | bytes 294920 | tf_op jit(solution)/shard_map/ppermute | solution.py:534
  19.8 6.8 %collective-permute-start.2 = (f32[3,8,8,128]{3,2,1,0:T(8,128)S(1)}, f32[3,8,8,128]{3,2,1,0:T(8,128)S(1)}, u32[]{:S(2)}, u32[]{:S(2)}) collective-permute-start(f32[3,8,8,128]{3,2,1,0:T(8,128)S(1)} %get-tuple-element.48), channel_id=1, source_target_pairs={{0,3},{1,2},{2,1},{3,0},{4,7},{5,6},{6,5},{7,4},{8,11},{9,10},{10,... | collective-permute-start | bytes 294920 | tf_op jit(solution)/shard_map/ppermute | solution.py:534
  26.5 9.9 %collective-permute-start.3 = (f32[12,8,8,128]{3,2,1,0:T(8,128)S(1)}, f32[12,8,8,128]{3,2,1,0:T(8,128)S(1)}, u32[]{:S(2)}, u32[]{:S(2)}) collective-permute-start(f32[12,8,8,128]{3,2,1,0:T(8,128)S(1)} %constant_dynamic-update-slice_fusion.own), channel_id=1, source_target_pairs={{0,4},{1,5},{2,6},{3,7},{4,0},{5,1},{6,2},{7,3},{8,12},{9,13},{10,... | collective-permute-start | bytes 1179656 | tf_op jit(solution)/shard_map/ppermute | solution.py:534
  27.9 13.9 %collective-permute-start.4 = (f32[12,8,8,128]{3,2,1,0:T(8,128)S(1)}, f32[12,8,8,128]{3,2,1,0:T(8,128)S(1)}, u32[]{:S(2)}, u32[]{:S(2)}) collective-permute-start(f32[12,8,8,128]{3,2,1,0:T(8,128)S(1)} %constant_dynamic-update-slice_fusion.own), channel_id=1, source_target_pairs={{4,8},{5,9},{6,10},{7,11},{8,4},{9,5},{10,6},{11,7},{12,16},{13,17... | collective-permute-start | bytes 1179656 | tf_op jit(solution)/shard_map/ppermute | solution.py:534
  36.5 0.7 copy-start.13
  42.6 1.0 copy-start.14
  43.5 1.0 copy-start.16
  46.6 78.3 %copy-start = (f32[3,16,8,128]{3,2,1,0:T(8,128)}, f32[3,16,8,128]{3,2,1,0:T(8,128)S(1)}, u32[]{:S(2)}) copy-start(f32[3,16,8,128]{3,2,1,0:T(8,128)S(1)} %get-tuple-element.65.cy.cy1) | copy-start | bytes 589828
  46.6 78.3 %copy-start.2 = (f32[3,16,8,128]{3,2,1,0:T(8,128)}, f32[3,16,8,128]{3,2,1,0:T(8,128)S(1)}, u32[]{:S(2)}) copy-start(f32[3,16,8,128]{3,2,1,0:T(8,128)S(1)} %get-tuple-element.66.cz.cz1) | copy-start | bytes 589828
  46.6 3.9 %collective-permute-start.5 = (f32[3,4,8,128]{3,2,1,0:T(8,128)S(1)}, f32[3,4,8,128]{3,2,1,0:T(8,128)S(1)}, u32[]{:S(2)}, u32[]{:S(2)}) collective-permute-start(f32[3,4,8,128]{3,2,1,0:T(8,128)S(1)} %get-tuple-element.50), channel_id=1, source_target_pairs={{0,1},{1,0},{2,3},{3,2},{4,5},{5,4},{6,7},{7,6},{8,9},{9,8},{10,11... | collective-permute-start | bytes 147464 | tf_op jit(solution)/shard_map/ppermute | solution.py:534
  46.7 4.5 %collective-permute-start.6 = (f32[3,4,8,128]{3,2,1,0:T(8,128)S(1)}, f32[3,4,8,128]{3,2,1,0:T(8,128)S(1)}, u32[]{:S(2)}, u32[]{:S(2)}) collective-permute-start(f32[3,4,8,128]{3,2,1,0:T(8,128)S(1)} %get-tuple-element.50), channel_id=1, source_target_pairs={{0,2},{1,3},{2,0},{3,1},{4,6},{5,7},{6,4},{7,5},{8,10},{9,11},{10,... | collective-permute-start | bytes 147464 | tf_op jit(solution)/shard_map/ppermute | solution.py:534
  47.9 4.2 %collective-permute-start.7 = (f32[3,4,8,128]{3,2,1,0:T(8,128)S(1)}, f32[3,4,8,128]{3,2,1,0:T(8,128)S(1)}, u32[]{:S(2)}, u32[]{:S(2)}) collective-permute-start(f32[3,4,8,128]{3,2,1,0:T(8,128)S(1)} %get-tuple-element.50), channel_id=1, source_target_pairs={{0,3},{1,2},{2,1},{3,0},{4,7},{5,6},{6,5},{7,4},{8,11},{9,10},{10,... | collective-permute-start | bytes 147464 | tf_op jit(solution)/shard_map/ppermute | solution.py:534
  52.1 7.3 %collective-permute-start.8 = (f32[12,4,8,128]{3,2,1,0:T(8,128)S(1)}, f32[12,4,8,128]{3,2,1,0:T(8,128)S(1)}, u32[]{:S(2)}, u32[]{:S(2)}) collective-permute-start(f32[12,4,8,128]{3,2,1,0:T(8,128)S(1)} %constant_dynamic-update-slice_fusion.4.own), channel_id=1, source_target_pairs={{0,4},{1,5},{2,6},{3,7},{4,0},{5,1},{6,2},{7,3},{8,12},{9,13},{10,... | collective-permute-start | bytes 589832 | tf_op jit(solution)/shard_map/ppermute | solution.py:534
  52.1 10.8 %collective-permute-start.9 = (f32[12,4,8,128]{3,2,1,0:T(8,128)S(1)}, f32[12,4,8,128]{3,2,1,0:T(8,128)S(1)}, u32[]{:S(2)}, u32[]{:S(2)}) collective-permute-start(f32[12,4,8,128]{3,2,1,0:T(8,128)S(1)} %constant_dynamic-update-slice_fusion.4.own), channel_id=1, source_target_pairs={{4,8},{5,9},{6,10},{7,11},{8,4},{9,5},{10,6},{11,7},{12,16},{13,17... | collective-permute-start | bytes 589832 | tf_op jit(solution)/shard_map/ppermute | solution.py:534
  64.6 22.5 %copy-start.7 = (f32[3,32,8,128]{3,2,1,0:T(8,128)}, f32[3,32,8,128]{3,2,1,0:T(8,128)S(1)}, u32[]{:S(2)}) copy-start(f32[3,32,8,128]{3,2,1,0:T(8,128)S(1)} %get-tuple-element.56.u.u0) | copy-start | bytes 1179652
  64.6 3.9 %collective-permute-start.10 = (f32[3,4,8,128]{3,2,1,0:T(8,128)S(1)}, f32[3,4,8,128]{3,2,1,0:T(8,128)S(1)}, u32[]{:S(2)}, u32[]{:S(2)}) collective-permute-start(f32[3,4,8,128]{3,2,1,0:T(8,128)S(1)} %get-tuple-element.57), channel_id=1, source_target_pairs={{0,1},{1,0},{2,3},{3,2},{4,5},{5,4},{6,7},{7,6},{8,9},{9,8},{10,11... | collective-permute-start | bytes 147464 | tf_op jit(solution)/shard_map/ppermute | solution.py:534
  65.3 5.4 %collective-permute-start.11 = (f32[3,4,8,128]{3,2,1,0:T(8,128)S(1)}, f32[3,4,8,128]{3,2,1,0:T(8,128)S(1)}, u32[]{:S(2)}, u32[]{:S(2)}) collective-permute-start(f32[3,4,8,128]{3,2,1,0:T(8,128)S(1)} %get-tuple-element.57), channel_id=1, source_target_pairs={{0,2},{1,3},{2,0},{3,1},{4,6},{5,7},{6,4},{7,5},{8,10},{9,11},{10,... | collective-permute-start | bytes 147464 | tf_op jit(solution)/shard_map/ppermute | solution.py:534
  68.5 4.2 %collective-permute-start.12 = (f32[3,4,8,128]{3,2,1,0:T(8,128)S(1)}, f32[3,4,8,128]{3,2,1,0:T(8,128)S(1)}, u32[]{:S(2)}, u32[]{:S(2)}) collective-permute-start(f32[3,4,8,128]{3,2,1,0:T(8,128)S(1)} %get-tuple-element.57), channel_id=1, source_target_pairs={{0,3},{1,2},{2,1},{3,0},{4,7},{5,6},{6,5},{7,4},{8,11},{9,10},{10,... | collective-permute-start | bytes 147464 | tf_op jit(solution)/shard_map/ppermute | solution.py:534
  72.7 7.8 %collective-permute-start.13 = (f32[12,4,8,128]{3,2,1,0:T(8,128)S(1)}, f32[12,4,8,128]{3,2,1,0:T(8,128)S(1)}, u32[]{:S(2)}, u32[]{:S(2)}) collective-permute-start(f32[12,4,8,128]{3,2,1,0:T(8,128)S(1)} %constant_dynamic-update-slice_fusion.8.own), channel_id=1, source_target_pairs={{0,4},{1,5},{2,6},{3,7},{4,0},{5,1},{6,2},{7,3},{8,12},{9,13},{10,... | collective-permute-start | bytes 589832 | tf_op jit(solution)/shard_map/ppermute | solution.py:534
  72.7 12.2 %collective-permute-start.14 = (f32[12,4,8,128]{3,2,1,0:T(8,128)S(1)}, f32[12,4,8,128]{3,2,1,0:T(8,128)S(1)}, u32[]{:S(2)}, u32[]{:S(2)}) collective-permute-start(f32[12,4,8,128]{3,2,1,0:T(8,128)S(1)} %constant_dynamic-update-slice_fusion.8.own), channel_id=1, source_target_pairs={{4,8},{5,9},{6,10},{7,11},{8,4},{9,5},{10,6},{11,7},{12,16},{13,17... | collective-permute-start | bytes 589832 | tf_op jit(solution)/shard_map/ppermute | solution.py:534
  87.1 5.6 %copy-start.17 = (f32[3,32,128]{2,1,0:T(8,128)}, f32[3,32,128]{2,1,0:T(8,128)S(1)}, u32[]{:S(2)}) copy-start(f32[3,32,128]{2,1,0:T(8,128)S(1)} %get-tuple-element.60.gy0) | copy-start | bytes 147460
  87.1 39.1 %copy-start.4 = (f32[3,16,8,128]{3,2,1,0:T(8,128)}, f32[3,16,8,128]{3,2,1,0:T(8,128)S(1)}, u32[]{:S(2)}) copy-start(f32[3,16,8,128]{3,2,1,0:T(8,128)S(1)} %get-tuple-element.61.t) | copy-start | bytes 589828
  87.1 3.9 %collective-permute-start.15 = (f32[3,4,8,128]{3,2,1,0:T(8,128)S(1)}, f32[3,4,8,128]{3,2,1,0:T(8,128)S(1)}, u32[]{:S(2)}, u32[]{:S(2)}) collective-permute-start(f32[3,4,8,128]{3,2,1,0:T(8,128)S(1)} %get-tuple-element.63), channel_id=1, source_target_pairs={{0,1},{1,0},{2,3},{3,2},{4,5},{5,4},{6,7},{7,6},{8,9},{9,8},{10,11... | collective-permute-start | bytes 147464 | tf_op jit(solution)/shard_map/ppermute | solution.py:534
  87.2 4.5 %collective-permute-start.16 = (f32[3,4,8,128]{3,2,1,0:T(8,128)S(1)}, f32[3,4,8,128]{3,2,1,0:T(8,128)S(1)}, u32[]{:S(2)}, u32[]{:S(2)}) collective-permute-start(f32[3,4,8,128]{3,2,1,0:T(8,128)S(1)} %get-tuple-element.63), channel_id=1, source_target_pairs={{0,2},{1,3},{2,0},{3,1},{4,6},{5,7},{6,4},{7,5},{8,10},{9,11},{10,... | collective-permute-start | bytes 147464 | tf_op jit(solution)/shard_map/ppermute | solution.py:534
  88.5 4.2 %collective-permute-start.17 = (f32[3,4,8,128]{3,2,1,0:T(8,128)S(1)}, f32[3,4,8,128]{3,2,1,0:T(8,128)S(1)}, u32[]{:S(2)}, u32[]{:S(2)}) collective-permute-start(f32[3,4,8,128]{3,2,1,0:T(8,128)S(1)} %get-tuple-element.63), channel_id=1, source_target_pairs={{0,3},{1,2},{2,1},{3,0},{4,7},{5,6},{6,5},{7,4},{8,11},{9,10},{10,... | collective-permute-start | bytes 147464 | tf_op jit(solution)/shard_map/ppermute | solution.py:534
  92.7 7.4 %collective-permute-start.18 = (f32[12,4,8,128]{3,2,1,0:T(8,128)S(1)}, f32[12,4,8,128]{3,2,1,0:T(8,128)S(1)}, u32[]{:S(2)}, u32[]{:S(2)}) collective-permute-start(f32[12,4,8,128]{3,2,1,0:T(8,128)S(1)} %constant_dynamic-update-slice_fusion.12.own), channel_id=1, source_target_pairs={{0,4},{1,5},{2,6},{3,7},{4,0},{5,1},{6,2},{7,3},{8,12},{9,13},{10,... | collective-permute-start | bytes 589832 | tf_op jit(solution)/shard_map/ppermute | solution.py:534
  92.8 11.5 %collective-permute-start.19 = (f32[12,4,8,128]{3,2,1,0:T(8,128)S(1)}, f32[12,4,8,128]{3,2,1,0:T(8,128)S(1)}, u32[]{:S(2)}, u32[]{:S(2)}) collective-permute-start(f32[12,4,8,128]{3,2,1,0:T(8,128)S(1)} %constant_dynamic-update-slice_fusion.12.own), channel_id=1, source_target_pairs={{4,8},{5,9},{6,10},{7,11},{8,4},{9,5},{10,6},{11,7},{12,16},{13,17... | collective-permute-start | bytes 589832 | tf_op jit(solution)/shard_map/ppermute | solution.py:534
  105.4 20.7 %copy-start.9 = (f32[3,16,8,128]{3,2,1,0:T(8,128)}, f32[3,16,8,128]{3,2,1,0:T(8,128)S(1)}, u32[]{:S(2)}) copy-start(f32[3,16,8,128]{3,2,1,0:T(8,128)S(1)} %get-tuple-element.68.u) | copy-start | bytes 589828
  105.4 3.9 %collective-permute-start.20 = (f32[3,4,8,128]{3,2,1,0:T(8,128)S(1)}, f32[3,4,8,128]{3,2,1,0:T(8,128)S(1)}, u32[]{:S(2)}, u32[]{:S(2)}) collective-permute-start(f32[3,4,8,128]{3,2,1,0:T(8,128)S(1)} %get-tuple-element.69), channel_id=1, source_target_pairs={{0,1},{1,0},{2,3},{3,2},{4,5},{5,4},{6,7},{7,6},{8,9},{9,8},{10,11... | collective-permute-start | bytes 147464 | tf_op jit(solution)/shard_map/ppermute | solution.py:534
  105.6 5.5 %collective-permute-start.21 = (f32[3,4,8,128]{3,2,1,0:T(8,128)S(1)}, f32[3,4,8,128]{3,2,1,0:T(8,128)S(1)}, u32[]{:S(2)}, u32[]{:S(2)}) collective-permute-start(f32[3,4,8,128]{3,2,1,0:T(8,128)S(1)} %get-tuple-element.69), channel_id=1, source_target_pairs={{0,2},{1,3},{2,0},{3,1},{4,6},{5,7},{6,4},{7,5},{8,10},{9,11},{10,... | collective-permute-start | bytes 147464 | tf_op jit(solution)/shard_map/ppermute | solution.py:534
  109.1 4.2 %collective-permute-start.22 = (f32[3,4,8,128]{3,2,1,0:T(8,128)S(1)}, f32[3,4,8,128]{3,2,1,0:T(8,128)S(1)}, u32[]{:S(2)}, u32[]{:S(2)}) collective-permute-start(f32[3,4,8,128]{3,2,1,0:T(8,128)S(1)} %get-tuple-element.69), channel_id=1, source_target_pairs={{0,3},{1,2},{2,1},{3,0},{4,7},{5,6},{6,5},{7,4},{8,11},{9,10},{10,... | collective-permute-start | bytes 147464 | tf_op jit(solution)/shard_map/ppermute | solution.py:534
  113.3 7.3 %collective-permute-start.23 = (f32[12,4,8,128]{3,2,1,0:T(8,128)S(1)}, f32[12,4,8,128]{3,2,1,0:T(8,128)S(1)}, u32[]{:S(2)}, u32[]{:S(2)}) collective-permute-start(f32[12,4,8,128]{3,2,1,0:T(8,128)S(1)} %constant_dynamic-update-slice_fusion.16.own), channel_id=1, source_target_pairs={{0,4},{1,5},{2,6},{3,7},{4,0},{5,1},{6,2},{7,3},{8,12},{9,13},{10,... | collective-permute-start | bytes 589832 | tf_op jit(solution)/shard_map/ppermute | solution.py:534
  113.3 11.5 %collective-permute-start.24 = (f32[12,4,8,128]{3,2,1,0:T(8,128)S(1)}, f32[12,4,8,128]{3,2,1,0:T(8,128)S(1)}, u32[]{:S(2)}, u32[]{:S(2)}) collective-permute-start(f32[12,4,8,128]{3,2,1,0:T(8,128)S(1)} %constant_dynamic-update-slice_fusion.16.own), channel_id=1, source_target_pairs={{4,8},{5,9},{6,10},{7,11},{8,4},{9,5},{10,6},{11,7},{12,16},{13,17... | collective-permute-start | bytes 589832 | tf_op jit(solution)/shard_map/ppermute | solution.py:534
  151.2 0.9 copy-start.1
  152.1 0.9 copy-start.3
  153.1 0.9 copy-start.5
  154.0 1.4 copy-start.6
  155.4 0.9 copy-start.10
  206.3 35.8 %copy-start.8 = (f32[3,32,8,128]{3,2,1,0:T(8,128)S(1)}, f32[3,32,8,128]{3,2,1,0:T(8,128)}, u32[]{:S(2)}) copy-start(f32[3,32,8,128]{3,2,1,0:T(8,128)} %copy-done.7) | copy-start | bytes 1179652
  206.4 35.8 %copy-start.18 = (f32[3,32,128]{2,1,0:T(8,128)S(1)}, f32[3,32,128]{2,1,0:T(8,128)}, u32[]{:S(2)}) copy-start(f32[3,32,128]{2,1,0:T(8,128)} %copy-done.17) | copy-start | bytes 147460
  206.4 3.9 %collective-permute-start.25 = (f32[3,4,8,128]{3,2,1,0:T(8,128)S(1)}, f32[3,4,8,128]{3,2,1,0:T(8,128)S(1)}, u32[]{:S(2)}, u32[]{:S(2)}) collective-permute-start(f32[3,4,8,128]{3,2,1,0:T(8,128)S(1)} %get-tuple-element.75), channel_id=1, source_target_pairs={{0,1},{1,0},{2,3},{3,2},{4,5},{5,4},{6,7},{7,6},{8,9},{9,8},{10,11... | collective-permute-start | bytes 147464 | tf_op jit(solution)/shard_map/ppermute | solution.py:534
  206.7 4.8 %collective-permute-start.26 = (f32[3,4,8,128]{3,2,1,0:T(8,128)S(1)}, f32[3,4,8,128]{3,2,1,0:T(8,128)S(1)}, u32[]{:S(2)}, u32[]{:S(2)}) collective-permute-start(f32[3,4,8,128]{3,2,1,0:T(8,128)S(1)} %get-tuple-element.75), channel_id=1, source_target_pairs={{0,2},{1,3},{2,0},{3,1},{4,6},{5,7},{6,4},{7,5},{8,10},{9,11},{10,... | collective-permute-start | bytes 147464 | tf_op jit(solution)/shard_map/ppermute | solution.py:534
  208.9 4.8 %collective-permute-start.27 = (f32[3,4,8,128]{3,2,1,0:T(8,128)S(1)}, f32[3,4,8,128]{3,2,1,0:T(8,128)S(1)}, u32[]{:S(2)}, u32[]{:S(2)}) collective-permute-start(f32[3,4,8,128]{3,2,1,0:T(8,128)S(1)} %get-tuple-element.75), channel_id=1, source_target_pairs={{0,3},{1,2},{2,1},{3,0},{4,7},{5,6},{6,5},{7,4},{8,11},{9,10},{10,... | collective-permute-start | bytes 147464 | tf_op jit(solution)/shard_map/ppermute | solution.py:534
  213.7 4.5 %collective-permute-start.28 = (f32[12,4,8,128]{3,2,1,0:T(8,128)S(1)}, f32[12,4,8,128]{3,2,1,0:T(8,128)S(1)}, u32[]{:S(2)}, u32[]{:S(2)}) collective-permute-start(f32[12,4,8,128]{3,2,1,0:T(8,128)S(1)} %constant_dynamic-update-slice_fusion.20.own), channel_id=1, source_target_pairs={{0,4},{1,5},{2,6},{3,7},{4,0},{5,1},{6,2},{7,3},{8,12},{9,13},{10,... | collective-permute-start | bytes 589832 | tf_op jit(solution)/shard_map/ppermute | solution.py:534
  213.7 8.9 %collective-permute-start.29 = (f32[12,4,8,128]{3,2,1,0:T(8,128)S(1)}, f32[12,4,8,128]{3,2,1,0:T(8,128)S(1)}, u32[]{:S(2)}, u32[]{:S(2)}) collective-permute-start(f32[12,4,8,128]{3,2,1,0:T(8,128)S(1)} %constant_dynamic-update-slice_fusion.20.own), channel_id=1, source_target_pairs={{4,8},{5,9},{6,10},{7,11},{8,4},{9,5},{10,6},{11,7},{12,16},{13,17... | collective-permute-start | bytes 589832 | tf_op jit(solution)/shard_map/ppermute | solution.py:534
  223.7 3.9 %collective-permute-start.30 = (f32[3,4,8,128]{3,2,1,0:T(8,128)S(1)}, f32[3,4,8,128]{3,2,1,0:T(8,128)S(1)}, u32[]{:S(2)}, u32[]{:S(2)}) collective-permute-start(f32[3,4,8,128]{3,2,1,0:T(8,128)S(1)} %get-tuple-element.77), channel_id=1, source_target_pairs={{0,1},{1,0},{2,3},{3,2},{4,5},{5,4},{6,7},{7,6},{8,9},{9,8},{10,11... | collective-permute-start | bytes 147464 | tf_op jit(solution)/shard_map/ppermute | solution.py:534
  223.8 5.5 %collective-permute-start.31 = (f32[3,4,8,128]{3,2,1,0:T(8,128)S(1)}, f32[3,4,8,128]{3,2,1,0:T(8,128)S(1)}, u32[]{:S(2)}, u32[]{:S(2)}) collective-permute-start(f32[3,4,8,128]{3,2,1,0:T(8,128)S(1)} %get-tuple-element.77), channel_id=1, source_target_pairs={{0,2},{1,3},{2,0},{3,1},{4,6},{5,7},{6,4},{7,5},{8,10},{9,11},{10,... | collective-permute-start | bytes 147464 | tf_op jit(solution)/shard_map/ppermute | solution.py:534
  227.2 4.2 %collective-permute-start.32 = (f32[3,4,8,128]{3,2,1,0:T(8,128)S(1)}, f32[3,4,8,128]{3,2,1,0:T(8,128)S(1)}, u32[]{:S(2)}, u32[]{:S(2)}) collective-permute-start(f32[3,4,8,128]{3,2,1,0:T(8,128)S(1)} %get-tuple-element.77), channel_id=1, source_target_pairs={{0,3},{1,2},{2,1},{3,0},{4,7},{5,6},{6,5},{7,4},{8,11},{9,10},{10,... | collective-permute-start | bytes 147464 | tf_op jit(solution)/shard_map/ppermute | solution.py:534
  231.4 7.3 %collective-permute-start.33 = (f32[12,4,8,128]{3,2,1,0:T(8,128)S(1)}, f32[12,4,8,128]{3,2,1,0:T(8,128)S(1)}, u32[]{:S(2)}, u32[]{:S(2)}) collective-permute-start(f32[12,4,8,128]{3,2,1,0:T(8,128)S(1)} %constant_dynamic-update-slice_fusion.24.own), channel_id=1, source_target_pairs={{0,4},{1,5},{2,6},{3,7},{4,0},{5,1},{6,2},{7,3},{8,12},{9,13},{10,... | collective-permute-start | bytes 589832 | tf_op jit(solution)/shard_map/ppermute | solution.py:534
  231.4 10.8 %collective-permute-start.34 = (f32[12,4,8,128]{3,2,1,0:T(8,128)S(1)}, f32[12,4,8,128]{3,2,1,0:T(8,128)S(1)}, u32[]{:S(2)}, u32[]{:S(2)}) collective-permute-start(f32[12,4,8,128]{3,2,1,0:T(8,128)S(1)} %constant_dynamic-update-slice_fusion.24.own), channel_id=1, source_target_pairs={{4,8},{5,9},{6,10},{7,11},{8,4},{9,5},{10,6},{11,7},{12,16},{13,17... | collective-permute-start | bytes 589832 | tf_op jit(solution)/shard_map/ppermute | solution.py:534
  243.8 3.9 %collective-permute-start.35 = (f32[3,4,8,128]{3,2,1,0:T(8,128)S(1)}, f32[3,4,8,128]{3,2,1,0:T(8,128)S(1)}, u32[]{:S(2)}, u32[]{:S(2)}) collective-permute-start(f32[3,4,8,128]{3,2,1,0:T(8,128)S(1)} %get-tuple-element.79), channel_id=1, source_target_pairs={{0,1},{1,0},{2,3},{3,2},{4,5},{5,4},{6,7},{7,6},{8,9},{9,8},{10,11... | collective-permute-start | bytes 147464 | tf_op jit(solution)/shard_map/ppermute | solution.py:534
  243.9 4.5 %collective-permute-start.36 = (f32[3,4,8,128]{3,2,1,0:T(8,128)S(1)}, f32[3,4,8,128]{3,2,1,0:T(8,128)S(1)}, u32[]{:S(2)}, u32[]{:S(2)}) collective-permute-start(f32[3,4,8,128]{3,2,1,0:T(8,128)S(1)} %get-tuple-element.79), channel_id=1, source_target_pairs={{0,2},{1,3},{2,0},{3,1},{4,6},{5,7},{6,4},{7,5},{8,10},{9,11},{10,... | collective-permute-start | bytes 147464 | tf_op jit(solution)/shard_map/ppermute | solution.py:534
  245.5 4.2 %collective-permute-start.37 = (f32[3,4,8,128]{3,2,1,0:T(8,128)S(1)}, f32[3,4,8,128]{3,2,1,0:T(8,128)S(1)}, u32[]{:S(2)}, u32[]{:S(2)}) collective-permute-start(f32[3,4,8,128]{3,2,1,0:T(8,128)S(1)} %get-tuple-element.79), channel_id=1, source_target_pairs={{0,3},{1,2},{2,1},{3,0},{4,7},{5,6},{6,5},{7,4},{8,11},{9,10},{10,... | collective-permute-start | bytes 147464 | tf_op jit(solution)/shard_map/ppermute | solution.py:534
  249.7 7.7 %collective-permute-start.38 = (f32[12,4,8,128]{3,2,1,0:T(8,128)S(1)}, f32[12,4,8,128]{3,2,1,0:T(8,128)S(1)}, u32[]{:S(2)}, u32[]{:S(2)}) collective-permute-start(f32[12,4,8,128]{3,2,1,0:T(8,128)S(1)} %constant_dynamic-update-slice_fusion.28.own), channel_id=1, source_target_pairs={{0,4},{1,5},{2,6},{3,7},{4,0},{5,1},{6,2},{7,3},{8,12},{9,13},{10,... | collective-permute-start | bytes 589832 | tf_op jit(solution)/shard_map/ppermute | solution.py:534
  249.7 11.3 %collective-permute-start.39 = (f32[12,4,8,128]{3,2,1,0:T(8,128)S(1)}, f32[12,4,8,128]{3,2,1,0:T(8,128)S(1)}, u32[]{:S(2)}, u32[]{:S(2)}) collective-permute-start(f32[12,4,8,128]{3,2,1,0:T(8,128)S(1)} %constant_dynamic-update-slice_fusion.28.own), channel_id=1, source_target_pairs={{4,8},{5,9},{6,10},{7,11},{8,4},{9,5},{10,6},{11,7},{12,16},{13,17... | collective-permute-start | bytes 589832 | tf_op jit(solution)/shard_map/ppermute | solution.py:534
  262.6 3.9 %collective-permute-start.40 = (f32[3,4,8,128]{3,2,1,0:T(8,128)S(1)}, f32[3,4,8,128]{3,2,1,0:T(8,128)S(1)}, u32[]{:S(2)}, u32[]{:S(2)}) collective-permute-start(f32[3,4,8,128]{3,2,1,0:T(8,128)S(1)} %get-tuple-element.81), channel_id=1, source_target_pairs={{0,1},{1,0},{2,3},{3,2},{4,5},{5,4},{6,7},{7,6},{8,9},{9,8},{10,11... | collective-permute-start | bytes 147464 | tf_op jit(solution)/shard_map/ppermute | solution.py:534
  262.7 5.4 %collective-permute-start.41 = (f32[3,4,8,128]{3,2,1,0:T(8,128)S(1)}, f32[3,4,8,128]{3,2,1,0:T(8,128)S(1)}, u32[]{:S(2)}, u32[]{:S(2)}) collective-permute-start(f32[3,4,8,128]{3,2,1,0:T(8,128)S(1)} %get-tuple-element.81), channel_id=1, source_target_pairs={{0,2},{1,3},{2,0},{3,1},{4,6},{5,7},{6,4},{7,5},{8,10},{9,11},{10,... | collective-permute-start | bytes 147464 | tf_op jit(solution)/shard_map/ppermute | solution.py:534
  266.1 4.2 %collective-permute-start.42 = (f32[3,4,8,128]{3,2,1,0:T(8,128)S(1)}, f32[3,4,8,128]{3,2,1,0:T(8,128)S(1)}, u32[]{:S(2)}, u32[]{:S(2)}) collective-permute-start(f32[3,4,8,128]{3,2,1,0:T(8,128)S(1)} %get-tuple-element.81), channel_id=1, source_target_pairs={{0,3},{1,2},{2,1},{3,0},{4,7},{5,6},{6,5},{7,4},{8,11},{9,10},{10,... | collective-permute-start | bytes 147464 | tf_op jit(solution)/shard_map/ppermute | solution.py:534
  270.3 7.3 %collective-permute-start.43 = (f32[12,4,8,128]{3,2,1,0:T(8,128)S(1)}, f32[12,4,8,128]{3,2,1,0:T(8,128)S(1)}, u32[]{:S(2)}, u32[]{:S(2)}) collective-permute-start(f32[12,4,8,128]{3,2,1,0:T(8,128)S(1)} %constant_dynamic-update-slice_fusion.32.own), channel_id=1, source_target_pairs={{0,4},{1,5},{2,6},{3,7},{4,0},{5,1},{6,2},{7,3},{8,12},{9,13},{10,... | collective-permute-start | bytes 589832 | tf_op jit(solution)/shard_map/ppermute | solution.py:534
  270.3 10.8 %collective-permute-start.44 = (f32[12,4,8,128]{3,2,1,0:T(8,128)S(1)}, f32[12,4,8,128]{3,2,1,0:T(8,128)S(1)}, u32[]{:S(2)}, u32[]{:S(2)}) collective-permute-start(f32[12,4,8,128]{3,2,1,0:T(8,128)S(1)} %constant_dynamic-update-slice_fusion.32.own), channel_id=1, source_target_pairs={{4,8},{5,9},{6,10},{7,11},{8,4},{9,5},{10,6},{11,7},{12,16},{13,17... | collective-permute-start | bytes 589832 | tf_op jit(solution)/shard_map/ppermute | solution.py:534
  (5 other events, 3.4 us)
Sparse Core Ops, SparseCore 0:
  19.9 69.0 all-gather.2

commit v2 on v1

v2 whole, which is shorter than its diff:
```python
import functools

import jax
import jax.numpy as jnp
from jax import lax
from jax.experimental import pallas as pl
from jax.experimental.pallas import tpu as pltpu
from jax.sharding import PartitionSpec as P

AX = ("gx", "gy")
DEVICES = 128
SLOTS = 3
BOTTOM_ITERS = 8
RELAXATION = 2.0 / 3.0
F32 = jnp.float32
I32 = jnp.int32

PLANES = (32, 16)


def iota(shape, dim):
    return lax.broadcasted_iota(I32, shape, dim)


def lanes():
    return iota((8, 128), 1)


def subs():
    return iota((8, 128), 0)


def roll(x, shift, axis):
    return pltpu.roll(x, shift, axis)


def lane_take(x, at):
    return jnp.take_along_axis(x, at, axis=1, mode="promise_in_bounds")


class Tile:
    def __init__(self, lv):
        self.zs, self.ys = 1 << lv, 32 << lv
        lane, sub = lanes(), subs()
        self.south_in = lane >= self.ys
        self.north_in = lane < 128 - self.ys
        self.first_row = sub == 0
        self.last_row = sub == 7
        self.south_edge = self.first_row & (lane < self.ys)
        self.z_low = (lane & 31) < self.zs

    def south(self, v, row):
        r = roll(v, self.ys, 1)
        return jnp.where(self.south_in, r, jnp.where(self.first_row, row, roll(r, 1, 0)))

    def north(self, v, edge):
        r = roll(v, 128 - self.ys, 1)
        return jnp.where(self.north_in, r, jnp.where(self.last_row, edge, roll(r, 7, 0)))

    def below(self, v):
        return roll(v, self.zs, 1)

    def above(self, v):
        return roll(v, 128 - self.zs, 1)


def pair_sum(t, lv):
    lane = lanes()
    zs, ys = 1 << lv, 32 << lv
    t = t + jnp.where((lane & zs) == 0, roll(t, 128 - zs, 1), roll(t, zs, 1))
    return t + jnp.where((lane & ys) == 0, roll(t, 128 - ys, 1), roll(t, ys, 1))


BOXES = 36
TWO_FACES = ((0, 2), (0, 3), (1, 2), (1, 3), (2, 0), (2, 1), (3, 0), (3, 1))


class Part:
    def __init__(self, lv, own=0, side=0):
        self.lv, self.own, self.side = lv, own, side
        self.tiles = (8, 3)[lv]
        self.ys = (4, 1)[lv]
        self.own_tiles = SLOTS * self.tiles
        self.side_tiles = (42, 18)[lv]


def pack_faces(v, s, part, out):
    lv = part.lv
    n = PLANES[lv]
    base = part.own + s * part.tiles
    planes = [v[s, 0], v[s, 1], v[s, n - 2], v[s, n - 1]]
    y0 = v[s, :, 0, :]
    y7 = v[s, :, 7, :]
    lane = iota((n, 128), 1)
    if lv == 0:
        for m in range(4):
            out[base + m] = planes[m]
        q = roll(jnp.where(lane >= 64, y7, y0), 64, 1)
    else:
        odd_k, odd_j = (lanes() & 1) == 1, (lanes() & 32) == 32
        out[base] = jnp.where(
            odd_k, jnp.where(odd_j, planes[3], planes[2]), jnp.where(odd_j, planes[1], planes[0])
        )
        q = jnp.where(
            lane < 32, y7, jnp.where(lane < 64, roll(y7, 96, 1), jnp.where(lane < 96, roll(y0, 64, 1), y0))
        )
    for t in range(n // 8):
        out[base + part.ys + t] = q[8 * t : 8 * t + 8]


def k_relay(parts, notes, par, *refs):
    got, (near, far) = refs[:4], refs[4:]
    even = par[0] == 1
    place = par[1]

    def of(m, t):
        low = jnp.where((m & 1) == 0, got[0][t], got[1][t])
        high = jnp.where((m & 1) == 0, got[2][t], got[3][t])
        return jnp.where(m < 2, low, high)

    def put(at, fwd, bwd):
        near[at] = jnp.where(even, fwd, bwd)
        far[at] = jnp.where(even, bwd, fwd)

    for part in parts:
        for s in range(SLOTS):
            base = part.own + s * part.tiles
            for m in range(4):
                box = m * SLOTS + s
                if part.lv == 0:
                    for x in range(2):
                        put(part.side + box * 2 + x, got[m][base + 2 + x], got[m][base + x])
                else:
                    put(part.side + box, got[m][base], got[m][base])
            if part.lv == 0:
                for x in range(2):
                    put(part.side + 24 + s * 6 + x, of(place ^ 3, base + x), of(place, base + 2 + x))
            for t in range(part.tiles - part.ys):
                at = part.side + (24 + s * 6 + 2 + t if part.lv == 0 else 12 + s * 2 + t)
                put(at, of(place ^ 3, base + part.ys + t), of(place, base + part.ys + t))
    if notes:
        own, side = notes
        for m in range(4):
            near[side + m] = got[m][own]
            far[side + m] = got[m][own]


def pick(tab, win, k, own, side):
    r = tab[k]
    low = jnp.where((r & 1) == 0, win[0][own], win[1][own])
    high = jnp.where((r & 1) == 0, win[2][own], win[3][own])
    beside = jnp.where((r & 1) == 0, win[4][side], win[5][side])
    return jnp.where(r < 4, jnp.where(r < 2, low, high), beside)


def pick_plane(tab, win, k, part, p):
    slot, m, delta = tab[BOXES + k], tab[2 * BOXES + k], tab[3 * BOXES + k]
    own = part.own + slot * part.tiles
    box = m * SLOTS + slot
    if part.lv == 0:
        x = p & 1
        direct = -1 if p >= 2 else 1
        side = part.side + jnp.where(delta == direct, box * 2 + x, 24 + slot * 6 + x)
        return pick(tab, win, k, own + p, side)
    lane = lanes()
    t = pick(tab, win, k, own, part.side + box)
    t = jnp.where(((lane & 1) == p >> 1) & ((lane & 32) == (p & 1) * 32), t, 0.0)
    return pair_sum(t, 0)


def pick_rows(tab, win, k, part, t):
    slot = tab[BOXES + k]
    own = part.own + slot * part.tiles + part.ys + t
    side = part.side + (24 + slot * 6 + 2 + t if part.lv == 0 else 12 + slot * 2 + t)
    return pick(tab, win, k, own, side)


def near_rows(y):
    lane = iota(y.shape, 1)
    return jnp.where(lane < 32, roll(y, 96, 1), jnp.where(lane < 96, y, roll(y, 32, 1)))


def take_ghosts(tab, win, part, xg, yg, ends):
    ys = 32 << part.lv
    low = iota((1, 128), 1) < 64
    for s in range(SLOTS):
        for g, (f, p) in enumerate(((0, 2), (0, 3), (1, 0), (1, 1))):
            xg[s, g] = pick_plane(tab, win, s * 4 + f, part, p)
        for t in range(part.tiles - part.ys):
            sv = pick_rows(tab, win, s * 4 + 2, part, t)
            nv = pick_rows(tab, win, s * 4 + 3, part, t)
            yg[s, 8 * t : 8 * t + 8, :] = jnp.where(lanes() < 64, sv, nv)

        def corner(q, p):
            return pick_plane(tab, win, 12 + s * 8 + q, part, p)

        for e, p in ((0, 3), (1, 0)):
            sp = corner(2 * e, p)[7:8]
            np = corner(2 * e + 1, p)[0:1]
            ends[s, e : e + 1, :] = jnp.where(low, roll(sp, ys, 1), roll(np, 128 - ys, 1))
            sp = corner(4 + e, p)[7:8]
            np = corner(6 + e, p)[0:1]
            ends[s, 2 + e : 3 + e, :] = jnp.where(low, roll(sp, 64, 1), roll(np, 64, 1))


def set_near(yg, gy, n):
    for s in range(SLOTS):
        for t in range(n // 8):
            gy[s, 8 * t : 8 * t + 8, :] = near_rows(yg[s, 8 * t : 8 * t + 8, :])


def planes_loop(n, body, carry, unroll=8):
    def chunk(c, carry):
        for u in range(unroll):
            carry = body(c * unroll + u, carry, u == unroll - 1)
        return carry

    return lax.fori_loop(0, n // unroll, chunk, carry)


def following(ref, s, i, n, edge, at_end):
    if not at_end:
        return ref[s, i + 1]
    return jnp.where(i == n - 1, edge, ref[s, jnp.minimum(i + 1, n - 1)])


def slab_sides(y, v, s, ends, n):
    lane = iota((n, 128), 1)
    row = iota((n, 128), 0)
    inner = jnp.where(lane < 64, roll(v[s, :, 0, :], 32, 1), roll(v[s, :, 7, :], 96, 1))
    outer = jnp.where(lane < 64, roll(y, 32, 1), roll(y, 96, 1))
    down = jnp.where(row == 0, ends[s, 2:3, :], roll(y, 1, 0))
    up = jnp.where(row == n - 1, ends[s, 3:4, :], roll(y, n - 1, 0))
    return outer, inner, down, up


def make_weights(b, xg, yg, ends, gy, tab, lv, w, extra):
    cx, cy, cz, wn, rd, slab = w
    n = PLANES[lv]
    h = 0.5 * 0.25**lv
    tl = Tile(lv)
    set_near(yg, gy, n)

    def has(k):
        return jnp.where(tab[4 * BOXES + k] == 1, 1.0, 0.0)

    def plane(s, i, here, w, nxt, wnext, row, south, north):
        wy = h * (here + tl.south(here, row))
        wy = jnp.where(tl.south_edge, wy * south, wy)
        wrow = h * (here + row) * north
        wz = jnp.where(tl.z_low, 0.0, h * (here + tl.below(here)))
        d = (w + wnext) + (wy + tl.north(wy, wrow)) + (wz + tl.above(wz))
        r = RELAXATION / d
        cx[s, i + 2] = wnext
        cy[s, i + 1] = wy
        cz[s, i + 1] = wz
        wn[s, pl.ds(i + 1, 1), :] = wrow[7:8, :]
        rd[s, i + 1] = r
        return r

    first = []
    for s in range(SLOTS):
        here, v = xg[s, 1], b[s, 0]
        w = h * (here + xg[s, 0])
        cx[s, 0] = w
        wnext = h * (here + v) * has(s * 4)
        plane(s, -1, here, w, v, wnext, ends[s, 0:1, :], has(12 + s * 8), has(13 + s * 8))
        first.append((v, wnext))

    def body(i, carry, at_end):
        out = []
        for s in range(SLOTS):
            v, w = carry[s]
            nxt = following(b, s, i, n, xg[s, 2], at_end)
            wnext = h * (v + nxt)
            if at_end:
                wnext = wnext * jnp.where(i == n - 1, has(s * 4 + 1), 1.0)
            r = plane(s, i, v, w, nxt, wnext, gy[s, pl.ds(i, 1), :], has(s * 4 + 2), has(s * 4 + 3))
            extra(s, i, r)
            out.append((nxt, wnext))
        return tuple(out)

    last = planes_loop(n, body, tuple(first))
    lane = iota((n, 128), 1)
    row = iota((n, 128), 0)
    for s in range(SLOTS):
        here, w = last[s]
        far = xg[s, 3]
        plane(s, n, here, w, far, h * (here + far), ends[s, 1:2, :], has(14 + s * 8), has(15 + s * 8))
        y = yg[s]
        outer, inner, down, up = (h * (y + t) for t in slab_sides(y, b, s, ends, n))
        k = 12 + s * 8
        down = down * jnp.where(row == 0, jnp.where(lane < 64, has(k + 4), has(k + 6)), 1.0)
        up = up * jnp.where(row == n - 1, jnp.where(lane < 64, has(k + 5), has(k + 7)), 1.0)
        zs = tl.zs
        wz = jnp.where((lane & 31) < zs, 0.0, h * (y + roll(y, zs, 1)))
        d = (outer + inner) + (down + up) + (wz + roll(wz, 128 - zs, 1))
        for m, t in enumerate((outer, inner, down, up, wz, RELAXATION / d)):
            slab[s, m] = t


def apply_level(v, before, after, gy, ends, lv, w, emit, wide=None):
    cx, cy, cz, wn = w[:4]
    n = PLANES[lv]
    tl = Tile(lv)

    def plane(s, i, here, fx, nxt, row):
        fnext = cx[s, i + 2] * (nxt - here)
        wrow = wn[s, pl.ds(i + 1, 1), :]
        fy = cy[s, i + 1] * (here - tl.south(here, row))
        fn = tl.north(fy, wrow * (row - here))
        fz = cz[s, i + 1] * (here - tl.below(here))
        return (fx - fnext) + (fy - fn) + (fz - tl.above(fz)), fnext

    first = []
    for s in range(SLOTS):
        v0, west = v[s, 0], before(s, 0)
        if wide:
            fx = cx[s, 0] * (west - before(s, 1))
            av, fx = plane(s, -1, west, fx, v0, ends[s, 0:1, :])
            wide(s, 0, west, av)
        else:
            fx = cx[s, 1] * (v0 - west)
        first.append((v0, fx))

    def body(i, carry, at_end):
        out = []
        for s in range(SLOTS):
            here, fx = carry[s]
            nxt = following(v, s, i, n, after(s, 0), at_end)
            av, fnext = plane(s, i, here, fx, nxt, gy[s, pl.ds(i, 1), :])
            emit(s, i, here, av)
            out.append((nxt, fnext))
        return tuple(out)

    last = planes_loop(n, body, tuple(first))
    if wide:
        for s in range(SLOTS):
            here, fx = last[s]
            av, fx = plane(s, n, here, fx, after(s, 1), ends[s, 1:2, :])
            wide(s, 1, here, av)


def apply_slab(yg, v, s, ends, lv, slab):
    n = PLANES[lv]
    zs = 1 << lv
    y = yg[s]
    outer, inner, down, up = slab_sides(y, v, s, ends, n)
    fz = slab[s, 4] * (y - roll(y, zs, 1))
    a = slab[s, 0] * (y - outer) + slab[s, 1] * (y - inner)
    b = slab[s, 2] * (y - down) + slab[s, 3] * (y - up)
    return y, a + b + (fz - roll(fz, 128 - zs, 1))


def sweep_wide(v, xg, yg, ends, gy, lv, w, first, first_x, first_y, out, out_x, out_y):
    rd, slab = w[4:]
    n = PLANES[lv]
    set_near(yg, gy, n)

    def emit(s, i, here, av):
        out[s, i] = here + (first[s, i] - av * rd[s, i + 1])

    def wide(s, e, here, av):
        out_x[s, e] = here + (first_x(s, e) - av * rd[s, (n + 1) * e])

    apply_level(v, lambda s, g: xg[s, 1 - g], lambda s, g: xg[s, 2 + g], gy, ends, lv, w, emit, wide)
    for s in range(SLOTS):
        y, a = apply_slab(yg, v, s, ends, lv, slab)
        out_y[s] = y + (first_y(s) - a * slab[s, 5])


def apply_near(v, gx, yg, gy, lv, w, emit):
    set_near(yg, gy, PLANES[lv])
    apply_level(v, lambda s, g: gx[s, 0], lambda s, g: gx[s, 1], gy, None, lv, w, emit)


def restrict_planes(v, s, lv, scale):
    out = []
    for c in range(PLANES[lv] // 2):
        out.append(pair_sum(v[s, 2 * c] + v[s, 2 * c + 1], lv) * scale)
    return out


def pack_bottom(planes, out):
    lane = lanes()
    at = (lane & 7) * 4
    part = lane >> 3
    top = None
    for s in range(2):
        for i in range(8):
            g = lane_take(planes[s][i], at)
            top = g if top is None else jnp.where(part == s * 8 + i, g, top)
    low = None
    for i in range(8):
        g = lane_take(planes[2][i], at)
        low = g if low is None else jnp.where((part & 7) == i, g, low)
    low = jnp.where(lane < 64, low, roll(low, 4, 0))
    out[0:8, :] = top
    out[8:12, :] = low[0:4]


PART0, PART1 = Part(0), Part(1)
FIRST = (Part(0), Part(1, 24, 42))
FIRST_NOTES = (33, 60)


def k_start(mask, src, inv, note, codes, s_out, b_out, b1_out, faces, gathered):
    bottom = []
    for s in range(SLOTS):
        s_out[s] = src[:, s, :].reshape(32, 8, 128) * mask[s]
        b_out[s] = inv[:, s, :].reshape(32, 8, 128)
        for c, t in enumerate(restrict_planes(b_out, s, 0, 0.125)):
            b1_out[s, c] = t
        bottom.append(restrict_planes(b1_out, s, 1, 0.125))
        pack_faces(b_out, s, FIRST[0], faces)
        pack_faces(b1_out, s, FIRST[1], faces)
    faces[FIRST_NOTES[0]] = jnp.broadcast_to(codes[...], (8, 128))
    pack_bottom(bottom, gathered)
    gathered[12:24, :] = jnp.zeros((12, 128), F32)
    gathered[12:13, :] = note[...]


def fill_table(par, notes, tab):
    even, place, block = par[0], par[1], par[2]

    def entry(k, code):
        owner = code >> 2
        delta = jnp.where(code >= 0, (owner >> 2) - block, 0)
        m = jnp.where(code >= 0, (owner & 3) ^ place, 0)
        slot = jnp.where(code >= 0, code & 3, 0)
        r = jnp.where(delta == 0, m, jnp.where(delta == 2 * even - 1, 4, 5))
        for x, value in enumerate((r, slot, m, delta, jnp.where(code >= 0, 1, 0))):
            tab[x * BOXES + k] = value
        return (jnp.where(r < 4, 0, r - 3) * 4 + m) * 12 + slot * 4

    for s in range(SLOTS):
        codes = [notes[s * 4 + f] for f in range(4)]
        rows = [entry(s * 4 + f, codes[f]) for f in range(4)]
        for q, (f, g) in enumerate(TWO_FACES):
            entry(12 + s * 8 + q, jnp.where(codes[f] >= 0, notes[rows[f] + g], -1))


def k_weights(par, notes, s_in, b, b1, *refs):
    win, refs = refs[:6], refs[6:]
    w, u, w1, faces, tab, (xg, yg, ends, gy, xg1, yg1, ends1, gy1) = (
        refs[:6], refs[6], refs[7:13], refs[13], refs[14], refs[15:]
    )
    fill_table(par, notes, tab)
    take_ghosts(tab, win, FIRST[0], xg, yg, ends)
    take_ghosts(tab, win, FIRST[1], xg1, yg1, ends1)

    def first(s, i, r):
        u[s, i] = s_in[s, i] * r

    make_weights(b, xg, yg, ends, gy, tab, 0, w, first)
    make_weights(b1, xg1, yg1, ends1, gy1, tab, 1, w1, lambda s, i, r: None)
    for s in range(SLOTS):
        pack_faces(u, s, PART0, faces)


def k_down(tab, t, u, *refs):
    win, w, rd1 = refs[:6], refs[6:12], refs[12]
    out, out_x, out_y, first_x, first_y, f1, u1, faces, xg, yg, ends, gy, res = refs[13:]
    take_ghosts(tab, win, PART0, xg, yg, ends)
    for s in range(SLOTS):
        for e in range(2):
            first_x[s, e] = xg[s, 1 + e]
        first_y[s] = yg[s]
    sweep_wide(u, xg, yg, ends, gy, 0, w, u, lambda s, e: xg[s, 1 + e], lambda s: yg[s], out, out_x, out_y)

    def emit(s, i, here, av):
        res[s, i] = t[s, i] - av

    apply_near(out, out_x, out_y, gy, 0, w, emit)
    for s in range(SLOTS):
        for c, p in enumerate(restrict_planes(res, s, 0, 0.125)):
            f1[s, c] = p
            u1[s, c] = p * rd1[s, c + 1]
        pack_faces(u1, s, PART1, faces)


def k_bottom_rhs(tab, t, u, *refs):
    win, w = refs[:6], refs[6:12]
    out, out_x, out_y, first_x, first_y, packed, xg, yg, ends, gy, res = refs[12:]
    take_ghosts(tab, win, PART1, xg, yg, ends)
    for s in range(SLOTS):
        for e in range(2):
            first_x[s, e] = xg[s, 1 + e]
        first_y[s] = yg[s]
    sweep_wide(u, xg, yg, ends, gy, 1, w, u, lambda s, e: xg[s, 1 + e], lambda s: yg[s], out, out_x, out_y)

    def emit(s, i, here, av):
        res[s, i] = t[s, i] - av

    apply_near(out, out_x, out_y, gy, 1, w, emit)
    pack_bottom([restrict_planes(res, s, 1, 0.125) for s in range(SLOTS)], packed)


def total(v):
    return jnp.sum(v, axis=(0, 1), keepdims=True)


def unpack_bottom(rows, put):
    for r in range(12):
        t = rows[:, r, :].T
        for half in range(2):
            s, j = (half, r) if r < 8 else (2, r - 8 + 4 * half)
            for i in range(8):
                put(s, j, i, t[half * 64 + i * 8 : half * 64 + i * 8 + 8, :])


def face_gather(v, dev_at, slot_at, place, s):
    out = lane_take(place(0), dev_at)
    for other in range(1, SLOTS):
        g = lane_take(place(other), dev_at)
        out = jnp.where(slot_at == other, g, out)
    return out


def k_bottom(place, first, u, gx0, gy0, *refs):
    w1, (beta_rows, rhs_rows) = refs[:6], refs[6:8]
    out, faces, boxes_out, p, r, x, q, cx, cy, cz, back, sq, v1, gx, yg, gy = refs[8:]
    note = beta_rows[:, 12, :].T
    at, slot, pres = [], [], []
    for f in range(12):
        gf = jnp.broadcast_to(note[f : f + 1, :], (8, 128))
        has = gf >= 0.0
        gf = jnp.where(has, gf, 0.0)
        dv = ((gf + 0.5) * (1.0 / 3.0)).astype(I32)
        at.append(dv)
        slot.append(gf.astype(I32) - 3 * dv)
        pres.append(jnp.where(has, 1.0, 0.0))
    counts = note[12:13, :]
    boxes = jnp.sum(counts, axis=1, keepdims=True)
    boxes_out[...] = jnp.broadcast_to(boxes, (8, 128))

    def fill_ghosts():
        def along(m, _):
            for s in range(SLOTS):
                for f, (src, dst) in enumerate(((7, 0), (0, 9))):
                    k = s * 4 + f
                    p[s, m + 1, dst] = face_gather(p, at[k], slot[k], lambda o: p[o, m + 1, src + 1], s)
                for f, (src, dst) in enumerate(((7, 0), (0, 9))):
                    k = s * 4 + 2 + f
                    p[s, dst, m + 1] = face_gather(p, at[k], slot[k], lambda o: p[o, src + 1, m + 1], s)
            return 0

        lax.fori_loop(0, 8, along, 0)

    def put_beta(s, j, i, tile):
        p[s, j + 1, i + 1] = tile

    unpack_bottom(beta_rows, put_beta)
    fill_ghosts()
    h = 0.5 * 0.0625
    low = subs() == 0

    def weights(m, _):
        for s in range(SLOTS):
            for i in range(9):
                w = h * (p[s, m + 1, i] + p[s, m + 1, i + 1])
                if i == 0:
                    w = w * pres[s * 4]
                if i == 8:
                    w = w * pres[s * 4 + 1]
                cx[s, m, i] = w
                w = h * (p[s, i, m + 1] + p[s, i + 1, m + 1])
                if i == 0:
                    w = w * pres[s * 4 + 2]
                if i == 8:
                    w = w * pres[s * 4 + 3]
                cy[s, i, m] = w
            for i in range(8):
                b = p[s, m + 1, i + 1]
                cz[s, m, i] = jnp.where(low, 0.0, h * (b + roll(b, 1, 0)))
        return 0

    lax.fori_loop(0, 8, weights, 0)

    def put_rhs(s, j, i, tile):
        r[s, j, i] = tile

    unpack_bottom(rhs_rows, put_rhs)

    def each(fn, init):
        def step(j, acc):
            for s in range(SLOTS):
                for i in range(8):
                    acc = fn(s, j, i, acc)
            return acc

        return lax.fori_loop(0, 8, step, init)

    zero = jnp.zeros((8, 128), F32)
    mean = total(each(lambda s, j, i, acc: acc + r[s, j, i], zero)) / (boxes * 512.0)
    valid = [jnp.where(jnp.broadcast_to(counts, (8, 128)) > s + 0.5, 1.0, 0.0) for s in range(SLOTS)]

    def shift(s, j, i, acc):
        v = (r[s, j, i] - mean) * valid[s]
        r[s, j, i] = v
        p[s, j + 1, i + 1] = v
        x[s, j, i] = zero
        return acc + v * v

    rr = total(each(shift, zero))

    def image(s, j, i, acc):
        here = p[s, j + 1, i + 1]
        a = cx[s, j, i] * (here - p[s, j + 1, i]) + cx[s, j, i + 1] * (here - p[s, j + 1, i + 2])
        b = cy[s, j, i] * (here - p[s, j, i + 1]) + cy[s, j + 1, i] * (here - p[s, j + 2, i + 1])
        fz = cz[s, j, i] * (here - roll(here, 1, 0))
        v = a + b + (fz - roll(fz, 7, 0))
        q[s, j, i] = v
        return acc + here * v

    def iteration(it, rr):
        fill_ghosts()
        alpha = rr / total(each(image, zero))

        def step(s, j, i, acc):
            x[s, j, i] = x[s, j, i] + alpha * p[s, j + 1, i + 1]
            v = r[s, j, i] - alpha * q[s, j, i]
            r[s, j, i] = v
            return acc + v * v

        rr_next = total(each(step, zero))
        ratio = rr_next / rr

        def turn(s, j, i, acc):
            p[s, j + 1, i + 1] = r[s, j, i] + ratio * p[s, j + 1, i + 1]
            return acc

        each(turn, 0)
        return rr_next

    rr = lax.fori_loop(0, BOTTOM_ITERS - 1, iteration, rr)
    fill_ghosts()
    alpha = rr / total(each(image, zero))

    def last(s, j, i, acc):
        x[s, j, i] = x[s, j, i] + alpha * p[s, j + 1, i + 1]
        return acc

    each(last, 0)

    for row in range(12):
        for half in range(2):
            s, j = (half, row) if row < 8 else (2, row - 8 + 4 * half)
            for i in range(8):
                sq[half * 64 + i * 8 : half * 64 + i * 8 + 8, :] = x[s, j, i]
        tr = sq[...].T
        if row < 8:
            back[:, row, :] = tr
            back[:, 8 + row, :] = roll(tr, 64, 1)
        else:
            back[:, 8 + row, :] = tr
            back[:, 12 + row, :] = roll(tr, 64, 1)

    lane, sub = lanes(), subs()
    kat = (lane & 31) >> 2

    def box(dev, s):
        return back[dev, pl.ds(pl.multiple_of(8 * s, 8), 8), :]

    for s in range(SLOTS):
        mine = box(place[24], s)
        for i in range(8):
            g = lane_take(mine, kat + i * 8)
            v1[s, 2 * i] = u[s, 2 * i] + g
            v1[s, 2 * i + 1] = u[s, 2 * i + 1] + g
        near = [box(place[s * 4 + f], place[12 + s * 4 + f]) for f in range(4)]
        for f, i in ((0, 7), (1, 0)):
            gx[s, f] = gx0[s, f] + lane_take(near[f], kat + i * 8)
        sb = jnp.broadcast_to(near[2][7:8, :], (8, 128))
        nb = jnp.broadcast_to(near[3][0:1, :], (8, 128))
        for part in range(2):
            idx = kat + (part * 4 + (sub >> 1)) * 8
            g = jnp.where(lane < 64, lane_take(sb, idx), lane_take(nb, idx))
            yg[s, 8 * part : 8 * part + 8, :] = gy0[s, 8 * part : 8 * part + 8, :] + g

    def emit(s, i, here, av):
        out[s, i] = here + (first[s, i] - av * w1[4][s, i + 1])

    apply_near(v1, gx, yg, gy, 1, w1, emit)
    for s in range(SLOTS):
        pack_faces(out, s, PART1, faces)


def k_up(tab, first1, first1_x, first1_y, u1, first, u0, u0_x, u0_y, *refs):
    win, w1, w = refs[:6], refs[6:12], refs[12:18]
    out, faces, c, c_x, c_y, xg, yg, ends, gy1, v, gx, y0, gy = refs[18:]
    take_ghosts(tab, win, PART1, xg, yg, ends)
    sweep_wide(u1, xg, yg, ends, gy1, 1, w1, first1, lambda s, e: first1_x[s, e], lambda s: first1_y[s], c, c_x, c_y)
    for s in range(SLOTS):
        for f in range(2):
            gx[s, f] = u0_x[s, f] + c_x[s, f]
        for i in range(16):
            t = c[s, i]
            v[s, 2 * i] = u0[s, 2 * i] + t
            v[s, 2 * i + 1] = u0[s, 2 * i + 1] + t
            y0[s, 2 * i : 2 * i + 2, :] = u0_y[s, 2 * i : 2 * i + 2, :] + c_y[s, i : i + 1, :]

    def emit(s, i, here, av):
        out[s, i] = here + (first[s, i] - av * w[4][s, i + 1])

    apply_near(v, gx, y0, gy, 0, w, emit)
    for s in range(SLOTS):
        pack_faces(out, s, PART0, faces)


def k_residual(tab, t, u, first, first_x, first_y, *refs):
    win, w = refs[:6], refs[6:12]
    out, res_out, sums, out_x, out_y, xg, yg, ends, gy, res = refs[12:]
    take_ghosts(tab, win, PART0, xg, yg, ends)
    sweep_wide(u, xg, yg, ends, gy, 0, w, first, lambda s, e: first_x[s, e], lambda s: first_y[s], out, out_x, out_y)

    def emit(s, i, here, av):
        res[s, i] = t[s, i] - av

    apply_near(out, out_x, out_y, gy, 0, w, emit)
    su = jnp.zeros((8, 128), F32)
    sr = jnp.zeros((8, 128), F32)
    for s in range(SLOTS):
        for i in range(32):
            d = res[s, i]
            sr = sr + d * d
            su = su + out[s, i]
        res_out[:, s, :] = res[s].reshape(256, 128)
    lane = iota((1, 128), 1)
    sums[...] = jnp.where(lane == 0, total(su), jnp.where(lane == 1, total(sr), 0.0))


def k_finish(mask, u, sums, boxes, corr, norm):
    tot = jnp.sum(sums[...], axis=0, keepdims=True)
    cells = boxes[0:1, 0:1] * 32768.0
    mean = tot[:, 0:1] / cells
    for s in range(SLOTS):
        corr[:, s, :] = ((u[s] - mean) * mask[s]).reshape(256, 128)
    norm[...] = jnp.broadcast_to(jnp.sqrt(tot[:, 1:2] / cells), (1, 128))


VMEM = pl.BlockSpec(memory_space=pltpu.VMEM)
SMEM = pl.BlockSpec(memory_space=pltpu.SMEM)


def call(kernel, smem, args, outs, scratch=(), vmem=24, tables=()):
    shape = lambda s: jax.ShapeDtypeStruct(s, F32)
    return pl.pallas_call(
        kernel,
        out_shape=[shape(s) for s in outs] + [jax.ShapeDtypeStruct(s, I32) for s in tables],
        in_specs=[SMEM] * smem + [VMEM] * (len(args) - smem),
        out_specs=[VMEM] * len(outs) + [SMEM] * len(tables),
        scratch_shapes=[pltpu.VMEM(s, F32) for s in scratch],
        compiler_params=pltpu.CompilerParams(vmem_limit_bytes=vmem * 1024 * 1024),
    )(*args)


def swapped(block, pairs):
    route = sorted([(a, b) for a, b in pairs] + [(b, a) for a, b in pairs])
    return lax.ppermute(block, AX, route)


def exchange(par, faces, parts, notes=()):
    got = [faces]
    for m in (1, 2, 3):
        got.append(swapped(faces, [(i, i ^ m) for i in range(DEVICES) if i < i ^ m]))
    tiles = parts[-1].side + parts[-1].side_tiles + (4 if notes else 0)
    sides = call(functools.partial(k_relay, parts, notes), 1, (par, *got), [(tiles, 8, 128)] * 2)
    for odd in (0, 1):
        pairs = [(i, i + 4) for i in range(DEVICES - 4) if (i // 4) % 2 == odd]
        got.append(swapped(sides[odd], pairs))
    return tuple(got)


def to_all(rows):
    spread = jnp.broadcast_to(rows[None], (DEVICES,) + rows.shape)
    return lax.all_to_all(spread, AX, 0, 0)


def shards(source_term, inverse_density, box_counts, ghost_from):
    dev = lax.axis_index(AX).astype(I32)
    mask = (jnp.arange(SLOTS, dtype=I32) < box_counts[0]).astype(F32)
    flat = ghost_from.reshape(-1)
    present = flat >= 0
    at = jnp.where(present, flat, dev * SLOTS)
    owner = at // SLOTS
    local = at - owner * SLOTS
    place = jnp.concatenate([owner, local, jnp.full((8,), dev)]).astype(I32)
    par = jnp.stack([1 - ((dev >> 2) & 1), dev & 3, dev >> 2])
    row = lambda a: jnp.concatenate([a, jnp.zeros((128 - a.shape[0],), I32)]).astype(F32).reshape(1, 128)
    note = row(jnp.concatenate([flat, box_counts]))
    codes = row(jnp.where(present, owner * 4 + local, -1))

    view = lambda a: a.reshape(SLOTS, 256, 128).transpose(1, 0, 2)
    fine, mid = (SLOTS, 32, 8, 128), (SLOTS, 16, 8, 128)
    gx, xg, ends = (SLOTS, 2, 8, 128), (SLOTS, 4, 8, 128), (SLOTS, 8, 128)
    gyf, gym = (SLOTS, 32, 128), (SLOTS, 16, 128)
    face0, face1 = (PART0.own_tiles, 8, 128), (PART1.own_tiles, 8, 128)

    def weight_shapes(n):
        wide = (SLOTS, n + 2, 8, 128)
        return [(SLOTS, n + 3, 8, 128), wide, wide, (SLOTS, n + 2, 128), wide, (SLOTS, 6, n, 128)]

    source, beta, beta1, faces, notes = call(
        k_start, 1, (mask, view(source_term), view(inverse_density), note, codes),
        [fine, fine, mid, (FIRST_NOTES[0] + 1, 8, 128), (24, 128)],
    )
    beta_rows = lax.all_gather(notes, AX)
    win = exchange(par, faces, FIRST, FIRST_NOTES)
    own, side = FIRST_NOTES
    codes = jnp.concatenate([a[own : own + 1, 0, :12] for a in win[:4]] + [a[side:, 0, :12] for a in win[4:]])
    outs = call(
        k_weights, 2, (par, codes.reshape(-1).astype(I32), source, beta, beta1) + win,
        weight_shapes(32) + [fine] + weight_shapes(16) + [face0],
        [xg, gyf, ends, gyf, xg, gym, ends, gym], tables=[(5 * BOXES,)],
    )
    w, first, w1, faces, tab = tuple(outs[:6]), outs[6], tuple(outs[7:13]), outs[13], outs[14]
    u, u_x, u_y, first_x, first_y, f1, first1, faces = call(
        k_down, 1, (tab, source, first) + exchange(par, faces, [PART0]) + w + (w1[4],),
        [fine, gx, gyf, gx, gyf, mid, mid, face1], [xg, gyf, ends, gyf, fine],
    )
    u1, u1_x, u1_y, first1_x, first1_y, rows = call(
        k_bottom_rhs, 1, (tab, f1, first1) + exchange(par, faces, [PART1]) + w1,
        [mid, gx, gym, gx, gym, (12, 128)], [xg, gym, ends, gym, mid],
    )
    cube = (SLOTS, 8, 8, 8, 128)
    u1, faces, boxes = call(
        k_bottom, 1, (place, first1, u1, u1_x, u1_y) + w1 + (beta_rows, to_all(rows)), [mid, face1, (8, 128)],
        [(SLOTS, 10, 10, 8, 128), cube, cube, cube, (SLOTS, 8, 9, 8, 128), (SLOTS, 9, 8, 8, 128), cube,
         (DEVICES, 24, 128), (128, 128), mid, gx, gym, gym],
    )
    u, faces = call(
        k_up, 1,
        (tab, first1, first1_x, first1_y, u1, first, u, u_x, u_y) + exchange(par, faces, [PART1]) + w1 + w,
        [fine, face0], [mid, gx, gym, xg, gym, ends, gym, fine, gx, gyf, gyf],
    )
    u, residual, sums = call(
        k_residual, 1, (tab, source, u, first, first_x, first_y) + exchange(par, faces, [PART0]) + w,
        [fine, (256, SLOTS, 128), (1, 128)], [gx, gyf, xg, gyf, ends, gyf, fine],
    )
    parts = to_all(sums).reshape(DEVICES, 128)
    correction, norm = call(k_finish, 1, (mask, u, parts, boxes), [(256, SLOTS, 128), (1, 128)])
    back = lambda a: a.transpose(1, 0, 2).reshape(SLOTS, 32768)
    return back(correction), back(residual), norm[0, 0]


def solution(mesh):
    rows = P(AX, None)
    return jax.shard_map(
        shards, mesh=mesh, in_specs=(rows, rows, P(AX), rows), out_specs=(rows, rows, P()), check_vma=False
    )
```

time: 309 us -> 250 us (0.81)
  starting transfers between devices: 99.7 us -> 58.7 us
  blocking collectives: 40.4 us -> 16.1 us
  local copies, waits for them, and re-layouts: 14.6 us -> 23.6 us
  waiting for transfers between devices: 69.6 us -> 60.6 us
  Pallas kernels: 68.5 us -> 72.9 us
    ppermute x45 -> x25, starting transfers between devices: 99.7 us -> 51.4 us  [swapped(): return lax.ppermute(block, AX, route)]
    ppermute x45 -> x25, waiting for transfers between devices: 69.6 us -> 42.9 us  [swapped(): return lax.ppermute(block, AX, route)]
    all_to_all x2 -> x1, blocking collectives: 40.4 us -> 16.1 us  [to_all(): return lax.all_to_all(spread, AX, 0, 0)]
    all_to_all x0 -> x1, waiting for transfers between devices: none -> 17.7 us  [to_all(): return lax.all_to_all(spread, AX, 0, 0)]
    unnamed x73 -> x114, local copies, waits for them, and re-layouts: 12.8 us -> 20.8 us
    all_to_all x0 -> x1, starting transfers between devices: none -> 7.22 us  [to_all(): return lax.all_to_all(spread, AX, 0, 0)]
    pallas_call x12 -> x13, Pallas kernels: 68.5 us -> 72.9 us  [call(): pl.pallas_call(kernel, out_shape=[shape(s) for s in outs] + [jax.ShapeDty...]
  transfers between devices with their start and end apart: 46 -> 27, of which waited for: 29 -> 19; matrix products, arithmetic and copies ran while one was open for 0% -> 1% of each run, Pallas kernels for 3% -> 5%
where the time goes in v2:
time: 250 us; the launch traced here: 249 us
  Pallas kernels  72.9 us (29%)
  waiting for transfers between devices  60.6 us (24%)
  starting transfers between devices  58.7 us (23%)
  local copies, waits for them, and re-layouts  23.6 us (9%)
  blocking collectives  16.1 us (6%)
  between operations  15.3 us (6%)
    pallas_call x13, Pallas kernels, call(): pl.pallas_call(kernel, out_shape=[shape(s) for s in outs] + [jax.ShapeDty...  72.9 us
    ppermute x25, starting transfers between devices, swapped(): return lax.ppermute(block, AX, route)  51.4 us
    ppermute x25, waiting for transfers between devices, swapped(): return lax.ppermute(block, AX, route)  42.9 us
    unnamed x114, local copies, waits for them, and re-layouts  20.8 us
    all_to_all x1, waiting for transfers between devices, to_all(): return lax.all_to_all(spread, AX, 0, 0)  17.7 us
    all_to_all x1, blocking collectives, to_all(): return lax.all_to_all(spread, AX, 0, 0)  16.1 us
    all_to_all x1, starting transfers between devices, to_all(): return lax.all_to_all(spread, AX, 0, 0)  7.22 us
  transfers between devices with their start and end apart: 27, of which 19 were waited for; matrix products, arithmetic and copies ran while one was open for 1% of the time, Pallas kernels for 5%

profile of v2, /device:TPU:1, one launch (start us, length us, event | category | flops | bytes accessed | tf_op | source)
XLA Modules:
  0.0 249.0 jit_solution(5790385783865870213)
XLA Ops:
  7.2 0.8 reshape.73
  8.0 0.8 concatenate.23
  10.0 1.0 copy-done.20
  11.1 1.0 copy-done.21
  12.1 3.1 %shard_map.67 = (f32[3,32,8,128]{3,2,1,0:T(8,128)S(1)}, f32[3,32,8,128]{3,2,1,0:T(8,128)S(1)}, f32[3,16,8,128]{3,2,1,0:T(8,128)S(1)}, f32[34,8,128]{2,1,0:T(8,128)S(1)}, f32[24,128]{1,0:T(8,128)}) custom-call(f32[3]{0:T(128)S(1)} %compare_convert_fusion.mask, f32[256,3,128]{2,1,0:T(4,128)S(1)} %bitcast.41, f32[256,3,128]{2,1,0:T(4,128)S(1)} %bitcast.42, ...), custom_call_target="tpu_custom_call" | custom-call | tf_op jit(solution)/shard_map/pallas_call | solution.py:748
  15.2 0.7 copy-done.30
  15.9 2.5 %collective-permute-start = (f32[34,8,128]{2,1,0:T(8,128)S(1)}, f32[34,8,128]{2,1,0:T(8,128)S(1)}, u32[]{:S(2)}, u32[]{:S(2)}) collective-permute-start(f32[34,8,128]{2,1,0:T(8,128)S(1)} %get-tuple-element.57.refs_0_), channel_id=1, source_target_pairs={{0,1},{1,0},{2,3},{3,2},{4,5},{5,4},{6,7},{7,6},{8,9},{9,8},{10,11... | collective-permute-start | bytes 417800 | tf_op jit(solution)/shard_map/ppermute | solution.py:760
  18.5 3.3 %collective-permute-start.1 = (f32[34,8,128]{2,1,0:T(8,128)S(1)}, f32[34,8,128]{2,1,0:T(8,128)S(1)}, u32[]{:S(2)}, u32[]{:S(2)}) collective-permute-start(f32[34,8,128]{2,1,0:T(8,128)S(1)} %get-tuple-element.57.refs_0_), channel_id=1, source_target_pairs={{0,2},{1,3},{2,0},{3,1},{4,6},{5,7},{6,4},{7,5},{8,10},{9,11},{10,... | collective-permute-start | bytes 417800 | tf_op jit(solution)/shard_map/ppermute | solution.py:760
  21.9 6.0 %collective-permute-done.1.refs_2_ = f32[34,8,128]{2,1,0:T(8,128)S(1)} collective-permute-done((f32[34,8,128]{2,1,0:T(8,128)S(1)}, f32[34,8,128]{2,1,0:T(8,128)S(1)}, u32[]{:S(2)}, u32[]{:S(2)}) %collective-permute-start.1) | collective-permute-done | bytes 139296 | tf_op jit(solution)/shard_map/ppermute | solution.py:760
  27.8 2.5 %collective-permute-done.2.refs_3_ = f32[34,8,128]{2,1,0:T(8,128)S(1)} collective-permute-done((f32[34,8,128]{2,1,0:T(8,128)S(1)}, f32[34,8,128]{2,1,0:T(8,128)S(1)}, u32[]{:S(2)}, u32[]{:S(2)}) %collective-permute-start.2) | collective-permute-done | bytes 139296 | tf_op jit(solution)/shard_map/ppermute | solution.py:760
  30.9 1.4 collective-permute-start.3
  32.3 5.3 %collective-permute-start.4 = (f32[64,8,128]{2,1,0:T(8,128)S(1)}, f32[64,8,128]{2,1,0:T(8,128)S(1)}, u32[]{:S(2)}, u32[]{:S(2)}) collective-permute-start(f32[64,8,128]{2,1,0:T(8,128)S(1)} %get-tuple-element.59), channel_id=1, source_target_pairs={{4,8},{5,9},{6,10},{7,11},{8,4},{9,5},{10,6},{11,7},{12,16},{13,17... | collective-permute-start | bytes 786440 | tf_op jit(solution)/shard_map/ppermute | solution.py:760
  37.7 0.7 copy-done.24
  38.4 5.3 %collective-permute-done.4.refs_5_ = f32[64,8,128]{2,1,0:T(8,128)S(1)} collective-permute-done((f32[64,8,128]{2,1,0:T(8,128)S(1)}, f32[64,8,128]{2,1,0:T(8,128)S(1)}, u32[]{:S(2)}, u32[]{:S(2)}) %collective-permute-start.4) | collective-permute-done | bytes 262176 | tf_op jit(solution)/shard_map/ppermute | solution.py:760
  43.7 0.7 copy-done.26
  44.6 0.9 copy-done.25
  45.5 0.9 copy-done.27
  46.4 0.9 copy-done.31
  48.0 3.9 %shard_map.69 = (f32[3,35,8,128]{3,2,1,0:T(8,128)S(1)}, f32[3,34,8,128]{3,2,1,0:T(8,128)S(1)}, f32[3,34,8,128]{3,2,1,0:T(8,128)S(1)}, f32[3,34,128]{2,1,0:T(8,12...) custom-call(s32[3]{0:T(128)S(1)} %copy-done.37, ...), custom_call_target="tpu_custom_call" | custom-call | tf_op jit(solution)/shard_map/pallas_call | solution.py:748
  52.2 1.0 collective-permute-start.6
  53.2 2.8 %collective-permute-start.7 = (f32[24,8,128]{2,1,0:T(8,128)S(1)}, f32[24,8,128]{2,1,0:T(8,128)S(1)}, u32[]{:S(2)}, u32[]{:S(2)}) collective-permute-start(f32[24,8,128]{2,1,0:T(8,128)S(1)} %get-tuple-element.65.refs_0_), channel_id=1, source_target_pairs={{0,3},{1,2},{2,1},{3,0},{4,7},{5,6},{6,5},{7,4},{8,11},{9,10},{10,... | collective-permute-start | bytes 294920 | tf_op jit(solution)/shard_map/ppermute | solution.py:760
  56.0 1.3 collective-permute-done.6.refs_2_
  57.3 1.3 collective-permute-done.7.refs_3_
  59.3 6.6 %collective-permute-start.9 = (f32[42,8,128]{2,1,0:T(8,128)S(1)}, f32[42,8,128]{2,1,0:T(8,128)S(1)}, u32[]{:S(2)}, u32[]{:S(2)}) collective-permute-start(f32[42,8,128]{2,1,0:T(8,128)S(1)} %get-tuple-element.67), channel_id=1, source_target_pairs={{4,8},{5,9},{6,10},{7,11},{8,4},{9,5},{10,6},{11,7},{12,16},{13,17... | collective-permute-start | bytes 516104 | tf_op jit(solution)/shard_map/ppermute | solution.py:760
  66.0 4.0 %collective-permute-done.9.refs_5_ = f32[42,8,128]{2,1,0:T(8,128)S(1)} collective-permute-done((f32[42,8,128]{2,1,0:T(8,128)S(1)}, f32[42,8,128]{2,1,0:T(8,128)S(1)}, u32[]{:S(2)}, u32[]{:S(2)}) %collective-permute-start.9) | collective-permute-done | bytes 172064 | tf_op jit(solution)/shard_map/ppermute | solution.py:760
  70.0 3.6 %shard_map.71 = (f32[3,32,8,128]{3,2,1,0:T(8,128)S(1)}, f32[3,2,8,128]{3,2,1,0:T(8,128)S(1)}, f32[3,32,128]{2,1,0:T(8,128)S(1)}, f32[3,2,8,128]{3,2,1,0:T(8,128)...) custom-call(s32[180]{0:T(256)S(1)} %get-tuple-element.63.tab, ...), custom_call_target="tpu_custom_call" | custom-call | tf_op jit(solution)/shard_map/pallas_call | solution.py:748
  73.8 3.8 %collective-permute-start.11 = (f32[9,8,128]{2,1,0:T(8,128)S(1)}, f32[9,8,128]{2,1,0:T(8,128)S(1)}, u32[]{:S(2)}, u32[]{:S(2)}) collective-permute-start(f32[9,8,128]{2,1,0:T(8,128)S(1)} %get-tuple-element.77.refs_0_), channel_id=1, source_target_pairs={{0,2},{1,3},{2,0},{3,1},{4,6},{5,7},{6,4},{7,5},{8,10},{9,11},{10,... | collective-permute-start | bytes 110600 | tf_op jit(solution)/shard_map/ppermute | solution.py:760
  77.7 2.0 collective-permute-done.11.refs_2_
  79.6 2.0 collective-permute-done.12.refs_3_
  82.3 7.3 %collective-permute-start.14 = (f32[18,8,128]{2,1,0:T(8,128)S(1)}, f32[18,8,128]{2,1,0:T(8,128)S(1)}, u32[]{:S(2)}, u32[]{:S(2)}) collective-permute-start(f32[18,8,128]{2,1,0:T(8,128)S(1)} %get-tuple-element.79), channel_id=1, source_target_pairs={{4,8},{5,9},{6,10},{7,11},{8,4},{9,5},{10,6},{11,7},{12,16},{13,17... | collective-permute-start | bytes 221192 | tf_op jit(solution)/shard_map/ppermute | solution.py:760
  89.6 2.1 collective-permute-done.14.refs_5_
  91.7 2.4 shard_map.73
  97.2 1.1 broadcast_in_dim.30
  98.3 7.2 %all-to-all-start = ((f32[128,12,128]{2,1,0:T(8,128)}), f32[128,12,128]{2,1,0:T(8,128)S(1)}, u32[]{:S(2)}, u32[]{:S(2)}) async-start(f32[128,12,128]{2,1,0:T(8,128)} %broadcast_in_dim.30), calls=%async_computation | async-start | bytes 2097152 | tf_op jit(solution)/shard_map/all_to_all | solution.py:777
  105.5 1.2 pad_add_fusion.1.place
  106.7 17.7 %all-to-all-done.refs_7_ = f32[128,12,128]{2,1,0:T(8,128)S(1)} async-done(((f32[128,12,128]{2,1,0:T(8,128)}), f32[128,12,128]{2,1,0:T(8,128)S(1)}, u32[]{:S(2)}, u32[]{:S(2)}) %all-to-all-start) | async-done | bytes 786464 | tf_op jit(solution)/shard_map/all_to_all | solution.py:777
  124.4 0.9 copy-done.1
  125.4 0.9 copy-done.5
  126.3 0.9 copy-done.8
  127.3 0.9 copy-done.11
  128.2 0.9 copy-done.13
  129.1 1.4 copy-done.15
  130.5 0.9 copy-done.17
  131.4 0.9 copy-done.29
  132.4 0.7 copy-done.48
  133.1 0.7 copy-done.50
  134.5 48.6 %shard_map.74 = (f32[3,16,8,128]{3,2,1,0:T(8,128)S(1)}, f32[9,8,128]{2,1,0:T(8,128)S(1)}, f32[8,128]{1,0:T(8,128)S(1)}) custom-call(s32[32]{0:T(128)S(1)} %copy-done.53, f32[3,16,8,128]{3,2,1,0:T(8,128)S(1)} %copy-done.13, f32[3,16,8,128]{3,2,1,0:T(8,128)S(1)} %copy-done.29, f32[3,2,8,128]{3,2,1,0:T(8,128)S(1)} %copy-done.48, f32[3,16,128]{2,1,0:T(8,128)S(1)} %copy-done.50, ...), custom_call_target="tpu_custom_call" | custom-call | tf_op jit(solution)/shard_map/pallas_call | solution.py:748
  183.5 2.2 collective-permute-start.16
  185.6 1.4 collective-permute-start.17
  187.0 1.0 collective-permute-done.16.refs_2_
  188.0 2.0 collective-permute-done.17.refs_3_
  190.6 4.4 %collective-permute-start.19 = (f32[18,8,128]{2,1,0:T(8,128)S(1)}, f32[18,8,128]{2,1,0:T(8,128)S(1)}, u32[]{:S(2)}, u32[]{:S(2)}) collective-permute-start(f32[18,8,128]{2,1,0:T(8,128)S(1)} %get-tuple-element.98), channel_id=1, source_target_pairs={{4,8},{5,9},{6,10},{7,11},{8,4},{9,5},{10,6},{11,7},{12,16},{13,17... | collective-permute-start | bytes 221192 | tf_op jit(solution)/shard_map/ppermute | solution.py:760
  195.1 2.4 collective-permute-done.19.refs_5_
  197.6 2.8 %shard_map.76 = (f32[3,32,8,128]{3,2,1,0:T(8,128)S(1)}, f32[24,8,128]{2,1,0:T(8,128)S(1)}) custom-call(s32[180]{0:T(256)S(1)} %copy-done.52, f32[3,16,8,128]{3,2,1,0:T(8,128)S(1)} %copy-done.14, f32[3,2,8,128]{3,2,1,0:T(8,128)S(1)} %copy-done.44, f32[3,16,128]{2,1,0:T(8,128)S(1)} %copy-done.46, f32[3,16,8,128]{3,2,1,0:T(8,128)S(1)} %get-tuple-element.92.u1, ...), custom_call_target="tpu_custom_call" | custom-call | tf_op jit(solution)/shard_map/pallas_call | solution.py:748
  200.4 3.3 %collective-permute-start.21 = (f32[24,8,128]{2,1,0:T(8,128)S(1)}, f32[24,8,128]{2,1,0:T(8,128)S(1)}, u32[]{:S(2)}, u32[]{:S(2)}) collective-permute-start(f32[24,8,128]{2,1,0:T(8,128)S(1)} %get-tuple-element.102.refs_0_), channel_id=1, source_target_pairs={{0,2},{1,3},{2,0},{3,1},{4,6},{5,7},{6,4},{7,5},{8,10},{9,11},{10,... | collective-permute-start | bytes 294920 | tf_op jit(solution)/shard_map/ppermute | solution.py:760
  204.3 0.7 collective-permute-done.20.refs_1_
  205.0 3.8 %collective-permute-done.21.refs_2_ = f32[24,8,128]{2,1,0:T(8,128)S(1)} collective-permute-done((f32[24,8,128]{2,1,0:T(8,128)S(1)}, f32[24,8,128]{2,1,0:T(8,128)S(1)}, u32[]{:S(2)}, u32[]{:S(2)}) %collective-permute-start.21) | collective-permute-done | bytes 98336 | tf_op jit(solution)/shard_map/ppermute | solution.py:760
  208.8 2.3 collective-permute-done.22.refs_3_
  211.7 4.5 %collective-permute-start.24 = (f32[42,8,128]{2,1,0:T(8,128)S(1)}, f32[42,8,128]{2,1,0:T(8,128)S(1)}, u32[]{:S(2)}, u32[]{:S(2)}) collective-permute-start(f32[42,8,128]{2,1,0:T(8,128)S(1)} %get-tuple-element.104), channel_id=1, source_target_pairs={{4,8},{5,9},{6,10},{7,11},{8,4},{9,5},{10,6},{11,7},{12,16},{13,17... | collective-permute-start | bytes 516104 | tf_op jit(solution)/shard_map/ppermute | solution.py:760
  216.3 1.0 collective-permute-done.23.refs_4_
  217.2 3.2 %collective-permute-done.24.refs_5_ = f32[42,8,128]{2,1,0:T(8,128)S(1)} collective-permute-done((f32[42,8,128]{2,1,0:T(8,128)S(1)}, f32[42,8,128]{2,1,0:T(8,128)S(1)}, u32[]{:S(2)}, u32[]{:S(2)}) %collective-permute-start.24) | collective-permute-done | bytes 172064 | tf_op jit(solution)/shard_map/ppermute | solution.py:760
  220.4 4.0 %shard_map.78 = (f32[3,32,8,128]{3,2,1,0:T(8,128)S(1)}, f32[256,3,128]{2,1,0:T(4,128)}, f32[1,128]{1,0:T(1,128)S(1)}) custom-call(s32[180]{0:T(256)S(1)} %copy-done.52, f32[3,32,8,128]{3,2,1,0:T(8,128)S(1)} %get-tuple-element.60.s_in.t, f32[3,32,8,128]{3,2,1,0:T(8,128)S(1)} %get-tuple-element.99.u, f32[3,32,8,128]{3,2,1,0:T(8,128)S(1)} %get-tuple-element.64.u.first, ...), custom_call_target="tpu_custom_call" | custom-call | tf_op jit(solution)/shard_map/pallas_call | solution.py:748
  224.5 16.1 %all_to_all.10 = f32[128,1,128]{2,1,0:T(1,128)S(1)} all-to-all(f32[128,1,128]{2,1,0:T(1,128)S(1)} %broadcast_in_dim.32), channel_id=1, replica_groups=mesh['gx'=8,'gy'=16] {'gx','gy'}, dimensions={0} | all-to-all | bytes 131072 | tf_op jit(solution)/shard_map/all_to_all | solution.py:777
  240.5 1.6 shard_map.79
  (141 shorter events, 10.0 us)
Async XLA Ops:
  7.2 117.3 %all-gather.3.cloned.1.call-start = ((), (), s32[]{:S(2)}) async-start(), calls=%async_computation.2 | async-start | bytes 1585152 | tf_op jit(solution)/shard_map/all_gather | solution.py:808
  9.9 5.3 %copy-start.54 = (f32[3]{0:T(128)}, f32[3]{0:T(128)S(1)}, u32[]{:S(2)}) copy-start(f32[3]{0:T(128)S(1)} %compare_convert_fusion.mask) | copy-start | bytes 40
  10.0 1.0 copy-start.20
  11.1 1.0 copy-start.21
  15.9 5.9 %collective-permute-start = (f32[34,8,128]{2,1,0:T(8,128)S(1)}, f32[34,8,128]{2,1,0:T(8,128)S(1)}, u32[]{:S(2)}, u32[]{:S(2)}) collective-permute-start(f32[34,8,128]{2,1,0:T(8,128)S(1)} %get-tuple-element.57.refs_0_), channel_id=1, source_target_pairs={{0,1},{1,0},{2,3},{3,2},{4,5},{5,4},{6,7},{7,6},{8,9},{9,8},{10,11... | collective-permute-start | bytes 417800 | tf_op jit(solution)/shard_map/ppermute | solution.py:760
  18.5 9.4 %collective-permute-start.1 = (f32[34,8,128]{2,1,0:T(8,128)S(1)}, f32[34,8,128]{2,1,0:T(8,128)S(1)}, u32[]{:S(2)}, u32[]{:S(2)}) collective-permute-start(f32[34,8,128]{2,1,0:T(8,128)S(1)} %get-tuple-element.57.refs_0_), channel_id=1, source_target_pairs={{0,2},{1,3},{2,0},{3,1},{4,6},{5,7},{6,4},{7,5},{8,10},{9,11},{10,... | collective-permute-start | bytes 417800 | tf_op jit(solution)/shard_map/ppermute | solution.py:760
  21.8 8.6 %collective-permute-start.2 = (f32[34,8,128]{2,1,0:T(8,128)S(1)}, f32[34,8,128]{2,1,0:T(8,128)S(1)}, u32[]{:S(2)}, u32[]{:S(2)}) collective-permute-start(f32[34,8,128]{2,1,0:T(8,128)S(1)} %get-tuple-element.57.refs_0_), channel_id=1, source_target_pairs={{0,3},{1,2},{2,1},{3,0},{4,7},{5,6},{6,5},{7,4},{8,11},{9,10},{10,... | collective-permute-start | bytes 417800 | tf_op jit(solution)/shard_map/ppermute | solution.py:760
  21.9 21.9 %copy-start.36 = (s32[3]{0:T(128)}, s32[3]{0:T(128)S(1)}, u32[]{:S(2)}) copy-start(s32[3]{0:T(128)S(1)} %pad_add_fusion.par) | copy-start | bytes 40
  30.9 6.7 %collective-permute-start.3 = (f32[64,8,128]{2,1,0:T(8,128)S(1)}, f32[64,8,128]{2,1,0:T(8,128)S(1)}, u32[]{:S(2)}, u32[]{:S(2)}) collective-permute-start(f32[64,8,128]{2,1,0:T(8,128)S(1)} %get-tuple-element.58), channel_id=1, source_target_pairs={{0,4},{1,5},{2,6},{3,7},{4,0},{5,1},{6,2},{7,3},{8,12},{9,13},{10,... | collective-permute-start | bytes 786440 | tf_op jit(solution)/shard_map/ppermute | solution.py:760
  32.3 11.4 %collective-permute-start.4 = (f32[64,8,128]{2,1,0:T(8,128)S(1)}, f32[64,8,128]{2,1,0:T(8,128)S(1)}, u32[]{:S(2)}, u32[]{:S(2)}) collective-permute-start(f32[64,8,128]{2,1,0:T(8,128)S(1)} %get-tuple-element.59), channel_id=1, source_target_pairs={{4,8},{5,9},{6,10},{7,11},{8,4},{9,5},{10,6},{11,7},{12,16},{13,17... | collective-permute-start | bytes 786440 | tf_op jit(solution)/shard_map/ppermute | solution.py:760
  44.5 1.0 copy-start.25
  45.5 0.9 copy-start.27
  52.0 21.6 %copy-start.2 = (f32[3,6,32,128]{3,2,1,0:T(8,128)}, f32[3,6,32,128]{3,2,1,0:T(8,128)S(1)}, u32[]{:S(2)}) copy-start(f32[3,6,32,128]{3,2,1,0:T(8,128)S(1)} %get-tuple-element.73.refs_11_.refs_17_) | copy-start | bytes 884740
  52.0 21.6 %copy-start.18 = (f32[3,34,128]{2,1,0:T(8,128)}, f32[3,34,128]{2,1,0:T(8,128)S(1)}, u32[]{:S(2)}) copy-start(f32[3,34,128]{2,1,0:T(8,128)S(1)} %get-tuple-element.71.refs_9_.refs_15_) | copy-start | bytes 156676
  52.0 39.7 %copy-start = (f32[3,18,8,128]{3,2,1,0:T(8,128)}, f32[3,18,8,128]{3,2,1,0:T(8,128)S(1)}, u32[]{:S(2)}) copy-start(f32[3,18,8,128]{3,2,1,0:T(8,128)S(1)} %get-tuple-element.74.refs_12_.refs_10_.refs_4_) | copy-start | bytes 663556
  52.0 39.7 %copy-start.4 = (f32[3,19,8,128]{3,2,1,0:T(8,128)}, f32[3,19,8,128]{3,2,1,0:T(8,128)S(1)}, u32[]{:S(2)}) copy-start(f32[3,19,8,128]{3,2,1,0:T(8,128)S(1)} %get-tuple-element.80.refs_6_.refs_0_) | copy-start | bytes 700420
  52.0 39.7 %copy-start.7 = (f32[3,18,8,128]{3,2,1,0:T(8,128)}, f32[3,18,8,128]{3,2,1,0:T(8,128)S(1)}, u32[]{:S(2)}) copy-start(f32[3,18,8,128]{3,2,1,0:T(8,128)S(1)} %get-tuple-element.81.refs_7_.refs_1_) | copy-start | bytes 663556
  52.0 39.7 %copy-start.10 = (f32[3,18,8,128]{3,2,1,0:T(8,128)}, f32[3,18,8,128]{3,2,1,0:T(8,128)S(1)}, u32[]{:S(2)}) copy-start(f32[3,18,8,128]{3,2,1,0:T(8,128)S(1)} %get-tuple-element.82.refs_8_.refs_2_) | copy-start | bytes 663556
  52.0 39.6 %copy-start.16 = (f32[3,6,16,128]{3,2,1,0:T(8,128)}, f32[3,6,16,128]{3,2,1,0:T(8,128)S(1)}, u32[]{:S(2)}) copy-start(f32[3,6,16,128]{3,2,1,0:T(8,128)S(1)} %get-tuple-element.84.refs_11_.refs_5_) | copy-start | bytes 442372
  52.1 39.6 %copy-start.51 = (s32[180]{0:T(256)}, s32[180]{0:T(256)S(1)}, u32[]{:S(2)}) copy-start(s32[180]{0:T(256)S(1)} %get-tuple-element.63.tab) | copy-start | bytes 2164
  52.1 3.9 %collective-permute-start.5 = (f32[24,8,128]{2,1,0:T(8,128)S(1)}, f32[24,8,128]{2,1,0:T(8,128)S(1)}, u32[]{:S(2)}, u32[]{:S(2)}) collective-permute-start(f32[24,8,128]{2,1,0:T(8,128)S(1)} %get-tuple-element.65.refs_0_), channel_id=1, source_target_pairs={{0,1},{1,0},{2,3},{3,2},{4,5},{5,4},{6,7},{7,6},{8,9},{9,8},{10,11... | collective-permute-start | bytes 294920 | tf_op jit(solution)/shard_map/ppermute | solution.py:760
  52.2 5.2 %collective-permute-start.6 = (f32[24,8,128]{2,1,0:T(8,128)S(1)}, f32[24,8,128]{2,1,0:T(8,128)S(1)}, u32[]{:S(2)}, u32[]{:S(2)}) collective-permute-start(f32[24,8,128]{2,1,0:T(8,128)S(1)} %get-tuple-element.65.refs_0_), channel_id=1, source_target_pairs={{0,2},{1,3},{2,0},{3,1},{4,6},{5,7},{6,4},{7,5},{8,10},{9,11},{10,... | collective-permute-start | bytes 294920 | tf_op jit(solution)/shard_map/ppermute | solution.py:760
  53.2 5.5 %collective-permute-start.7 = (f32[24,8,128]{2,1,0:T(8,128)S(1)}, f32[24,8,128]{2,1,0:T(8,128)S(1)}, u32[]{:S(2)}, u32[]{:S(2)}) collective-permute-start(f32[24,8,128]{2,1,0:T(8,128)S(1)} %get-tuple-element.65.refs_0_), channel_id=1, source_target_pairs={{0,3},{1,2},{2,1},{3,0},{4,7},{5,6},{6,5},{7,4},{8,11},{9,10},{10,... | collective-permute-start | bytes 294920 | tf_op jit(solution)/shard_map/ppermute | solution.py:760
  59.2 6.7 %collective-permute-start.8 = (f32[42,8,128]{2,1,0:T(8,128)S(1)}, f32[42,8,128]{2,1,0:T(8,128)S(1)}, u32[]{:S(2)}, u32[]{:S(2)}) collective-permute-start(f32[42,8,128]{2,1,0:T(8,128)S(1)} %get-tuple-element.66), channel_id=1, source_target_pairs={{0,4},{1,5},{2,6},{3,7},{4,0},{5,1},{6,2},{7,3},{8,12},{9,13},{10,... | collective-permute-start | bytes 516104 | tf_op jit(solution)/shard_map/ppermute | solution.py:760
  59.3 10.7 %collective-permute-start.9 = (f32[42,8,128]{2,1,0:T(8,128)S(1)}, f32[42,8,128]{2,1,0:T(8,128)S(1)}, u32[]{:S(2)}, u32[]{:S(2)}) collective-permute-start(f32[42,8,128]{2,1,0:T(8,128)S(1)} %get-tuple-element.67), channel_id=1, source_target_pairs={{4,8},{5,9},{6,10},{7,11},{8,4},{9,5},{10,6},{11,7},{12,16},{13,17... | collective-permute-start | bytes 516104 | tf_op jit(solution)/shard_map/ppermute | solution.py:760
  73.6 20.4 %copy-start.12 = (f32[3,16,8,128]{3,2,1,0:T(8,128)}, f32[3,16,8,128]{3,2,1,0:T(8,128)S(1)}, u32[]{:S(2)}) copy-start(f32[3,16,8,128]{3,2,1,0:T(8,128)S(1)} %get-tuple-element.75.u.first.first1) | copy-start | bytes 589828
  73.7 23.6 %copy-start.22 = (f32[3,32,8,128]{3,2,1,0:T(8,128)}, f32[3,32,8,128]{3,2,1,0:T(8,128)S(1)}, u32[]{:S(2)}) copy-start(f32[3,32,8,128]{3,2,1,0:T(8,128)S(1)} %get-tuple-element.93.u0) | copy-start | bytes 1179652
  73.7 23.6 %copy-start.32 = (f32[3,32,128]{2,1,0:T(8,128)}, f32[3,32,128]{2,1,0:T(8,128)S(1)}, u32[]{:S(2)}) copy-start(f32[3,32,128]{2,1,0:T(8,128)S(1)} %get-tuple-element.101.first_y) | copy-start | bytes 147460
  73.7 23.5 %copy-start.34 = (f32[3,32,128]{2,1,0:T(8,128)}, f32[3,32,128]{2,1,0:T(8,128)S(1)}, u32[]{:S(2)}) copy-start(f32[3,32,128]{2,1,0:T(8,128)S(1)} %get-tuple-element.95.u0_y) | copy-start | bytes 147460
  73.7 23.5 %copy-start.39 = (f32[3,2,8,128]{3,2,1,0:T(8,128)}, f32[3,2,8,128]{3,2,1,0:T(8,128)S(1)}, u32[]{:S(2)}) copy-start(f32[3,2,8,128]{3,2,1,0:T(8,128)S(1)} %get-tuple-element.100.first_x) | copy-start | bytes 73732
  73.7 23.5 %copy-start.41 = (f32[3,2,8,128]{3,2,1,0:T(8,128)}, f32[3,2,8,128]{3,2,1,0:T(8,128)S(1)}, u32[]{:S(2)}) copy-start(f32[3,2,8,128]{3,2,1,0:T(8,128)S(1)} %get-tuple-element.94.u0_x) | copy-start | bytes 73732
  73.7 3.9 %collective-permute-start.10 = (f32[9,8,128]{2,1,0:T(8,128)S(1)}, f32[9,8,128]{2,1,0:T(8,128)S(1)}, u32[]{:S(2)}, u32[]{:S(2)}) collective-permute-start(f32[9,8,128]{2,1,0:T(8,128)S(1)} %get-tuple-element.77.refs_0_), channel_id=1, source_target_pairs={{0,1},{1,0},{2,3},{3,2},{4,5},{5,4},{6,7},{7,6},{8,9},{9,8},{10,11... | collective-permute-start | bytes 110600 | tf_op jit(solution)/shard_map/ppermute | solution.py:760
  73.8 5.8 %collective-permute-start.11 = (f32[9,8,128]{2,1,0:T(8,128)S(1)}, f32[9,8,128]{2,1,0:T(8,128)S(1)}, u32[]{:S(2)}, u32[]{:S(2)}) collective-permute-start(f32[9,8,128]{2,1,0:T(8,128)S(1)} %get-tuple-element.77.refs_0_), channel_id=1, source_target_pairs={{0,2},{1,3},{2,0},{3,1},{4,6},{5,7},{6,4},{7,5},{8,10},{9,11},{10,... | collective-permute-start | bytes 110600 | tf_op jit(solution)/shard_map/ppermute | solution.py:760
  77.6 4.0 %collective-permute-start.12 = (f32[9,8,128]{2,1,0:T(8,128)S(1)}, f32[9,8,128]{2,1,0:T(8,128)S(1)}, u32[]{:S(2)}, u32[]{:S(2)}) collective-permute-start(f32[9,8,128]{2,1,0:T(8,128)S(1)} %get-tuple-element.77.refs_0_), channel_id=1, source_target_pairs={{0,3},{1,2},{2,1},{3,0},{4,7},{5,6},{6,5},{7,4},{8,11},{9,10},{10,... | collective-permute-start | bytes 110600 | tf_op jit(solution)/shard_map/ppermute | solution.py:760
  82.2 7.4 %collective-permute-start.13 = (f32[18,8,128]{2,1,0:T(8,128)S(1)}, f32[18,8,128]{2,1,0:T(8,128)S(1)}, u32[]{:S(2)}, u32[]{:S(2)}) collective-permute-start(f32[18,8,128]{2,1,0:T(8,128)S(1)} %get-tuple-element.78), channel_id=1, source_target_pairs={{0,4},{1,5},{2,6},{3,7},{4,0},{5,1},{6,2},{7,3},{8,12},{9,13},{10,... | collective-permute-start | bytes 221192 | tf_op jit(solution)/shard_map/ppermute | solution.py:760
  82.3 9.4 %collective-permute-start.14 = (f32[18,8,128]{2,1,0:T(8,128)S(1)}, f32[18,8,128]{2,1,0:T(8,128)S(1)}, u32[]{:S(2)}, u32[]{:S(2)}) collective-permute-start(f32[18,8,128]{2,1,0:T(8,128)S(1)} %get-tuple-element.79), channel_id=1, source_target_pairs={{4,8},{5,9},{6,10},{7,11},{8,4},{9,5},{10,6},{11,7},{12,16},{13,17... | collective-permute-start | bytes 221192 | tf_op jit(solution)/shard_map/ppermute | solution.py:760
  98.3 26.1 %all-to-all-start = ((f32[128,12,128]{2,1,0:T(8,128)}), f32[128,12,128]{2,1,0:T(8,128)S(1)}, u32[]{:S(2)}, u32[]{:S(2)}) async-start(f32[128,12,128]{2,1,0:T(8,128)} %broadcast_in_dim.30), calls=%async_computation | async-start | bytes 2097152 | tf_op jit(solution)/shard_map/all_to_all | solution.py:777
  125.4 0.9 copy-start.5
  129.1 1.4 copy-start.15
  134.4 55.5 %copy-start.38 = (s32[3]{0:T(128)S(1)}, s32[3]{0:T(128)}, u32[]{:S(2)}) copy-start(s32[3]{0:T(128)} %copy-done.36) | copy-start | bytes 40
  134.4 63.1 %copy-start.3 = (f32[3,6,32,128]{3,2,1,0:T(8,128)S(1)}, f32[3,6,32,128]{3,2,1,0:T(8,128)}, u32[]{:S(2)}) copy-start(f32[3,6,32,128]{3,2,1,0:T(8,128)} %copy-done.2) | copy-start | bytes 884740
  134.4 63.1 %copy-start.6 = (f32[3,19,8,128]{3,2,1,0:T(8,128)S(1)}, f32[3,19,8,128]{3,2,1,0:T(8,128)}, u32[]{:S(2)}) copy-start(f32[3,19,8,128]{3,2,1,0:T(8,128)} %copy-done.4) | copy-start | bytes 700420
  134.4 63.1 %copy-start.9 = (f32[3,18,8,128]{3,2,1,0:T(8,128)S(1)}, f32[3,18,8,128]{3,2,1,0:T(8,128)}, u32[]{:S(2)}) copy-start(f32[3,18,8,128]{3,2,1,0:T(8,128)} %copy-done.7) | copy-start | bytes 663556
  134.4 63.1 %copy-start.14 = (f32[3,16,8,128]{3,2,1,0:T(8,128)S(1)}, f32[3,16,8,128]{3,2,1,0:T(8,128)}, u32[]{:S(2)}) copy-start(f32[3,16,8,128]{3,2,1,0:T(8,128)} %copy-done.12) | copy-start | bytes 589828
  134.4 63.1 %copy-start.19 = (f32[3,34,128]{2,1,0:T(8,128)S(1)}, f32[3,34,128]{2,1,0:T(8,128)}, u32[]{:S(2)}) copy-start(f32[3,34,128]{2,1,0:T(8,128)} %copy-done.18) | copy-start | bytes 156676
  134.4 63.1 %copy-start.23 = (f32[3,32,8,128]{3,2,1,0:T(8,128)S(1)}, f32[3,32,8,128]{3,2,1,0:T(8,128)}, u32[]{:S(2)}) copy-start(f32[3,32,8,128]{3,2,1,0:T(8,128)} %copy-done.22) | copy-start | bytes 1179652
  134.5 63.1 %copy-start.35 = (f32[3,32,128]{2,1,0:T(8,128)S(1)}, f32[3,32,128]{2,1,0:T(8,128)}, u32[]{:S(2)}) copy-start(f32[3,32,128]{2,1,0:T(8,128)} %copy-done.34) | copy-start | bytes 147460
  134.5 63.1 %copy-start.42 = (f32[3,2,8,128]{3,2,1,0:T(8,128)S(1)}, f32[3,2,8,128]{3,2,1,0:T(8,128)}, u32[]{:S(2)}) copy-start(f32[3,2,8,128]{3,2,1,0:T(8,128)} %copy-done.41) | copy-start | bytes 73732
  134.5 63.1 %copy-start.44 = (f32[3,2,8,128]{3,2,1,0:T(8,128)S(1)}, f32[3,2,8,128]{3,2,1,0:T(8,128)}, u32[]{:S(2)}) copy-start(f32[3,2,8,128]{3,2,1,0:T(8,128)} %copy-done.43) | copy-start | bytes 73732
  134.5 63.1 %copy-start.46 = (f32[3,16,128]{2,1,0:T(8,128)S(1)}, f32[3,16,128]{2,1,0:T(8,128)}, u32[]{:S(2)}) copy-start(f32[3,16,128]{2,1,0:T(8,128)} %copy-done.45) | copy-start | bytes 73732
  134.5 63.1 %copy-start.52 = (s32[180]{0:T(256)S(1)}, s32[180]{0:T(256)}, u32[]{:S(2)}) copy-start(s32[180]{0:T(256)} %copy-done.51) | copy-start | bytes 2164
  183.1 3.9 %collective-permute-start.15 = (f32[9,8,128]{2,1,0:T(8,128)S(1)}, f32[9,8,128]{2,1,0:T(8,128)S(1)}, u32[]{:S(2)}, u32[]{:S(2)}) collective-permute-start(f32[9,8,128]{2,1,0:T(8,128)S(1)} %get-tuple-element.96.refs_0_), channel_id=1, source_target_pairs={{0,1},{1,0},{2,3},{3,2},{4,5},{5,4},{6,7},{7,6},{8,9},{9,8},{10,11... | collective-permute-start | bytes 110600 | tf_op jit(solution)/shard_map/ppermute | solution.py:760
  183.5 4.5 %collective-permute-start.16 = (f32[9,8,128]{2,1,0:T(8,128)S(1)}, f32[9,8,128]{2,1,0:T(8,128)S(1)}, u32[]{:S(2)}, u32[]{:S(2)}) collective-permute-start(f32[9,8,128]{2,1,0:T(8,128)S(1)} %get-tuple-element.96.refs_0_), channel_id=1, source_target_pairs={{0,2},{1,3},{2,0},{3,1},{4,6},{5,7},{6,4},{7,5},{8,10},{9,11},{10,... | collective-permute-start | bytes 110600 | tf_op jit(solution)/shard_map/ppermute | solution.py:760
  185.6 4.3 %collective-permute-start.17 = (f32[9,8,128]{2,1,0:T(8,128)S(1)}, f32[9,8,128]{2,1,0:T(8,128)S(1)}, u32[]{:S(2)}, u32[]{:S(2)}) collective-permute-start(f32[9,8,128]{2,1,0:T(8,128)S(1)} %get-tuple-element.96.refs_0_), channel_id=1, source_target_pairs={{0,3},{1,2},{2,1},{3,0},{4,7},{5,6},{6,5},{7,4},{8,11},{9,10},{10,... | collective-permute-start | bytes 110600 | tf_op jit(solution)/shard_map/ppermute | solution.py:760
  190.5 4.5 %collective-permute-start.18 = (f32[18,8,128]{2,1,0:T(8,128)S(1)}, f32[18,8,128]{2,1,0:T(8,128)S(1)}, u32[]{:S(2)}, u32[]{:S(2)}) collective-permute-start(f32[18,8,128]{2,1,0:T(8,128)S(1)} %get-tuple-element.97), channel_id=1, source_target_pairs={{0,4},{1,5},{2,6},{3,7},{4,0},{5,1},{6,2},{7,3},{8,12},{9,13},{10,... | collective-permute-start | bytes 221192 | tf_op jit(solution)/shard_map/ppermute | solution.py:760
  190.6 6.9 %collective-permute-start.19 = (f32[18,8,128]{2,1,0:T(8,128)S(1)}, f32[18,8,128]{2,1,0:T(8,128)S(1)}, u32[]{:S(2)}, u32[]{:S(2)}) collective-permute-start(f32[18,8,128]{2,1,0:T(8,128)S(1)} %get-tuple-element.98), channel_id=1, source_target_pairs={{4,8},{5,9},{6,10},{7,11},{8,4},{9,5},{10,6},{11,7},{12,16},{13,17... | collective-permute-start | bytes 221192 | tf_op jit(solution)/shard_map/ppermute | solution.py:760
  197.6 22.9 %copy-start.33 = (f32[3,32,128]{2,1,0:T(8,128)S(1)}, f32[3,32,128]{2,1,0:T(8,128)}, u32[]{:S(2)}) copy-start(f32[3,32,128]{2,1,0:T(8,128)} %copy-done.32) | copy-start | bytes 147460
  197.6 22.9 %copy-start.40 = (f32[3,2,8,128]{3,2,1,0:T(8,128)S(1)}, f32[3,2,8,128]{3,2,1,0:T(8,128)}, u32[]{:S(2)}) copy-start(f32[3,2,8,128]{3,2,1,0:T(8,128)} %copy-done.39) | copy-start | bytes 73732
  200.4 4.6 %collective-permute-start.20 = (f32[24,8,128]{2,1,0:T(8,128)S(1)}, f32[24,8,128]{2,1,0:T(8,128)S(1)}, u32[]{:S(2)}, u32[]{:S(2)}) collective-permute-start(f32[24,8,128]{2,1,0:T(8,128)S(1)} %get-tuple-element.102.refs_0_), channel_id=1, source_target_pairs={{0,1},{1,0},{2,3},{3,2},{4,5},{5,4},{6,7},{7,6},{8,9},{9,8},{10,11... | collective-permute-start | bytes 294920 | tf_op jit(solution)/shard_map/ppermute | solution.py:760
  200.4 8.3 %collective-permute-start.21 = (f32[24,8,128]{2,1,0:T(8,128)S(1)}, f32[24,8,128]{2,1,0:T(8,128)S(1)}, u32[]{:S(2)}, u32[]{:S(2)}) collective-permute-start(f32[24,8,128]{2,1,0:T(8,128)S(1)} %get-tuple-element.102.refs_0_), channel_id=1, source_target_pairs={{0,2},{1,3},{2,0},{3,1},{4,6},{5,7},{6,4},{7,5},{8,10},{9,11},{10,... | collective-permute-start | bytes 294920 | tf_op jit(solution)/shard_map/ppermute | solution.py:760
  203.7 7.3 %collective-permute-start.22 = (f32[24,8,128]{2,1,0:T(8,128)S(1)}, f32[24,8,128]{2,1,0:T(8,128)S(1)}, u32[]{:S(2)}, u32[]{:S(2)}) collective-permute-start(f32[24,8,128]{2,1,0:T(8,128)S(1)} %get-tuple-element.102.refs_0_), channel_id=1, source_target_pairs={{0,3},{1,2},{2,1},{3,0},{4,7},{5,6},{6,5},{7,4},{8,11},{9,10},{10,... | collective-permute-start | bytes 294920 | tf_op jit(solution)/shard_map/ppermute | solution.py:760
  211.6 5.6 %collective-permute-start.23 = (f32[42,8,128]{2,1,0:T(8,128)S(1)}, f32[42,8,128]{2,1,0:T(8,128)S(1)}, u32[]{:S(2)}, u32[]{:S(2)}) collective-permute-start(f32[42,8,128]{2,1,0:T(8,128)S(1)} %get-tuple-element.103), channel_id=1, source_target_pairs={{0,4},{1,5},{2,6},{3,7},{4,0},{5,1},{6,2},{7,3},{8,12},{9,13},{10,... | collective-permute-start | bytes 516104 | tf_op jit(solution)/shard_map/ppermute | solution.py:760
  211.7 8.7 %collective-permute-start.24 = (f32[42,8,128]{2,1,0:T(8,128)S(1)}, f32[42,8,128]{2,1,0:T(8,128)S(1)}, u32[]{:S(2)}, u32[]{:S(2)}) collective-permute-start(f32[42,8,128]{2,1,0:T(8,128)S(1)} %get-tuple-element.104), channel_id=1, source_target_pairs={{4,8},{5,9},{6,10},{7,11},{8,4},{9,5},{10,6},{11,7},{12,16},{13,17... | collective-permute-start | bytes 516104 | tf_op jit(solution)/shard_map/ppermute | solution.py:760
  220.4 20.1 %copy-start.55 = (f32[3]{0:T(128)S(1)}, f32[3]{0:T(128)}, u32[]{:S(2)}) copy-start(f32[3]{0:T(128)} %copy-done.54) | copy-start | bytes 40
  (20 other events, 15.2 us)
Sparse Core Ops, SparseCore 0:
  16.0 71.0 all-gather.2

commit v3 on v2

--- a/solution.py
+++ b/solution.py
@@ -108,10 +108,10 @@
         out[base + part.ys + t] = q[8 * t : 8 * t + 8]
 
 
-def k_relay(parts, notes, par, *refs):
+def k_relay(parts, notes, *refs):
     got, (near, far) = refs[:4], refs[4:]
-    even = par[0] == 1
-    place = par[1]
+    _, even, place, _ = place_of_device()
+    even = even == 1
 
     def of(m, t):
         low = jnp.where((m & 1) == 0, got[0][t], got[1][t])
@@ -396,7 +396,7 @@
         low = g if low is None else jnp.where((part & 7) == i, g, low)
     low = jnp.where(lane < 64, low, roll(low, 4, 0))
     out[0:8, :] = top
-    out[8:12, :] = low[0:4]
+    out[8:16, :] = low
 
 
 PART0, PART1 = Part(0), Part(1)
@@ -404,24 +404,61 @@
 FIRST_NOTES = (33, 60)
 
 
-def k_start(mask, src, inv, note, codes, s_out, b_out, b1_out, faces, gathered):
+def place_of_device():
+    dev = lax.axis_index("gx") * 16 + lax.axis_index("gy")
+    return dev, 1 - ((dev >> 2) & 1), dev & 3, dev >> 2
+
+
+def used(count, s):
+    return jnp.where(s < count, 1.0, 0.0)
+
+
+def load_beta(inv, s, b, b1):
+    b[s] = inv[:, s, :].reshape(32, 8, 128)
+    for c, t in enumerate(restrict_planes(b, s, 0, 0.125)):
+        b1[s, c] = t
+
+
+def k_start(ghost, count, inv, faces, gathered, place, b, b1):
     bottom = []
-    for s in range(SLOTS):
-        s_out[s] = src[:, s, :].reshape(32, 8, 128) * mask[s]
-        b_out[s] = inv[:, s, :].reshape(32, 8, 128)
-        for c, t in enumerate(restrict_planes(b_out, s, 0, 0.125)):
-            b1_out[s, c] = t
-        bottom.append(restrict_planes(b1_out, s, 1, 0.125))
-        pack_faces(b_out, s, FIRST[0], faces)
-        pack_faces(b1_out, s, FIRST[1], faces)
-    faces[FIRST_NOTES[0]] = jnp.broadcast_to(codes[...], (8, 128))
+    dev = place_of_device()[0]
+    lane = lanes()
+    note = jnp.where(lane == 12, jnp.full((8, 128), count[0]), 0)
+    codes = jnp.zeros((8, 128), I32)
+    for s in range(SLOTS):
+        for f in range(4):
+            k = s * 4 + f
+            g = ghost[s, f]
+            has = g >= 0
+            owner = jnp.where(has, (g * 21846) >> 16, dev)
+            local = jnp.where(has, g - 3 * owner, 0)
+            place[k] = owner
+            place[12 + k] = local
+            note = jnp.where(lane == k, jnp.full((8, 128), g), note)
+            codes = jnp.where(lane == k, jnp.full((8, 128), jnp.where(has, owner * 4 + local, -1)), codes)
+    place[24] = dev
+    note = note.astype(F32)
+    for s in range(SLOTS):
+        load_beta(inv, s, b, b1)
+        bottom.append(restrict_planes(b1, s, 1, 0.125))
+        pack_faces(b, s, FIRST[0], faces)
+        pack_faces(b1, s, FIRST[1], faces)
+    faces[FIRST_NOTES[0]] = codes.astype(F32)
     pack_bottom(bottom, gathered)
-    gathered[12:24, :] = jnp.zeros((12, 128), F32)
-    gathered[12:13, :] = note[...]
-
-
-def fill_table(par, notes, tab):
-    even, place, block = par[0], par[1], par[2]
+    gathered[16:24, :] = note
+
+
+def fill_table(win, rows, notes, sem, tab):
+    _, even, place, block = place_of_device()
+    own, side = FIRST_NOTES
+    rows[...] = jnp.zeros((16, 128), I32)
+    for m in range(4):
+        rows[m : m + 1, :] = win[m][own][0:1].astype(I32)
+        for x in range(2):
+            rows[4 + 4 * x + m : 5 + 4 * x + m, :] = win[4 + x][side + m][0:1].astype(I32)
+    copy = pltpu.make_async_copy(rows, notes, sem)
+    copy.start()
+    copy.wait()
 
     def entry(k, code):
         owner = code >> 2
@@ -431,31 +468,38 @@
         r = jnp.where(delta == 0, m, jnp.where(delta == 2 * even - 1, 4, 5))
         for x, value in enumerate((r, slot, m, delta, jnp.where(code >= 0, 1, 0))):
             tab[x * BOXES + k] = value
-        return (jnp.where(r < 4, 0, r - 3) * 4 + m) * 12 + slot * 4
-
-    for s in range(SLOTS):
-        codes = [notes[s * 4 + f] for f in range(4)]
-        rows = [entry(s * 4 + f, codes[f]) for f in range(4)]
+        return jnp.where(r < 4, 0, r - 3) * 4 + m, slot * 4
+
+    for s in range(SLOTS):
+        codes = [notes[0, s * 4 + f] for f in range(4)]
+        found = [entry(s * 4 + f, codes[f]) for f in range(4)]
         for q, (f, g) in enumerate(TWO_FACES):
-            entry(12 + s * 8 + q, jnp.where(codes[f] >= 0, notes[rows[f] + g], -1))
-
-
-def k_weights(par, notes, s_in, b, b1, *refs):
+            entry(12 + s * 8 + q, jnp.where(codes[f] >= 0, notes[found[f][0], found[f][1] + g], -1))
+
+
+def k_weights(count, src, inv, *refs):
     win, refs = refs[:6], refs[6:]
-    w, u, w1, faces, tab, (xg, yg, ends, gy, xg1, yg1, ends1, gy1) = (
-        refs[:6], refs[6], refs[7:13], refs[13], refs[14], refs[15:]
+    w, s_out, u, b1, faces, tab, (b, xg, yg, ends, gy, rows, notes, sem) = (
+        refs[:6], refs[6], refs[7], refs[8], refs[9], refs[10], refs[11:]
     )
-    fill_table(par, notes, tab)
+    fill_table(win, rows, notes, sem, tab)
+    for s in range(SLOTS):
+        s_out[s] = src[:, s, :].reshape(32, 8, 128) * used(count[0], s)
+        load_beta(inv, s, b, b1)
     take_ghosts(tab, win, FIRST[0], xg, yg, ends)
-    take_ghosts(tab, win, FIRST[1], xg1, yg1, ends1)
 
     def first(s, i, r):
-        u[s, i] = s_in[s, i] * r
+        u[s, i] = s_out[s, i] * r
 
     make_weights(b, xg, yg, ends, gy, tab, 0, w, first)
-    make_weights(b1, xg1, yg1, ends1, gy1, tab, 1, w1, lambda s, i, r: None)
     for s in range(SLOTS):
         pack_faces(u, s, PART0, faces)
+
+
+def k_weights_next(tab, b1, *refs):
+    win, w1, (xg, yg, ends, gy) = refs[:6], refs[6:12], refs[12:]
+    take_ghosts(tab, win, FIRST[1], xg, yg, ends)
+    make_weights(b1, xg, yg, ends, gy, tab, 1, w1, lambda s, i, r: None)
 
 
 def k_down(tab, t, u, *refs):
@@ -509,18 +553,26 @@
                 put(s, j, i, t[half * 64 + i * 8 : half * 64 + i * 8 + 8, :])
 
 
-def face_gather(v, dev_at, slot_at, place, s):
+def face_gather(dev_at, slot_at, place):
     out = lane_take(place(0), dev_at)
     for other in range(1, SLOTS):
-        g = lane_take(place(other), dev_at)
-        out = jnp.where(slot_at == other, g, out)
+        out = jnp.where(slot_at == other, lane_take(place(other), dev_at), out)
     return out
 
 
-def k_bottom(place, first, u, gx0, gy0, *refs):
-    w1, (beta_rows, rhs_rows) = refs[:6], refs[6:8]
-    out, faces, boxes_out, p, r, x, q, cx, cy, cz, back, sq, v1, gx, yg, gy = refs[8:]
-    note = beta_rows[:, 12, :].T
+def fill_bottom_ghosts(p, at, slot):
+    for s in range(SLOTS):
+        for f, (src, dst) in enumerate(((7, 0), (0, 9))):
+            k = s * 4 + f
+            for m in range(1, 9):
+                p[s, m, dst] = face_gather(at[k], slot[k], lambda o: p[o, m, src + 1])
+            k = s * 4 + 2 + f
+            for m in range(1, 9):
+                p[s, dst, m] = face_gather(at[k], slot[k], lambda o: p[o, src + 1, m])
+
+
+def k_bottom_weights(beta_rows, cx, cy, cz, at_out, slot_out, counts_out, p):
+    note = beta_rows[:, 16, :].T
     at, slot, pres = [], [], []
     for f in range(12):
         gf = jnp.broadcast_to(note[f : f + 1, :], (8, 128))
@@ -530,28 +582,15 @@
         at.append(dv)
         slot.append(gf.astype(I32) - 3 * dv)
         pres.append(jnp.where(has, 1.0, 0.0))
-    counts = note[12:13, :]
-    boxes = jnp.sum(counts, axis=1, keepdims=True)
-    boxes_out[...] = jnp.broadcast_to(boxes, (8, 128))
-
-    def fill_ghosts():
-        def along(m, _):
-            for s in range(SLOTS):
-                for f, (src, dst) in enumerate(((7, 0), (0, 9))):
-                    k = s * 4 + f
-                    p[s, m + 1, dst] = face_gather(p, at[k], slot[k], lambda o: p[o, m + 1, src + 1], s)
-                for f, (src, dst) in enumerate(((7, 0), (0, 9))):
-                    k = s * 4 + 2 + f
-                    p[s, dst, m + 1] = face_gather(p, at[k], slot[k], lambda o: p[o, src + 1, m + 1], s)
-            return 0
-
-        lax.fori_loop(0, 8, along, 0)
+        at_out[f] = dv.astype(F32)
+        slot_out[f] = slot[f].astype(F32)
+    counts_out[...] = jnp.broadcast_to(note[12:13, :], (8, 128))
 
     def put_beta(s, j, i, tile):
         p[s, j + 1, i + 1] = tile
 
     unpack_bottom(beta_rows, put_beta)
-    fill_ghosts()
+    fill_bottom_ghosts(p, at, slot)
     h = 0.5 * 0.0625
     low = subs() == 0
 
@@ -577,23 +616,51 @@
 
     lax.fori_loop(0, 8, weights, 0)
 
+
+def k_bottom(place, cx, cy, cz, at_in, slot_in, counts_in, mine64, other64, *refs):
+    far, (out, faces, boxes_out) = refs[:9], refs[9:12]
+    p, r, x, q, back, sq, rhs_rows, v1, gx, yg, gy = refs[12:23]
+    kept, sem = refs[23:32], refs[32]
+    copies = [pltpu.make_async_copy(a, b, sem.at[n]) for n, (a, b) in enumerate(zip(far, kept))]
+    for c in copies:
+        c.start()
+    first, u, gx0, gy0 = kept[:4]
+    w1 = kept[4:]
+    me = place[24]
+    for m in range(64):
+        here = me ^ ((m & 15) | ((m >> 4) << 5))
+        rhs_rows[here] = mine64[m]
+        rhs_rows[here ^ 16] = other64[m]
+    at = [at_in[f].astype(I32) for f in range(12)]
+    slot = [slot_in[f].astype(I32) for f in range(12)]
+    counts = counts_in[...]
+    boxes = jnp.sum(counts[0:1], axis=1, keepdims=True)
+    boxes_out[...] = jnp.broadcast_to(boxes, (8, 128))
+
+    def fill_ghosts():
+        fill_bottom_ghosts(p, at, slot)
+
     def put_rhs(s, j, i, tile):
         r[s, j, i] = tile
 
     unpack_bottom(rhs_rows, put_rhs)
 
-    def each(fn, init):
+    zero = jnp.zeros((8, 128), F32)
+
+    def each(fn):
         def step(j, acc):
+            acc = list(acc)
             for s in range(SLOTS):
                 for i in range(8):
-                    acc = fn(s, j, i, acc)
-            return acc
-
-        return lax.fori_loop(0, 8, step, init)
-
-    zero = jnp.zeros((8, 128), F32)
-    mean = total(each(lambda s, j, i, acc: acc + r[s, j, i], zero)) / (boxes * 512.0)
-    valid = [jnp.where(jnp.broadcast_to(counts, (8, 128)) > s + 0.5, 1.0, 0.0) for s in range(SLOTS)]
+                    acc[i] = fn(s, j, i, acc[i])
+            return tuple(acc)
+
+        a = lax.fori_loop(0, 8, step, (zero,) * 8, unroll=2)
+        a = ((a[0] + a[1]) + (a[2] + a[3])) + ((a[4] + a[5]) + (a[6] + a[7]))
+        return jnp.broadcast_to(total(a), (8, 128))
+
+    mean = each(lambda s, j, i, acc: acc + r[s, j, i]) / jnp.broadcast_to(boxes * 512.0, (8, 128))
+    valid = [jnp.where(counts > s + 0.5, 1.0, 0.0) for s in range(SLOTS)]
 
     def shift(s, j, i, acc):
         v = (r[s, j, i] - mean) * valid[s]
@@ -602,7 +669,7 @@
         x[s, j, i] = zero
         return acc + v * v
 
-    rr = total(each(shift, zero))
+    rr = each(shift)
 
     def image(s, j, i, acc):
         here = p[s, j + 1, i + 1]
@@ -615,7 +682,7 @@
 
     def iteration(it, rr):
         fill_ghosts()
-        alpha = rr / total(each(image, zero))
+        alpha = rr / each(image)
 
         def step(s, j, i, acc):
             x[s, j, i] = x[s, j, i] + alpha * p[s, j + 1, i + 1]
@@ -623,31 +690,27 @@
             r[s, j, i] = v
             return acc + v * v
 
-        rr_next = total(each(step, zero))
+        rr_next = each(step)
         ratio = rr_next / rr
 
-        def turn(s, j, i, acc):
-            p[s, j + 1, i + 1] = r[s, j, i] + ratio * p[s, j + 1, i + 1]
-            return acc
-
-        each(turn, 0)
+        def turn(j, _):
+            for s in range(SLOTS):
+                for i in range(8):
+                    p[s, j + 1, i + 1] = r[s, j, i] + ratio * p[s, j + 1, i + 1]
+            return 0
+
+        lax.fori_loop(0, 8, turn, 0)
         return rr_next
 
     rr = lax.fori_loop(0, BOTTOM_ITERS - 1, iteration, rr)
     fill_ghosts()
-    alpha = rr / total(each(image, zero))
-
-    def last(s, j, i, acc):
-        x[s, j, i] = x[s, j, i] + alpha * p[s, j + 1, i + 1]
-        return acc
-
-    each(last, 0)
+    alpha = rr / each(image)
 
     for row in range(12):
         for half in range(2):
             s, j = (half, row) if row < 8 else (2, row - 8 + 4 * half)
             for i in range(8):
-                sq[half * 64 + i * 8 : half * 64 + i * 8 + 8, :] = x[s, j, i]
+                sq[half * 64 + i * 8 : half * 64 + i * 8 + 8, :] = x[s, j, i] + alpha * p[s, j + 1, i + 1]
         tr = sq[...].T
         if row < 8:
             back[:, row, :] = tr
@@ -656,6 +719,8 @@
             back[:, 8 + row, :] = tr
             back[:, 12 + row, :] = roll(tr, 64, 1)
 
+    for c in copies:
+        c.wait()
     lane, sub = lanes(), subs()
     kat = (lane & 31) >> 2
 
@@ -663,7 +728,7 @@
         return back[dev, pl.ds(pl.multiple_of(8 * s, 8), 8), :]
 
     for s in range(SLOTS):
-        mine = box(place[24], s)
+        mine = box(me, s)
         for i in range(8):
             g = lane_take(mine, kat + i * 8)
             v1[s, 2 * i] = u[s, 2 * i] + g
@@ -730,27 +795,28 @@
     sums[...] = jnp.where(lane == 0, total(su), jnp.where(lane == 1, total(sr), 0.0))
 
 
-def k_finish(mask, u, sums, boxes, corr, norm):
+def k_finish(count, u, sums, boxes, corr, norm):
     tot = jnp.sum(sums[...], axis=0, keepdims=True)
     cells = boxes[0:1, 0:1] * 32768.0
     mean = tot[:, 0:1] / cells
     for s in range(SLOTS):
-        corr[:, s, :] = ((u[s] - mean) * mask[s]).reshape(256, 128)
+        corr[:, s, :] = ((u[s] - mean) * used(count[0], s)).reshape(256, 128)
     norm[...] = jnp.broadcast_to(jnp.sqrt(tot[:, 1:2] / cells), (1, 128))
 
 
 VMEM = pl.BlockSpec(memory_space=pltpu.VMEM)
 SMEM = pl.BlockSpec(memory_space=pltpu.SMEM)
-
-
-def call(kernel, smem, args, outs, scratch=(), vmem=24, tables=()):
+HBM = pl.BlockSpec(memory_space=pltpu.HBM)
+
+
+def call(kernel, smem, args, outs, scratch=(), vmem=16, tables=(), hbm=0, extra=()):
     shape = lambda s: jax.ShapeDtypeStruct(s, F32)
     return pl.pallas_call(
         kernel,
         out_shape=[shape(s) for s in outs] + [jax.ShapeDtypeStruct(s, I32) for s in tables],
-        in_specs=[SMEM] * smem + [VMEM] * (len(args) - smem),
+        in_specs=[SMEM] * smem + [VMEM] * (len(args) - smem - hbm) + [HBM] * hbm,
         out_specs=[VMEM] * len(outs) + [SMEM] * len(tables),
-        scratch_shapes=[pltpu.VMEM(s, F32) for s in scratch],
+        scratch_shapes=[pltpu.VMEM(s, F32) for s in scratch] + list(extra),
         compiler_params=pltpu.CompilerParams(vmem_limit_bytes=vmem * 1024 * 1024),
     )(*args)
 
@@ -760,37 +826,44 @@
     return lax.ppermute(block, AX, route)
 
 
-def exchange(par, faces, parts, notes=()):
+def xor_pairs(m):
+    return [(i, i ^ m) for i in range(DEVICES) if i < i ^ m]
+
+
+def exchange(faces, parts, notes=()):
     got = [faces]
     for m in (1, 2, 3):
-        got.append(swapped(faces, [(i, i ^ m) for i in range(DEVICES) if i < i ^ m]))
+        got.append(swapped(faces, xor_pairs(m)))
     tiles = parts[-1].side + parts[-1].side_tiles + (4 if notes else 0)
-    sides = call(functools.partial(k_relay, parts, notes), 1, (par, *got), [(tiles, 8, 128)] * 2)
+    sides = call(functools.partial(k_relay, parts, notes), 0, got, [(tiles, 8, 128)] * 2)
     for odd in (0, 1):
         pairs = [(i, i + 4) for i in range(DEVICES - 4) if (i // 4) % 2 == odd]
         got.append(swapped(sides[odd], pairs))
     return tuple(got)
 
 
+def k_join(*refs):
+    n = refs[0].shape[0]
+    for m in range(4):
+        refs[4][m * n : (m + 1) * n] = refs[m][...]
+
+
+def gather_rows(rows, beside):
+    rows = rows[None]
+    for unit in (1, 4, 32):
+        if unit == 32:
+            rows, beside = lax.optimization_barrier((rows, beside))
+        got = [rows] + [swapped(rows, xor_pairs(m * unit)) for m in (1, 2, 3)]
+        rows = call(k_join, 0, got, [(4 * rows.shape[0],) + rows.shape[1:]])[0]
+    return tuple(beside) + (rows, swapped(rows, xor_pairs(16)))
+
+
 def to_all(rows):
     spread = jnp.broadcast_to(rows[None], (DEVICES,) + rows.shape)
     return lax.all_to_all(spread, AX, 0, 0)
 
 
 def shards(source_term, inverse_density, box_counts, ghost_from):
-    dev = lax.axis_index(AX).astype(I32)
-    mask = (jnp.arange(SLOTS, dtype=I32) < box_counts[0]).astype(F32)
-    flat = ghost_from.reshape(-1)
-    present = flat >= 0
-    at = jnp.where(present, flat, dev * SLOTS)
-    owner = at // SLOTS
-    local = at - owner * SLOTS
-    place = jnp.concatenate([owner, local, jnp.full((8,), dev)]).astype(I32)
-    par = jnp.stack([1 - ((dev >> 2) & 1), dev & 3, dev >> 2])
-    row = lambda a: jnp.concatenate([a, jnp.zeros((128 - a.shape[0],), I32)]).astype(F32).reshape(1, 128)
-    note = row(jnp.concatenate([flat, box_counts]))
-    codes = row(jnp.where(present, owner * 4 + local, -1))
-
     view = lambda a: a.reshape(SLOTS, 256, 128).transpose(1, 0, 2)
     fine, mid = (SLOTS, 32, 8, 128), (SLOTS, 16, 8, 128)
     gx, xg, ends = (SLOTS, 2, 8, 128), (SLOTS, 4, 8, 128), (SLOTS, 8, 128)
@@ -801,45 +874,50 @@
         wide = (SLOTS, n + 2, 8, 128)
         return [(SLOTS, n + 3, 8, 128), wide, wide, (SLOTS, n + 2, 128), wide, (SLOTS, 6, n, 128)]
 
-    source, beta, beta1, faces, notes = call(
-        k_start, 1, (mask, view(source_term), view(inverse_density), note, codes),
-        [fine, fine, mid, (FIRST_NOTES[0] + 1, 8, 128), (24, 128)],
+    faces, notes, place = call(
+        k_start, 2, (ghost_from, box_counts, view(inverse_density)),
+        [(FIRST_NOTES[0] + 1, 8, 128), (24, 128)], [fine, mid], tables=[(25,)],
     )
     beta_rows = lax.all_gather(notes, AX)
-    win = exchange(par, faces, FIRST, FIRST_NOTES)
-    own, side = FIRST_NOTES
-    codes = jnp.concatenate([a[own : own + 1, 0, :12] for a in win[:4]] + [a[side:, 0, :12] for a in win[4:]])
+    win = exchange(faces, FIRST, FIRST_NOTES)
     outs = call(
-        k_weights, 2, (par, codes.reshape(-1).astype(I32), source, beta, beta1) + win,
-        weight_shapes(32) + [fine] + weight_shapes(16) + [face0],
-        [xg, gyf, ends, gyf, xg, gym, ends, gym], tables=[(5 * BOXES,)],
+        k_weights, 1, (box_counts, view(source_term), view(inverse_density)) + win,
+        weight_shapes(32) + [fine, fine, mid, face0], [fine, xg, gyf, ends, gyf], tables=[(5 * BOXES,)],
+        extra=[pltpu.VMEM((16, 128), I32), pltpu.SMEM((16, 128), I32), pltpu.SemaphoreType.DMA],
     )
-    w, first, w1, faces, tab = tuple(outs[:6]), outs[6], tuple(outs[7:13]), outs[13], outs[14]
+    w, (source, first, beta1, faces, tab) = tuple(outs[:6]), outs[6:]
+    w1 = tuple(call(k_weights_next, 1, (tab, beta1) + win, weight_shapes(16), [xg, gym, ends, gym]))
     u, u_x, u_y, first_x, first_y, f1, first1, faces = call(
-        k_down, 1, (tab, source, first) + exchange(par, faces, [PART0]) + w + (w1[4],),
+        k_down, 1, (tab, source, first) + exchange(faces, [PART0]) + w + (w1[4],),
         [fine, gx, gyf, gx, gyf, mid, mid, face1], [xg, gyf, ends, gyf, fine],
     )
     u1, u1_x, u1_y, first1_x, first1_y, rows = call(
-        k_bottom_rhs, 1, (tab, f1, first1) + exchange(par, faces, [PART1]) + w1,
-        [mid, gx, gym, gx, gym, (12, 128)], [xg, gym, ends, gym, mid],
+        k_bottom_rhs, 1, (tab, f1, first1) + exchange(faces, [PART1]) + w1,
+        [mid, gx, gym, gx, gym, (16, 128)], [xg, gym, ends, gym, mid],
     )
-    cube = (SLOTS, 8, 8, 8, 128)
+    cube, padded = (SLOTS, 8, 8, 8, 128), (SLOTS, 10, 10, 8, 128)
+    bottom_w = call(
+        k_bottom_weights, 0, (beta_rows,),
+        [(SLOTS, 8, 9, 8, 128), (SLOTS, 9, 8, 8, 128), cube, (12, 8, 128), (12, 8, 128), (8, 128)], [padded],
+    )
+    kept = [first1, u1, u1_x, u1_y] + list(w1[:5])
     u1, faces, boxes = call(
-        k_bottom, 1, (place, first1, u1, u1_x, u1_y) + w1 + (beta_rows, to_all(rows)), [mid, face1, (8, 128)],
-        [(SLOTS, 10, 10, 8, 128), cube, cube, cube, (SLOTS, 8, 9, 8, 128), (SLOTS, 9, 8, 8, 128), cube,
-         (DEVICES, 24, 128), (128, 128), mid, gx, gym, gym],
+        k_bottom, 1, (place,) + gather_rows(rows, tuple(bottom_w)) + tuple(kept), [mid, face1, (8, 128)],
+        [padded, cube, cube, cube, (DEVICES, 24, 128), (128, 128), (DEVICES, 16, 128), mid, gx, gym, gym]
+        + [a.shape for a in kept],
+        hbm=len(kept), extra=[pltpu.SemaphoreType.DMA((len(kept),))],
     )
     u, faces = call(
         k_up, 1,
-        (tab, first1, first1_x, first1_y, u1, first, u, u_x, u_y) + exchange(par, faces, [PART1]) + w1 + w,
+        (tab, first1, first1_x, first1_y, u1, first, u, u_x, u_y) + exchange(faces, [PART1]) + w1 + w,
         [fine, face0], [mid, gx, gym, xg, gym, ends, gym, fine, gx, gyf, gyf],
     )
     u, residual, sums = call(
-        k_residual, 1, (tab, source, u, first, first_x, first_y) + exchange(par, faces, [PART0]) + w,
+        k_residual, 1, (tab, source, u, first, first_x, first_y) + exchange(faces, [PART0]) + w,
         [fine, (256, SLOTS, 128), (1, 128)], [gx, gyf, xg, gyf, ends, gyf, fine],
     )
     parts = to_all(sums).reshape(DEVICES, 128)
-    correction, norm = call(k_finish, 1, (mask, u, parts, boxes), [(256, SLOTS, 128), (1, 128)])
+    correction, norm = call(k_finish, 1, (box_counts, u, parts, boxes), [(256, SLOTS, 128), (1, 128)])
     back = lambda a: a.transpose(1, 0, 2).reshape(SLOTS, 32768)
     return back(correction), back(residual), norm[0, 0]
 

time: 250 us -> 199 us (0.80)
  Pallas kernels: 72.9 us -> 41.6 us
  local copies, waits for them, and re-layouts: 23.6 us -> 9.03 us
  waiting for transfers between devices: 60.6 us -> 46.1 us
  starting transfers between devices: 58.7 us -> 68.7 us
    pallas_call x13 -> x18, Pallas kernels: 72.9 us -> 41.6 us  [call(): pl.pallas_call(kernel, out_shape=[shape(s) for s in outs] + [jax.ShapeDty...]
    all_to_all x1 -> x0, waiting for transfers between devices: 17.7 us -> none  [to_all(): return lax.all_to_all(spread, AX, 0, 0)]
    ppermute x25 -> x35, starting transfers between devices: 51.4 us -> 68.6 us  [swapped(): return lax.ppermute(block, AX, route)]
    unnamed x114 -> x66, local copies, waits for them, and re-layouts: 20.8 us -> 8.99 us
    all_to_all x1 -> x0, starting transfers between devices: 7.22 us -> none  [to_all(): return lax.all_to_all(spread, AX, 0, 0)]
    ppermute x25 -> x35, waiting for transfers between devices: 42.9 us -> 46.1 us  [swapped(): return lax.ppermute(block, AX, route)]
  transfers between devices with their start and end apart: 27 -> 36, of which waited for: 19 -> 23; matrix products, arithmetic and copies ran while one was open for 1% -> 0% of each run, Pallas kernels for 5% -> 7%
where the time goes in v3:
time: 199 us; the launch traced here: 198 us
  starting transfers between devices  68.7 us (35%)
  waiting for transfers between devices  46.1 us (23%)
  Pallas kernels  41.6 us (21%)
  blocking collectives  17.8 us (9%)
  between operations  15.1 us (8%)
  local copies, waits for them, and re-layouts  9.03 us (5%)
    ppermute x35, starting transfers between devices, swapped(): return lax.ppermute(block, AX, route)  68.6 us
    ppermute x35, waiting for transfers between devices, swapped(): return lax.ppermute(block, AX, route)  46.1 us
    pallas_call x18, Pallas kernels, call(): pl.pallas_call(kernel, out_shape=[shape(s) for s in outs] + [jax.ShapeDty...  41.6 us
    all_to_all x1, blocking collectives, to_all(): return lax.all_to_all(spread, AX, 0, 0)  17.8 us
    unnamed x66, local copies, waits for them, and re-layouts  8.99 us
  transfers between devices with their start and end apart: 36, of which 23 were waited for; matrix products, arithmetic and copies ran while one was open for 0% of the time, Pallas kernels for 7%

profile of v3, /device:TPU:1, one launch (start us, length us, event | category | flops | bytes accessed | tf_op | source)
XLA Modules:
  0.0 198.4 jit_solution(659603367643086542)
XLA Ops:
  7.9 1.0 copy-done
  8.9 0.7 copy-done.30
  9.6 2.8 %shard_map.67 = (f32[34,8,128]{2,1,0:T(8,128)S(1)}, f32[24,128]{1,0:T(8,128)}, s32[25]{0:T(128)S(1)}) custom-call(s32[3,4]{1,0:T(4,128)S(1)} %copy-done.30, s32[1]{0:T(128)S(6)} %copy.7.count, f32[256,3,128]{2,1,0:T(4,128)S(1)} %bitcast.18), custom_call_target="tpu_custom_call" | custom-call | tf_op jit(solution)/shard_map/pallas_call | solution.py:814
  12.9 4.7 %collective-permute-start.2 = (f32[34,8,128]{2,1,0:T(8,128)S(1)}, f32[34,8,128]{2,1,0:T(8,128)S(1)}, u32[]{:S(2)}, u32[]{:S(2)}) collective-permute-start(f32[34,8,128]{2,1,0:T(8,128)S(1)} %get-tuple-element.70.refs_0_), channel_id=1, source_target_pairs={{0,3},{1,2},{2,1},{3,0},{4,7},{5,6},{6,5},{7,4},{8,11},{9,10},{10,... | collective-permute-start | bytes 417800 | tf_op jit(solution)/shard_map/ppermute | solution.py:826
  18.3 5.2 %collective-permute-done.2.refs_3_ = f32[34,8,128]{2,1,0:T(8,128)S(1)} collective-permute-done((f32[34,8,128]{2,1,0:T(8,128)S(1)}, f32[34,8,128]{2,1,0:T(8,128)S(1)}, u32[]{:S(2)}, u32[]{:S(2)}) %collective-permute-start.2) | collective-permute-done | bytes 139296 | tf_op jit(solution)/shard_map/ppermute | solution.py:826
  23.4 1.0 collective-permute-done.refs_1_
  24.5 1.4 collective-permute-start.3
  25.8 6.2 %collective-permute-start.4 = (f32[64,8,128]{2,1,0:T(8,128)S(1)}, f32[64,8,128]{2,1,0:T(8,128)S(1)}, u32[]{:S(2)}, u32[]{:S(2)}) collective-permute-start(f32[64,8,128]{2,1,0:T(8,128)S(1)} %get-tuple-element.72), channel_id=1, source_target_pairs={{4,8},{5,9},{6,10},{7,11},{8,4},{9,5},{10,6},{11,7},{12,16},{13,17... | collective-permute-start | bytes 786440 | tf_op jit(solution)/shard_map/ppermute | solution.py:826
  32.1 5.5 %collective-permute-done.4.refs_5_ = f32[64,8,128]{2,1,0:T(8,128)S(1)} collective-permute-done((f32[64,8,128]{2,1,0:T(8,128)S(1)}, f32[64,8,128]{2,1,0:T(8,128)S(1)}, u32[]{:S(2)}, u32[]{:S(2)}) %collective-permute-start.4) | collective-permute-done | bytes 262176 | tf_op jit(solution)/shard_map/ppermute | solution.py:826
  37.6 1.0 copy-done.1
  38.6 1.0 copy-done.7
  39.7 5.1 %shard_map.69 = (f32[3,35,8,128]{3,2,1,0:T(8,128)S(1)}, f32[3,34,8,128]{3,2,1,0:T(8,128)S(1)}, f32[3,34,8,128]{3,2,1,0:T(8,128)S(1)}, f32[3,34,128]{2,1,0:T(8,12...) custom-call(s32[1]{0:T(128)S(6)} %copy.7.count, ...), custom_call_target="tpu_custom_call" | custom-call | tf_op jit(solution)/shard_map/pallas_call | solution.py:814
  44.8 2.3 %collective-permute-start.7 = (f32[24,8,128]{2,1,0:T(8,128)S(1)}, f32[24,8,128]{2,1,0:T(8,128)S(1)}, u32[]{:S(2)}, u32[]{:S(2)}) collective-permute-start(f32[24,8,128]{2,1,0:T(8,128)S(1)} %get-tuple-element.76.refs_0_), channel_id=1, source_target_pairs={{0,3},{1,2},{2,1},{3,0},{4,7},{5,6},{6,5},{7,4},{8,11},{9,10},{10,... | collective-permute-start | bytes 294920 | tf_op jit(solution)/shard_map/ppermute | solution.py:826
  47.2 1.0 collective-permute-start.5
  48.1 1.8 collective-permute-done.7.refs_3_
  50.0 2.3 %collective-permute-done.6.refs_2_ = f32[24,8,128]{2,1,0:T(8,128)S(1)} collective-permute-done((f32[24,8,128]{2,1,0:T(8,128)S(1)}, f32[24,8,128]{2,1,0:T(8,128)S(1)}, u32[]{:S(2)}, u32[]{:S(2)}) %collective-permute-start.6) | collective-permute-done | bytes 98336 | tf_op jit(solution)/shard_map/ppermute | solution.py:826
  52.4 7.0 %collective-permute-start.9 = (f32[42,8,128]{2,1,0:T(8,128)S(1)}, f32[42,8,128]{2,1,0:T(8,128)S(1)}, u32[]{:S(2)}, u32[]{:S(2)}) collective-permute-start(f32[42,8,128]{2,1,0:T(8,128)S(1)} %get-tuple-element.78), channel_id=1, source_target_pairs={{4,8},{5,9},{6,10},{7,11},{8,4},{9,5},{10,6},{11,7},{12,16},{13,17... | collective-permute-start | bytes 516104 | tf_op jit(solution)/shard_map/ppermute | solution.py:826
  59.4 1.7 shard_map.71
  61.1 1.9 collective-permute-done.9.refs_5_
  63.0 3.7 %shard_map.72 = (f32[3,32,8,128]{3,2,1,0:T(8,128)S(1)}, f32[3,2,8,128]{3,2,1,0:T(8,128)S(1)}, f32[3,32,128]{2,1,0:T(8,128)S(1)}, f32[3,2,8,128]{3,2,1,0:T(8,128)...) custom-call(s32[180]{0:T(256)S(1)} %get-tuple-element.73.tab, ...), custom_call_target="tpu_custom_call" | custom-call | tf_op jit(solution)/shard_map/pallas_call | solution.py:814
  66.7 1.8 collective-permute-start.12
  68.5 1.5 collective-permute-start.10
  70.0 1.6 collective-permute-done.12.refs_3_
  71.6 1.2 collective-permute-done.11.refs_2_
  72.9 7.1 %collective-permute-start.14 = (f32[18,8,128]{2,1,0:T(8,128)S(1)}, f32[18,8,128]{2,1,0:T(8,128)S(1)}, u32[]{:S(2)}, u32[]{:S(2)}) collective-permute-start(f32[18,8,128]{2,1,0:T(8,128)S(1)} %get-tuple-element.91), channel_id=1, source_target_pairs={{4,8},{5,9},{6,10},{7,11},{8,4},{9,5},{10,6},{11,7},{12,16},{13,17... | collective-permute-start | bytes 221192 | tf_op jit(solution)/shard_map/ppermute | solution.py:826
  80.1 2.4 %collective-permute-done.14.refs_5_ = f32[18,8,128]{2,1,0:T(8,128)S(1)} collective-permute-done((f32[18,8,128]{2,1,0:T(8,128)S(1)}, f32[18,8,128]{2,1,0:T(8,128)S(1)}, u32[]{:S(2)}, u32[]{:S(2)}) %collective-permute-start.14) | collective-permute-done | bytes 73760 | tf_op jit(solution)/shard_map/ppermute | solution.py:826
  82.4 2.4 %shard_map.74 = (f32[3,16,8,128]{3,2,1,0:T(8,128)S(1)}, f32[3,2,8,128]{3,2,1,0:T(8,128)S(1)}, f32[3,16,128]{2,1,0:T(8,128)S(1)}, f32[3,2,8,128]{3,2,1,0:T(8,128)...) custom-call(s32[180]{0:T(256)S(1)} %get-tuple-element.73.tab, f32[3,16,8,128]{3,2,1,0:T(8,128)S(1)} %get-tuple-element.88.t, ...), custom_call_target="tpu_custom_call" | custom-call | tf_op jit(solution)/shard_map/pallas_call | solution.py:814
  84.8 0.7 copy-done.14
  86.7 1.0 collective-permute-start.17
  87.7 1.0 collective-permute-start.16
  88.7 1.2 collective-permute-start.15
  90.4 1.3 collective-permute-done.16.refs_2_
  91.7 2.5 %collective-permute-start.20 = (f32[4,16,128]{2,1,0:T(8,128)S(1)}, f32[4,16,128]{2,1,0:T(8,128)S(1)}, u32[]{:S(2)}, u32[]{:S(2)}) collective-permute-start(f32[4,16,128]{2,1,0:T(8,128)S(1)} %shard_map.75.refs_0_), channel_id=1, source_target_pairs={{0,12},{1,13},{2,14},{3,15},{4,8},{5,9},{6,10},{7,11},{8,4},{9,5},... | collective-permute-start | bytes 98312 | tf_op jit(solution)/shard_map/ppermute | solution.py:826
  94.2 0.8 collective-permute-start.18
  94.9 0.7 collective-permute-done.20.refs_3_
  95.7 2.9 %collective-permute-done.19.refs_2_ = f32[4,16,128]{2,1,0:T(8,128)S(1)} collective-permute-done((f32[4,16,128]{2,1,0:T(8,128)S(1)}, f32[4,16,128]{2,1,0:T(8,128)S(1)}, u32[]{:S(2)}, u32[]{:S(2)}) %collective-permute-start.19) | collective-permute-done | bytes 32800 | tf_op jit(solution)/shard_map/ppermute | solution.py:826
  99.3 1.4 copy-done.4
  100.7 1.2 shard_map.77
  101.9 1.4 collective-permute-start.23
  103.3 1.5 collective-permute-start.22
  105.3 1.8 collective-permute-done.23.refs_3_
  107.0 1.6 collective-permute-done.22.refs_2_
  109.1 6.2 %collective-permute-start.24 = (f32[64,16,128]{2,1,0:T(8,128)S(1)}, f32[64,16,128]{2,1,0:T(8,128)S(1)}, u32[]{:S(2)}, u32[]{:S(2)}) collective-permute-start(f32[64,16,128]{2,1,0:T(8,128)S(1)} %shard_map.78.mine64), channel_id=1, source_target_pairs={{0,16},{1,17},{2,18},{3,19},{4,20},{5,21},{6,22},{7,23},{8,24},{9,... | collective-permute-start | bytes 1572872 | tf_op jit(solution)/shard_map/ppermute | solution.py:826
  115.2 1.5 collective-permute-done.24.other64
  117.5 16.7 %shard_map.79 = (f32[3,16,8,128]{3,2,1,0:T(8,128)S(1)}, f32[9,8,128]{2,1,0:T(8,128)S(1)}, f32[8,128]{1,0:T(8,128)S(1)}) custom-call(s32[25]{0:T(128)S(1)} %copy-done.32, f32[3,8,9,8,128]{4,3,2,1,0:T(8,128)S(1)} %get-tuple-element.108.cx, f32[3,9,8,8,128]{4,3,2,1,0:T(8,128)S(1)} %get-tuple-element.109.cy, f32[3,8,8,8,128]{4,3,2,1,0:T(8,128)S(1)} %get-tuple-element.110.cz, ...), custom_call_target="tpu_custom_call" | custom-call | tf_op jit(solution)/shard_map/pallas_call | solution.py:814
  134.2 1.5 collective-permute-start.27
  135.7 1.1 collective-permute-start.26
  136.8 0.7 collective-permute-start.25
  137.5 0.8 collective-permute-done.27.refs_3_
  138.3 1.7 collective-permute-done.26.refs_2_
  140.0 1.5 collective-permute-start.28
  141.5 4.3 %collective-permute-start.29 = (f32[18,8,128]{2,1,0:T(8,128)S(1)}, f32[18,8,128]{2,1,0:T(8,128)S(1)}, u32[]{:S(2)}, u32[]{:S(2)}) collective-permute-start(f32[18,8,128]{2,1,0:T(8,128)S(1)} %get-tuple-element.124), channel_id=1, source_target_pairs={{4,8},{5,9},{6,10},{7,11},{8,4},{9,5},{10,6},{11,7},{12,16},{13,17... | collective-permute-start | bytes 221192 | tf_op jit(solution)/shard_map/ppermute | solution.py:826
  145.8 2.5 %collective-permute-done.29.refs_5_ = f32[18,8,128]{2,1,0:T(8,128)S(1)} collective-permute-done((f32[18,8,128]{2,1,0:T(8,128)S(1)}, f32[18,8,128]{2,1,0:T(8,128)S(1)}, u32[]{:S(2)}, u32[]{:S(2)}) %collective-permute-start.29) | collective-permute-done | bytes 73760 | tf_op jit(solution)/shard_map/ppermute | solution.py:826
  148.4 2.8 %shard_map.81 = (f32[3,32,8,128]{3,2,1,0:T(8,128)S(1)}, f32[24,8,128]{2,1,0:T(8,128)S(1)}) custom-call(s32[180]{0:T(256)S(1)} %get-tuple-element.73.tab, f32[3,16,8,128]{3,2,1,0:T(8,128)S(1)} %get-tuple-element.87.u.refs_0_.first1, f32[3,2,8,128]{3,2,1,0:T(8,128)S(1)} %copy-done.23, f32[3,16,128]{2,1,0:T(8,128)S(1)} %copy-done.25, ...), custom_call_target="tpu_custom_call" | custom-call | tf_op jit(solution)/shard_map/pallas_call | solution.py:814
  151.2 1.4 collective-permute-start.32
  152.5 1.0 collective-permute-start.31
  153.5 1.0 collective-permute-start.30
  154.5 3.0 %collective-permute-done.32.refs_3_ = f32[24,8,128]{2,1,0:T(8,128)S(1)} collective-permute-done((f32[24,8,128]{2,1,0:T(8,128)S(1)}, f32[24,8,128]{2,1,0:T(8,128)S(1)}, u32[]{:S(2)}, u32[]{:S(2)}) %collective-permute-start.32) | collective-permute-done | bytes 98336 | tf_op jit(solution)/shard_map/ppermute | solution.py:826
  157.4 0.9 collective-permute-done.31.refs_2_
  158.5 6.3 %collective-permute-start.34 = (f32[42,8,128]{2,1,0:T(8,128)S(1)}, f32[42,8,128]{2,1,0:T(8,128)S(1)}, u32[]{:S(2)}, u32[]{:S(2)}) collective-permute-start(f32[42,8,128]{2,1,0:T(8,128)S(1)} %get-tuple-element.130), channel_id=1, source_target_pairs={{4,8},{5,9},{6,10},{7,11},{8,4},{9,5},{10,6},{11,7},{12,16},{13,17... | collective-permute-start | bytes 516104 | tf_op jit(solution)/shard_map/ppermute | solution.py:826
  164.8 3.8 %collective-permute-done.34.refs_5_ = f32[42,8,128]{2,1,0:T(8,128)S(1)} collective-permute-done((f32[42,8,128]{2,1,0:T(8,128)S(1)}, f32[42,8,128]{2,1,0:T(8,128)S(1)}, u32[]{:S(2)}, u32[]{:S(2)}) %collective-permute-start.34) | collective-permute-done | bytes 172064 | tf_op jit(solution)/shard_map/ppermute | solution.py:826
  168.6 4.0 %shard_map.83 = (f32[3,32,8,128]{3,2,1,0:T(8,128)S(1)}, f32[256,3,128]{2,1,0:T(4,128)}, f32[1,128]{1,0:T(1,128)S(1)}) custom-call(s32[180]{0:T(256)S(1)} %get-tuple-element.73.tab, f32[3,32,8,128]{3,2,1,0:T(8,128)S(1)} %copy-done.3, f32[3,32,8,128]{3,2,1,0:T(8,128)S(1)} %get-tuple-element.125.u, f32[3,32,8,128]{3,2,1,0:T(8,128)S(1)} %get-tuple-element.75.u.first, ...), custom_call_target="tpu_custom_call" | custom-call | tf_op jit(solution)/shard_map/pallas_call | solution.py:814
  172.7 17.8 %all_to_all.5 = f32[128,1,128]{2,1,0:T(1,128)S(1)} all-to-all(f32[128,1,128]{2,1,0:T(1,128)S(1)} %broadcast_in_dim.13), channel_id=1, replica_groups=mesh['gx'=8,'gy'=16] {'gx','gy'}, dimensions={0} | all-to-all | bytes 131072 | tf_op jit(solution)/shard_map/all_to_all | solution.py:863
  190.4 1.1 shard_map.84
  (95 shorter events, 5.7 us)
Async XLA Ops:
  7.2 92.1 %all-gather.3.cloned.1.call-start = ((), (), s32[]{:S(2)}) async-start(), calls=%async_computation.1 | async-start | bytes 1585152 | tf_op jit(solution)/shard_map/all_gather | solution.py:881
  7.9 1.0 copy-start
  8.9 0.7 copy-start.30
  12.9 10.5 %collective-permute-start.2 = (f32[34,8,128]{2,1,0:T(8,128)S(1)}, f32[34,8,128]{2,1,0:T(8,128)S(1)}, u32[]{:S(2)}, u32[]{:S(2)}) collective-permute-start(f32[34,8,128]{2,1,0:T(8,128)S(1)} %get-tuple-element.70.refs_0_), channel_id=1, source_target_pairs={{0,3},{1,2},{2,1},{3,0},{4,7},{5,6},{6,5},{7,4},{8,11},{9,10},{10,... | collective-permute-start | bytes 417800 | tf_op jit(solution)/shard_map/ppermute | solution.py:826
  17.6 5.8 %collective-permute-start.1 = (f32[34,8,128]{2,1,0:T(8,128)S(1)}, f32[34,8,128]{2,1,0:T(8,128)S(1)}, u32[]{:S(2)}, u32[]{:S(2)}) collective-permute-start(f32[34,8,128]{2,1,0:T(8,128)S(1)} %get-tuple-element.70.refs_0_), channel_id=1, source_target_pairs={{0,2},{1,3},{2,0},{3,1},{4,6},{5,7},{6,4},{7,5},{8,10},{9,11},{10,... | collective-permute-start | bytes 417800 | tf_op jit(solution)/shard_map/ppermute | solution.py:826
  17.6 6.8 %collective-permute-start = (f32[34,8,128]{2,1,0:T(8,128)S(1)}, f32[34,8,128]{2,1,0:T(8,128)S(1)}, u32[]{:S(2)}, u32[]{:S(2)}) collective-permute-start(f32[34,8,128]{2,1,0:T(8,128)S(1)} %get-tuple-element.70.refs_0_), channel_id=1, source_target_pairs={{0,1},{1,0},{2,3},{3,2},{4,5},{5,4},{6,7},{7,6},{8,9},{9,8},{10,11... | collective-permute-start | bytes 417800 | tf_op jit(solution)/shard_map/ppermute | solution.py:826
  24.5 7.6 %collective-permute-start.3 = (f32[64,8,128]{2,1,0:T(8,128)S(1)}, f32[64,8,128]{2,1,0:T(8,128)S(1)}, u32[]{:S(2)}, u32[]{:S(2)}) collective-permute-start(f32[64,8,128]{2,1,0:T(8,128)S(1)} %get-tuple-element.71), channel_id=1, source_target_pairs={{0,4},{1,5},{2,6},{3,7},{4,0},{5,1},{6,2},{7,3},{8,12},{9,13},{10,... | collective-permute-start | bytes 786440 | tf_op jit(solution)/shard_map/ppermute | solution.py:826
  25.8 11.7 %collective-permute-start.4 = (f32[64,8,128]{2,1,0:T(8,128)S(1)}, f32[64,8,128]{2,1,0:T(8,128)S(1)}, u32[]{:S(2)}, u32[]{:S(2)}) collective-permute-start(f32[64,8,128]{2,1,0:T(8,128)S(1)} %get-tuple-element.72), channel_id=1, source_target_pairs={{4,8},{5,9},{6,10},{7,11},{8,4},{9,5},{10,6},{11,7},{12,16},{13,17... | collective-permute-start | bytes 786440 | tf_op jit(solution)/shard_map/ppermute | solution.py:826
  37.6 1.0 copy-start.1
  38.6 1.0 copy-start.7
  44.8 21.9 %copy-start.2 = (f32[3,32,8,128]{3,2,1,0:T(8,128)}, f32[3,32,8,128]{3,2,1,0:T(8,128)S(1)}, u32[]{:S(2)}) copy-start(f32[3,32,8,128]{3,2,1,0:T(8,128)S(1)} %get-tuple-element.74.t) | copy-start | bytes 1179652
  44.8 5.2 %collective-permute-start.7 = (f32[24,8,128]{2,1,0:T(8,128)S(1)}, f32[24,8,128]{2,1,0:T(8,128)S(1)}, u32[]{:S(2)}, u32[]{:S(2)}) collective-permute-start(f32[24,8,128]{2,1,0:T(8,128)S(1)} %get-tuple-element.76.refs_0_), channel_id=1, source_target_pairs={{0,3},{1,2},{2,1},{3,0},{4,7},{5,6},{6,5},{7,4},{8,11},{9,10},{10,... | collective-permute-start | bytes 294920 | tf_op jit(solution)/shard_map/ppermute | solution.py:826
  47.1 5.1 %collective-permute-start.6 = (f32[24,8,128]{2,1,0:T(8,128)S(1)}, f32[24,8,128]{2,1,0:T(8,128)S(1)}, u32[]{:S(2)}, u32[]{:S(2)}) collective-permute-start(f32[24,8,128]{2,1,0:T(8,128)S(1)} %get-tuple-element.76.refs_0_), channel_id=1, source_target_pairs={{0,2},{1,3},{2,0},{3,1},{4,6},{5,7},{6,4},{7,5},{8,10},{9,11},{10,... | collective-permute-start | bytes 294920 | tf_op jit(solution)/shard_map/ppermute | solution.py:826
  47.2 5.1 %collective-permute-start.5 = (f32[24,8,128]{2,1,0:T(8,128)S(1)}, f32[24,8,128]{2,1,0:T(8,128)S(1)}, u32[]{:S(2)}, u32[]{:S(2)}) collective-permute-start(f32[24,8,128]{2,1,0:T(8,128)S(1)} %get-tuple-element.76.refs_0_), channel_id=1, source_target_pairs={{0,1},{1,0},{2,3},{3,2},{4,5},{5,4},{6,7},{7,6},{8,9},{9,8},{10,11... | collective-permute-start | bytes 294920 | tf_op jit(solution)/shard_map/ppermute | solution.py:826
  52.3 8.8 %collective-permute-start.8 = (f32[42,8,128]{2,1,0:T(8,128)S(1)}, f32[42,8,128]{2,1,0:T(8,128)S(1)}, u32[]{:S(2)}, u32[]{:S(2)}) collective-permute-start(f32[42,8,128]{2,1,0:T(8,128)S(1)} %get-tuple-element.77), channel_id=1, source_target_pairs={{0,4},{1,5},{2,6},{3,7},{4,0},{5,1},{6,2},{7,3},{8,12},{9,13},{10,... | collective-permute-start | bytes 516104 | tf_op jit(solution)/shard_map/ppermute | solution.py:826
  52.4 10.6 %collective-permute-start.9 = (f32[42,8,128]{2,1,0:T(8,128)S(1)}, f32[42,8,128]{2,1,0:T(8,128)S(1)}, u32[]{:S(2)}, u32[]{:S(2)}) collective-permute-start(f32[42,8,128]{2,1,0:T(8,128)S(1)} %get-tuple-element.78), channel_id=1, source_target_pairs={{4,8},{5,9},{6,10},{7,11},{8,4},{9,5},{10,6},{11,7},{12,16},{13,17... | collective-permute-start | bytes 516104 | tf_op jit(solution)/shard_map/ppermute | solution.py:826
  61.1 21.4 %copy-start.5 = (f32[3,6,16,128]{3,2,1,0:T(8,128)}, f32[3,6,16,128]{3,2,1,0:T(8,128)S(1)}, u32[]{:S(2)}) copy-start(f32[3,6,16,128]{3,2,1,0:T(8,128)S(1)} %get-tuple-element.96.refs_11_) | copy-start | bytes 442372
  61.1 21.3 %copy-start.12 = (f32[3,18,128]{2,1,0:T(8,128)}, f32[3,18,128]{2,1,0:T(8,128)S(1)}, u32[]{:S(2)}) copy-start(f32[3,18,128]{2,1,0:T(8,128)S(1)} %get-tuple-element.95.refs_9_.refs_7_) | copy-start | bytes 82948
  66.6 31.9 %copy-start.10 = (f32[3,32,8,128]{3,2,1,0:T(8,128)}, f32[3,32,8,128]{3,2,1,0:T(8,128)S(1)}, u32[]{:S(2)}) copy-start(f32[3,32,8,128]{3,2,1,0:T(8,128)S(1)} %get-tuple-element.119.u0) | copy-start | bytes 1179652
  66.7 31.9 %copy-start.16 = (f32[3,32,128]{2,1,0:T(8,128)}, f32[3,32,128]{2,1,0:T(8,128)S(1)}, u32[]{:S(2)}) copy-start(f32[3,32,128]{2,1,0:T(8,128)S(1)} %get-tuple-element.127.first_y) | copy-start | bytes 147460
  66.7 31.9 %copy-start.18 = (f32[3,32,128]{2,1,0:T(8,128)}, f32[3,32,128]{2,1,0:T(8,128)S(1)}, u32[]{:S(2)}) copy-start(f32[3,32,128]{2,1,0:T(8,128)S(1)} %get-tuple-element.121.u0_y) | copy-start | bytes 147460
  66.7 31.9 %copy-start.20 = (f32[3,2,8,128]{3,2,1,0:T(8,128)}, f32[3,2,8,128]{3,2,1,0:T(8,128)S(1)}, u32[]{:S(2)}) copy-start(f32[3,2,8,128]{3,2,1,0:T(8,128)S(1)} %get-tuple-element.120.u0_x) | copy-start | bytes 73732
  66.7 4.9 %collective-permute-start.12 = (f32[9,8,128]{2,1,0:T(8,128)S(1)}, f32[9,8,128]{2,1,0:T(8,128)S(1)}, u32[]{:S(2)}, u32[]{:S(2)}) collective-permute-start(f32[9,8,128]{2,1,0:T(8,128)S(1)} %get-tuple-element.89.refs_0_), channel_id=1, source_target_pairs={{0,3},{1,2},{2,1},{3,0},{4,7},{5,6},{6,5},{7,4},{8,11},{9,10},{10,... | collective-permute-start | bytes 110600 | tf_op jit(solution)/shard_map/ppermute | solution.py:826
  68.5 4.3 %collective-permute-start.11 = (f32[9,8,128]{2,1,0:T(8,128)S(1)}, f32[9,8,128]{2,1,0:T(8,128)S(1)}, u32[]{:S(2)}, u32[]{:S(2)}) collective-permute-start(f32[9,8,128]{2,1,0:T(8,128)S(1)} %get-tuple-element.89.refs_0_), channel_id=1, source_target_pairs={{0,2},{1,3},{2,0},{3,1},{4,6},{5,7},{6,4},{7,5},{8,10},{9,11},{10,... | collective-permute-start | bytes 110600 | tf_op jit(solution)/shard_map/ppermute | solution.py:826
  68.5 4.3 %collective-permute-start.10 = (f32[9,8,128]{2,1,0:T(8,128)S(1)}, f32[9,8,128]{2,1,0:T(8,128)S(1)}, u32[]{:S(2)}, u32[]{:S(2)}) collective-permute-start(f32[9,8,128]{2,1,0:T(8,128)S(1)} %get-tuple-element.89.refs_0_), channel_id=1, source_target_pairs={{0,1},{1,0},{2,3},{3,2},{4,5},{5,4},{6,7},{7,6},{8,9},{9,8},{10,11... | collective-permute-start | bytes 110600 | tf_op jit(solution)/shard_map/ppermute | solution.py:826
  72.8 7.2 %collective-permute-start.13 = (f32[18,8,128]{2,1,0:T(8,128)S(1)}, f32[18,8,128]{2,1,0:T(8,128)S(1)}, u32[]{:S(2)}, u32[]{:S(2)}) collective-permute-start(f32[18,8,128]{2,1,0:T(8,128)S(1)} %get-tuple-element.90), channel_id=1, source_target_pairs={{0,4},{1,5},{2,6},{3,7},{4,0},{5,1},{6,2},{7,3},{8,12},{9,13},{10,... | collective-permute-start | bytes 221192 | tf_op jit(solution)/shard_map/ppermute | solution.py:826
  72.9 9.5 %collective-permute-start.14 = (f32[18,8,128]{2,1,0:T(8,128)S(1)}, f32[18,8,128]{2,1,0:T(8,128)S(1)}, u32[]{:S(2)}, u32[]{:S(2)}) collective-permute-start(f32[18,8,128]{2,1,0:T(8,128)S(1)} %get-tuple-element.91), channel_id=1, source_target_pairs={{4,8},{5,9},{6,10},{7,11},{8,4},{9,5},{10,6},{11,7},{12,16},{13,17... | collective-permute-start | bytes 221192 | tf_op jit(solution)/shard_map/ppermute | solution.py:826
  84.8 0.7 copy-start.14
  86.7 11.9 %copy-start.22 = (f32[3,2,8,128]{3,2,1,0:T(8,128)}, f32[3,2,8,128]{3,2,1,0:T(8,128)S(1)}, u32[]{:S(2)}) copy-start(f32[3,2,8,128]{3,2,1,0:T(8,128)S(1)} %get-tuple-element.97.first1_x) | copy-start | bytes 73732
  86.7 11.9 %copy-start.24 = (f32[3,16,128]{2,1,0:T(8,128)}, f32[3,16,128]{2,1,0:T(8,128)S(1)}, u32[]{:S(2)}) copy-start(f32[3,16,128]{2,1,0:T(8,128)S(1)} %get-tuple-element.98.first1_y) | copy-start | bytes 73732
  86.7 3.7 %collective-permute-start.17 = (f32[1,16,128]{2,1,0:T(8,128)S(1)}, f32[1,16,128]{2,1,0:T(8,128)S(1)}, u32[]{:S(2)}, u32[]{:S(2)}) collective-permute-start(f32[1,16,128]{2,1,0:T(8,128)S(1)} %bitcast.23), channel_id=1, source_target_pairs={{0,3},{1,2},{2,1},{3,0},{4,7},{5,6},{6,5},{7,4},{8,11},{9,10},{10,... | collective-permute-start | bytes 24584 | tf_op jit(solution)/shard_map/ppermute | solution.py:826
  87.7 4.0 %collective-permute-start.16 = (f32[1,16,128]{2,1,0:T(8,128)S(1)}, f32[1,16,128]{2,1,0:T(8,128)S(1)}, u32[]{:S(2)}, u32[]{:S(2)}) collective-permute-start(f32[1,16,128]{2,1,0:T(8,128)S(1)} %bitcast.24), channel_id=1, source_target_pairs={{0,2},{1,3},{2,0},{3,1},{4,6},{5,7},{6,4},{7,5},{8,10},{9,11},{10,... | collective-permute-start | bytes 24584 | tf_op jit(solution)/shard_map/ppermute | solution.py:826
  88.7 3.0 %collective-permute-start.15 = (f32[1,16,128]{2,1,0:T(8,128)S(1)}, f32[1,16,128]{2,1,0:T(8,128)S(1)}, u32[]{:S(2)}, u32[]{:S(2)}) collective-permute-start(f32[1,16,128]{2,1,0:T(8,128)S(1)} %bitcast.25), channel_id=1, source_target_pairs={{0,1},{1,0},{2,3},{3,2},{4,5},{5,4},{6,7},{7,6},{8,9},{9,8},{10,11... | collective-permute-start | bytes 24584 | tf_op jit(solution)/shard_map/ppermute | solution.py:826
  91.7 4.0 %collective-permute-start.20 = (f32[4,16,128]{2,1,0:T(8,128)S(1)}, f32[4,16,128]{2,1,0:T(8,128)S(1)}, u32[]{:S(2)}, u32[]{:S(2)}) collective-permute-start(f32[4,16,128]{2,1,0:T(8,128)S(1)} %shard_map.75.refs_0_), channel_id=1, source_target_pairs={{0,12},{1,13},{2,14},{3,15},{4,8},{5,9},{6,10},{7,11},{8,4},{9,5},... | collective-permute-start | bytes 98312 | tf_op jit(solution)/shard_map/ppermute | solution.py:826
  94.2 4.4 %collective-permute-start.19 = (f32[4,16,128]{2,1,0:T(8,128)S(1)}, f32[4,16,128]{2,1,0:T(8,128)S(1)}, u32[]{:S(2)}, u32[]{:S(2)}) collective-permute-start(f32[4,16,128]{2,1,0:T(8,128)S(1)} %shard_map.75.refs_0_), channel_id=1, source_target_pairs={{0,8},{1,9},{2,10},{3,11},{4,12},{5,13},{6,14},{7,15},{8,0},{9,1},... | collective-permute-start | bytes 98312 | tf_op jit(solution)/shard_map/ppermute | solution.py:826
  94.2 4.4 %collective-permute-start.18 = (f32[4,16,128]{2,1,0:T(8,128)S(1)}, f32[4,16,128]{2,1,0:T(8,128)S(1)}, u32[]{:S(2)}, u32[]{:S(2)}) collective-permute-start(f32[4,16,128]{2,1,0:T(8,128)S(1)} %shard_map.75.refs_0_), channel_id=1, source_target_pairs={{0,4},{1,5},{2,6},{3,7},{4,0},{5,1},{6,2},{7,3},{8,12},{9,13},{10,... | collective-permute-start | bytes 98312 | tf_op jit(solution)/shard_map/ppermute | solution.py:826
  99.3 1.4 copy-start.4
  100.7 1.3 copy-start.9
  100.7 16.1 %copy-start.13 = (f32[3,18,128]{2,1,0:T(8,128)S(1)}, f32[3,18,128]{2,1,0:T(8,128)}, u32[]{:S(2)}) copy-start(f32[3,18,128]{2,1,0:T(8,128)} %copy-done.12) | copy-start | bytes 82948
  100.7 16.1 %copy-start.15 = (f32[3,16,8,128]{3,2,1,0:T(8,128)S(1)}, f32[3,16,8,128]{3,2,1,0:T(8,128)}, u32[]{:S(2)}) copy-start(f32[3,16,8,128]{3,2,1,0:T(8,128)} %copy-done.14) | copy-start | bytes 589828
  100.7 16.1 %copy-start.27 = (f32[3,2,8,128]{3,2,1,0:T(8,128)S(1)}, f32[3,2,8,128]{3,2,1,0:T(8,128)}, u32[]{:S(2)}) copy-start(f32[3,2,8,128]{3,2,1,0:T(8,128)} %copy-done.26) | copy-start | bytes 73732
  100.7 16.1 %copy-start.29 = (f32[3,16,128]{2,1,0:T(8,128)S(1)}, f32[3,16,128]{2,1,0:T(8,128)}, u32[]{:S(2)}) copy-start(f32[3,16,128]{2,1,0:T(8,128)} %copy-done.28) | copy-start | bytes 73732
  101.9 5.1 %collective-permute-start.23 = (f32[16,16,128]{2,1,0:T(8,128)S(1)}, f32[16,16,128]{2,1,0:T(8,128)S(1)}, u32[]{:S(2)}, u32[]{:S(2)}) collective-permute-start(f32[16,16,128]{2,1,0:T(8,128)S(1)} %copy-done.9), channel_id=1, source_target_pairs={{0,96},{1,97},{2,98},{3,99},{4,100},{5,101},{6,102},{7,103},{8,104... | collective-permute-start | bytes 393224 | tf_op jit(solution)/shard_map/ppermute | solution.py:826
  103.3 5.3 %collective-permute-start.22 = (f32[16,16,128]{2,1,0:T(8,128)S(1)}, f32[16,16,128]{2,1,0:T(8,128)S(1)}, u32[]{:S(2)}, u32[]{:S(2)}) collective-permute-start(f32[16,16,128]{2,1,0:T(8,128)S(1)} %copy-done.9), channel_id=1, source_target_pairs={{0,64},{1,65},{2,66},{3,67},{4,68},{5,69},{6,70},{7,71},{8,72},{9,... | collective-permute-start | bytes 393224 | tf_op jit(solution)/shard_map/ppermute | solution.py:826
  104.9 4.1 %collective-permute-start.21 = (f32[16,16,128]{2,1,0:T(8,128)S(1)}, f32[16,16,128]{2,1,0:T(8,128)S(1)}, u32[]{:S(2)}, u32[]{:S(2)}) collective-permute-start(f32[16,16,128]{2,1,0:T(8,128)S(1)} %copy-done.9), channel_id=1, source_target_pairs={{0,32},{1,33},{2,34},{3,35},{4,36},{5,37},{6,38},{7,39},{8,40},{9,... | collective-permute-start | bytes 393224 | tf_op jit(solution)/shard_map/ppermute | solution.py:826
  109.1 7.7 %collective-permute-start.24 = (f32[64,16,128]{2,1,0:T(8,128)S(1)}, f32[64,16,128]{2,1,0:T(8,128)S(1)}, u32[]{:S(2)}, u32[]{:S(2)}) collective-permute-start(f32[64,16,128]{2,1,0:T(8,128)S(1)} %shard_map.78.mine64), channel_id=1, source_target_pairs={{0,16},{1,17},{2,18},{3,19},{4,20},{5,21},{6,22},{7,23},{8,24},{9,... | collective-permute-start | bytes 1572872 | tf_op jit(solution)/shard_map/ppermute | solution.py:826
  117.4 30.9 %copy-start.6 = (f32[3,6,16,128]{3,2,1,0:T(8,128)S(1)}, f32[3,6,16,128]{3,2,1,0:T(8,128)}, u32[]{:S(2)}) copy-start(f32[3,6,16,128]{3,2,1,0:T(8,128)} %copy-done.5) | copy-start | bytes 442372
  117.4 30.9 %copy-start.11 = (f32[3,32,8,128]{3,2,1,0:T(8,128)S(1)}, f32[3,32,8,128]{3,2,1,0:T(8,128)}, u32[]{:S(2)}) copy-start(f32[3,32,8,128]{3,2,1,0:T(8,128)} %copy-done.10) | copy-start | bytes 1179652
  117.4 30.9 %copy-start.19 = (f32[3,32,128]{2,1,0:T(8,128)S(1)}, f32[3,32,128]{2,1,0:T(8,128)}, u32[]{:S(2)}) copy-start(f32[3,32,128]{2,1,0:T(8,128)} %copy-done.18) | copy-start | bytes 147460
  117.4 30.9 %copy-start.21 = (f32[3,2,8,128]{3,2,1,0:T(8,128)S(1)}, f32[3,2,8,128]{3,2,1,0:T(8,128)}, u32[]{:S(2)}) copy-start(f32[3,2,8,128]{3,2,1,0:T(8,128)} %copy-done.20) | copy-start | bytes 73732
  117.4 30.9 %copy-start.23 = (f32[3,2,8,128]{3,2,1,0:T(8,128)S(1)}, f32[3,2,8,128]{3,2,1,0:T(8,128)}, u32[]{:S(2)}) copy-start(f32[3,2,8,128]{3,2,1,0:T(8,128)} %copy-done.22) | copy-start | bytes 73732
  117.5 30.9 %copy-start.25 = (f32[3,16,128]{2,1,0:T(8,128)S(1)}, f32[3,16,128]{2,1,0:T(8,128)}, u32[]{:S(2)}) copy-start(f32[3,16,128]{2,1,0:T(8,128)} %copy-done.24) | copy-start | bytes 73732
  134.2 4.1 %collective-permute-start.27 = (f32[9,8,128]{2,1,0:T(8,128)S(1)}, f32[9,8,128]{2,1,0:T(8,128)S(1)}, u32[]{:S(2)}, u32[]{:S(2)}) collective-permute-start(f32[9,8,128]{2,1,0:T(8,128)S(1)} %get-tuple-element.122.refs_0_), channel_id=1, source_target_pairs={{0,3},{1,2},{2,1},{3,0},{4,7},{5,6},{6,5},{7,4},{8,11},{9,10},{10,... | collective-permute-start | bytes 110600 | tf_op jit(solution)/shard_map/ppermute | solution.py:826
  135.7 4.3 %collective-permute-start.26 = (f32[9,8,128]{2,1,0:T(8,128)S(1)}, f32[9,8,128]{2,1,0:T(8,128)S(1)}, u32[]{:S(2)}, u32[]{:S(2)}) collective-permute-start(f32[9,8,128]{2,1,0:T(8,128)S(1)} %get-tuple-element.122.refs_0_), channel_id=1, source_target_pairs={{0,2},{1,3},{2,0},{3,1},{4,6},{5,7},{6,4},{7,5},{8,10},{9,11},{10,... | collective-permute-start | bytes 110600 | tf_op jit(solution)/shard_map/ppermute | solution.py:826
  136.8 3.2 %collective-permute-start.25 = (f32[9,8,128]{2,1,0:T(8,128)S(1)}, f32[9,8,128]{2,1,0:T(8,128)S(1)}, u32[]{:S(2)}, u32[]{:S(2)}) collective-permute-start(f32[9,8,128]{2,1,0:T(8,128)S(1)} %get-tuple-element.122.refs_0_), channel_id=1, source_target_pairs={{0,1},{1,0},{2,3},{3,2},{4,5},{5,4},{6,7},{7,6},{8,9},{9,8},{10,11... | collective-permute-start | bytes 110600 | tf_op jit(solution)/shard_map/ppermute | solution.py:826
  140.0 5.8 %collective-permute-start.28 = (f32[18,8,128]{2,1,0:T(8,128)S(1)}, f32[18,8,128]{2,1,0:T(8,128)S(1)}, u32[]{:S(2)}, u32[]{:S(2)}) collective-permute-start(f32[18,8,128]{2,1,0:T(8,128)S(1)} %get-tuple-element.123), channel_id=1, source_target_pairs={{0,4},{1,5},{2,6},{3,7},{4,0},{5,1},{6,2},{7,3},{8,12},{9,13},{10,... | collective-permute-start | bytes 221192 | tf_op jit(solution)/shard_map/ppermute | solution.py:826
  141.5 6.9 %collective-permute-start.29 = (f32[18,8,128]{2,1,0:T(8,128)S(1)}, f32[18,8,128]{2,1,0:T(8,128)S(1)}, u32[]{:S(2)}, u32[]{:S(2)}) collective-permute-start(f32[18,8,128]{2,1,0:T(8,128)S(1)} %get-tuple-element.124), channel_id=1, source_target_pairs={{4,8},{5,9},{6,10},{7,11},{8,4},{9,5},{10,6},{11,7},{12,16},{13,17... | collective-permute-start | bytes 221192 | tf_op jit(solution)/shard_map/ppermute | solution.py:826
  148.4 20.2 %copy-start.3 = (f32[3,32,8,128]{3,2,1,0:T(8,128)S(1)}, f32[3,32,8,128]{3,2,1,0:T(8,128)}, u32[]{:S(2)}) copy-start(f32[3,32,8,128]{3,2,1,0:T(8,128)} %copy-done.2) | copy-start | bytes 1179652
  148.4 20.2 %copy-start.17 = (f32[3,32,128]{2,1,0:T(8,128)S(1)}, f32[3,32,128]{2,1,0:T(8,128)}, u32[]{:S(2)}) copy-start(f32[3,32,128]{2,1,0:T(8,128)} %copy-done.16) | copy-start | bytes 147460
  151.2 6.3 %collective-permute-start.32 = (f32[24,8,128]{2,1,0:T(8,128)S(1)}, f32[24,8,128]{2,1,0:T(8,128)S(1)}, u32[]{:S(2)}, u32[]{:S(2)}) collective-permute-start(f32[24,8,128]{2,1,0:T(8,128)S(1)} %get-tuple-element.128.refs_0_), channel_id=1, source_target_pairs={{0,3},{1,2},{2,1},{3,0},{4,7},{5,6},{6,5},{7,4},{8,11},{9,10},{10,... | collective-permute-start | bytes 294920 | tf_op jit(solution)/shard_map/ppermute | solution.py:826
  152.5 5.8 %collective-permute-start.31 = (f32[24,8,128]{2,1,0:T(8,128)S(1)}, f32[24,8,128]{2,1,0:T(8,128)S(1)}, u32[]{:S(2)}, u32[]{:S(2)}) collective-permute-start(f32[24,8,128]{2,1,0:T(8,128)S(1)} %get-tuple-element.128.refs_0_), channel_id=1, source_target_pairs={{0,2},{1,3},{2,0},{3,1},{4,6},{5,7},{6,4},{7,5},{8,10},{9,11},{10,... | collective-permute-start | bytes 294920 | tf_op jit(solution)/shard_map/ppermute | solution.py:826
  153.5 4.9 %collective-permute-start.30 = (f32[24,8,128]{2,1,0:T(8,128)S(1)}, f32[24,8,128]{2,1,0:T(8,128)S(1)}, u32[]{:S(2)}, u32[]{:S(2)}) collective-permute-start(f32[24,8,128]{2,1,0:T(8,128)S(1)} %get-tuple-element.128.refs_0_), channel_id=1, source_target_pairs={{0,1},{1,0},{2,3},{3,2},{4,5},{5,4},{6,7},{7,6},{8,9},{9,8},{10,11... | collective-permute-start | bytes 294920 | tf_op jit(solution)/shard_map/ppermute | solution.py:826
  158.4 6.4 %collective-permute-start.33 = (f32[42,8,128]{2,1,0:T(8,128)S(1)}, f32[42,8,128]{2,1,0:T(8,128)S(1)}, u32[]{:S(2)}, u32[]{:S(2)}) collective-permute-start(f32[42,8,128]{2,1,0:T(8,128)S(1)} %get-tuple-element.129), channel_id=1, source_target_pairs={{0,4},{1,5},{2,6},{3,7},{4,0},{5,1},{6,2},{7,3},{8,12},{9,13},{10,... | collective-permute-start | bytes 516104 | tf_op jit(solution)/shard_map/ppermute | solution.py:826
  158.5 10.1 %collective-permute-start.34 = (f32[42,8,128]{2,1,0:T(8,128)S(1)}, f32[42,8,128]{2,1,0:T(8,128)S(1)}, u32[]{:S(2)}, u32[]{:S(2)}) collective-permute-start(f32[42,8,128]{2,1,0:T(8,128)S(1)} %get-tuple-element.130), channel_id=1, source_target_pairs={{4,8},{5,9},{6,10},{7,11},{8,4},{9,5},{10,6},{11,7},{12,16},{13,17... | collective-permute-start | bytes 516104 | tf_op jit(solution)/shard_map/ppermute | solution.py:826
  (5 other events, 3.0 us)
Sparse Core Ops, SparseCore 0:
  13.0 70.9 all-gather.2

commit v4 on v3

--- a/solution.py
+++ b/solution.py
@@ -413,13 +413,12 @@
     return jnp.where(s < count, 1.0, 0.0)
 
 
-def load_beta(inv, s, b, b1):
-    b[s] = inv[:, s, :].reshape(32, 8, 128)
-    for c, t in enumerate(restrict_planes(b, s, 0, 0.125)):
-        b1[s, c] = t
-
-
-def k_start(ghost, count, inv, faces, gathered, place, b, b1):
+def k_source(count, src, out):
+    for s in range(SLOTS):
+        out[s] = src[:, s, :].reshape(32, 8, 128) * used(count[0], s)
+
+
+def k_start(ghost, count, inv, b, b1, faces, gathered, place):
     bottom = []
     dev = place_of_device()[0]
     lane = lanes()
@@ -439,7 +438,9 @@
     place[24] = dev
     note = note.astype(F32)
     for s in range(SLOTS):
-        load_beta(inv, s, b, b1)
+        b[s] = inv[:, s, :].reshape(32, 8, 128)
+        for c, t in enumerate(restrict_planes(b, s, 0, 0.125)):
+            b1[s, c] = t
         bottom.append(restrict_planes(b1, s, 1, 0.125))
         pack_faces(b, s, FIRST[0], faces)
         pack_faces(b1, s, FIRST[1], faces)
@@ -477,19 +478,14 @@
             entry(12 + s * 8 + q, jnp.where(codes[f] >= 0, notes[found[f][0], found[f][1] + g], -1))
 
 
-def k_weights(count, src, inv, *refs):
+def k_weights(source, b, *refs):
     win, refs = refs[:6], refs[6:]
-    w, s_out, u, b1, faces, tab, (b, xg, yg, ends, gy, rows, notes, sem) = (
-        refs[:6], refs[6], refs[7], refs[8], refs[9], refs[10], refs[11:]
-    )
+    w, u, faces, tab, (xg, yg, ends, gy, rows, notes, sem) = refs[:6], refs[6], refs[7], refs[8], refs[9:]
     fill_table(win, rows, notes, sem, tab)
-    for s in range(SLOTS):
-        s_out[s] = src[:, s, :].reshape(32, 8, 128) * used(count[0], s)
-        load_beta(inv, s, b, b1)
     take_ghosts(tab, win, FIRST[0], xg, yg, ends)
 
     def first(s, i, r):
-        u[s, i] = s_out[s, i] * r
+        u[s, i] = source[s, i] * r
 
     make_weights(b, xg, yg, ends, gy, tab, 0, w, first)
     for s in range(SLOTS):
@@ -523,7 +519,7 @@
         pack_faces(u1, s, PART1, faces)
 
 
-def k_bottom_rhs(tab, t, u, *refs):
+def k_bottom_rhs(tab, t, u, beta_rows, *refs):
     win, w = refs[:6], refs[6:12]
     out, out_x, out_y, first_x, first_y, packed, xg, yg, ends, gy, res = refs[12:]
     take_ghosts(tab, win, PART1, xg, yg, ends)
@@ -538,15 +534,17 @@
 
     apply_near(out, out_x, out_y, gy, 1, w, emit)
     pack_bottom([restrict_planes(res, s, 1, 0.125) for s in range(SLOTS)], packed)
+    packed[12:24, :] = beta_rows[0:12, :]
+    packed[24:32, :] = beta_rows[16:24, :]
 
 
 def total(v):
     return jnp.sum(v, axis=(0, 1), keepdims=True)
 
 
-def unpack_bottom(rows, put):
+def unpack_bottom(rows, at, put):
     for r in range(12):
-        t = rows[:, r, :].T
+        t = rows[:, at + r, :].T
         for half in range(2):
             s, j = (half, r) if r < 8 else (2, r - 8 + 4 * half)
             for i in range(8):
@@ -571,8 +569,22 @@
                 p[s, dst, m] = face_gather(at[k], slot[k], lambda o: p[o, src + 1, m])
 
 
-def k_bottom_weights(beta_rows, cx, cy, cz, at_out, slot_out, counts_out, p):
-    note = beta_rows[:, 16, :].T
+def k_bottom(place, mine64, other64, *refs):
+    far, (out, faces, boxes_out) = refs[:9], refs[9:12]
+    p, r, x, q, cx, cy, cz, back, sq, rows, v1, gx, yg, gy = refs[12:26]
+    kept, sem = refs[26:35], refs[35]
+    copies = [pltpu.make_async_copy(a, b, sem.at[n]) for n, (a, b) in enumerate(zip(far, kept))]
+    for c in copies:
+        c.start()
+    first, u, gx0, gy0 = kept[:4]
+    w1 = kept[4:]
+    me = place[24]
+    for m in range(64):
+        here = me ^ ((m & 15) | ((m >> 4) << 5))
+        for half, there in ((mine64, here), (other64, here ^ 16)):
+            rows[there] = half[24 * m : 24 * m + 24, :]
+            sq[pl.ds(there, 1), :] = half[1536 + m : 1537 + m, :]
+    note = sq[...].T
     at, slot, pres = [], [], []
     for f in range(12):
         gf = jnp.broadcast_to(note[f : f + 1, :], (8, 128))
@@ -582,15 +594,18 @@
         at.append(dv)
         slot.append(gf.astype(I32) - 3 * dv)
         pres.append(jnp.where(has, 1.0, 0.0))
-        at_out[f] = dv.astype(F32)
-        slot_out[f] = slot[f].astype(F32)
-    counts_out[...] = jnp.broadcast_to(note[12:13, :], (8, 128))
+    counts = jnp.broadcast_to(note[12:13, :], (8, 128))
+    boxes = jnp.sum(counts[0:1], axis=1, keepdims=True)
+    boxes_out[...] = jnp.broadcast_to(boxes, (8, 128))
+
+    def fill_ghosts():
+        fill_bottom_ghosts(p, at, slot)
 
     def put_beta(s, j, i, tile):
         p[s, j + 1, i + 1] = tile
 
-    unpack_bottom(beta_rows, put_beta)
-    fill_bottom_ghosts(p, at, slot)
+    unpack_bottom(rows, 12, put_beta)
+    fill_ghosts()
     h = 0.5 * 0.0625
     low = subs() == 0
 
@@ -616,34 +631,10 @@
 
     lax.fori_loop(0, 8, weights, 0)
 
-
-def k_bottom(place, cx, cy, cz, at_in, slot_in, counts_in, mine64, other64, *refs):
-    far, (out, faces, boxes_out) = refs[:9], refs[9:12]
-    p, r, x, q, back, sq, rhs_rows, v1, gx, yg, gy = refs[12:23]
-    kept, sem = refs[23:32], refs[32]
-    copies = [pltpu.make_async_copy(a, b, sem.at[n]) for n, (a, b) in enumerate(zip(far, kept))]
-    for c in copies:
-        c.start()
-    first, u, gx0, gy0 = kept[:4]
-    w1 = kept[4:]
-    me = place[24]
-    for m in range(64):
-        here = me ^ ((m & 15) | ((m >> 4) << 5))
-        rhs_rows[here] = mine64[m]
-        rhs_rows[here ^ 16] = other64[m]
-    at = [at_in[f].astype(I32) for f in range(12)]
-    slot = [slot_in[f].astype(I32) for f in range(12)]
-    counts = counts_in[...]
-    boxes = jnp.sum(counts[0:1], axis=1, keepdims=True)
-    boxes_out[...] = jnp.broadcast_to(boxes, (8, 128))
-
-    def fill_ghosts():
-        fill_bottom_ghosts(p, at, slot)
-
     def put_rhs(s, j, i, tile):
         r[s, j, i] = tile
 
-    unpack_bottom(rhs_rows, put_rhs)
+    unpack_bottom(rows, 0, put_rhs)
 
     zero = jnp.zeros((8, 128), F32)
 
@@ -843,19 +834,20 @@
 
 
 def k_join(*refs):
-    n = refs[0].shape[0]
+    out = refs[4]
+    each = (out.shape[0] // 100) * 24
+    notes = each // 24
     for m in range(4):
-        refs[4][m * n : (m + 1) * n] = refs[m][...]
-
-
-def gather_rows(rows, beside):
-    rows = rows[None]
-    for unit in (1, 4, 32):
-        if unit == 32:
-            rows, beside = lax.optimization_barrier((rows, beside))
+        out[m * each : (m + 1) * each, :] = refs[m][0:each, :]
+        at = 4 * each + m * notes
+        out[at : at + notes, :] = refs[m][each : each + notes, :]
+
+
+def gather_rows(rows):
+    for unit, count in ((1, 104), (4, 400), (32, 1600)):
         got = [rows] + [swapped(rows, xor_pairs(m * unit)) for m in (1, 2, 3)]
-        rows = call(k_join, 0, got, [(4 * rows.shape[0],) + rows.shape[1:]])[0]
-    return tuple(beside) + (rows, swapped(rows, xor_pairs(16)))
+        rows = call(k_join, 0, got, [(count, 128)])[0]
+    return rows, swapped(rows, xor_pairs(16))
 
 
 def to_all(rows):
@@ -874,37 +866,34 @@
         wide = (SLOTS, n + 2, 8, 128)
         return [(SLOTS, n + 3, 8, 128), wide, wide, (SLOTS, n + 2, 128), wide, (SLOTS, 6, n, 128)]
 
-    faces, notes, place = call(
+    beta, beta1, faces, beta_rows, place = call(
         k_start, 2, (ghost_from, box_counts, view(inverse_density)),
-        [(FIRST_NOTES[0] + 1, 8, 128), (24, 128)], [fine, mid], tables=[(25,)],
+        [fine, mid, (FIRST_NOTES[0] + 1, 8, 128), (24, 128)], tables=[(25,)],
     )
-    beta_rows = lax.all_gather(notes, AX)
+    later, faces = lax.optimization_barrier((view(source_term), faces))
+    source = call(k_source, 1, (box_counts, later), [fine])[0]
     win = exchange(faces, FIRST, FIRST_NOTES)
     outs = call(
-        k_weights, 1, (box_counts, view(source_term), view(inverse_density)) + win,
-        weight_shapes(32) + [fine, fine, mid, face0], [fine, xg, gyf, ends, gyf], tables=[(5 * BOXES,)],
+        k_weights, 0, (source, beta) + win, weight_shapes(32) + [fine, face0], [xg, gyf, ends, gyf],
+        tables=[(5 * BOXES,)],
         extra=[pltpu.VMEM((16, 128), I32), pltpu.SMEM((16, 128), I32), pltpu.SemaphoreType.DMA],
     )
-    w, (source, first, beta1, faces, tab) = tuple(outs[:6]), outs[6:]
+    w, (first, faces, tab) = tuple(outs[:6]), outs[6:]
     w1 = tuple(call(k_weights_next, 1, (tab, beta1) + win, weight_shapes(16), [xg, gym, ends, gym]))
     u, u_x, u_y, first_x, first_y, f1, first1, faces = call(
         k_down, 1, (tab, source, first) + exchange(faces, [PART0]) + w + (w1[4],),
         [fine, gx, gyf, gx, gyf, mid, mid, face1], [xg, gyf, ends, gyf, fine],
     )
     u1, u1_x, u1_y, first1_x, first1_y, rows = call(
-        k_bottom_rhs, 1, (tab, f1, first1) + exchange(faces, [PART1]) + w1,
-        [mid, gx, gym, gx, gym, (16, 128)], [xg, gym, ends, gym, mid],
+        k_bottom_rhs, 1, (tab, f1, first1, beta_rows) + exchange(faces, [PART1]) + w1,
+        [mid, gx, gym, gx, gym, (32, 128)], [xg, gym, ends, gym, mid],
     )
     cube, padded = (SLOTS, 8, 8, 8, 128), (SLOTS, 10, 10, 8, 128)
-    bottom_w = call(
-        k_bottom_weights, 0, (beta_rows,),
-        [(SLOTS, 8, 9, 8, 128), (SLOTS, 9, 8, 8, 128), cube, (12, 8, 128), (12, 8, 128), (8, 128)], [padded],
-    )
     kept = [first1, u1, u1_x, u1_y] + list(w1[:5])
     u1, faces, boxes = call(
-        k_bottom, 1, (place,) + gather_rows(rows, tuple(bottom_w)) + tuple(kept), [mid, face1, (8, 128)],
-        [padded, cube, cube, cube, (DEVICES, 24, 128), (128, 128), (DEVICES, 16, 128), mid, gx, gym, gym]
-        + [a.shape for a in kept],
+        k_bottom, 1, (place,) + gather_rows(rows) + tuple(kept), [mid, face1, (8, 128)],
+        [padded, cube, cube, cube, (SLOTS, 8, 9, 8, 128), (SLOTS, 9, 8, 8, 128), cube, (DEVICES, 24, 128),
+         (128, 128), (DEVICES, 24, 128), mid, gx, gym, gym] + [a.shape for a in kept],
         hbm=len(kept), extra=[pltpu.SemaphoreType.DMA((len(kept),))],
     )
     u, faces = call(

time: 199 us -> 177 us (0.89)
  between operations: 15.1 us -> 1.54 us
  local copies, waits for them, and re-layouts: 9.03 us -> 1.09 us
  waiting for transfers between devices: 46.1 us -> 48.2 us
    unnamed x66 -> x6, local copies, waits for them, and re-layouts: 8.99 us -> 1.06 us
    ppermute x35, waiting for transfers between devices: 46.1 us -> 48.2 us  [swapped(): return lax.ppermute(block, AX, route)]
  transfers between devices with their start and end apart: 36 -> 35, of which waited for: 23 -> 23; matrix products, arithmetic and copies ran while one was open for 0% -> 0% of each run, Pallas kernels for 7% -> 1%
where the time goes in v4:
time: 177 us
  starting transfers between devices  68.3 us (39%)
  waiting for transfers between devices  48.2 us (27%)
  Pallas kernels  39.7 us (22%)
  blocking collectives  17.9 us (10%)
    ppermute x35, starting transfers between devices, swapped(): return lax.ppermute(block, AX, route)  68.3 us
    ppermute x35, waiting for transfers between devices, swapped(): return lax.ppermute(block, AX, route)  48.2 us
    pallas_call x18, Pallas kernels, call(): pl.pallas_call(kernel, out_shape=[shape(s) for s in outs] + [jax.ShapeDty...  39.7 us
    all_to_all x1, blocking collectives, to_all(): return lax.all_to_all(spread, AX, 0, 0)  17.9 us
  transfers between devices with their start and end apart: 35, of which 23 were waited for; matrix products, arithmetic and copies ran while one was open for 0% of the time, Pallas kernels for 1%

profile of v4, /device:TPU:1, one launch (start us, length us, event | category | flops | bytes accessed | tf_op | source)
XLA Modules:
  0.0 176.8 jit_solution(11464051769184550214)
XLA Ops:
  1.3 1.0 copy-done
  2.4 2.7 %shard_map.67 = (f32[3,32,8,128]{3,2,1,0:T(8,128)S(1)}, f32[3,16,8,128]{3,2,1,0:T(8,128)S(1)}, f32[34,8,128]{2,1,0:T(8,128)S(1)}, f32[24,128]{1,0:T(8,128)S(1)}, s32[25]{0:T(128)S(1)}) custom-call(s32[3,4]{1,0:T(4,128)S(1)} %copy-done.2, s32[1]{0:T(128)S(6)} %copy.7.count, f32[256,3,128]{2,1,0:T(4,128)S(1)} %bitcast.16), custom_call_target="tpu_custom_call" | custom-call | tf_op jit(solution)/shard_map/pallas_call | solution.py:805
  5.1 4.7 %collective-permute-start.2 = (f32[34,8,128]{2,1,0:T(8,128)S(1)}, f32[34,8,128]{2,1,0:T(8,128)S(1)}, u32[]{:S(2)}, u32[]{:S(2)}) collective-permute-start(f32[34,8,128]{2,1,0:T(8,128)S(1)} %get-tuple-element.62.refs_0_), channel_id=1, source_target_pairs={{0,3},{1,2},{2,1},{3,0},{4,7},{5,6},{6,5},{7,4},{8,11},{9,10},{10,... | collective-permute-start | bytes 417800 | tf_op jit(solution)/shard_map/ppermute | solution.py:817
  9.8 0.7 collective-permute-start
  10.4 5.2 %collective-permute-done.2.refs_3_ = f32[34,8,128]{2,1,0:T(8,128)S(1)} collective-permute-done((f32[34,8,128]{2,1,0:T(8,128)S(1)}, f32[34,8,128]{2,1,0:T(8,128)S(1)}, u32[]{:S(2)}, u32[]{:S(2)}) %collective-permute-start.2) | collective-permute-done | bytes 139296 | tf_op jit(solution)/shard_map/ppermute | solution.py:817
  15.6 1.0 collective-permute-done.refs_1_
  16.7 1.4 collective-permute-start.3
  18.0 6.2 %collective-permute-start.4 = (f32[64,8,128]{2,1,0:T(8,128)S(1)}, f32[64,8,128]{2,1,0:T(8,128)S(1)}, u32[]{:S(2)}, u32[]{:S(2)}) collective-permute-start(f32[64,8,128]{2,1,0:T(8,128)S(1)} %get-tuple-element.64), channel_id=1, source_target_pairs={{4,8},{5,9},{6,10},{7,11},{8,4},{9,5},{10,6},{11,7},{12,16},{13,17... | collective-permute-start | bytes 786440 | tf_op jit(solution)/shard_map/ppermute | solution.py:817
  24.3 0.3 shard_map.68.source.t
  24.6 5.1 %collective-permute-done.4.refs_5_ = f32[64,8,128]{2,1,0:T(8,128)S(1)} collective-permute-done((f32[64,8,128]{2,1,0:T(8,128)S(1)}, f32[64,8,128]{2,1,0:T(8,128)S(1)}, u32[]{:S(2)}, u32[]{:S(2)}) %collective-permute-start.4) | collective-permute-done | bytes 262176 | tf_op jit(solution)/shard_map/ppermute | solution.py:817
  29.7 3.0 %shard_map.70 = (f32[3,35,8,128]{3,2,1,0:T(8,128)S(1)}, f32[3,34,8,128]{3,2,1,0:T(8,128)S(1)}, f32[3,34,8,128]{3,2,1,0:T(8,128)S(1)}, f32[3,34,128]{2,1,0:T(8,12...) custom-call(f32[3,32,8,128]{3,2,1,0:T(8,128)S(1)} %shard_map.68.sour, ...), custom_call_target="tpu_custom_call" | custom-call | tf_op jit(solution)/shard_map/pallas_call | solution.py:805
  32.7 2.4 %collective-permute-start.7 = (f32[24,8,128]{2,1,0:T(8,128)S(1)}, f32[24,8,128]{2,1,0:T(8,128)S(1)}, u32[]{:S(2)}, u32[]{:S(2)}) collective-permute-start(f32[24,8,128]{2,1,0:T(8,128)S(1)} %get-tuple-element.67.refs_0_), channel_id=1, source_target_pairs={{0,3},{1,2},{2,1},{3,0},{4,7},{5,6},{6,5},{7,4},{8,11},{9,10},{10,... | collective-permute-start | bytes 294920 | tf_op jit(solution)/shard_map/ppermute | solution.py:817
  35.1 0.9 collective-permute-start.5
  36.0 1.9 %collective-permute-done.7.refs_3_ = f32[24,8,128]{2,1,0:T(8,128)S(1)} collective-permute-done((f32[24,8,128]{2,1,0:T(8,128)S(1)}, f32[24,8,128]{2,1,0:T(8,128)S(1)}, u32[]{:S(2)}, u32[]{:S(2)}) %collective-permute-start.7) | collective-permute-done | bytes 98336 | tf_op jit(solution)/shard_map/ppermute | solution.py:817
  37.9 2.2 %collective-permute-done.6.refs_2_ = f32[24,8,128]{2,1,0:T(8,128)S(1)} collective-permute-done((f32[24,8,128]{2,1,0:T(8,128)S(1)}, f32[24,8,128]{2,1,0:T(8,128)S(1)}, u32[]{:S(2)}, u32[]{:S(2)}) %collective-permute-start.6) | collective-permute-done | bytes 98336 | tf_op jit(solution)/shard_map/ppermute | solution.py:817
  40.2 7.0 %collective-permute-start.9 = (f32[42,8,128]{2,1,0:T(8,128)S(1)}, f32[42,8,128]{2,1,0:T(8,128)S(1)}, u32[]{:S(2)}, u32[]{:S(2)}) collective-permute-start(f32[42,8,128]{2,1,0:T(8,128)S(1)} %get-tuple-element.69), channel_id=1, source_target_pairs={{4,8},{5,9},{6,10},{7,11},{8,4},{9,5},{10,6},{11,7},{12,16},{13,17... | collective-permute-start | bytes 516104 | tf_op jit(solution)/shard_map/ppermute | solution.py:817
  47.2 1.7 shard_map.72
  48.9 1.8 %collective-permute-done.9.refs_5_ = f32[42,8,128]{2,1,0:T(8,128)S(1)} collective-permute-done((f32[42,8,128]{2,1,0:T(8,128)S(1)}, f32[42,8,128]{2,1,0:T(8,128)S(1)}, u32[]{:S(2)}, u32[]{:S(2)}) %collective-permute-start.9) | collective-permute-done | bytes 172064 | tf_op jit(solution)/shard_map/ppermute | solution.py:817
  50.7 3.6 %shard_map.73 = (f32[3,32,8,128]{3,2,1,0:T(8,128)S(1)}, f32[3,2,8,128]{3,2,1,0:T(8,128)S(1)}, f32[3,32,128]{2,1,0:T(8,128)S(1)}, f32[3,2,8,128]{3,2,1,0:T(8,128)...) custom-call(s32[180]{0:T(256)S(1)} %get-tuple-element.65.tab, ...), custom_call_target="tpu_custom_call" | custom-call | tf_op jit(solution)/shard_map/pallas_call | solution.py:805
  54.3 1.8 %collective-permute-start.12 = (f32[9,8,128]{2,1,0:T(8,128)S(1)}, f32[9,8,128]{2,1,0:T(8,128)S(1)}, u32[]{:S(2)}, u32[]{:S(2)}) collective-permute-start(f32[9,8,128]{2,1,0:T(8,128)S(1)} %get-tuple-element.81.refs_0_), channel_id=1, source_target_pairs={{0,3},{1,2},{2,1},{3,0},{4,7},{5,6},{6,5},{7,4},{8,11},{9,10},{10,... | collective-permute-start | bytes 110600 | tf_op jit(solution)/shard_map/ppermute | solution.py:817
  56.1 0.1 collective-permute-start.11
  56.2 1.4 collective-permute-start.10
  57.6 0.8 collective-permute-done.12.refs_3_
  58.4 2.0 %collective-permute-done.11.refs_2_ = f32[9,8,128]{2,1,0:T(8,128)S(1)} collective-permute-done((f32[9,8,128]{2,1,0:T(8,128)S(1)}, f32[9,8,128]{2,1,0:T(8,128)S(1)}, u32[]{:S(2)}, u32[]{:S(2)}) %collective-permute-start.11) | collective-permute-done | bytes 36896 | tf_op jit(solution)/shard_map/ppermute | solution.py:817
  60.6 7.0 %collective-permute-start.14 = (f32[18,8,128]{2,1,0:T(8,128)S(1)}, f32[18,8,128]{2,1,0:T(8,128)S(1)}, u32[]{:S(2)}, u32[]{:S(2)}) collective-permute-start(f32[18,8,128]{2,1,0:T(8,128)S(1)} %get-tuple-element.83), channel_id=1, source_target_pairs={{4,8},{5,9},{6,10},{7,11},{8,4},{9,5},{10,6},{11,7},{12,16},{13,17... | collective-permute-start | bytes 221192 | tf_op jit(solution)/shard_map/ppermute | solution.py:817
  67.6 2.1 %collective-permute-done.14.refs_5_ = f32[18,8,128]{2,1,0:T(8,128)S(1)} collective-permute-done((f32[18,8,128]{2,1,0:T(8,128)S(1)}, f32[18,8,128]{2,1,0:T(8,128)S(1)}, u32[]{:S(2)}, u32[]{:S(2)}) %collective-permute-start.14) | collective-permute-done | bytes 73760 | tf_op jit(solution)/shard_map/ppermute | solution.py:817
  69.7 2.4 %shard_map.75 = (f32[3,16,8,128]{3,2,1,0:T(8,128)S(1)}, f32[3,2,8,128]{3,2,1,0:T(8,128)S(1)}, f32[3,16,128]{2,1,0:T(8,128)S(1)}, f32[3,2,8,128]{3,2,1,0:T(8,128)...) custom-call(s32[180]{0:T(256)S(1)} %get-tuple-element.65.tab, f32[3,16,8,128]{3,2,1,0:T(8,128)S(1)} %get-tuple-element.79.t, ...), custom_call_target="tpu_custom_call" | custom-call | tf_op jit(solution)/shard_map/pallas_call | solution.py:805
  72.0 1.2 collective-permute-start.17
  73.2 1.1 collective-permute-start.16
  74.4 1.0 collective-permute-start.15
  75.4 0.5 collective-permute-done.17.refs_3_
  75.9 1.4 collective-permute-done.16.refs_2_
  77.3 2.4 %collective-permute-start.20 = (f32[104,128]{1,0:T(8,128)S(1)}, f32[104,128]{1,0:T(8,128)S(1)}, u32[]{:S(2)}, u32[]{:S(2)}) collective-permute-start(f32[104,128]{1,0:T(8,128)S(1)} %shard_map.76.refs_0_), channel_id=1, source_target_pairs={{0,12},{1,13},{2,14},{3,15},{4,8},{5,9},{6,10},{7,11},{8,4},{9,5},... | collective-permute-start | bytes 159752 | tf_op jit(solution)/shard_map/ppermute | solution.py:817
  79.7 0.9 collective-permute-start.18
  80.7 0.9 collective-permute-done.20.refs_3_
  81.6 2.7 %collective-permute-done.19.refs_2_ = f32[104,128]{1,0:T(8,128)S(1)} collective-permute-done((f32[104,128]{1,0:T(8,128)S(1)}, f32[104,128]{1,0:T(8,128)S(1)}, u32[]{:S(2)}, u32[]{:S(2)}) %collective-permute-start.19) | collective-permute-done | bytes 53280 | tf_op jit(solution)/shard_map/ppermute | solution.py:817
  84.3 1.2 collective-permute-start.23
  85.5 1.8 %collective-permute-start.22 = (f32[400,128]{1,0:T(8,128)S(1)}, f32[400,128]{1,0:T(8,128)S(1)}, u32[]{:S(2)}, u32[]{:S(2)}) collective-permute-start(f32[400,128]{1,0:T(8,128)S(1)} %shard_map.77.refs_0_), channel_id=1, source_target_pairs={{0,64},{1,65},{2,66},{3,67},{4,68},{5,69},{6,70},{7,71},{8,72},{9,... | collective-permute-start | bytes 614408 | tf_op jit(solution)/shard_map/ppermute | solution.py:817
  87.3 0.3 collective-permute-start.21
  87.6 4.8 %collective-permute-done.23.refs_3_ = f32[400,128]{1,0:T(8,128)S(1)} collective-permute-done((f32[400,128]{1,0:T(8,128)S(1)}, f32[400,128]{1,0:T(8,128)S(1)}, u32[]{:S(2)}, u32[]{:S(2)}) %collective-permute-start.23) | collective-permute-done | bytes 204832 | tf_op jit(solution)/shard_map/ppermute | solution.py:817
  92.4 0.9 collective-permute-done.21.refs_1_
  93.4 5.6 %collective-permute-start.24 = (f32[1600,128]{1,0:T(8,128)S(1)}, f32[1600,128]{1,0:T(8,128)S(1)}, u32[]{:S(2)}, u32[]{:S(2)}) collective-permute-start(f32[1600,128]{1,0:T(8,128)S(1)} %shard_map.78.mine64), channel_id=1, source_target_pairs={{0,16},{1,17},{2,18},{3,19},{4,20},{5,21},{6,22},{7,23},{8,24},{9,... | collective-permute-start | bytes 2457608 | tf_op jit(solution)/shard_map/ppermute | solution.py:817
  99.0 2.0 %collective-permute-done.24.other64 = f32[1600,128]{1,0:T(8,128)S(1)} collective-permute-done((f32[1600,128]{1,0:T(8,128)S(1)}, f32[1600,128]{1,0:T(8,128)S(1)}, u32[]{:S(2)}, u32[]{:S(2)}) %collective-permute-start.24) | collective-permute-done | bytes 819232 | tf_op jit(solution)/shard_map/ppermute | solution.py:817
  100.9 18.0 %shard_map.79 = (f32[3,16,8,128]{3,2,1,0:T(8,128)S(1)}, f32[9,8,128]{2,1,0:T(8,128)S(1)}, f32[8,128]{1,0:T(8,128)S(1)}) custom-call(s32[25]{0:T(128)S(1)} %get-tuple-element.91.place, f32[1600,128]{1,0:T(8,128)S(1)} %shard_map.78.mine64, f32[1600,128]{1,0:T(8,128)S(1)} %collective-permute-done.24.other64, ...), custom_call_target="tpu_custom_call" | custom-call | tf_op jit(solution)/shard_map/pallas_call | solution.py:805
  118.9 1.7 collective-permute-start.27
  120.6 1.1 collective-permute-start.26
  121.7 0.5 collective-permute-start.25
  122.2 0.8 collective-permute-done.27.refs_3_
  123.0 1.9 %collective-permute-done.26.refs_2_ = f32[9,8,128]{2,1,0:T(8,128)S(1)} collective-permute-done((f32[9,8,128]{2,1,0:T(8,128)S(1)}, f32[9,8,128]{2,1,0:T(8,128)S(1)}, u32[]{:S(2)}, u32[]{:S(2)}) %collective-permute-start.26) | collective-permute-done | bytes 36896 | tf_op jit(solution)/shard_map/ppermute | solution.py:817
  125.0 1.0 collective-permute-start.28
  126.0 4.9 %collective-permute-start.29 = (f32[18,8,128]{2,1,0:T(8,128)S(1)}, f32[18,8,128]{2,1,0:T(8,128)S(1)}, u32[]{:S(2)}, u32[]{:S(2)}) collective-permute-start(f32[18,8,128]{2,1,0:T(8,128)S(1)} %get-tuple-element.102), channel_id=1, source_target_pairs={{4,8},{5,9},{6,10},{7,11},{8,4},{9,5},{10,6},{11,7},{12,16},{13,17... | collective-permute-start | bytes 221192 | tf_op jit(solution)/shard_map/ppermute | solution.py:817
  131.0 2.1 %collective-permute-done.29.refs_5_ = f32[18,8,128]{2,1,0:T(8,128)S(1)} collective-permute-done((f32[18,8,128]{2,1,0:T(8,128)S(1)}, f32[18,8,128]{2,1,0:T(8,128)S(1)}, u32[]{:S(2)}, u32[]{:S(2)}) %collective-permute-start.29) | collective-permute-done | bytes 73760 | tf_op jit(solution)/shard_map/ppermute | solution.py:817
  133.0 2.7 %shard_map.81 = (f32[3,32,8,128]{3,2,1,0:T(8,128)S(1)}, f32[24,8,128]{2,1,0:T(8,128)S(1)}) custom-call(s32[180]{0:T(256)S(1)} %get-tuple-element.65.tab, f32[3,16,8,128]{3,2,1,0:T(8,128)S(1)} %get-tuple-element.78.u.refs_0_.first1, f32[3,2,8,128]{3,2,1,0:T(8,128)S(1)} %get-tuple-element.89.first1_x, f32[3,16,128]{2,1,0:T(8,128)S(1)} %get-tuple-element.90.first1_y, ...), custom_call_target="tpu_custom_call" | custom-call | tf_op jit(solution)/shard_map/pallas_call | solution.py:805
  135.7 1.3 collective-permute-start.32
  137.0 0.9 collective-permute-start.31
  138.0 1.1 collective-permute-start.30
  139.1 3.1 %collective-permute-done.32.refs_3_ = f32[24,8,128]{2,1,0:T(8,128)S(1)} collective-permute-done((f32[24,8,128]{2,1,0:T(8,128)S(1)}, f32[24,8,128]{2,1,0:T(8,128)S(1)}, u32[]{:S(2)}, u32[]{:S(2)}) %collective-permute-start.32) | collective-permute-done | bytes 98336 | tf_op jit(solution)/shard_map/ppermute | solution.py:817
  142.1 0.9 collective-permute-done.31.refs_2_
  143.1 0.1 collective-permute-done.30.refs_1_
  143.3 6.2 %collective-permute-start.34 = (f32[42,8,128]{2,1,0:T(8,128)S(1)}, f32[42,8,128]{2,1,0:T(8,128)S(1)}, u32[]{:S(2)}, u32[]{:S(2)}) collective-permute-start(f32[42,8,128]{2,1,0:T(8,128)S(1)} %get-tuple-element.108), channel_id=1, source_target_pairs={{4,8},{5,9},{6,10},{7,11},{8,4},{9,5},{10,6},{11,7},{12,16},{13,17... | collective-permute-start | bytes 516104 | tf_op jit(solution)/shard_map/ppermute | solution.py:817
  149.5 4.2 %collective-permute-done.34.refs_5_ = f32[42,8,128]{2,1,0:T(8,128)S(1)} collective-permute-done((f32[42,8,128]{2,1,0:T(8,128)S(1)}, f32[42,8,128]{2,1,0:T(8,128)S(1)}, u32[]{:S(2)}, u32[]{:S(2)}) %collective-permute-start.34) | collective-permute-done | bytes 172064 | tf_op jit(solution)/shard_map/ppermute | solution.py:817
  153.7 4.0 %shard_map.83 = (f32[3,32,8,128]{3,2,1,0:T(8,128)S(1)}, f32[256,3,128]{2,1,0:T(4,128)}, f32[1,128]{1,0:T(1,128)S(1)}) custom-call(s32[180]{0:T(256)S(1)} %get-tuple-element.65.tab, f32[3,32,8,128]{3,2,1,0:T(8,128)S(1)} %shard_map.68.source.t, f32[3,32,8,128]{3,2,1,0:T(8,128)S(1)} %get-tuple-element.103.u, f32[3,32,8,128]{3,2,1,0:T(8,128)S(1)} %get-tuple-element.66.u.first, ...), custom_call_target="tpu_custom_call" | custom-call | tf_op jit(solution)/shard_map/pallas_call | solution.py:805
  157.7 17.9 %all_to_all.5 = f32[128,1,128]{2,1,0:T(1,128)S(1)} all-to-all(f32[128,1,128]{2,1,0:T(1,128)S(1)} %broadcast_in_dim.9), channel_id=1, replica_groups=mesh['gx'=8,'gy'=16] {'gx','gy'}, dimensions={0} | all-to-all | bytes 131072 | tf_op jit(solution)/shard_map/all_to_all | solution.py:855
  175.7 1.1 shard_map.84
  (32 shorter events, 0.6 us)
Async XLA Ops:
  0.6 0.7 copy-start.2
  1.3 1.0 copy-start
  2.4 21.9 %copy-start.1 = (f32[3,32768]{1,0:T(4,128)S(1)}, f32[3,32768]{1,0:T(4,128)}, u32[]{:S(2)}) copy-start(f32[3,32768]{1,0:T(4,128)} %param.4) | copy-start | bytes 1179652
  5.1 10.5 %collective-permute-start.2 = (f32[34,8,128]{2,1,0:T(8,128)S(1)}, f32[34,8,128]{2,1,0:T(8,128)S(1)}, u32[]{:S(2)}, u32[]{:S(2)}) collective-permute-start(f32[34,8,128]{2,1,0:T(8,128)S(1)} %get-tuple-element.62.refs_0_), channel_id=1, source_target_pairs={{0,3},{1,2},{2,1},{3,0},{4,7},{5,6},{6,5},{7,4},{8,11},{9,10},{10,... | collective-permute-start | bytes 417800 | tf_op jit(solution)/shard_map/ppermute | solution.py:817
  9.8 5.8 %collective-permute-start.1 = (f32[34,8,128]{2,1,0:T(8,128)S(1)}, f32[34,8,128]{2,1,0:T(8,128)S(1)}, u32[]{:S(2)}, u32[]{:S(2)}) collective-permute-start(f32[34,8,128]{2,1,0:T(8,128)S(1)} %get-tuple-element.62.refs_0_), channel_id=1, source_target_pairs={{0,2},{1,3},{2,0},{3,1},{4,6},{5,7},{6,4},{7,5},{8,10},{9,11},{10,... | collective-permute-start | bytes 417800 | tf_op jit(solution)/shard_map/ppermute | solution.py:817
  9.8 6.8 %collective-permute-start = (f32[34,8,128]{2,1,0:T(8,128)S(1)}, f32[34,8,128]{2,1,0:T(8,128)S(1)}, u32[]{:S(2)}, u32[]{:S(2)}) collective-permute-start(f32[34,8,128]{2,1,0:T(8,128)S(1)} %get-tuple-element.62.refs_0_), channel_id=1, source_target_pairs={{0,1},{1,0},{2,3},{3,2},{4,5},{5,4},{6,7},{7,6},{8,9},{9,8},{10,11... | collective-permute-start | bytes 417800 | tf_op jit(solution)/shard_map/ppermute | solution.py:817
  16.7 7.9 %collective-permute-start.3 = (f32[64,8,128]{2,1,0:T(8,128)S(1)}, f32[64,8,128]{2,1,0:T(8,128)S(1)}, u32[]{:S(2)}, u32[]{:S(2)}) collective-permute-start(f32[64,8,128]{2,1,0:T(8,128)S(1)} %get-tuple-element.63), channel_id=1, source_target_pairs={{0,4},{1,5},{2,6},{3,7},{4,0},{5,1},{6,2},{7,3},{8,12},{9,13},{10,... | collective-permute-start | bytes 786440 | tf_op jit(solution)/shard_map/ppermute | solution.py:817
  18.0 11.6 %collective-permute-start.4 = (f32[64,8,128]{2,1,0:T(8,128)S(1)}, f32[64,8,128]{2,1,0:T(8,128)S(1)}, u32[]{:S(2)}, u32[]{:S(2)}) collective-permute-start(f32[64,8,128]{2,1,0:T(8,128)S(1)} %get-tuple-element.64), channel_id=1, source_target_pairs={{4,8},{5,9},{6,10},{7,11},{8,4},{9,5},{10,6},{11,7},{12,16},{13,17... | collective-permute-start | bytes 786440 | tf_op jit(solution)/shard_map/ppermute | solution.py:817
  32.7 5.2 %collective-permute-start.7 = (f32[24,8,128]{2,1,0:T(8,128)S(1)}, f32[24,8,128]{2,1,0:T(8,128)S(1)}, u32[]{:S(2)}, u32[]{:S(2)}) collective-permute-start(f32[24,8,128]{2,1,0:T(8,128)S(1)} %get-tuple-element.67.refs_0_), channel_id=1, source_target_pairs={{0,3},{1,2},{2,1},{3,0},{4,7},{5,6},{6,5},{7,4},{8,11},{9,10},{10,... | collective-permute-start | bytes 294920 | tf_op jit(solution)/shard_map/ppermute | solution.py:817
  35.1 5.0 %collective-permute-start.6 = (f32[24,8,128]{2,1,0:T(8,128)S(1)}, f32[24,8,128]{2,1,0:T(8,128)S(1)}, u32[]{:S(2)}, u32[]{:S(2)}) collective-permute-start(f32[24,8,128]{2,1,0:T(8,128)S(1)} %get-tuple-element.67.refs_0_), channel_id=1, source_target_pairs={{0,2},{1,3},{2,0},{3,1},{4,6},{5,7},{6,4},{7,5},{8,10},{9,11},{10,... | collective-permute-start | bytes 294920 | tf_op jit(solution)/shard_map/ppermute | solution.py:817
  35.1 5.0 %collective-permute-start.5 = (f32[24,8,128]{2,1,0:T(8,128)S(1)}, f32[24,8,128]{2,1,0:T(8,128)S(1)}, u32[]{:S(2)}, u32[]{:S(2)}) collective-permute-start(f32[24,8,128]{2,1,0:T(8,128)S(1)} %get-tuple-element.67.refs_0_), channel_id=1, source_target_pairs={{0,1},{1,0},{2,3},{3,2},{4,5},{5,4},{6,7},{7,6},{8,9},{9,8},{10,11... | collective-permute-start | bytes 294920 | tf_op jit(solution)/shard_map/ppermute | solution.py:817
  40.1 8.8 %collective-permute-start.8 = (f32[42,8,128]{2,1,0:T(8,128)S(1)}, f32[42,8,128]{2,1,0:T(8,128)S(1)}, u32[]{:S(2)}, u32[]{:S(2)}) collective-permute-start(f32[42,8,128]{2,1,0:T(8,128)S(1)} %get-tuple-element.68), channel_id=1, source_target_pairs={{0,4},{1,5},{2,6},{3,7},{4,0},{5,1},{6,2},{7,3},{8,12},{9,13},{10,... | collective-permute-start | bytes 516104 | tf_op jit(solution)/shard_map/ppermute | solution.py:817
  40.2 10.5 %collective-permute-start.9 = (f32[42,8,128]{2,1,0:T(8,128)S(1)}, f32[42,8,128]{2,1,0:T(8,128)S(1)}, u32[]{:S(2)}, u32[]{:S(2)}) collective-permute-start(f32[42,8,128]{2,1,0:T(8,128)S(1)} %get-tuple-element.69), channel_id=1, source_target_pairs={{4,8},{5,9},{6,10},{7,11},{8,4},{9,5},{10,6},{11,7},{12,16},{13,17... | collective-permute-start | bytes 516104 | tf_op jit(solution)/shard_map/ppermute | solution.py:817
  54.3 4.1 %collective-permute-start.12 = (f32[9,8,128]{2,1,0:T(8,128)S(1)}, f32[9,8,128]{2,1,0:T(8,128)S(1)}, u32[]{:S(2)}, u32[]{:S(2)}) collective-permute-start(f32[9,8,128]{2,1,0:T(8,128)S(1)} %get-tuple-element.81.refs_0_), channel_id=1, source_target_pairs={{0,3},{1,2},{2,1},{3,0},{4,7},{5,6},{6,5},{7,4},{8,11},{9,10},{10,... | collective-permute-start | bytes 110600 | tf_op jit(solution)/shard_map/ppermute | solution.py:817
  56.1 4.3 %collective-permute-start.11 = (f32[9,8,128]{2,1,0:T(8,128)S(1)}, f32[9,8,128]{2,1,0:T(8,128)S(1)}, u32[]{:S(2)}, u32[]{:S(2)}) collective-permute-start(f32[9,8,128]{2,1,0:T(8,128)S(1)} %get-tuple-element.81.refs_0_), channel_id=1, source_target_pairs={{0,2},{1,3},{2,0},{3,1},{4,6},{5,7},{6,4},{7,5},{8,10},{9,11},{10,... | collective-permute-start | bytes 110600 | tf_op jit(solution)/shard_map/ppermute | solution.py:817
  56.2 4.2 %collective-permute-start.10 = (f32[9,8,128]{2,1,0:T(8,128)S(1)}, f32[9,8,128]{2,1,0:T(8,128)S(1)}, u32[]{:S(2)}, u32[]{:S(2)}) collective-permute-start(f32[9,8,128]{2,1,0:T(8,128)S(1)} %get-tuple-element.81.refs_0_), channel_id=1, source_target_pairs={{0,1},{1,0},{2,3},{3,2},{4,5},{5,4},{6,7},{7,6},{8,9},{9,8},{10,11... | collective-permute-start | bytes 110600 | tf_op jit(solution)/shard_map/ppermute | solution.py:817
  60.5 7.1 %collective-permute-start.13 = (f32[18,8,128]{2,1,0:T(8,128)S(1)}, f32[18,8,128]{2,1,0:T(8,128)S(1)}, u32[]{:S(2)}, u32[]{:S(2)}) collective-permute-start(f32[18,8,128]{2,1,0:T(8,128)S(1)} %get-tuple-element.82), channel_id=1, source_target_pairs={{0,4},{1,5},{2,6},{3,7},{4,0},{5,1},{6,2},{7,3},{8,12},{9,13},{10,... | collective-permute-start | bytes 221192 | tf_op jit(solution)/shard_map/ppermute | solution.py:817
  60.6 9.1 %collective-permute-start.14 = (f32[18,8,128]{2,1,0:T(8,128)S(1)}, f32[18,8,128]{2,1,0:T(8,128)S(1)}, u32[]{:S(2)}, u32[]{:S(2)}) collective-permute-start(f32[18,8,128]{2,1,0:T(8,128)S(1)} %get-tuple-element.83), channel_id=1, source_target_pairs={{4,8},{5,9},{6,10},{7,11},{8,4},{9,5},{10,6},{11,7},{12,16},{13,17... | collective-permute-start | bytes 221192 | tf_op jit(solution)/shard_map/ppermute | solution.py:817
  72.0 3.9 %collective-permute-start.17 = (f32[32,128]{1,0:T(8,128)S(1)}, f32[32,128]{1,0:T(8,128)S(1)}, u32[]{:S(2)}, u32[]{:S(2)}) collective-permute-start(f32[32,128]{1,0:T(8,128)S(1)} %get-tuple-element.92.refs_0_), channel_id=1, source_target_pairs={{0,3},{1,2},{2,1},{3,0},{4,7},{5,6},{6,5},{7,4},{8,11},{9,10},{10,... | collective-permute-start | bytes 49160 | tf_op jit(solution)/shard_map/ppermute | solution.py:817
  73.2 4.1 %collective-permute-start.16 = (f32[32,128]{1,0:T(8,128)S(1)}, f32[32,128]{1,0:T(8,128)S(1)}, u32[]{:S(2)}, u32[]{:S(2)}) collective-permute-start(f32[32,128]{1,0:T(8,128)S(1)} %get-tuple-element.92.refs_0_), channel_id=1, source_target_pairs={{0,2},{1,3},{2,0},{3,1},{4,6},{5,7},{6,4},{7,5},{8,10},{9,11},{10,... | collective-permute-start | bytes 49160 | tf_op jit(solution)/shard_map/ppermute | solution.py:817
  74.4 3.0 %collective-permute-start.15 = (f32[32,128]{1,0:T(8,128)S(1)}, f32[32,128]{1,0:T(8,128)S(1)}, u32[]{:S(2)}, u32[]{:S(2)}) collective-permute-start(f32[32,128]{1,0:T(8,128)S(1)} %get-tuple-element.92.refs_0_), channel_id=1, source_target_pairs={{0,1},{1,0},{2,3},{3,2},{4,5},{5,4},{6,7},{7,6},{8,9},{9,8},{10,11... | collective-permute-start | bytes 49160 | tf_op jit(solution)/shard_map/ppermute | solution.py:817
  77.3 4.3 %collective-permute-start.20 = (f32[104,128]{1,0:T(8,128)S(1)}, f32[104,128]{1,0:T(8,128)S(1)}, u32[]{:S(2)}, u32[]{:S(2)}) collective-permute-start(f32[104,128]{1,0:T(8,128)S(1)} %shard_map.76.refs_0_), channel_id=1, source_target_pairs={{0,12},{1,13},{2,14},{3,15},{4,8},{5,9},{6,10},{7,11},{8,4},{9,5},... | collective-permute-start | bytes 159752 | tf_op jit(solution)/shard_map/ppermute | solution.py:817
  79.7 4.5 %collective-permute-start.19 = (f32[104,128]{1,0:T(8,128)S(1)}, f32[104,128]{1,0:T(8,128)S(1)}, u32[]{:S(2)}, u32[]{:S(2)}) collective-permute-start(f32[104,128]{1,0:T(8,128)S(1)} %shard_map.76.refs_0_), channel_id=1, source_target_pairs={{0,8},{1,9},{2,10},{3,11},{4,12},{5,13},{6,14},{7,15},{8,0},{9,1},... | collective-permute-start | bytes 159752 | tf_op jit(solution)/shard_map/ppermute | solution.py:817
  79.7 4.5 %collective-permute-start.18 = (f32[104,128]{1,0:T(8,128)S(1)}, f32[104,128]{1,0:T(8,128)S(1)}, u32[]{:S(2)}, u32[]{:S(2)}) collective-permute-start(f32[104,128]{1,0:T(8,128)S(1)} %shard_map.76.refs_0_), channel_id=1, source_target_pairs={{0,4},{1,5},{2,6},{3,7},{4,0},{5,1},{6,2},{7,3},{8,12},{9,13},{10,... | collective-permute-start | bytes 159752 | tf_op jit(solution)/shard_map/ppermute | solution.py:817
  84.3 8.1 %collective-permute-start.23 = (f32[400,128]{1,0:T(8,128)S(1)}, f32[400,128]{1,0:T(8,128)S(1)}, u32[]{:S(2)}, u32[]{:S(2)}) collective-permute-start(f32[400,128]{1,0:T(8,128)S(1)} %shard_map.77.refs_0_), channel_id=1, source_target_pairs={{0,96},{1,97},{2,98},{3,99},{4,100},{5,101},{6,102},{7,103},{8,104... | collective-permute-start | bytes 614408 | tf_op jit(solution)/shard_map/ppermute | solution.py:817
  85.5 6.9 %collective-permute-start.22 = (f32[400,128]{1,0:T(8,128)S(1)}, f32[400,128]{1,0:T(8,128)S(1)}, u32[]{:S(2)}, u32[]{:S(2)}) collective-permute-start(f32[400,128]{1,0:T(8,128)S(1)} %shard_map.77.refs_0_), channel_id=1, source_target_pairs={{0,64},{1,65},{2,66},{3,67},{4,68},{5,69},{6,70},{7,71},{8,72},{9,... | collective-permute-start | bytes 614408 | tf_op jit(solution)/shard_map/ppermute | solution.py:817
  87.3 6.0 %collective-permute-start.21 = (f32[400,128]{1,0:T(8,128)S(1)}, f32[400,128]{1,0:T(8,128)S(1)}, u32[]{:S(2)}, u32[]{:S(2)}) collective-permute-start(f32[400,128]{1,0:T(8,128)S(1)} %shard_map.77.refs_0_), channel_id=1, source_target_pairs={{0,32},{1,33},{2,34},{3,35},{4,36},{5,37},{6,38},{7,39},{8,40},{9,... | collective-permute-start | bytes 614408 | tf_op jit(solution)/shard_map/ppermute | solution.py:817
  93.4 7.6 %collective-permute-start.24 = (f32[1600,128]{1,0:T(8,128)S(1)}, f32[1600,128]{1,0:T(8,128)S(1)}, u32[]{:S(2)}, u32[]{:S(2)}) collective-permute-start(f32[1600,128]{1,0:T(8,128)S(1)} %shard_map.78.mine64), channel_id=1, source_target_pairs={{0,16},{1,17},{2,18},{3,19},{4,20},{5,21},{6,22},{7,23},{8,24},{9,... | collective-permute-start | bytes 2457608 | tf_op jit(solution)/shard_map/ppermute | solution.py:817
  118.9 4.1 %collective-permute-start.27 = (f32[9,8,128]{2,1,0:T(8,128)S(1)}, f32[9,8,128]{2,1,0:T(8,128)S(1)}, u32[]{:S(2)}, u32[]{:S(2)}) collective-permute-start(f32[9,8,128]{2,1,0:T(8,128)S(1)} %get-tuple-element.100.refs_0_), channel_id=1, source_target_pairs={{0,3},{1,2},{2,1},{3,0},{4,7},{5,6},{6,5},{7,4},{8,11},{9,10},{10,... | collective-permute-start | bytes 110600 | tf_op jit(solution)/shard_map/ppermute | solution.py:817
  120.6 4.3 %collective-permute-start.26 = (f32[9,8,128]{2,1,0:T(8,128)S(1)}, f32[9,8,128]{2,1,0:T(8,128)S(1)}, u32[]{:S(2)}, u32[]{:S(2)}) collective-permute-start(f32[9,8,128]{2,1,0:T(8,128)S(1)} %get-tuple-element.100.refs_0_), channel_id=1, source_target_pairs={{0,2},{1,3},{2,0},{3,1},{4,6},{5,7},{6,4},{7,5},{8,10},{9,11},{10,... | collective-permute-start | bytes 110600 | tf_op jit(solution)/shard_map/ppermute | solution.py:817
  121.7 3.3 %collective-permute-start.25 = (f32[9,8,128]{2,1,0:T(8,128)S(1)}, f32[9,8,128]{2,1,0:T(8,128)S(1)}, u32[]{:S(2)}, u32[]{:S(2)}) collective-permute-start(f32[9,8,128]{2,1,0:T(8,128)S(1)} %get-tuple-element.100.refs_0_), channel_id=1, source_target_pairs={{0,1},{1,0},{2,3},{3,2},{4,5},{5,4},{6,7},{7,6},{8,9},{9,8},{10,11... | collective-permute-start | bytes 110600 | tf_op jit(solution)/shard_map/ppermute | solution.py:817
  125.0 6.0 %collective-permute-start.28 = (f32[18,8,128]{2,1,0:T(8,128)S(1)}, f32[18,8,128]{2,1,0:T(8,128)S(1)}, u32[]{:S(2)}, u32[]{:S(2)}) collective-permute-start(f32[18,8,128]{2,1,0:T(8,128)S(1)} %get-tuple-element.101), channel_id=1, source_target_pairs={{0,4},{1,5},{2,6},{3,7},{4,0},{5,1},{6,2},{7,3},{8,12},{9,13},{10,... | collective-permute-start | bytes 221192 | tf_op jit(solution)/shard_map/ppermute | solution.py:817
  126.0 7.0 %collective-permute-start.29 = (f32[18,8,128]{2,1,0:T(8,128)S(1)}, f32[18,8,128]{2,1,0:T(8,128)S(1)}, u32[]{:S(2)}, u32[]{:S(2)}) collective-permute-start(f32[18,8,128]{2,1,0:T(8,128)S(1)} %get-tuple-element.102), channel_id=1, source_target_pairs={{4,8},{5,9},{6,10},{7,11},{8,4},{9,5},{10,6},{11,7},{12,16},{13,17... | collective-permute-start | bytes 221192 | tf_op jit(solution)/shard_map/ppermute | solution.py:817
  135.7 6.4 %collective-permute-start.32 = (f32[24,8,128]{2,1,0:T(8,128)S(1)}, f32[24,8,128]{2,1,0:T(8,128)S(1)}, u32[]{:S(2)}, u32[]{:S(2)}) collective-permute-start(f32[24,8,128]{2,1,0:T(8,128)S(1)} %get-tuple-element.106.refs_0_), channel_id=1, source_target_pairs={{0,3},{1,2},{2,1},{3,0},{4,7},{5,6},{6,5},{7,4},{8,11},{9,10},{10,... | collective-permute-start | bytes 294920 | tf_op jit(solution)/shard_map/ppermute | solution.py:817
  137.0 6.0 %collective-permute-start.31 = (f32[24,8,128]{2,1,0:T(8,128)S(1)}, f32[24,8,128]{2,1,0:T(8,128)S(1)}, u32[]{:S(2)}, u32[]{:S(2)}) collective-permute-start(f32[24,8,128]{2,1,0:T(8,128)S(1)} %get-tuple-element.106.refs_0_), channel_id=1, source_target_pairs={{0,2},{1,3},{2,0},{3,1},{4,6},{5,7},{6,4},{7,5},{8,10},{9,11},{10,... | collective-permute-start | bytes 294920 | tf_op jit(solution)/shard_map/ppermute | solution.py:817
  138.0 5.2 %collective-permute-start.30 = (f32[24,8,128]{2,1,0:T(8,128)S(1)}, f32[24,8,128]{2,1,0:T(8,128)S(1)}, u32[]{:S(2)}, u32[]{:S(2)}) collective-permute-start(f32[24,8,128]{2,1,0:T(8,128)S(1)} %get-tuple-element.106.refs_0_), channel_id=1, source_target_pairs={{0,1},{1,0},{2,3},{3,2},{4,5},{5,4},{6,7},{7,6},{8,9},{9,8},{10,11... | collective-permute-start | bytes 294920 | tf_op jit(solution)/shard_map/ppermute | solution.py:817
  143.2 6.3 %collective-permute-start.33 = (f32[42,8,128]{2,1,0:T(8,128)S(1)}, f32[42,8,128]{2,1,0:T(8,128)S(1)}, u32[]{:S(2)}, u32[]{:S(2)}) collective-permute-start(f32[42,8,128]{2,1,0:T(8,128)S(1)} %get-tuple-element.107), channel_id=1, source_target_pairs={{0,4},{1,5},{2,6},{3,7},{4,0},{5,1},{6,2},{7,3},{8,12},{9,13},{10,... | collective-permute-start | bytes 516104 | tf_op jit(solution)/shard_map/ppermute | solution.py:817
  143.3 10.4 %collective-permute-start.34 = (f32[42,8,128]{2,1,0:T(8,128)S(1)}, f32[42,8,128]{2,1,0:T(8,128)S(1)}, u32[]{:S(2)}, u32[]{:S(2)}) collective-permute-start(f32[42,8,128]{2,1,0:T(8,128)S(1)} %get-tuple-element.108), channel_id=1, source_target_pairs={{4,8},{5,9},{6,10},{7,11},{8,4},{9,5},{10,6},{11,7},{12,16},{13,17... | collective-permute-start | bytes 516104 | tf_op jit(solution)/shard_map/ppermute | solution.py:817

commit v5 on v4

--- a/solution.py
+++ b/solution.py
@@ -299,7 +299,7 @@
             slab[s, m] = t
 
 
-def apply_level(v, before, after, gy, ends, lv, w, emit, wide=None):
+def apply_level(v, before, after, gy, ends, lv, w, emit, wide=None, unroll=8):
     cx, cy, cz, wn = w[:4]
     n = PLANES[lv]
     tl = Tile(lv)
@@ -333,7 +333,7 @@
             out.append((nxt, fnext))
         return tuple(out)
 
-    last = planes_loop(n, body, tuple(first))
+    last = planes_loop(n, body, tuple(first), unroll)
     if wide:
         for s in range(SLOTS):
             here, fx = last[s]
@@ -352,7 +352,7 @@
     return y, a + b + (fz - roll(fz, 128 - zs, 1))
 
 
-def sweep_wide(v, xg, yg, ends, gy, lv, w, first, first_x, first_y, out, out_x, out_y):
+def sweep_wide(v, xg, yg, ends, gy, lv, w, first, first_x, first_y, out, out_x, out_y, unroll=8):
     rd, slab = w[4:]
     n = PLANES[lv]
     set_near(yg, gy, n)
@@ -363,15 +363,15 @@
     def wide(s, e, here, av):
         out_x[s, e] = here + (first_x(s, e) - av * rd[s, (n + 1) * e])
 
-    apply_level(v, lambda s, g: xg[s, 1 - g], lambda s, g: xg[s, 2 + g], gy, ends, lv, w, emit, wide)
+    apply_level(v, lambda s, g: xg[s, 1 - g], lambda s, g: xg[s, 2 + g], gy, ends, lv, w, emit, wide, unroll)
     for s in range(SLOTS):
         y, a = apply_slab(yg, v, s, ends, lv, slab)
         out_y[s] = y + (first_y(s) - a * slab[s, 5])
 
 
-def apply_near(v, gx, yg, gy, lv, w, emit):
+def apply_near(v, gx, yg, gy, lv, w, emit, unroll=8):
     set_near(yg, gy, PLANES[lv])
-    apply_level(v, lambda s, g: gx[s, 0], lambda s, g: gx[s, 1], gy, None, lv, w, emit)
+    apply_level(v, lambda s, g: gx[s, 0], lambda s, g: gx[s, 1], gy, None, lv, w, emit, None, unroll)
 
 
 def restrict_planes(v, s, lv, scale):
@@ -418,11 +418,19 @@
         out[s] = src[:, s, :].reshape(32, 8, 128) * used(count[0], s)
 
 
-def k_start(ghost, count, inv, b, b1, faces, gathered, place):
-    bottom = []
+def k_bottom_beta(ghost, count, b1, out):
+    lane = lanes()
+    note = jnp.where(lane == 12, jnp.full((8, 128), count[0]), 0)
+    for s in range(SLOTS):
+        for f in range(4):
+            note = jnp.where(lane == s * 4 + f, jnp.full((8, 128), ghost[s, f]), note)
+    pack_bottom([restrict_planes(b1, s, 1, 0.125) for s in range(SLOTS)], out)
+    out[16:24, :] = note.astype(F32)
+
+
+def k_start(ghost, inv, b, b1, faces, place):
     dev = place_of_device()[0]
     lane = lanes()
-    note = jnp.where(lane == 12, jnp.full((8, 128), count[0]), 0)
     codes = jnp.zeros((8, 128), I32)
     for s in range(SLOTS):
         for f in range(4):
@@ -433,20 +441,15 @@
             local = jnp.where(has, g - 3 * owner, 0)
             place[k] = owner
             place[12 + k] = local
-            note = jnp.where(lane == k, jnp.full((8, 128), g), note)
             codes = jnp.where(lane == k, jnp.full((8, 128), jnp.where(has, owner * 4 + local, -1)), codes)
     place[24] = dev
-    note = note.astype(F32)
     for s in range(SLOTS):
         b[s] = inv[:, s, :].reshape(32, 8, 128)
         for c, t in enumerate(restrict_planes(b, s, 0, 0.125)):
             b1[s, c] = t
-        bottom.append(restrict_planes(b1, s, 1, 0.125))
         pack_faces(b, s, FIRST[0], faces)
         pack_faces(b1, s, FIRST[1], faces)
     faces[FIRST_NOTES[0]] = codes.astype(F32)
-    pack_bottom(bottom, gathered)
-    gathered[16:24, :] = note
 
 
 def fill_table(win, rows, notes, sem, tab):
@@ -629,7 +632,7 @@
                 cz[s, m, i] = jnp.where(low, 0.0, h * (b + roll(b, 1, 0)))
         return 0
 
-    lax.fori_loop(0, 8, weights, 0)
+    lax.fori_loop(0, 8, weights, 0, unroll=8)
 
     def put_rhs(s, j, i, tile):
         r[s, j, i] = tile
@@ -637,6 +640,12 @@
     unpack_bottom(rows, 0, put_rhs)
 
     zero = jnp.zeros((8, 128), F32)
+
+    def whole(a):
+        a = ((a[0] + a[1]) + (a[2] + a[3])) + ((a[4] + a[5]) + (a[6] + a[7]))
+        for sh in (4, 2, 1):
+            a = a + roll(a, sh, 0)
+        return jnp.broadcast_to(jnp.sum(a, axis=1, keepdims=True), (8, 128))
 
     def each(fn):
         def step(j, acc):
@@ -646,9 +655,7 @@
                     acc[i] = fn(s, j, i, acc[i])
             return tuple(acc)
 
-        a = lax.fori_loop(0, 8, step, (zero,) * 8, unroll=2)
-        a = ((a[0] + a[1]) + (a[2] + a[3])) + ((a[4] + a[5]) + (a[6] + a[7]))
-        return jnp.broadcast_to(total(a), (8, 128))
+        return whole(lax.fori_loop(0, 8, step, (zero,) * 8, unroll=8))
 
     mean = each(lambda s, j, i, acc: acc + r[s, j, i]) / jnp.broadcast_to(boxes * 512.0, (8, 128))
     valid = [jnp.where(counts > s + 0.5, 1.0, 0.0) for s in range(SLOTS)]
@@ -662,18 +669,28 @@
 
     rr = each(shift)
 
-    def image(s, j, i, acc):
-        here = p[s, j + 1, i + 1]
-        a = cx[s, j, i] * (here - p[s, j + 1, i]) + cx[s, j, i + 1] * (here - p[s, j + 1, i + 2])
-        b = cy[s, j, i] * (here - p[s, j, i + 1]) + cy[s, j + 1, i] * (here - p[s, j + 2, i + 1])
-        fz = cz[s, j, i] * (here - roll(here, 1, 0))
-        v = a + b + (fz - roll(fz, 7, 0))
-        q[s, j, i] = v
-        return acc + here * v
+    def image():
+        def step(j, acc):
+            acc = list(acc)
+            for s in range(SLOTS):
+                here = p[s, j + 1, 1]
+                fx = cx[s, j, 0] * (here - p[s, j + 1, 0])
+                for i in range(8):
+                    nxt = p[s, j + 1, i + 2]
+                    fnext = cx[s, j, i + 1] * (nxt - here)
+                    b = cy[s, j, i] * (here - p[s, j, i + 1]) + cy[s, j + 1, i] * (here - p[s, j + 2, i + 1])
+                    fz = cz[s, j, i] * (here - roll(here, 1, 0))
+                    v = (fx - fnext) + b + (fz - roll(fz, 7, 0))
+                    q[s, j, i] = v
+                    acc[i] = acc[i] + here * v
+                    here, fx = nxt, fnext
+            return tuple(acc)
+
+        return whole(lax.fori_loop(0, 8, step, (zero,) * 8, unroll=8))
 
     def iteration(it, rr):
         fill_ghosts()
-        alpha = rr / each(image)
+        alpha = rr / image()
 
         def step(s, j, i, acc):
             x[s, j, i] = x[s, j, i] + alpha * p[s, j + 1, i + 1]
@@ -690,12 +707,12 @@
                     p[s, j + 1, i + 1] = r[s, j, i] + ratio * p[s, j + 1, i + 1]
             return 0
 
-        lax.fori_loop(0, 8, turn, 0)
+        lax.fori_loop(0, 8, turn, 0, unroll=8)
         return rr_next
 
     rr = lax.fori_loop(0, BOTTOM_ITERS - 1, iteration, rr)
     fill_ghosts()
-    alpha = rr / each(image)
+    alpha = rr / image()
 
     for row in range(12):
         for half in range(2):
@@ -768,12 +785,12 @@
     win, w = refs[:6], refs[6:12]
     out, res_out, sums, out_x, out_y, xg, yg, ends, gy, res = refs[12:]
     take_ghosts(tab, win, PART0, xg, yg, ends)
-    sweep_wide(u, xg, yg, ends, gy, 0, w, first, lambda s, e: first_x[s, e], lambda s: first_y[s], out, out_x, out_y)
+    sweep_wide(u, xg, yg, ends, gy, 0, w, first, lambda s, e: first_x[s, e], lambda s: first_y[s], out, out_x, out_y, 32)
 
     def emit(s, i, here, av):
         res[s, i] = t[s, i] - av
 
-    apply_near(out, out_x, out_y, gy, 0, w, emit)
+    apply_near(out, out_x, out_y, gy, 0, w, emit, 32)
     su = jnp.zeros((8, 128), F32)
     sr = jnp.zeros((8, 128), F32)
     for s in range(SLOTS):
@@ -827,10 +844,11 @@
         got.append(swapped(faces, xor_pairs(m)))
     tiles = parts[-1].side + parts[-1].side_tiles + (4 if notes else 0)
     sides = call(functools.partial(k_relay, parts, notes), 0, got, [(tiles, 8, 128)] * 2)
-    for odd in (0, 1):
+    beside = [None, None]
+    for odd in (1, 0):
         pairs = [(i, i + 4) for i in range(DEVICES - 4) if (i // 4) % 2 == odd]
-        got.append(swapped(sides[odd], pairs))
-    return tuple(got)
+        beside[odd] = swapped(sides[odd], pairs)
+    return tuple(got + beside)
 
 
 def k_join(*refs):
@@ -866,10 +884,11 @@
         wide = (SLOTS, n + 2, 8, 128)
         return [(SLOTS, n + 3, 8, 128), wide, wide, (SLOTS, n + 2, 128), wide, (SLOTS, 6, n, 128)]
 
-    beta, beta1, faces, beta_rows, place = call(
-        k_start, 2, (ghost_from, box_counts, view(inverse_density)),
-        [fine, mid, (FIRST_NOTES[0] + 1, 8, 128), (24, 128)], tables=[(25,)],
+    beta, beta1, faces, place = call(
+        k_start, 1, (ghost_from, view(inverse_density)),
+        [fine, mid, (FIRST_NOTES[0] + 1, 8, 128)], tables=[(25,)],
     )
+    beta_rows = call(k_bottom_beta, 2, (ghost_from, box_counts, beta1), [(24, 128)])[0]
     later, faces = lax.optimization_barrier((view(source_term), faces))
     source = call(k_source, 1, (box_counts, later), [fine])[0]
     win = exchange(faces, FIRST, FIRST_NOTES)

time: 177 us -> 171 us (0.966)
  Pallas kernels: 39.7 us -> 34.3 us
    pallas_call x18 -> x19, Pallas kernels: 39.7 us -> 34.3 us  [call(): pl.pallas_call(kernel, out_shape=[shape(s) for s in outs] + [jax.ShapeDty...]
  transfers between devices with their start and end apart: 35 -> 35, of which waited for: 23 -> 23; matrix products, arithmetic and copies ran while one was open for 0% -> 0% of each run, Pallas kernels for 1% -> 2%
where the time goes in v5:
time: 171 us
  starting transfers between devices  68.3 us (40%)
  waiting for transfers between devices  46.7 us (27%)
  Pallas kernels  34.3 us (20%)
  blocking collectives  17.9 us (10%)
  local copies, waits for them, and re-layouts  1.76 us (1%)
    ppermute x35, starting transfers between devices, swapped(): return lax.ppermute(block, AX, route)  68.3 us
    ppermute x35, waiting for transfers between devices, swapped(): return lax.ppermute(block, AX, route)  46.7 us
    pallas_call x19, Pallas kernels, call(): pl.pallas_call(kernel, out_shape=[shape(s) for s in outs] + [jax.ShapeDty...  34.3 us
    all_to_all x1, blocking collectives, to_all(): return lax.all_to_all(spread, AX, 0, 0)  17.9 us
  transfers between devices with their start and end apart: 35, of which 23 were waited for; matrix products, arithmetic and copies ran while one was open for 0% of the time, Pallas kernels for 2%

profile of v5, /device:TPU:1, one launch (start us, length us, event | category | flops | bytes accessed | tf_op | source)
XLA Modules:
  0.0 170.6 jit_solution(3548849266266661662)
XLA Ops:
  0.6 1.0 copy-done
  1.7 0.7 copy-done.2
  2.4 2.0 %shard_map.67 = (f32[3,32,8,128]{3,2,1,0:T(8,128)S(1)}, f32[3,16,8,128]{3,2,1,0:T(8,128)S(1)}, f32[34,8,128]{2,1,0:T(8,128)S(1)}, s32[25]{0:T(128)S(1)}) custom-call(s32[3,4]{1,0:T(4,128)S(1)} %copy-done.2, f32[256,3,128]{2,1,0:T(4,128)S(1)} %bitcast.16), custom_call_target="tpu_custom_call" | custom-call | tf_op jit(solution)/shard_map/pallas_call | solution.py:822
  4.4 4.7 %collective-permute-start.2 = (f32[34,8,128]{2,1,0:T(8,128)S(1)}, f32[34,8,128]{2,1,0:T(8,128)S(1)}, u32[]{:S(2)}, u32[]{:S(2)}) collective-permute-start(f32[34,8,128]{2,1,0:T(8,128)S(1)} %get-tuple-element.61.refs_0_), channel_id=1, source_target_pairs={{0,3},{1,2},{2,1},{3,0},{4,7},{5,6},{6,5},{7,4},{8,11},{9,10},{10,... | collective-permute-start | bytes 417800 | tf_op jit(solution)/shard_map/ppermute | solution.py:834
  9.0 0.7 collective-permute-start
  9.7 5.2 %collective-permute-done.2.refs_3_ = f32[34,8,128]{2,1,0:T(8,128)S(1)} collective-permute-done((f32[34,8,128]{2,1,0:T(8,128)S(1)}, f32[34,8,128]{2,1,0:T(8,128)S(1)}, u32[]{:S(2)}, u32[]{:S(2)}) %collective-permute-start.2) | collective-permute-done | bytes 139296 | tf_op jit(solution)/shard_map/ppermute | solution.py:834
  14.9 1.0 collective-permute-done.refs_1_
  15.9 1.4 collective-permute-start.3
  17.3 6.2 %collective-permute-start.4 = (f32[64,8,128]{2,1,0:T(8,128)S(1)}, f32[64,8,128]{2,1,0:T(8,128)S(1)}, u32[]{:S(2)}, u32[]{:S(2)}) collective-permute-start(f32[64,8,128]{2,1,0:T(8,128)S(1)} %get-tuple-element.63), channel_id=1, source_target_pairs={{4,8},{5,9},{6,10},{7,11},{8,4},{9,5},{10,6},{11,7},{12,16},{13,17... | collective-permute-start | bytes 786440 | tf_op jit(solution)/shard_map/ppermute | solution.py:834
  24.2 0.3 shard_map.68.source.t
  24.5 4.5 %collective-permute-done.4.refs_5_ = f32[64,8,128]{2,1,0:T(8,128)S(1)} collective-permute-done((f32[64,8,128]{2,1,0:T(8,128)S(1)}, f32[64,8,128]{2,1,0:T(8,128)S(1)}, u32[]{:S(2)}, u32[]{:S(2)}) %collective-permute-start.4) | collective-permute-done | bytes 262176 | tf_op jit(solution)/shard_map/ppermute | solution.py:834
  28.9 3.0 %shard_map.70 = (f32[3,35,8,128]{3,2,1,0:T(8,128)S(1)}, f32[3,34,8,128]{3,2,1,0:T(8,128)S(1)}, f32[3,34,8,128]{3,2,1,0:T(8,128)S(1)}, f32[3,34,128]{2,1,0:T(8,12...) custom-call(f32[3,32,8,128]{3,2,1,0:T(8,128)S(1)} %shard_map.68.sour, ...), custom_call_target="tpu_custom_call" | custom-call | tf_op jit(solution)/shard_map/pallas_call | solution.py:822
  31.9 2.4 %collective-permute-start.7 = (f32[24,8,128]{2,1,0:T(8,128)S(1)}, f32[24,8,128]{2,1,0:T(8,128)S(1)}, u32[]{:S(2)}, u32[]{:S(2)}) collective-permute-start(f32[24,8,128]{2,1,0:T(8,128)S(1)} %get-tuple-element.66.refs_0_), channel_id=1, source_target_pairs={{0,3},{1,2},{2,1},{3,0},{4,7},{5,6},{6,5},{7,4},{8,11},{9,10},{10,... | collective-permute-start | bytes 294920 | tf_op jit(solution)/shard_map/ppermute | solution.py:834
  34.3 0.9 collective-permute-start.5
  35.3 1.9 %collective-permute-done.7.refs_3_ = f32[24,8,128]{2,1,0:T(8,128)S(1)} collective-permute-done((f32[24,8,128]{2,1,0:T(8,128)S(1)}, f32[24,8,128]{2,1,0:T(8,128)S(1)}, u32[]{:S(2)}, u32[]{:S(2)}) %collective-permute-start.7) | collective-permute-done | bytes 98336 | tf_op jit(solution)/shard_map/ppermute | solution.py:834
  37.1 2.2 %collective-permute-done.6.refs_2_ = f32[24,8,128]{2,1,0:T(8,128)S(1)} collective-permute-done((f32[24,8,128]{2,1,0:T(8,128)S(1)}, f32[24,8,128]{2,1,0:T(8,128)S(1)}, u32[]{:S(2)}, u32[]{:S(2)}) %collective-permute-start.6) | collective-permute-done | bytes 98336 | tf_op jit(solution)/shard_map/ppermute | solution.py:834
  39.4 7.0 %collective-permute-start.9 = (f32[42,8,128]{2,1,0:T(8,128)S(1)}, f32[42,8,128]{2,1,0:T(8,128)S(1)}, u32[]{:S(2)}, u32[]{:S(2)}) collective-permute-start(f32[42,8,128]{2,1,0:T(8,128)S(1)} %get-tuple-element.68), channel_id=1, source_target_pairs={{4,8},{5,9},{6,10},{7,11},{8,4},{9,5},{10,6},{11,7},{12,16},{13,17... | collective-permute-start | bytes 516104 | tf_op jit(solution)/shard_map/ppermute | solution.py:834
  46.5 1.7 shard_map.72
  48.1 1.8 %collective-permute-done.9.refs_5_ = f32[42,8,128]{2,1,0:T(8,128)S(1)} collective-permute-done((f32[42,8,128]{2,1,0:T(8,128)S(1)}, f32[42,8,128]{2,1,0:T(8,128)S(1)}, u32[]{:S(2)}, u32[]{:S(2)}) %collective-permute-start.9) | collective-permute-done | bytes 172064 | tf_op jit(solution)/shard_map/ppermute | solution.py:834
  49.9 3.6 %shard_map.73 = (f32[3,32,8,128]{3,2,1,0:T(8,128)S(1)}, f32[3,2,8,128]{3,2,1,0:T(8,128)S(1)}, f32[3,32,128]{2,1,0:T(8,128)S(1)}, f32[3,2,8,128]{3,2,1,0:T(8,128)...) custom-call(s32[180]{0:T(256)S(1)} %get-tuple-element.64.tab, ...), custom_call_target="tpu_custom_call" | custom-call | tf_op jit(solution)/shard_map/pallas_call | solution.py:822
  53.6 1.8 %collective-permute-start.12 = (f32[9,8,128]{2,1,0:T(8,128)S(1)}, f32[9,8,128]{2,1,0:T(8,128)S(1)}, u32[]{:S(2)}, u32[]{:S(2)}) collective-permute-start(f32[9,8,128]{2,1,0:T(8,128)S(1)} %get-tuple-element.79.refs_0_), channel_id=1, source_target_pairs={{0,3},{1,2},{2,1},{3,0},{4,7},{5,6},{6,5},{7,4},{8,11},{9,10},{10,... | collective-permute-start | bytes 110600 | tf_op jit(solution)/shard_map/ppermute | solution.py:834
  55.5 1.4 collective-permute-start.10
  56.9 0.8 collective-permute-done.12.refs_3_
  57.7 2.0 %collective-permute-done.11.refs_2_ = f32[9,8,128]{2,1,0:T(8,128)S(1)} collective-permute-done((f32[9,8,128]{2,1,0:T(8,128)S(1)}, f32[9,8,128]{2,1,0:T(8,128)S(1)}, u32[]{:S(2)}, u32[]{:S(2)}) %collective-permute-start.11) | collective-permute-done | bytes 36896 | tf_op jit(solution)/shard_map/ppermute | solution.py:834
  59.8 7.0 %collective-permute-start.14 = (f32[18,8,128]{2,1,0:T(8,128)S(1)}, f32[18,8,128]{2,1,0:T(8,128)S(1)}, u32[]{:S(2)}, u32[]{:S(2)}) collective-permute-start(f32[18,8,128]{2,1,0:T(8,128)S(1)} %get-tuple-element.81), channel_id=1, source_target_pairs={{4,8},{5,9},{6,10},{7,11},{8,4},{9,5},{10,6},{11,7},{12,16},{13,17... | collective-permute-start | bytes 221192 | tf_op jit(solution)/shard_map/ppermute | solution.py:834
  66.9 0.8 shard_map.74.beta_rows
  67.7 1.2 collective-permute-done.14.refs_5_
  68.9 2.4 %shard_map.76 = (f32[3,16,8,128]{3,2,1,0:T(8,128)S(1)}, f32[3,2,8,128]{3,2,1,0:T(8,128)S(1)}, f32[3,16,128]{2,1,0:T(8,128)S(1)}, f32[3,2,8,128]{3,2,1,0:T(8,128)...) custom-call(s32[180]{0:T(256)S(1)} %get-tuple-element.64.tab, f32[3,16,8,128]{3,2,1,0:T(8,128)S(1)} %get-tuple-element.78.t, ...), custom_call_target="tpu_custom_call" | custom-call | tf_op jit(solution)/shard_map/pallas_call | solution.py:822
  71.3 1.2 collective-permute-start.17
  72.5 1.1 collective-permute-start.16
  73.6 1.0 collective-permute-start.15
  74.6 0.5 collective-permute-done.17.refs_3_
  75.2 1.4 collective-permute-done.16.refs_2_
  76.6 2.4 %collective-permute-start.20 = (f32[104,128]{1,0:T(8,128)S(1)}, f32[104,128]{1,0:T(8,128)S(1)}, u32[]{:S(2)}, u32[]{:S(2)}) collective-permute-start(f32[104,128]{1,0:T(8,128)S(1)} %shard_map.77.refs_0_), channel_id=1, source_target_pairs={{0,12},{1,13},{2,14},{3,15},{4,8},{5,9},{6,10},{7,11},{8,4},{9,5},... | collective-permute-start | bytes 159752 | tf_op jit(solution)/shard_map/ppermute | solution.py:834
  79.0 0.9 collective-permute-start.18
  79.9 0.9 collective-permute-done.20.refs_3_
  80.9 2.7 %collective-permute-done.19.refs_2_ = f32[104,128]{1,0:T(8,128)S(1)} collective-permute-done((f32[104,128]{1,0:T(8,128)S(1)}, f32[104,128]{1,0:T(8,128)S(1)}, u32[]{:S(2)}, u32[]{:S(2)}) %collective-permute-start.19) | collective-permute-done | bytes 53280 | tf_op jit(solution)/shard_map/ppermute | solution.py:834
  83.6 1.2 collective-permute-start.23
  84.8 1.8 %collective-permute-start.22 = (f32[400,128]{1,0:T(8,128)S(1)}, f32[400,128]{1,0:T(8,128)S(1)}, u32[]{:S(2)}, u32[]{:S(2)}) collective-permute-start(f32[400,128]{1,0:T(8,128)S(1)} %shard_map.78.refs_0_), channel_id=1, source_target_pairs={{0,64},{1,65},{2,66},{3,67},{4,68},{5,69},{6,70},{7,71},{8,72},{9,... | collective-permute-start | bytes 614408 | tf_op jit(solution)/shard_map/ppermute | solution.py:834
  86.6 0.3 collective-permute-start.21
  86.9 4.8 %collective-permute-done.23.refs_3_ = f32[400,128]{1,0:T(8,128)S(1)} collective-permute-done((f32[400,128]{1,0:T(8,128)S(1)}, f32[400,128]{1,0:T(8,128)S(1)}, u32[]{:S(2)}, u32[]{:S(2)}) %collective-permute-start.23) | collective-permute-done | bytes 204832 | tf_op jit(solution)/shard_map/ppermute | solution.py:834
  91.7 0.9 collective-permute-done.21.refs_1_
  92.6 5.6 %collective-permute-start.24 = (f32[1600,128]{1,0:T(8,128)S(1)}, f32[1600,128]{1,0:T(8,128)S(1)}, u32[]{:S(2)}, u32[]{:S(2)}) collective-permute-start(f32[1600,128]{1,0:T(8,128)S(1)} %shard_map.79.mine64), channel_id=1, source_target_pairs={{0,16},{1,17},{2,18},{3,19},{4,20},{5,21},{6,22},{7,23},{8,24},{9,... | collective-permute-start | bytes 2457608 | tf_op jit(solution)/shard_map/ppermute | solution.py:834
  98.2 2.0 %collective-permute-done.24.other64 = f32[1600,128]{1,0:T(8,128)S(1)} collective-permute-done((f32[1600,128]{1,0:T(8,128)S(1)}, f32[1600,128]{1,0:T(8,128)S(1)}, u32[]{:S(2)}, u32[]{:S(2)}) %collective-permute-start.24) | collective-permute-done | bytes 819232 | tf_op jit(solution)/shard_map/ppermute | solution.py:834
  100.2 13.2 %shard_map.80 = (f32[3,16,8,128]{3,2,1,0:T(8,128)S(1)}, f32[9,8,128]{2,1,0:T(8,128)S(1)}, f32[8,128]{1,0:T(8,128)S(1)}) custom-call(s32[25]{0:T(128)S(1)} %get-tuple-element.89.place, f32[1600,128]{1,0:T(8,128)S(1)} %shard_map.79.mine64, f32[1600,128]{1,0:T(8,128)S(1)} %collective-permute-done.24.other64, ...), custom_call_target="tpu_custom_call" | custom-call | tf_op jit(solution)/shard_map/pallas_call | solution.py:822
  113.4 1.7 %collective-permute-start.27 = (f32[9,8,128]{2,1,0:T(8,128)S(1)}, f32[9,8,128]{2,1,0:T(8,128)S(1)}, u32[]{:S(2)}, u32[]{:S(2)}) collective-permute-start(f32[9,8,128]{2,1,0:T(8,128)S(1)} %get-tuple-element.98.refs_0_), channel_id=1, source_target_pairs={{0,3},{1,2},{2,1},{3,0},{4,7},{5,6},{6,5},{7,4},{8,11},{9,10},{10,... | collective-permute-start | bytes 110600 | tf_op jit(solution)/shard_map/ppermute | solution.py:834
  115.2 1.1 collective-permute-start.26
  116.2 0.6 collective-permute-start.25
  116.8 0.8 collective-permute-done.27.refs_3_
  117.5 1.9 %collective-permute-done.26.refs_2_ = f32[9,8,128]{2,1,0:T(8,128)S(1)} collective-permute-done((f32[9,8,128]{2,1,0:T(8,128)S(1)}, f32[9,8,128]{2,1,0:T(8,128)S(1)}, u32[]{:S(2)}, u32[]{:S(2)}) %collective-permute-start.26) | collective-permute-done | bytes 36896 | tf_op jit(solution)/shard_map/ppermute | solution.py:834
  119.5 1.0 collective-permute-start.28
  120.6 4.9 %collective-permute-start.29 = (f32[18,8,128]{2,1,0:T(8,128)S(1)}, f32[18,8,128]{2,1,0:T(8,128)S(1)}, u32[]{:S(2)}, u32[]{:S(2)}) collective-permute-start(f32[18,8,128]{2,1,0:T(8,128)S(1)} %get-tuple-element.100), channel_id=1, source_target_pairs={{4,8},{5,9},{6,10},{7,11},{8,4},{9,5},{10,6},{11,7},{12,16},{13,17... | collective-permute-start | bytes 221192 | tf_op jit(solution)/shard_map/ppermute | solution.py:834
  125.5 2.1 %collective-permute-done.29.refs_5_ = f32[18,8,128]{2,1,0:T(8,128)S(1)} collective-permute-done((f32[18,8,128]{2,1,0:T(8,128)S(1)}, f32[18,8,128]{2,1,0:T(8,128)S(1)}, u32[]{:S(2)}, u32[]{:S(2)}) %collective-permute-start.29) | collective-permute-done | bytes 73760 | tf_op jit(solution)/shard_map/ppermute | solution.py:834
  127.6 2.7 %shard_map.82 = (f32[3,32,8,128]{3,2,1,0:T(8,128)S(1)}, f32[24,8,128]{2,1,0:T(8,128)S(1)}) custom-call(s32[180]{0:T(256)S(1)} %get-tuple-element.64.tab, f32[3,16,8,128]{3,2,1,0:T(8,128)S(1)} %get-tuple-element.77.u.refs_0_.first1, f32[3,2,8,128]{3,2,1,0:T(8,128)S(1)} %get-tuple-element.87.first1_x, f32[3,16,128]{2,1,0:T(8,128)S(1)} %get-tuple-element.88.first1_y, ...), custom_call_target="tpu_custom_call" | custom-call | tf_op jit(solution)/shard_map/pallas_call | solution.py:822
  130.3 1.3 collective-permute-start.32
  131.6 0.9 collective-permute-start.31
  132.5 1.1 collective-permute-start.30
  133.6 3.1 %collective-permute-done.32.refs_3_ = f32[24,8,128]{2,1,0:T(8,128)S(1)} collective-permute-done((f32[24,8,128]{2,1,0:T(8,128)S(1)}, f32[24,8,128]{2,1,0:T(8,128)S(1)}, u32[]{:S(2)}, u32[]{:S(2)}) %collective-permute-start.32) | collective-permute-done | bytes 98336 | tf_op jit(solution)/shard_map/ppermute | solution.py:834
  136.6 0.9 collective-permute-done.31.refs_2_
  137.9 6.2 %collective-permute-start.34 = (f32[42,8,128]{2,1,0:T(8,128)S(1)}, f32[42,8,128]{2,1,0:T(8,128)S(1)}, u32[]{:S(2)}, u32[]{:S(2)}) collective-permute-start(f32[42,8,128]{2,1,0:T(8,128)S(1)} %get-tuple-element.106), channel_id=1, source_target_pairs={{4,8},{5,9},{6,10},{7,11},{8,4},{9,5},{10,6},{11,7},{12,16},{13,17... | collective-permute-start | bytes 516104 | tf_op jit(solution)/shard_map/ppermute | solution.py:834
  144.1 4.2 %collective-permute-done.34.refs_5_ = f32[42,8,128]{2,1,0:T(8,128)S(1)} collective-permute-done((f32[42,8,128]{2,1,0:T(8,128)S(1)}, f32[42,8,128]{2,1,0:T(8,128)S(1)}, u32[]{:S(2)}, u32[]{:S(2)}) %collective-permute-start.34) | collective-permute-done | bytes 172064 | tf_op jit(solution)/shard_map/ppermute | solution.py:834
  148.2 3.3 %shard_map.84 = (f32[3,32,8,128]{3,2,1,0:T(8,128)S(1)}, f32[256,3,128]{2,1,0:T(4,128)}, f32[1,128]{1,0:T(1,128)S(1)}) custom-call(s32[180]{0:T(256)S(1)} %get-tuple-element.64.tab, f32[3,32,8,128]{3,2,1,0:T(8,128)S(1)} %shard_map.68.source.t, f32[3,32,8,128]{3,2,1,0:T(8,128)S(1)} %get-tuple-element.101.u, f32[3,32,8,128]{3,2,1,0:T(8,128)S(1)} %get-tuple-element.65.u.first, ...), custom_call_target="tpu_custom_call" | custom-call | tf_op jit(solution)/shard_map/pallas_call | solution.py:822
  151.5 17.9 %all_to_all.5 = f32[128,1,128]{2,1,0:T(1,128)S(1)} all-to-all(f32[128,1,128]{2,1,0:T(1,128)S(1)} %broadcast_in_dim.9), channel_id=1, replica_groups=mesh['gx'=8,'gy'=16] {'gx','gy'}, dimensions={0} | all-to-all | bytes 131072 | tf_op jit(solution)/shard_map/all_to_all | solution.py:873
  169.5 1.1 shard_map.85
  (35 shorter events, 0.9 us)
Async XLA Ops:
  0.6 1.0 copy-start
  1.7 0.7 copy-start.2
  2.4 21.8 %copy-start.1 = (f32[3,32768]{1,0:T(4,128)S(1)}, f32[3,32768]{1,0:T(4,128)}, u32[]{:S(2)}) copy-start(f32[3,32768]{1,0:T(4,128)} %param.4) | copy-start | bytes 1179652
  4.4 10.5 %collective-permute-start.2 = (f32[34,8,128]{2,1,0:T(8,128)S(1)}, f32[34,8,128]{2,1,0:T(8,128)S(1)}, u32[]{:S(2)}, u32[]{:S(2)}) collective-permute-start(f32[34,8,128]{2,1,0:T(8,128)S(1)} %get-tuple-element.61.refs_0_), channel_id=1, source_target_pairs={{0,3},{1,2},{2,1},{3,0},{4,7},{5,6},{6,5},{7,4},{8,11},{9,10},{10,... | collective-permute-start | bytes 417800 | tf_op jit(solution)/shard_map/ppermute | solution.py:834
  9.0 5.8 %collective-permute-start.1 = (f32[34,8,128]{2,1,0:T(8,128)S(1)}, f32[34,8,128]{2,1,0:T(8,128)S(1)}, u32[]{:S(2)}, u32[]{:S(2)}) collective-permute-start(f32[34,8,128]{2,1,0:T(8,128)S(1)} %get-tuple-element.61.refs_0_), channel_id=1, source_target_pairs={{0,2},{1,3},{2,0},{3,1},{4,6},{5,7},{6,4},{7,5},{8,10},{9,11},{10,... | collective-permute-start | bytes 417800 | tf_op jit(solution)/shard_map/ppermute | solution.py:834
  9.0 6.8 %collective-permute-start = (f32[34,8,128]{2,1,0:T(8,128)S(1)}, f32[34,8,128]{2,1,0:T(8,128)S(1)}, u32[]{:S(2)}, u32[]{:S(2)}) collective-permute-start(f32[34,8,128]{2,1,0:T(8,128)S(1)} %get-tuple-element.61.refs_0_), channel_id=1, source_target_pairs={{0,1},{1,0},{2,3},{3,2},{4,5},{5,4},{6,7},{7,6},{8,9},{9,8},{10,11... | collective-permute-start | bytes 417800 | tf_op jit(solution)/shard_map/ppermute | solution.py:834
  15.9 8.5 %collective-permute-start.3 = (f32[64,8,128]{2,1,0:T(8,128)S(1)}, f32[64,8,128]{2,1,0:T(8,128)S(1)}, u32[]{:S(2)}, u32[]{:S(2)}) collective-permute-start(f32[64,8,128]{2,1,0:T(8,128)S(1)} %get-tuple-element.62), channel_id=1, source_target_pairs={{0,4},{1,5},{2,6},{3,7},{4,0},{5,1},{6,2},{7,3},{8,12},{9,13},{10,... | collective-permute-start | bytes 786440 | tf_op jit(solution)/shard_map/ppermute | solution.py:834
  17.3 11.6 %collective-permute-start.4 = (f32[64,8,128]{2,1,0:T(8,128)S(1)}, f32[64,8,128]{2,1,0:T(8,128)S(1)}, u32[]{:S(2)}, u32[]{:S(2)}) collective-permute-start(f32[64,8,128]{2,1,0:T(8,128)S(1)} %get-tuple-element.63), channel_id=1, source_target_pairs={{4,8},{5,9},{6,10},{7,11},{8,4},{9,5},{10,6},{11,7},{12,16},{13,17... | collective-permute-start | bytes 786440 | tf_op jit(solution)/shard_map/ppermute | solution.py:834
  31.9 5.2 %collective-permute-start.7 = (f32[24,8,128]{2,1,0:T(8,128)S(1)}, f32[24,8,128]{2,1,0:T(8,128)S(1)}, u32[]{:S(2)}, u32[]{:S(2)}) collective-permute-start(f32[24,8,128]{2,1,0:T(8,128)S(1)} %get-tuple-element.66.refs_0_), channel_id=1, source_target_pairs={{0,3},{1,2},{2,1},{3,0},{4,7},{5,6},{6,5},{7,4},{8,11},{9,10},{10,... | collective-permute-start | bytes 294920 | tf_op jit(solution)/shard_map/ppermute | solution.py:834
  34.3 5.0 %collective-permute-start.6 = (f32[24,8,128]{2,1,0:T(8,128)S(1)}, f32[24,8,128]{2,1,0:T(8,128)S(1)}, u32[]{:S(2)}, u32[]{:S(2)}) collective-permute-start(f32[24,8,128]{2,1,0:T(8,128)S(1)} %get-tuple-element.66.refs_0_), channel_id=1, source_target_pairs={{0,2},{1,3},{2,0},{3,1},{4,6},{5,7},{6,4},{7,5},{8,10},{9,11},{10,... | collective-permute-start | bytes 294920 | tf_op jit(solution)/shard_map/ppermute | solution.py:834
  34.3 5.0 %collective-permute-start.5 = (f32[24,8,128]{2,1,0:T(8,128)S(1)}, f32[24,8,128]{2,1,0:T(8,128)S(1)}, u32[]{:S(2)}, u32[]{:S(2)}) collective-permute-start(f32[24,8,128]{2,1,0:T(8,128)S(1)} %get-tuple-element.66.refs_0_), channel_id=1, source_target_pairs={{0,1},{1,0},{2,3},{3,2},{4,5},{5,4},{6,7},{7,6},{8,9},{9,8},{10,11... | collective-permute-start | bytes 294920 | tf_op jit(solution)/shard_map/ppermute | solution.py:834
  39.3 8.8 %collective-permute-start.8 = (f32[42,8,128]{2,1,0:T(8,128)S(1)}, f32[42,8,128]{2,1,0:T(8,128)S(1)}, u32[]{:S(2)}, u32[]{:S(2)}) collective-permute-start(f32[42,8,128]{2,1,0:T(8,128)S(1)} %get-tuple-element.67), channel_id=1, source_target_pairs={{0,4},{1,5},{2,6},{3,7},{4,0},{5,1},{6,2},{7,3},{8,12},{9,13},{10,... | collective-permute-start | bytes 516104 | tf_op jit(solution)/shard_map/ppermute | solution.py:834
  39.4 10.5 %collective-permute-start.9 = (f32[42,8,128]{2,1,0:T(8,128)S(1)}, f32[42,8,128]{2,1,0:T(8,128)S(1)}, u32[]{:S(2)}, u32[]{:S(2)}) collective-permute-start(f32[42,8,128]{2,1,0:T(8,128)S(1)} %get-tuple-element.68), channel_id=1, source_target_pairs={{4,8},{5,9},{6,10},{7,11},{8,4},{9,5},{10,6},{11,7},{12,16},{13,17... | collective-permute-start | bytes 516104 | tf_op jit(solution)/shard_map/ppermute | solution.py:834
  53.6 4.1 %collective-permute-start.12 = (f32[9,8,128]{2,1,0:T(8,128)S(1)}, f32[9,8,128]{2,1,0:T(8,128)S(1)}, u32[]{:S(2)}, u32[]{:S(2)}) collective-permute-start(f32[9,8,128]{2,1,0:T(8,128)S(1)} %get-tuple-element.79.refs_0_), channel_id=1, source_target_pairs={{0,3},{1,2},{2,1},{3,0},{4,7},{5,6},{6,5},{7,4},{8,11},{9,10},{10,... | collective-permute-start | bytes 110600 | tf_op jit(solution)/shard_map/ppermute | solution.py:834
  55.4 4.3 %collective-permute-start.11 = (f32[9,8,128]{2,1,0:T(8,128)S(1)}, f32[9,8,128]{2,1,0:T(8,128)S(1)}, u32[]{:S(2)}, u32[]{:S(2)}) collective-permute-start(f32[9,8,128]{2,1,0:T(8,128)S(1)} %get-tuple-element.79.refs_0_), channel_id=1, source_target_pairs={{0,2},{1,3},{2,0},{3,1},{4,6},{5,7},{6,4},{7,5},{8,10},{9,11},{10,... | collective-permute-start | bytes 110600 | tf_op jit(solution)/shard_map/ppermute | solution.py:834
  55.5 4.2 %collective-permute-start.10 = (f32[9,8,128]{2,1,0:T(8,128)S(1)}, f32[9,8,128]{2,1,0:T(8,128)S(1)}, u32[]{:S(2)}, u32[]{:S(2)}) collective-permute-start(f32[9,8,128]{2,1,0:T(8,128)S(1)} %get-tuple-element.79.refs_0_), channel_id=1, source_target_pairs={{0,1},{1,0},{2,3},{3,2},{4,5},{5,4},{6,7},{7,6},{8,9},{9,8},{10,11... | collective-permute-start | bytes 110600 | tf_op jit(solution)/shard_map/ppermute | solution.py:834
  59.7 7.1 %copy-start.3 = (s32[3,4]{1,0:T(4,128)S(1)}, s32[3,4]{1,0:T(4,128)}, u32[]{:S(2)}) copy-start(s32[3,4]{1,0:T(4,128)} %ghost.3) | copy-start | bytes 148
  59.7 8.0 %collective-permute-start.13 = (f32[18,8,128]{2,1,0:T(8,128)S(1)}, f32[18,8,128]{2,1,0:T(8,128)S(1)}, u32[]{:S(2)}, u32[]{:S(2)}) collective-permute-start(f32[18,8,128]{2,1,0:T(8,128)S(1)} %get-tuple-element.80), channel_id=1, source_target_pairs={{0,4},{1,5},{2,6},{3,7},{4,0},{5,1},{6,2},{7,3},{8,12},{9,13},{10,... | collective-permute-start | bytes 221192 | tf_op jit(solution)/shard_map/ppermute | solution.py:834
  59.8 9.1 %collective-permute-start.14 = (f32[18,8,128]{2,1,0:T(8,128)S(1)}, f32[18,8,128]{2,1,0:T(8,128)S(1)}, u32[]{:S(2)}, u32[]{:S(2)}) collective-permute-start(f32[18,8,128]{2,1,0:T(8,128)S(1)} %get-tuple-element.81), channel_id=1, source_target_pairs={{4,8},{5,9},{6,10},{7,11},{8,4},{9,5},{10,6},{11,7},{12,16},{13,17... | collective-permute-start | bytes 221192 | tf_op jit(solution)/shard_map/ppermute | solution.py:834
  71.3 3.9 %collective-permute-start.17 = (f32[32,128]{1,0:T(8,128)S(1)}, f32[32,128]{1,0:T(8,128)S(1)}, u32[]{:S(2)}, u32[]{:S(2)}) collective-permute-start(f32[32,128]{1,0:T(8,128)S(1)} %get-tuple-element.90.refs_0_), channel_id=1, source_target_pairs={{0,3},{1,2},{2,1},{3,0},{4,7},{5,6},{6,5},{7,4},{8,11},{9,10},{10,... | collective-permute-start | bytes 49160 | tf_op jit(solution)/shard_map/ppermute | solution.py:834
  72.5 4.1 %collective-permute-start.16 = (f32[32,128]{1,0:T(8,128)S(1)}, f32[32,128]{1,0:T(8,128)S(1)}, u32[]{:S(2)}, u32[]{:S(2)}) collective-permute-start(f32[32,128]{1,0:T(8,128)S(1)} %get-tuple-element.90.refs_0_), channel_id=1, source_target_pairs={{0,2},{1,3},{2,0},{3,1},{4,6},{5,7},{6,4},{7,5},{8,10},{9,11},{10,... | collective-permute-start | bytes 49160 | tf_op jit(solution)/shard_map/ppermute | solution.py:834
  73.6 3.0 %collective-permute-start.15 = (f32[32,128]{1,0:T(8,128)S(1)}, f32[32,128]{1,0:T(8,128)S(1)}, u32[]{:S(2)}, u32[]{:S(2)}) collective-permute-start(f32[32,128]{1,0:T(8,128)S(1)} %get-tuple-element.90.refs_0_), channel_id=1, source_target_pairs={{0,1},{1,0},{2,3},{3,2},{4,5},{5,4},{6,7},{7,6},{8,9},{9,8},{10,11... | collective-permute-start | bytes 49160 | tf_op jit(solution)/shard_map/ppermute | solution.py:834
  76.6 4.3 %collective-permute-start.20 = (f32[104,128]{1,0:T(8,128)S(1)}, f32[104,128]{1,0:T(8,128)S(1)}, u32[]{:S(2)}, u32[]{:S(2)}) collective-permute-start(f32[104,128]{1,0:T(8,128)S(1)} %shard_map.77.refs_0_), channel_id=1, source_target_pairs={{0,12},{1,13},{2,14},{3,15},{4,8},{5,9},{6,10},{7,11},{8,4},{9,5},... | collective-permute-start | bytes 159752 | tf_op jit(solution)/shard_map/ppermute | solution.py:834
  79.0 4.5 %collective-permute-start.19 = (f32[104,128]{1,0:T(8,128)S(1)}, f32[104,128]{1,0:T(8,128)S(1)}, u32[]{:S(2)}, u32[]{:S(2)}) collective-permute-start(f32[104,128]{1,0:T(8,128)S(1)} %shard_map.77.refs_0_), channel_id=1, source_target_pairs={{0,8},{1,9},{2,10},{3,11},{4,12},{5,13},{6,14},{7,15},{8,0},{9,1},... | collective-permute-start | bytes 159752 | tf_op jit(solution)/shard_map/ppermute | solution.py:834
  79.0 4.5 %collective-permute-start.18 = (f32[104,128]{1,0:T(8,128)S(1)}, f32[104,128]{1,0:T(8,128)S(1)}, u32[]{:S(2)}, u32[]{:S(2)}) collective-permute-start(f32[104,128]{1,0:T(8,128)S(1)} %shard_map.77.refs_0_), channel_id=1, source_target_pairs={{0,4},{1,5},{2,6},{3,7},{4,0},{5,1},{6,2},{7,3},{8,12},{9,13},{10,... | collective-permute-start | bytes 159752 | tf_op jit(solution)/shard_map/ppermute | solution.py:834
  83.6 8.1 %collective-permute-start.23 = (f32[400,128]{1,0:T(8,128)S(1)}, f32[400,128]{1,0:T(8,128)S(1)}, u32[]{:S(2)}, u32[]{:S(2)}) collective-permute-start(f32[400,128]{1,0:T(8,128)S(1)} %shard_map.78.refs_0_), channel_id=1, source_target_pairs={{0,96},{1,97},{2,98},{3,99},{4,100},{5,101},{6,102},{7,103},{8,104... | collective-permute-start | bytes 614408 | tf_op jit(solution)/shard_map/ppermute | solution.py:834
  84.8 6.9 %collective-permute-start.22 = (f32[400,128]{1,0:T(8,128)S(1)}, f32[400,128]{1,0:T(8,128)S(1)}, u32[]{:S(2)}, u32[]{:S(2)}) collective-permute-start(f32[400,128]{1,0:T(8,128)S(1)} %shard_map.78.refs_0_), channel_id=1, source_target_pairs={{0,64},{1,65},{2,66},{3,67},{4,68},{5,69},{6,70},{7,71},{8,72},{9,... | collective-permute-start | bytes 614408 | tf_op jit(solution)/shard_map/ppermute | solution.py:834
  86.6 6.0 %collective-permute-start.21 = (f32[400,128]{1,0:T(8,128)S(1)}, f32[400,128]{1,0:T(8,128)S(1)}, u32[]{:S(2)}, u32[]{:S(2)}) collective-permute-start(f32[400,128]{1,0:T(8,128)S(1)} %shard_map.78.refs_0_), channel_id=1, source_target_pairs={{0,32},{1,33},{2,34},{3,35},{4,36},{5,37},{6,38},{7,39},{8,40},{9,... | collective-permute-start | bytes 614408 | tf_op jit(solution)/shard_map/ppermute | solution.py:834
  92.6 7.6 %collective-permute-start.24 = (f32[1600,128]{1,0:T(8,128)S(1)}, f32[1600,128]{1,0:T(8,128)S(1)}, u32[]{:S(2)}, u32[]{:S(2)}) collective-permute-start(f32[1600,128]{1,0:T(8,128)S(1)} %shard_map.79.mine64), channel_id=1, source_target_pairs={{0,16},{1,17},{2,18},{3,19},{4,20},{5,21},{6,22},{7,23},{8,24},{9,... | collective-permute-start | bytes 2457608 | tf_op jit(solution)/shard_map/ppermute | solution.py:834
  113.4 4.1 %collective-permute-start.27 = (f32[9,8,128]{2,1,0:T(8,128)S(1)}, f32[9,8,128]{2,1,0:T(8,128)S(1)}, u32[]{:S(2)}, u32[]{:S(2)}) collective-permute-start(f32[9,8,128]{2,1,0:T(8,128)S(1)} %get-tuple-element.98.refs_0_), channel_id=1, source_target_pairs={{0,3},{1,2},{2,1},{3,0},{4,7},{5,6},{6,5},{7,4},{8,11},{9,10},{10,... | collective-permute-start | bytes 110600 | tf_op jit(solution)/shard_map/ppermute | solution.py:834
  115.2 4.3 %collective-permute-start.26 = (f32[9,8,128]{2,1,0:T(8,128)S(1)}, f32[9,8,128]{2,1,0:T(8,128)S(1)}, u32[]{:S(2)}, u32[]{:S(2)}) collective-permute-start(f32[9,8,128]{2,1,0:T(8,128)S(1)} %get-tuple-element.98.refs_0_), channel_id=1, source_target_pairs={{0,2},{1,3},{2,0},{3,1},{4,6},{5,7},{6,4},{7,5},{8,10},{9,11},{10,... | collective-permute-start | bytes 110600 | tf_op jit(solution)/shard_map/ppermute | solution.py:834
  116.2 3.3 %collective-permute-start.25 = (f32[9,8,128]{2,1,0:T(8,128)S(1)}, f32[9,8,128]{2,1,0:T(8,128)S(1)}, u32[]{:S(2)}, u32[]{:S(2)}) collective-permute-start(f32[9,8,128]{2,1,0:T(8,128)S(1)} %get-tuple-element.98.refs_0_), channel_id=1, source_target_pairs={{0,1},{1,0},{2,3},{3,2},{4,5},{5,4},{6,7},{7,6},{8,9},{9,8},{10,11... | collective-permute-start | bytes 110600 | tf_op jit(solution)/shard_map/ppermute | solution.py:834
  119.5 6.0 %collective-permute-start.28 = (f32[18,8,128]{2,1,0:T(8,128)S(1)}, f32[18,8,128]{2,1,0:T(8,128)S(1)}, u32[]{:S(2)}, u32[]{:S(2)}) collective-permute-start(f32[18,8,128]{2,1,0:T(8,128)S(1)} %get-tuple-element.99), channel_id=1, source_target_pairs={{0,4},{1,5},{2,6},{3,7},{4,0},{5,1},{6,2},{7,3},{8,12},{9,13},{10,... | collective-permute-start | bytes 221192 | tf_op jit(solution)/shard_map/ppermute | solution.py:834
  120.6 7.0 %collective-permute-start.29 = (f32[18,8,128]{2,1,0:T(8,128)S(1)}, f32[18,8,128]{2,1,0:T(8,128)S(1)}, u32[]{:S(2)}, u32[]{:S(2)}) collective-permute-start(f32[18,8,128]{2,1,0:T(8,128)S(1)} %get-tuple-element.100), channel_id=1, source_target_pairs={{4,8},{5,9},{6,10},{7,11},{8,4},{9,5},{10,6},{11,7},{12,16},{13,17... | collective-permute-start | bytes 221192 | tf_op jit(solution)/shard_map/ppermute | solution.py:834
  130.3 6.4 %collective-permute-start.32 = (f32[24,8,128]{2,1,0:T(8,128)S(1)}, f32[24,8,128]{2,1,0:T(8,128)S(1)}, u32[]{:S(2)}, u32[]{:S(2)}) collective-permute-start(f32[24,8,128]{2,1,0:T(8,128)S(1)} %get-tuple-element.104.refs_0_), channel_id=1, source_target_pairs={{0,3},{1,2},{2,1},{3,0},{4,7},{5,6},{6,5},{7,4},{8,11},{9,10},{10,... | collective-permute-start | bytes 294920 | tf_op jit(solution)/shard_map/ppermute | solution.py:834
  131.6 6.0 %collective-permute-start.31 = (f32[24,8,128]{2,1,0:T(8,128)S(1)}, f32[24,8,128]{2,1,0:T(8,128)S(1)}, u32[]{:S(2)}, u32[]{:S(2)}) collective-permute-start(f32[24,8,128]{2,1,0:T(8,128)S(1)} %get-tuple-element.104.refs_0_), channel_id=1, source_target_pairs={{0,2},{1,3},{2,0},{3,1},{4,6},{5,7},{6,4},{7,5},{8,10},{9,11},{10,... | collective-permute-start | bytes 294920 | tf_op jit(solution)/shard_map/ppermute | solution.py:834
  132.5 5.2 %collective-permute-start.30 = (f32[24,8,128]{2,1,0:T(8,128)S(1)}, f32[24,8,128]{2,1,0:T(8,128)S(1)}, u32[]{:S(2)}, u32[]{:S(2)}) collective-permute-start(f32[24,8,128]{2,1,0:T(8,128)S(1)} %get-tuple-element.104.refs_0_), channel_id=1, source_target_pairs={{0,1},{1,0},{2,3},{3,2},{4,5},{5,4},{6,7},{7,6},{8,9},{9,8},{10,11... | collective-permute-start | bytes 294920 | tf_op jit(solution)/shard_map/ppermute | solution.py:834
  137.8 6.3 %collective-permute-start.33 = (f32[42,8,128]{2,1,0:T(8,128)S(1)}, f32[42,8,128]{2,1,0:T(8,128)S(1)}, u32[]{:S(2)}, u32[]{:S(2)}) collective-permute-start(f32[42,8,128]{2,1,0:T(8,128)S(1)} %get-tuple-element.105), channel_id=1, source_target_pairs={{0,4},{1,5},{2,6},{3,7},{4,0},{5,1},{6,2},{7,3},{8,12},{9,13},{10,... | collective-permute-start | bytes 516104 | tf_op jit(solution)/shard_map/ppermute | solution.py:834
  137.9 10.4 %collective-permute-start.34 = (f32[42,8,128]{2,1,0:T(8,128)S(1)}, f32[42,8,128]{2,1,0:T(8,128)S(1)}, u32[]{:S(2)}, u32[]{:S(2)}) collective-permute-start(f32[42,8,128]{2,1,0:T(8,128)S(1)} %get-tuple-element.106), channel_id=1, source_target_pairs={{4,8},{5,9},{6,10},{7,11},{8,4},{9,5},{10,6},{11,7},{12,16},{13,17... | collective-permute-start | bytes 516104 | tf_op jit(solution)/shard_map/ppermute | solution.py:834

commit v6 on v5

--- a/solution.py
+++ b/solution.py
@@ -65,7 +65,7 @@
 
 
 def pair_sum(t, lv):
-    lane = lanes()
+    lane = iota(t.shape, 1)
     zs, ys = 1 << lv, 32 << lv
     t = t + jnp.where((lane & zs) == 0, roll(t, 128 - zs, 1), roll(t, zs, 1))
     return t + jnp.where((lane & ys) == 0, roll(t, 128 - ys, 1), roll(t, ys, 1))
@@ -85,12 +85,14 @@
 
 
 def pack_faces(v, s, part, out):
+    n = PLANES[part.lv]
+    pack_tiles([v[s, 0], v[s, 1], v[s, n - 2], v[s, n - 1]], v[s, :, 0, :], v[s, :, 7, :], s, part, out)
+
+
+def pack_tiles(planes, y0, y7, s, part, out):
     lv = part.lv
     n = PLANES[lv]
     base = part.own + s * part.tiles
-    planes = [v[s, 0], v[s, 1], v[s, n - 2], v[s, n - 1]]
-    y0 = v[s, :, 0, :]
-    y7 = v[s, :, 7, :]
     lane = iota((n, 128), 1)
     if lv == 0:
         for m in range(4):
@@ -413,53 +415,57 @@
     return jnp.where(s < count, 1.0, 0.0)
 
 
-def k_source(count, src, out):
+def k_load(count, src, inv, out, b, b1):
     for s in range(SLOTS):
         out[s] = src[:, s, :].reshape(32, 8, 128) * used(count[0], s)
-
-
-def k_bottom_beta(ghost, count, b1, out):
-    lane = lanes()
-    note = jnp.where(lane == 12, jnp.full((8, 128), count[0]), 0)
-    for s in range(SLOTS):
-        for f in range(4):
-            note = jnp.where(lane == s * 4 + f, jnp.full((8, 128), ghost[s, f]), note)
-    pack_bottom([restrict_planes(b1, s, 1, 0.125) for s in range(SLOTS)], out)
-    out[16:24, :] = note.astype(F32)
-
-
-def k_start(ghost, inv, b, b1, faces, place):
-    dev = place_of_device()[0]
-    lane = lanes()
-    codes = jnp.zeros((8, 128), I32)
-    for s in range(SLOTS):
-        for f in range(4):
-            k = s * 4 + f
-            g = ghost[s, f]
-            has = g >= 0
-            owner = jnp.where(has, (g * 21846) >> 16, dev)
-            local = jnp.where(has, g - 3 * owner, 0)
-            place[k] = owner
-            place[12 + k] = local
-            codes = jnp.where(lane == k, jnp.full((8, 128), jnp.where(has, owner * 4 + local, -1)), codes)
-    place[24] = dev
-    for s in range(SLOTS):
         b[s] = inv[:, s, :].reshape(32, 8, 128)
         for c, t in enumerate(restrict_planes(b, s, 0, 0.125)):
             b1[s, c] = t
-        pack_faces(b, s, FIRST[0], faces)
-        pack_faces(b1, s, FIRST[1], faces)
-    faces[FIRST_NOTES[0]] = codes.astype(F32)
+
+
+def k_bottom_beta(ghost, count, b1, out, place):
+    lane = lanes()
+    dev = place_of_device()[0]
+    place[24] = dev
+    note = jnp.where(lane == 12, jnp.full((8, 128), count[0]), 0)
+    for s in range(SLOTS):
+        for f in range(4):
+            k, g = s * 4 + f, ghost[s, f]
+            note = jnp.where(lane == k, jnp.full((8, 128), g), note)
+            owner = jnp.where(g >= 0, (g * 21846) >> 16, dev)
+            place[k] = owner
+            place[12 + k] = jnp.where(g >= 0, g - 3 * owner, 0)
+    pack_bottom([restrict_planes(b1, s, 1, 0.125) for s in range(SLOTS)], out)
+    out[16:24, :] = note.astype(F32)
+
+
+def k_start(ghost, inv, faces):
+    g = ghost[...]
+    owner = (g * 21846) >> 16
+    codes = jnp.where(g >= 0, g + owner, -1)
+    faces[FIRST_NOTES[0]] = jnp.zeros((8, 128), F32)
+    faces[FIRST_NOTES[0], 0:SLOTS, 0:4] = codes.astype(F32)
+    for s in range(SLOTS):
+        plane = lambda i: inv[8 * i : 8 * i + 8, s, :]
+        y = [inv[pl.ds(at, 32, stride=8), s, :] for at in (0, 7)]
+        pack_tiles([plane(i) for i in (0, 1, 30, 31)], y[0], y[1], s, FIRST[0], faces)
+        near = [pair_sum(plane(2 * c) + plane(2 * c + 1), 0) * 0.125 for c in (0, 1, 14, 15)]
+        y = [
+            pair_sum(inv[pl.ds(at, 16, stride=16), s, :] + inv[pl.ds(at + 8, 16, stride=16), s, :], 0) * 0.125
+            for at in (0, 7)
+        ]
+        pack_tiles(near, y[0], y[1], s, FIRST[1], faces)
 
 
 def fill_table(win, rows, notes, sem, tab):
     _, even, place, block = place_of_device()
     own, side = FIRST_NOTES
-    rows[...] = jnp.zeros((16, 128), I32)
+    rows[...] = jnp.zeros((40, 128), I32)
     for m in range(4):
-        rows[m : m + 1, :] = win[m][own][0:1].astype(I32)
+        rows[3 * m : 3 * m + 3, :] = win[m][own][0:3].astype(I32)
         for x in range(2):
-            rows[4 + 4 * x + m : 5 + 4 * x + m, :] = win[4 + x][side + m][0:1].astype(I32)
+            at = 3 * (4 + 4 * x + m)
+            rows[at : at + 3, :] = win[4 + x][side + m][0:3].astype(I32)
     copy = pltpu.make_async_copy(rows, notes, sem)
     copy.start()
     copy.wait()
@@ -472,13 +478,13 @@
         r = jnp.where(delta == 0, m, jnp.where(delta == 2 * even - 1, 4, 5))
         for x, value in enumerate((r, slot, m, delta, jnp.where(code >= 0, 1, 0))):
             tab[x * BOXES + k] = value
-        return jnp.where(r < 4, 0, r - 3) * 4 + m, slot * 4
-
-    for s in range(SLOTS):
-        codes = [notes[0, s * 4 + f] for f in range(4)]
+        return (jnp.where(r < 4, 0, r - 3) * 4 + m) * 3 + slot
+
+    for s in range(SLOTS):
+        codes = [notes[s, f] for f in range(4)]
         found = [entry(s * 4 + f, codes[f]) for f in range(4)]
         for q, (f, g) in enumerate(TWO_FACES):
-            entry(12 + s * 8 + q, jnp.where(codes[f] >= 0, notes[found[f][0], found[f][1] + g], -1))
+            entry(12 + s * 8 + q, jnp.where(codes[f] >= 0, notes[found[f], g], -1))
 
 
 def k_weights(source, b, *refs):
@@ -884,18 +890,15 @@
         wide = (SLOTS, n + 2, 8, 128)
         return [(SLOTS, n + 3, 8, 128), wide, wide, (SLOTS, n + 2, 128), wide, (SLOTS, 6, n, 128)]
 
-    beta, beta1, faces, place = call(
-        k_start, 1, (ghost_from, view(inverse_density)),
-        [fine, mid, (FIRST_NOTES[0] + 1, 8, 128)], tables=[(25,)],
-    )
-    beta_rows = call(k_bottom_beta, 2, (ghost_from, box_counts, beta1), [(24, 128)])[0]
-    later, faces = lax.optimization_barrier((view(source_term), faces))
-    source = call(k_source, 1, (box_counts, later), [fine])[0]
+    faces = call(k_start, 0, (ghost_from, view(inverse_density)), [(FIRST_NOTES[0] + 1, 8, 128)])[0]
+    *later, faces = lax.optimization_barrier((view(source_term), view(inverse_density), faces))
+    source, beta, beta1 = call(k_load, 1, (box_counts, *later), [fine, fine, mid])
+    beta_rows, place = call(k_bottom_beta, 2, (ghost_from, box_counts, beta1), [(24, 128)], tables=[(25,)])
     win = exchange(faces, FIRST, FIRST_NOTES)
     outs = call(
         k_weights, 0, (source, beta) + win, weight_shapes(32) + [fine, face0], [xg, gyf, ends, gyf],
         tables=[(5 * BOXES,)],
-        extra=[pltpu.VMEM((16, 128), I32), pltpu.SMEM((16, 128), I32), pltpu.SemaphoreType.DMA],
+        extra=[pltpu.VMEM((40, 128), I32), pltpu.SMEM((40, 128), I32), pltpu.SemaphoreType.DMA],
     )
     w, (first, faces, tab) = tuple(outs[:6]), outs[6:]
     w1 = tuple(call(k_weights_next, 1, (tab, beta1) + win, weight_shapes(16), [xg, gym, ends, gym]))

time: 171 us -> 169 us (0.988)
  transfers between devices with their start and end apart: 35 -> 35, of which waited for: 23 -> 23; matrix products, arithmetic and copies ran while one was open for 0% -> 0% of each run, Pallas kernels for 2% -> 3%
where the time goes in v6:
time: 169 us
  starting transfers between devices  68.3 us (40%)
  waiting for transfers between devices  45 us (27%)
  Pallas kernels  34.4 us (20%)
  blocking collectives  17.9 us (11%)
  local copies, waits for them, and re-layouts  1.76 us (1%)
    ppermute x35, starting transfers between devices, swapped(): return lax.ppermute(block, AX, route)  68.3 us
    ppermute x35, waiting for transfers between devices, swapped(): return lax.ppermute(block, AX, route)  45 us
    pallas_call x19, Pallas kernels, call(): pl.pallas_call(kernel, out_shape=[shape(s) for s in outs] + [jax.ShapeDty...  34.4 us
    all_to_all x1, blocking collectives, to_all(): return lax.all_to_all(spread, AX, 0, 0)  17.9 us
  transfers between devices with their start and end apart: 35, of which 23 were waited for; matrix products, arithmetic and copies ran while one was open for 0% of the time, Pallas kernels for 3%

profile of v6, /device:TPU:1, one launch (start us, length us, event | category | flops | bytes accessed | tf_op | source)
XLA Modules:
  0.0 169.0 jit_solution(11775367184437287284)
XLA Ops:
  0.6 1.0 copy-done
  1.7 0.7 copy-done.3
  2.4 0.3 shard_map.67.refs_0_
  2.7 4.7 %collective-permute-start.2 = (f32[34,8,128]{2,1,0:T(8,128)S(1)}, f32[34,8,128]{2,1,0:T(8,128)S(1)}, u32[]{:S(2)}, u32[]{:S(2)}) collective-permute-start(f32[34,8,128]{2,1,0:T(8,128)S(1)} %shard_map.67.refs_0_), channel_id=1, source_target_pairs={{0,3},{1,2},{2,1},{3,0},{4,7},{5,6},{6,5},{7,4},{8,11},{9,10},{10,... | collective-permute-start | bytes 417800 | tf_op jit(solution)/shard_map/ppermute | solution.py:840
  7.3 0.7 collective-permute-start
  8.0 5.2 %collective-permute-done.2.refs_3_ = f32[34,8,128]{2,1,0:T(8,128)S(1)} collective-permute-done((f32[34,8,128]{2,1,0:T(8,128)S(1)}, f32[34,8,128]{2,1,0:T(8,128)S(1)}, u32[]{:S(2)}, u32[]{:S(2)}) %collective-permute-start.2) | collective-permute-done | bytes 139296 | tf_op jit(solution)/shard_map/ppermute | solution.py:840
  13.2 1.0 collective-permute-done.refs_1_
  14.2 1.4 collective-permute-start.3
  15.6 6.2 %collective-permute-start.4 = (f32[64,8,128]{2,1,0:T(8,128)S(1)}, f32[64,8,128]{2,1,0:T(8,128)S(1)}, u32[]{:S(2)}, u32[]{:S(2)}) collective-permute-start(f32[64,8,128]{2,1,0:T(8,128)S(1)} %get-tuple-element.66), channel_id=1, source_target_pairs={{4,8},{5,9},{6,10},{7,11},{8,4},{9,5},{10,6},{11,7},{12,16},{13,17... | collective-permute-start | bytes 786440 | tf_op jit(solution)/shard_map/ppermute | solution.py:840
  22.5 1.4 shard_map.68
  23.9 3.3 %collective-permute-done.4.refs_5_ = f32[64,8,128]{2,1,0:T(8,128)S(1)} collective-permute-done((f32[64,8,128]{2,1,0:T(8,128)S(1)}, f32[64,8,128]{2,1,0:T(8,128)S(1)}, u32[]{:S(2)}, u32[]{:S(2)}) %collective-permute-start.4) | collective-permute-done | bytes 262176 | tf_op jit(solution)/shard_map/ppermute | solution.py:840
  27.2 3.1 %shard_map.70 = (f32[3,35,8,128]{3,2,1,0:T(8,128)S(1)}, f32[3,34,8,128]{3,2,1,0:T(8,128)S(1)}, f32[3,34,8,128]{3,2,1,0:T(8,128)S(1)}, f32[3,34,128]{2,1,0:T(8,12...) custom-call(f32[3,32,8,128]{3,2,1,0:T(8,128)S(1)} %get-tuple-element, ...), custom_call_target="tpu_custom_call" | custom-call | tf_op jit(solution)/shard_map/pallas_call | solution.py:828
  30.4 2.4 %collective-permute-start.7 = (f32[24,8,128]{2,1,0:T(8,128)S(1)}, f32[24,8,128]{2,1,0:T(8,128)S(1)}, u32[]{:S(2)}, u32[]{:S(2)}) collective-permute-start(f32[24,8,128]{2,1,0:T(8,128)S(1)} %get-tuple-element.69.refs_0_), channel_id=1, source_target_pairs={{0,3},{1,2},{2,1},{3,0},{4,7},{5,6},{6,5},{7,4},{8,11},{9,10},{10,... | collective-permute-start | bytes 294920 | tf_op jit(solution)/shard_map/ppermute | solution.py:840
  32.8 0.9 collective-permute-start.5
  33.7 1.9 %collective-permute-done.7.refs_3_ = f32[24,8,128]{2,1,0:T(8,128)S(1)} collective-permute-done((f32[24,8,128]{2,1,0:T(8,128)S(1)}, f32[24,8,128]{2,1,0:T(8,128)S(1)}, u32[]{:S(2)}, u32[]{:S(2)}) %collective-permute-start.7) | collective-permute-done | bytes 98336 | tf_op jit(solution)/shard_map/ppermute | solution.py:840
  35.6 2.2 %collective-permute-done.6.refs_2_ = f32[24,8,128]{2,1,0:T(8,128)S(1)} collective-permute-done((f32[24,8,128]{2,1,0:T(8,128)S(1)}, f32[24,8,128]{2,1,0:T(8,128)S(1)}, u32[]{:S(2)}, u32[]{:S(2)}) %collective-permute-start.6) | collective-permute-done | bytes 98336 | tf_op jit(solution)/shard_map/ppermute | solution.py:840
  37.9 7.0 %collective-permute-start.9 = (f32[42,8,128]{2,1,0:T(8,128)S(1)}, f32[42,8,128]{2,1,0:T(8,128)S(1)}, u32[]{:S(2)}, u32[]{:S(2)}) collective-permute-start(f32[42,8,128]{2,1,0:T(8,128)S(1)} %get-tuple-element.71), channel_id=1, source_target_pairs={{4,8},{5,9},{6,10},{7,11},{8,4},{9,5},{10,6},{11,7},{12,16},{13,17... | collective-permute-start | bytes 516104 | tf_op jit(solution)/shard_map/ppermute | solution.py:840
  44.9 1.7 shard_map.72
  46.6 1.8 %collective-permute-done.9.refs_5_ = f32[42,8,128]{2,1,0:T(8,128)S(1)} collective-permute-done((f32[42,8,128]{2,1,0:T(8,128)S(1)}, f32[42,8,128]{2,1,0:T(8,128)S(1)}, u32[]{:S(2)}, u32[]{:S(2)}) %collective-permute-start.9) | collective-permute-done | bytes 172064 | tf_op jit(solution)/shard_map/ppermute | solution.py:840
  48.4 3.6 %shard_map.73 = (f32[3,32,8,128]{3,2,1,0:T(8,128)S(1)}, f32[3,2,8,128]{3,2,1,0:T(8,128)S(1)}, f32[3,32,128]{2,1,0:T(8,128)S(1)}, f32[3,2,8,128]{3,2,1,0:T(8,128)...) custom-call(s32[180]{0:T(256)S(1)} %get-tuple-element.67.tab, ...), custom_call_target="tpu_custom_call" | custom-call | tf_op jit(solution)/shard_map/pallas_call | solution.py:828
  52.0 1.8 %collective-permute-start.12 = (f32[9,8,128]{2,1,0:T(8,128)S(1)}, f32[9,8,128]{2,1,0:T(8,128)S(1)}, u32[]{:S(2)}, u32[]{:S(2)}) collective-permute-start(f32[9,8,128]{2,1,0:T(8,128)S(1)} %get-tuple-element.83.refs_0_), channel_id=1, source_target_pairs={{0,3},{1,2},{2,1},{3,0},{4,7},{5,6},{6,5},{7,4},{8,11},{9,10},{10,... | collective-permute-start | bytes 110600 | tf_op jit(solution)/shard_map/ppermute | solution.py:840
  53.9 1.4 collective-permute-start.10
  55.3 0.8 collective-permute-done.12.refs_3_
  56.1 2.0 %collective-permute-done.11.refs_2_ = f32[9,8,128]{2,1,0:T(8,128)S(1)} collective-permute-done((f32[9,8,128]{2,1,0:T(8,128)S(1)}, f32[9,8,128]{2,1,0:T(8,128)S(1)}, u32[]{:S(2)}, u32[]{:S(2)}) %collective-permute-start.11) | collective-permute-done | bytes 36896 | tf_op jit(solution)/shard_map/ppermute | solution.py:840
  58.3 7.0 %collective-permute-start.14 = (f32[18,8,128]{2,1,0:T(8,128)S(1)}, f32[18,8,128]{2,1,0:T(8,128)S(1)}, u32[]{:S(2)}, u32[]{:S(2)}) collective-permute-start(f32[18,8,128]{2,1,0:T(8,128)S(1)} %get-tuple-element.85), channel_id=1, source_target_pairs={{4,8},{5,9},{6,10},{7,11},{8,4},{9,5},{10,6},{11,7},{12,16},{13,17... | collective-permute-start | bytes 221192 | tf_op jit(solution)/shard_map/ppermute | solution.py:840
  65.3 1.4 shard_map.74
  66.7 0.7 collective-permute-done.14.refs_5_
  67.4 2.4 %shard_map.76 = (f32[3,16,8,128]{3,2,1,0:T(8,128)S(1)}, f32[3,2,8,128]{3,2,1,0:T(8,128)S(1)}, f32[3,16,128]{2,1,0:T(8,128)S(1)}, f32[3,2,8,128]{3,2,1,0:T(8,128)...) custom-call(s32[180]{0:T(256)S(1)} %get-tuple-element.67.tab, f32[3,16,8,128]{3,2,1,0:T(8,128)S(1)} %get-tuple-element.81.t, ...), custom_call_target="tpu_custom_call" | custom-call | tf_op jit(solution)/shard_map/pallas_call | solution.py:828
  69.8 1.2 collective-permute-start.17
  70.9 1.1 collective-permute-start.16
  72.1 1.0 collective-permute-start.15
  73.1 0.5 collective-permute-done.17.refs_3_
  73.6 1.4 collective-permute-done.16.refs_2_
  75.0 2.4 %collective-permute-start.20 = (f32[104,128]{1,0:T(8,128)S(1)}, f32[104,128]{1,0:T(8,128)S(1)}, u32[]{:S(2)}, u32[]{:S(2)}) collective-permute-start(f32[104,128]{1,0:T(8,128)S(1)} %shard_map.77.refs_0_), channel_id=1, source_target_pairs={{0,12},{1,13},{2,14},{3,15},{4,8},{5,9},{6,10},{7,11},{8,4},{9,5},... | collective-permute-start | bytes 159752 | tf_op jit(solution)/shard_map/ppermute | solution.py:840
  77.5 0.9 collective-permute-start.18
  78.4 0.9 collective-permute-done.20.refs_3_
  79.3 2.7 %collective-permute-done.19.refs_2_ = f32[104,128]{1,0:T(8,128)S(1)} collective-permute-done((f32[104,128]{1,0:T(8,128)S(1)}, f32[104,128]{1,0:T(8,128)S(1)}, u32[]{:S(2)}, u32[]{:S(2)}) %collective-permute-start.19) | collective-permute-done | bytes 53280 | tf_op jit(solution)/shard_map/ppermute | solution.py:840
  82.0 1.2 collective-permute-start.23
  83.2 1.8 %collective-permute-start.22 = (f32[400,128]{1,0:T(8,128)S(1)}, f32[400,128]{1,0:T(8,128)S(1)}, u32[]{:S(2)}, u32[]{:S(2)}) collective-permute-start(f32[400,128]{1,0:T(8,128)S(1)} %shard_map.78.refs_0_), channel_id=1, source_target_pairs={{0,64},{1,65},{2,66},{3,67},{4,68},{5,69},{6,70},{7,71},{8,72},{9,... | collective-permute-start | bytes 614408 | tf_op jit(solution)/shard_map/ppermute | solution.py:840
  85.0 0.3 collective-permute-start.21
  85.4 4.8 %collective-permute-done.23.refs_3_ = f32[400,128]{1,0:T(8,128)S(1)} collective-permute-done((f32[400,128]{1,0:T(8,128)S(1)}, f32[400,128]{1,0:T(8,128)S(1)}, u32[]{:S(2)}, u32[]{:S(2)}) %collective-permute-start.23) | collective-permute-done | bytes 204832 | tf_op jit(solution)/shard_map/ppermute | solution.py:840
  90.1 0.9 collective-permute-done.21.refs_1_
  91.1 5.6 %collective-permute-start.24 = (f32[1600,128]{1,0:T(8,128)S(1)}, f32[1600,128]{1,0:T(8,128)S(1)}, u32[]{:S(2)}, u32[]{:S(2)}) collective-permute-start(f32[1600,128]{1,0:T(8,128)S(1)} %shard_map.79.mine64), channel_id=1, source_target_pairs={{0,16},{1,17},{2,18},{3,19},{4,20},{5,21},{6,22},{7,23},{8,24},{9,... | collective-permute-start | bytes 2457608 | tf_op jit(solution)/shard_map/ppermute | solution.py:840
  96.7 2.0 %collective-permute-done.24.other64 = f32[1600,128]{1,0:T(8,128)S(1)} collective-permute-done((f32[1600,128]{1,0:T(8,128)S(1)}, f32[1600,128]{1,0:T(8,128)S(1)}, u32[]{:S(2)}, u32[]{:S(2)}) %collective-permute-start.24) | collective-permute-done | bytes 819232 | tf_op jit(solution)/shard_map/ppermute | solution.py:840
  98.7 13.2 %shard_map.80 = (f32[3,16,8,128]{3,2,1,0:T(8,128)S(1)}, f32[9,8,128]{2,1,0:T(8,128)S(1)}, f32[8,128]{1,0:T(8,128)S(1)}) custom-call(s32[25]{0:T(128)S(1)} %get-tuple-element.93.place, f32[1600,128]{1,0:T(8,128)S(1)} %shard_map.79.mine64, f32[1600,128]{1,0:T(8,128)S(1)} %collective-permute-done.24.other64, ...), custom_call_target="tpu_custom_call" | custom-call | tf_op jit(solution)/shard_map/pallas_call | solution.py:828
  111.9 1.7 %collective-permute-start.27 = (f32[9,8,128]{2,1,0:T(8,128)S(1)}, f32[9,8,128]{2,1,0:T(8,128)S(1)}, u32[]{:S(2)}, u32[]{:S(2)}) collective-permute-start(f32[9,8,128]{2,1,0:T(8,128)S(1)} %get-tuple-element.102.refs_0_), channel_id=1, source_target_pairs={{0,3},{1,2},{2,1},{3,0},{4,7},{5,6},{6,5},{7,4},{8,11},{9,10},{10,... | collective-permute-start | bytes 110600 | tf_op jit(solution)/shard_map/ppermute | solution.py:840
  113.6 1.1 collective-permute-start.26
  114.7 0.6 collective-permute-start.25
  115.2 0.8 collective-permute-done.27.refs_3_
  116.0 1.9 %collective-permute-done.26.refs_2_ = f32[9,8,128]{2,1,0:T(8,128)S(1)} collective-permute-done((f32[9,8,128]{2,1,0:T(8,128)S(1)}, f32[9,8,128]{2,1,0:T(8,128)S(1)}, u32[]{:S(2)}, u32[]{:S(2)}) %collective-permute-start.26) | collective-permute-done | bytes 36896 | tf_op jit(solution)/shard_map/ppermute | solution.py:840
  118.0 1.0 collective-permute-start.28
  119.0 4.9 %collective-permute-start.29 = (f32[18,8,128]{2,1,0:T(8,128)S(1)}, f32[18,8,128]{2,1,0:T(8,128)S(1)}, u32[]{:S(2)}, u32[]{:S(2)}) collective-permute-start(f32[18,8,128]{2,1,0:T(8,128)S(1)} %get-tuple-element.104), channel_id=1, source_target_pairs={{4,8},{5,9},{6,10},{7,11},{8,4},{9,5},{10,6},{11,7},{12,16},{13,17... | collective-permute-start | bytes 221192 | tf_op jit(solution)/shard_map/ppermute | solution.py:840
  123.9 2.1 %collective-permute-done.29.refs_5_ = f32[18,8,128]{2,1,0:T(8,128)S(1)} collective-permute-done((f32[18,8,128]{2,1,0:T(8,128)S(1)}, f32[18,8,128]{2,1,0:T(8,128)S(1)}, u32[]{:S(2)}, u32[]{:S(2)}) %collective-permute-start.29) | collective-permute-done | bytes 73760 | tf_op jit(solution)/shard_map/ppermute | solution.py:840
  126.0 2.7 %shard_map.82 = (f32[3,32,8,128]{3,2,1,0:T(8,128)S(1)}, f32[24,8,128]{2,1,0:T(8,128)S(1)}) custom-call(s32[180]{0:T(256)S(1)} %get-tuple-element.67.tab, f32[3,16,8,128]{3,2,1,0:T(8,128)S(1)} %get-tuple-element.80.u.refs_0_.first1, f32[3,2,8,128]{3,2,1,0:T(8,128)S(1)} %get-tuple-element.91.first1_x, f32[3,16,128]{2,1,0:T(8,128)S(1)} %get-tuple-element.92.first1_y, ...), custom_call_target="tpu_custom_call" | custom-call | tf_op jit(solution)/shard_map/pallas_call | solution.py:828
  128.7 1.3 collective-permute-start.32
  130.0 0.9 collective-permute-start.31
  130.9 1.1 collective-permute-start.30
  132.0 3.1 %collective-permute-done.32.refs_3_ = f32[24,8,128]{2,1,0:T(8,128)S(1)} collective-permute-done((f32[24,8,128]{2,1,0:T(8,128)S(1)}, f32[24,8,128]{2,1,0:T(8,128)S(1)}, u32[]{:S(2)}, u32[]{:S(2)}) %collective-permute-start.32) | collective-permute-done | bytes 98336 | tf_op jit(solution)/shard_map/ppermute | solution.py:840
  135.1 0.9 collective-permute-done.31.refs_2_
  136.3 6.2 %collective-permute-start.34 = (f32[42,8,128]{2,1,0:T(8,128)S(1)}, f32[42,8,128]{2,1,0:T(8,128)S(1)}, u32[]{:S(2)}, u32[]{:S(2)}) collective-permute-start(f32[42,8,128]{2,1,0:T(8,128)S(1)} %get-tuple-element.110), channel_id=1, source_target_pairs={{4,8},{5,9},{6,10},{7,11},{8,4},{9,5},{10,6},{11,7},{12,16},{13,17... | collective-permute-start | bytes 516104 | tf_op jit(solution)/shard_map/ppermute | solution.py:840
  142.5 4.2 %collective-permute-done.34.refs_5_ = f32[42,8,128]{2,1,0:T(8,128)S(1)} collective-permute-done((f32[42,8,128]{2,1,0:T(8,128)S(1)}, f32[42,8,128]{2,1,0:T(8,128)S(1)}, u32[]{:S(2)}, u32[]{:S(2)}) %collective-permute-start.34) | collective-permute-done | bytes 172064 | tf_op jit(solution)/shard_map/ppermute | solution.py:840
  146.7 3.2 %shard_map.84 = (f32[3,32,8,128]{3,2,1,0:T(8,128)S(1)}, f32[256,3,128]{2,1,0:T(4,128)}, f32[1,128]{1,0:T(1,128)S(1)}) custom-call(s32[180]{0:T(256)S(1)} %get-tuple-element.67.tab, f32[3,32,8,128]{3,2,1,0:T(8,128)S(1)} %get-tuple-element.62.source.t, f32[3,32,8,128]{3,2,1,0:T(8,128)S(1)} %get-tuple-element.105.u, ...), custom_call_target="tpu_custom_call" | custom-call | tf_op jit(solution)/shard_map/pallas_call | solution.py:828
  150.0 17.9 %all_to_all.5 = f32[128,1,128]{2,1,0:T(1,128)S(1)} all-to-all(f32[128,1,128]{2,1,0:T(1,128)S(1)} %broadcast_in_dim.9), channel_id=1, replica_groups=mesh['gx'=8,'gy'=16] {'gx','gy'}, dimensions={0} | all-to-all | bytes 131072 | tf_op jit(solution)/shard_map/all_to_all | solution.py:879
  167.9 1.1 shard_map.85
  (37 shorter events, 0.9 us)
Async XLA Ops:
  0.6 1.0 copy-start
  1.7 0.7 copy-start.3
  2.4 20.1 %copy-start.1 = (f32[3,32768]{1,0:T(4,128)S(1)}, f32[3,32768]{1,0:T(4,128)}, u32[]{:S(2)}) copy-start(f32[3,32768]{1,0:T(4,128)} %param.5) | copy-start | bytes 1179652
  2.4 20.1 %copy-start.2 = (f32[3,32768]{1,0:T(4,128)S(1)}, f32[3,32768]{1,0:T(4,128)}, u32[]{:S(2)}) copy-start(f32[3,32768]{1,0:T(4,128)} %param.4) | copy-start | bytes 1179652
  2.7 10.5 %collective-permute-start.2 = (f32[34,8,128]{2,1,0:T(8,128)S(1)}, f32[34,8,128]{2,1,0:T(8,128)S(1)}, u32[]{:S(2)}, u32[]{:S(2)}) collective-permute-start(f32[34,8,128]{2,1,0:T(8,128)S(1)} %shard_map.67.refs_0_), channel_id=1, source_target_pairs={{0,3},{1,2},{2,1},{3,0},{4,7},{5,6},{6,5},{7,4},{8,11},{9,10},{10,... | collective-permute-start | bytes 417800 | tf_op jit(solution)/shard_map/ppermute | solution.py:840
  7.3 5.8 %collective-permute-start.1 = (f32[34,8,128]{2,1,0:T(8,128)S(1)}, f32[34,8,128]{2,1,0:T(8,128)S(1)}, u32[]{:S(2)}, u32[]{:S(2)}) collective-permute-start(f32[34,8,128]{2,1,0:T(8,128)S(1)} %shard_map.67.refs_0_), channel_id=1, source_target_pairs={{0,2},{1,3},{2,0},{3,1},{4,6},{5,7},{6,4},{7,5},{8,10},{9,11},{10,... | collective-permute-start | bytes 417800 | tf_op jit(solution)/shard_map/ppermute | solution.py:840
  7.3 6.8 %collective-permute-start = (f32[34,8,128]{2,1,0:T(8,128)S(1)}, f32[34,8,128]{2,1,0:T(8,128)S(1)}, u32[]{:S(2)}, u32[]{:S(2)}) collective-permute-start(f32[34,8,128]{2,1,0:T(8,128)S(1)} %shard_map.67.refs_0_), channel_id=1, source_target_pairs={{0,1},{1,0},{2,3},{3,2},{4,5},{5,4},{6,7},{7,6},{8,9},{9,8},{10,11... | collective-permute-start | bytes 417800 | tf_op jit(solution)/shard_map/ppermute | solution.py:840
  14.2 9.7 %collective-permute-start.3 = (f32[64,8,128]{2,1,0:T(8,128)S(1)}, f32[64,8,128]{2,1,0:T(8,128)S(1)}, u32[]{:S(2)}, u32[]{:S(2)}) collective-permute-start(f32[64,8,128]{2,1,0:T(8,128)S(1)} %get-tuple-element.65), channel_id=1, source_target_pairs={{0,4},{1,5},{2,6},{3,7},{4,0},{5,1},{6,2},{7,3},{8,12},{9,13},{10,... | collective-permute-start | bytes 786440 | tf_op jit(solution)/shard_map/ppermute | solution.py:840
  15.6 11.6 %collective-permute-start.4 = (f32[64,8,128]{2,1,0:T(8,128)S(1)}, f32[64,8,128]{2,1,0:T(8,128)S(1)}, u32[]{:S(2)}, u32[]{:S(2)}) collective-permute-start(f32[64,8,128]{2,1,0:T(8,128)S(1)} %get-tuple-element.66), channel_id=1, source_target_pairs={{4,8},{5,9},{6,10},{7,11},{8,4},{9,5},{10,6},{11,7},{12,16},{13,17... | collective-permute-start | bytes 786440 | tf_op jit(solution)/shard_map/ppermute | solution.py:840
  30.4 5.2 %collective-permute-start.7 = (f32[24,8,128]{2,1,0:T(8,128)S(1)}, f32[24,8,128]{2,1,0:T(8,128)S(1)}, u32[]{:S(2)}, u32[]{:S(2)}) collective-permute-start(f32[24,8,128]{2,1,0:T(8,128)S(1)} %get-tuple-element.69.refs_0_), channel_id=1, source_target_pairs={{0,3},{1,2},{2,1},{3,0},{4,7},{5,6},{6,5},{7,4},{8,11},{9,10},{10,... | collective-permute-start | bytes 294920 | tf_op jit(solution)/shard_map/ppermute | solution.py:840
  32.8 5.0 %collective-permute-start.6 = (f32[24,8,128]{2,1,0:T(8,128)S(1)}, f32[24,8,128]{2,1,0:T(8,128)S(1)}, u32[]{:S(2)}, u32[]{:S(2)}) collective-permute-start(f32[24,8,128]{2,1,0:T(8,128)S(1)} %get-tuple-element.69.refs_0_), channel_id=1, source_target_pairs={{0,2},{1,3},{2,0},{3,1},{4,6},{5,7},{6,4},{7,5},{8,10},{9,11},{10,... | collective-permute-start | bytes 294920 | tf_op jit(solution)/shard_map/ppermute | solution.py:840
  32.8 5.0 %collective-permute-start.5 = (f32[24,8,128]{2,1,0:T(8,128)S(1)}, f32[24,8,128]{2,1,0:T(8,128)S(1)}, u32[]{:S(2)}, u32[]{:S(2)}) collective-permute-start(f32[24,8,128]{2,1,0:T(8,128)S(1)} %get-tuple-element.69.refs_0_), channel_id=1, source_target_pairs={{0,1},{1,0},{2,3},{3,2},{4,5},{5,4},{6,7},{7,6},{8,9},{9,8},{10,11... | collective-permute-start | bytes 294920 | tf_op jit(solution)/shard_map/ppermute | solution.py:840
  37.8 8.8 %collective-permute-start.8 = (f32[42,8,128]{2,1,0:T(8,128)S(1)}, f32[42,8,128]{2,1,0:T(8,128)S(1)}, u32[]{:S(2)}, u32[]{:S(2)}) collective-permute-start(f32[42,8,128]{2,1,0:T(8,128)S(1)} %get-tuple-element.70), channel_id=1, source_target_pairs={{0,4},{1,5},{2,6},{3,7},{4,0},{5,1},{6,2},{7,3},{8,12},{9,13},{10,... | collective-permute-start | bytes 516104 | tf_op jit(solution)/shard_map/ppermute | solution.py:840
  37.9 10.5 %collective-permute-start.9 = (f32[42,8,128]{2,1,0:T(8,128)S(1)}, f32[42,8,128]{2,1,0:T(8,128)S(1)}, u32[]{:S(2)}, u32[]{:S(2)}) collective-permute-start(f32[42,8,128]{2,1,0:T(8,128)S(1)} %get-tuple-element.71), channel_id=1, source_target_pairs={{4,8},{5,9},{6,10},{7,11},{8,4},{9,5},{10,6},{11,7},{12,16},{13,17... | collective-permute-start | bytes 516104 | tf_op jit(solution)/shard_map/ppermute | solution.py:840
  52.0 4.1 %collective-permute-start.12 = (f32[9,8,128]{2,1,0:T(8,128)S(1)}, f32[9,8,128]{2,1,0:T(8,128)S(1)}, u32[]{:S(2)}, u32[]{:S(2)}) collective-permute-start(f32[9,8,128]{2,1,0:T(8,128)S(1)} %get-tuple-element.83.refs_0_), channel_id=1, source_target_pairs={{0,3},{1,2},{2,1},{3,0},{4,7},{5,6},{6,5},{7,4},{8,11},{9,10},{10,... | collective-permute-start | bytes 110600 | tf_op jit(solution)/shard_map/ppermute | solution.py:840
  53.8 4.3 %collective-permute-start.11 = (f32[9,8,128]{2,1,0:T(8,128)S(1)}, f32[9,8,128]{2,1,0:T(8,128)S(1)}, u32[]{:S(2)}, u32[]{:S(2)}) collective-permute-start(f32[9,8,128]{2,1,0:T(8,128)S(1)} %get-tuple-element.83.refs_0_), channel_id=1, source_target_pairs={{0,2},{1,3},{2,0},{3,1},{4,6},{5,7},{6,4},{7,5},{8,10},{9,11},{10,... | collective-permute-start | bytes 110600 | tf_op jit(solution)/shard_map/ppermute | solution.py:840
  53.9 4.2 %collective-permute-start.10 = (f32[9,8,128]{2,1,0:T(8,128)S(1)}, f32[9,8,128]{2,1,0:T(8,128)S(1)}, u32[]{:S(2)}, u32[]{:S(2)}) collective-permute-start(f32[9,8,128]{2,1,0:T(8,128)S(1)} %get-tuple-element.83.refs_0_), channel_id=1, source_target_pairs={{0,1},{1,0},{2,3},{3,2},{4,5},{5,4},{6,7},{7,6},{8,9},{9,8},{10,11... | collective-permute-start | bytes 110600 | tf_op jit(solution)/shard_map/ppermute | solution.py:840
  58.2 7.1 %copy-start.4 = (s32[3,4]{1,0:T(4,128)S(1)}, s32[3,4]{1,0:T(4,128)}, u32[]{:S(2)}) copy-start(s32[3,4]{1,0:T(4,128)} %ghost.3) | copy-start | bytes 148
  58.2 8.5 %collective-permute-start.13 = (f32[18,8,128]{2,1,0:T(8,128)S(1)}, f32[18,8,128]{2,1,0:T(8,128)S(1)}, u32[]{:S(2)}, u32[]{:S(2)}) collective-permute-start(f32[18,8,128]{2,1,0:T(8,128)S(1)} %get-tuple-element.84), channel_id=1, source_target_pairs={{0,4},{1,5},{2,6},{3,7},{4,0},{5,1},{6,2},{7,3},{8,12},{9,13},{10,... | collective-permute-start | bytes 221192 | tf_op jit(solution)/shard_map/ppermute | solution.py:840
  58.3 9.1 %collective-permute-start.14 = (f32[18,8,128]{2,1,0:T(8,128)S(1)}, f32[18,8,128]{2,1,0:T(8,128)S(1)}, u32[]{:S(2)}, u32[]{:S(2)}) collective-permute-start(f32[18,8,128]{2,1,0:T(8,128)S(1)} %get-tuple-element.85), channel_id=1, source_target_pairs={{4,8},{5,9},{6,10},{7,11},{8,4},{9,5},{10,6},{11,7},{12,16},{13,17... | collective-permute-start | bytes 221192 | tf_op jit(solution)/shard_map/ppermute | solution.py:840
  69.8 3.9 %collective-permute-start.17 = (f32[32,128]{1,0:T(8,128)S(1)}, f32[32,128]{1,0:T(8,128)S(1)}, u32[]{:S(2)}, u32[]{:S(2)}) collective-permute-start(f32[32,128]{1,0:T(8,128)S(1)} %get-tuple-element.94.refs_0_), channel_id=1, source_target_pairs={{0,3},{1,2},{2,1},{3,0},{4,7},{5,6},{6,5},{7,4},{8,11},{9,10},{10,... | collective-permute-start | bytes 49160 | tf_op jit(solution)/shard_map/ppermute | solution.py:840
  70.9 4.1 %collective-permute-start.16 = (f32[32,128]{1,0:T(8,128)S(1)}, f32[32,128]{1,0:T(8,128)S(1)}, u32[]{:S(2)}, u32[]{:S(2)}) collective-permute-start(f32[32,128]{1,0:T(8,128)S(1)} %get-tuple-element.94.refs_0_), channel_id=1, source_target_pairs={{0,2},{1,3},{2,0},{3,1},{4,6},{5,7},{6,4},{7,5},{8,10},{9,11},{10,... | collective-permute-start | bytes 49160 | tf_op jit(solution)/shard_map/ppermute | solution.py:840
  72.1 3.0 %collective-permute-start.15 = (f32[32,128]{1,0:T(8,128)S(1)}, f32[32,128]{1,0:T(8,128)S(1)}, u32[]{:S(2)}, u32[]{:S(2)}) collective-permute-start(f32[32,128]{1,0:T(8,128)S(1)} %get-tuple-element.94.refs_0_), channel_id=1, source_target_pairs={{0,1},{1,0},{2,3},{3,2},{4,5},{5,4},{6,7},{7,6},{8,9},{9,8},{10,11... | collective-permute-start | bytes 49160 | tf_op jit(solution)/shard_map/ppermute | solution.py:840
  75.0 4.3 %collective-permute-start.20 = (f32[104,128]{1,0:T(8,128)S(1)}, f32[104,128]{1,0:T(8,128)S(1)}, u32[]{:S(2)}, u32[]{:S(2)}) collective-permute-start(f32[104,128]{1,0:T(8,128)S(1)} %shard_map.77.refs_0_), channel_id=1, source_target_pairs={{0,12},{1,13},{2,14},{3,15},{4,8},{5,9},{6,10},{7,11},{8,4},{9,5},... | collective-permute-start | bytes 159752 | tf_op jit(solution)/shard_map/ppermute | solution.py:840
  77.5 4.5 %collective-permute-start.19 = (f32[104,128]{1,0:T(8,128)S(1)}, f32[104,128]{1,0:T(8,128)S(1)}, u32[]{:S(2)}, u32[]{:S(2)}) collective-permute-start(f32[104,128]{1,0:T(8,128)S(1)} %shard_map.77.refs_0_), channel_id=1, source_target_pairs={{0,8},{1,9},{2,10},{3,11},{4,12},{5,13},{6,14},{7,15},{8,0},{9,1},... | collective-permute-start | bytes 159752 | tf_op jit(solution)/shard_map/ppermute | solution.py:840
  77.5 4.5 %collective-permute-start.18 = (f32[104,128]{1,0:T(8,128)S(1)}, f32[104,128]{1,0:T(8,128)S(1)}, u32[]{:S(2)}, u32[]{:S(2)}) collective-permute-start(f32[104,128]{1,0:T(8,128)S(1)} %shard_map.77.refs_0_), channel_id=1, source_target_pairs={{0,4},{1,5},{2,6},{3,7},{4,0},{5,1},{6,2},{7,3},{8,12},{9,13},{10,... | collective-permute-start | bytes 159752 | tf_op jit(solution)/shard_map/ppermute | solution.py:840
  82.0 8.1 %collective-permute-start.23 = (f32[400,128]{1,0:T(8,128)S(1)}, f32[400,128]{1,0:T(8,128)S(1)}, u32[]{:S(2)}, u32[]{:S(2)}) collective-permute-start(f32[400,128]{1,0:T(8,128)S(1)} %shard_map.78.refs_0_), channel_id=1, source_target_pairs={{0,96},{1,97},{2,98},{3,99},{4,100},{5,101},{6,102},{7,103},{8,104... | collective-permute-start | bytes 614408 | tf_op jit(solution)/shard_map/ppermute | solution.py:840
  83.2 6.9 %collective-permute-start.22 = (f32[400,128]{1,0:T(8,128)S(1)}, f32[400,128]{1,0:T(8,128)S(1)}, u32[]{:S(2)}, u32[]{:S(2)}) collective-permute-start(f32[400,128]{1,0:T(8,128)S(1)} %shard_map.78.refs_0_), channel_id=1, source_target_pairs={{0,64},{1,65},{2,66},{3,67},{4,68},{5,69},{6,70},{7,71},{8,72},{9,... | collective-permute-start | bytes 614408 | tf_op jit(solution)/shard_map/ppermute | solution.py:840
  85.0 6.0 %collective-permute-start.21 = (f32[400,128]{1,0:T(8,128)S(1)}, f32[400,128]{1,0:T(8,128)S(1)}, u32[]{:S(2)}, u32[]{:S(2)}) collective-permute-start(f32[400,128]{1,0:T(8,128)S(1)} %shard_map.78.refs_0_), channel_id=1, source_target_pairs={{0,32},{1,33},{2,34},{3,35},{4,36},{5,37},{6,38},{7,39},{8,40},{9,... | collective-permute-start | bytes 614408 | tf_op jit(solution)/shard_map/ppermute | solution.py:840
  91.1 7.6 %collective-permute-start.24 = (f32[1600,128]{1,0:T(8,128)S(1)}, f32[1600,128]{1,0:T(8,128)S(1)}, u32[]{:S(2)}, u32[]{:S(2)}) collective-permute-start(f32[1600,128]{1,0:T(8,128)S(1)} %shard_map.79.mine64), channel_id=1, source_target_pairs={{0,16},{1,17},{2,18},{3,19},{4,20},{5,21},{6,22},{7,23},{8,24},{9,... | collective-permute-start | bytes 2457608 | tf_op jit(solution)/shard_map/ppermute | solution.py:840
  111.9 4.1 %collective-permute-start.27 = (f32[9,8,128]{2,1,0:T(8,128)S(1)}, f32[9,8,128]{2,1,0:T(8,128)S(1)}, u32[]{:S(2)}, u32[]{:S(2)}) collective-permute-start(f32[9,8,128]{2,1,0:T(8,128)S(1)} %get-tuple-element.102.refs_0_), channel_id=1, source_target_pairs={{0,3},{1,2},{2,1},{3,0},{4,7},{5,6},{6,5},{7,4},{8,11},{9,10},{10,... | collective-permute-start | bytes 110600 | tf_op jit(solution)/shard_map/ppermute | solution.py:840
  113.6 4.3 %collective-permute-start.26 = (f32[9,8,128]{2,1,0:T(8,128)S(1)}, f32[9,8,128]{2,1,0:T(8,128)S(1)}, u32[]{:S(2)}, u32[]{:S(2)}) collective-permute-start(f32[9,8,128]{2,1,0:T(8,128)S(1)} %get-tuple-element.102.refs_0_), channel_id=1, source_target_pairs={{0,2},{1,3},{2,0},{3,1},{4,6},{5,7},{6,4},{7,5},{8,10},{9,11},{10,... | collective-permute-start | bytes 110600 | tf_op jit(solution)/shard_map/ppermute | solution.py:840
  114.7 3.3 %collective-permute-start.25 = (f32[9,8,128]{2,1,0:T(8,128)S(1)}, f32[9,8,128]{2,1,0:T(8,128)S(1)}, u32[]{:S(2)}, u32[]{:S(2)}) collective-permute-start(f32[9,8,128]{2,1,0:T(8,128)S(1)} %get-tuple-element.102.refs_0_), channel_id=1, source_target_pairs={{0,1},{1,0},{2,3},{3,2},{4,5},{5,4},{6,7},{7,6},{8,9},{9,8},{10,11... | collective-permute-start | bytes 110600 | tf_op jit(solution)/shard_map/ppermute | solution.py:840
  118.0 6.0 %collective-permute-start.28 = (f32[18,8,128]{2,1,0:T(8,128)S(1)}, f32[18,8,128]{2,1,0:T(8,128)S(1)}, u32[]{:S(2)}, u32[]{:S(2)}) collective-permute-start(f32[18,8,128]{2,1,0:T(8,128)S(1)} %get-tuple-element.103), channel_id=1, source_target_pairs={{0,4},{1,5},{2,6},{3,7},{4,0},{5,1},{6,2},{7,3},{8,12},{9,13},{10,... | collective-permute-start | bytes 221192 | tf_op jit(solution)/shard_map/ppermute | solution.py:840
  119.0 7.0 %collective-permute-start.29 = (f32[18,8,128]{2,1,0:T(8,128)S(1)}, f32[18,8,128]{2,1,0:T(8,128)S(1)}, u32[]{:S(2)}, u32[]{:S(2)}) collective-permute-start(f32[18,8,128]{2,1,0:T(8,128)S(1)} %get-tuple-element.104), channel_id=1, source_target_pairs={{4,8},{5,9},{6,10},{7,11},{8,4},{9,5},{10,6},{11,7},{12,16},{13,17... | collective-permute-start | bytes 221192 | tf_op jit(solution)/shard_map/ppermute | solution.py:840
  128.7 6.4 %collective-permute-start.32 = (f32[24,8,128]{2,1,0:T(8,128)S(1)}, f32[24,8,128]{2,1,0:T(8,128)S(1)}, u32[]{:S(2)}, u32[]{:S(2)}) collective-permute-start(f32[24,8,128]{2,1,0:T(8,128)S(1)} %get-tuple-element.108.refs_0_), channel_id=1, source_target_pairs={{0,3},{1,2},{2,1},{3,0},{4,7},{5,6},{6,5},{7,4},{8,11},{9,10},{10,... | collective-permute-start | bytes 294920 | tf_op jit(solution)/shard_map/ppermute | solution.py:840
  130.0 6.0 %collective-permute-start.31 = (f32[24,8,128]{2,1,0:T(8,128)S(1)}, f32[24,8,128]{2,1,0:T(8,128)S(1)}, u32[]{:S(2)}, u32[]{:S(2)}) collective-permute-start(f32[24,8,128]{2,1,0:T(8,128)S(1)} %get-tuple-element.108.refs_0_), channel_id=1, source_target_pairs={{0,2},{1,3},{2,0},{3,1},{4,6},{5,7},{6,4},{7,5},{8,10},{9,11},{10,... | collective-permute-start | bytes 294920 | tf_op jit(solution)/shard_map/ppermute | solution.py:840
  130.9 5.2 %collective-permute-start.30 = (f32[24,8,128]{2,1,0:T(8,128)S(1)}, f32[24,8,128]{2,1,0:T(8,128)S(1)}, u32[]{:S(2)}, u32[]{:S(2)}) collective-permute-start(f32[24,8,128]{2,1,0:T(8,128)S(1)} %get-tuple-element.108.refs_0_), channel_id=1, source_target_pairs={{0,1},{1,0},{2,3},{3,2},{4,5},{5,4},{6,7},{7,6},{8,9},{9,8},{10,11... | collective-permute-start | bytes 294920 | tf_op jit(solution)/shard_map/ppermute | solution.py:840
  136.2 6.3 %collective-permute-start.33 = (f32[42,8,128]{2,1,0:T(8,128)S(1)}, f32[42,8,128]{2,1,0:T(8,128)S(1)}, u32[]{:S(2)}, u32[]{:S(2)}) collective-permute-start(f32[42,8,128]{2,1,0:T(8,128)S(1)} %get-tuple-element.109), channel_id=1, source_target_pairs={{0,4},{1,5},{2,6},{3,7},{4,0},{5,1},{6,2},{7,3},{8,12},{9,13},{10,... | collective-permute-start | bytes 516104 | tf_op jit(solution)/shard_map/ppermute | solution.py:840
  136.3 10.4 %collective-permute-start.34 = (f32[42,8,128]{2,1,0:T(8,128)S(1)}, f32[42,8,128]{2,1,0:T(8,128)S(1)}, u32[]{:S(2)}, u32[]{:S(2)}) collective-permute-start(f32[42,8,128]{2,1,0:T(8,128)S(1)} %get-tuple-element.110), channel_id=1, source_target_pairs={{4,8},{5,9},{6,10},{7,11},{8,4},{9,5},{10,6},{11,7},{12,16},{13,17... | collective-permute-start | bytes 516104 | tf_op jit(solution)/shard_map/ppermute | solution.py:840
